TPU v7x, 32 devices: a whole 2x2x4 slice. The times are simulated.
32 devices in a mesh: dp: 8 (over y, x, core), seq: 4 (over z).
Axes of the slice: x: 2, y: 2, z: 4, core: 2. Of those that a mesh axis runs over, the one named last changes fastest.
Arguments:
- long_tokens: bfloat16 [8, 512, 512], P('dp', 'seq'), may hold values from -6 to 6
- short_tokens: bfloat16 [16, 256, 512], P('dp', 'seq'), may hold values from -6 to 6
- long_cot: bfloat16 [8, 512, 512], P('dp', 'seq'), may hold values from -6 to 6
- short_cot: bfloat16 [16, 256, 512], P('dp', 'seq'), may hold values from -6 to 6
- long_lengths: int32 [8], P('dp'), may hold values from 1 to 512, as said below
- short_lengths: int32 [16], P('dp'), may hold values from 1 to 256, as said below
- w_query: bfloat16 [512, 512], P(('dp', 'seq')), may hold values from -0.375 to 0.375
- w_key: bfloat16 [512, 512], P(('dp', 'seq')), may hold values from -0.25 to 0.25
- w_value: bfloat16 [512, 512], P(('dp', 'seq')), may hold values from -0.25 to 0.25
- w_out: bfloat16 [512, 512], P(('dp', 'seq')), may hold values from -2 to 2
- w_up: bfloat16 [512, 2048], P(('dp', 'seq')), may hold values from -0.25 to 0.25
- w_down: bfloat16 [2048, 512], P(None, ('dp', 'seq')), may hold values from -0.125 to 0.125
- pos_table: bfloat16 [512, 512], P(None, ('dp', 'seq')), may hold values from -3 to 3
- norm_gain: bfloat16 [2, 512], P(None, ('dp', 'seq')), may hold values from 0.5 to 1.5
- norm_bias: bfloat16 [2, 512], P(None, ('dp', 'seq')), may hold values from -1.5 to 1.5
Outputs:
- long_out: bfloat16 [8, 512, 512], P('dp', 'seq')
- short_out: bfloat16 [16, 256, 512], P('dp', 'seq')
- long_grad: bfloat16 [8, 512, 512], P('dp', 'seq')
- short_grad: bfloat16 [16, 256, 512], P('dp', 'seq')
- grad_query: float32 [512, 512], P(('dp', 'seq'))
- grad_key: float32 [512, 512], P(('dp', 'seq'))
- grad_value: float32 [512, 512], P(('dp', 'seq'))
- grad_out: float32 [512, 512], P(('dp', 'seq'))
- grad_up: float32 [512, 2048], P(('dp', 'seq'))
- grad_down: float32 [2048, 512], P(None, ('dp', 'seq'))
- grad_pos: float32 [512, 512], P(None, ('dp', 'seq'))
- grad_gain: float32 [2, 512], P(None, ('dp', 'seq'))
- grad_bias: float32 [2, 512], P(None, ('dp', 'seq'))
Inputs may be any that keep to these rules, and one draw needn't show every extreme that they name: `long_lengths`: characters at or after a window's length are padding: no query attends to them. Some long window has length exactly 512. `short_lengths`: characters at or after a window's length are padding: no query attends to them. Some short window has length exactly 256.
All inputs are finite; a program needn't handle non-finite values.
Results may differ from a plain program's by a relative error of at most 0.014.
The roundings to bfloat16 on the way count: a program that leaves them out, or rounds other values in their place, can miss the bound.
Values may be sent and summed in bfloat16 or wider, within the bound.
No kernel may reach another device: no remote copies, remote signals or barrier semaphores. Data moves between devices by JAX's collectives and lax.ppermute only.
A program may use at most 128 MiB of HBM per device.

v0:
```python
import math

import jax
import jax.numpy as jnp
from jax import lax
from jax.sharding import PartitionSpec as P

HEAD_DIM = 64


def layer_norm(values, gain, bias):
    row_mean = jnp.mean(values, axis=-1, keepdims=True)
    centred = values - row_mean
    variance = jnp.mean(centred * centred, axis=-1, keepdims=True)
    return centred * lax.rsqrt(variance + 1e-05) * gain + bias


def exact_gelu(values):
    return jax.nn.gelu(values, approximate=False)


def rows_product(left, right):
    return lax.dot_general(
        left, right, (((0,), (0,)), ((), ())), preferred_element_type=jnp.float32
    )


def back_product(grad_rows, weight):
    return lax.dot_general(
        grad_rows, weight, (((1,), (1,)), ((), ())), preferred_element_type=jnp.float32
    )


def block_split(heads, lengths):
    windows, window_len, _, head_width = heads.shape
    per_block = math.gcd(windows, max(1, 512 // window_len))
    shaped = heads.reshape(
        windows // per_block, per_block, window_len, 3, head_width // HEAD_DIM, HEAD_DIM
    )
    return (shaped, lengths.reshape(windows // per_block, per_block), per_block)


def window_scores(queries, key_rows, lengths):
    window_len = queries.shape[1]
    scores = jnp.einsum(
        "bqhd,bkhd->bhqk", queries, key_rows, preferred_element_type=jnp.float32
    ) * HEAD_DIM ** (-0.5)
    row_ids = jnp.arange(window_len)[:, None]
    col_ids = jnp.arange(window_len)[None, :]
    allowed = (col_ids <= row_ids)[None, None] & (
        col_ids[None, None] < lengths[:, None, None, None]
    )
    return jnp.where(allowed, scores, -1e30)


def attend(heads, lengths):
    shaped, len_blocks, per_block = block_split(heads, lengths)

    def one_block(block_args):
        block, len_block = block_args
        queries, key_rows, values = (block[:, :, 0], block[:, :, 1], block[:, :, 2])
        scores = window_scores(queries, key_rows, len_block)
        row_max = jnp.max(scores, axis=-1, keepdims=True)
        shifted = jnp.exp(scores - row_max)
        row_total = jnp.sum(shifted, axis=-1, keepdims=True)
        attn_weights = shifted / row_total
        mixed = jnp.einsum(
            "bhqk,bkhd->bqhd",
            attn_weights.astype(jnp.bfloat16),
            values,
            preferred_element_type=jnp.float32,
        )
        return (mixed.astype(jnp.bfloat16), (row_max + jnp.log(row_total))[..., 0])

    mixed, log_total = lax.map(one_block, (shaped, len_blocks))
    windows, window_len, _, head_width = heads.shape
    return (mixed.reshape(windows, window_len, head_width), log_total)


def attend_back(heads, log_total, grad_mixed, lengths):
    shaped, len_blocks, per_block = block_split(heads, lengths)
    windows, window_len, _, head_width = heads.shape
    grad_blocks = grad_mixed.reshape(
        windows // per_block, per_block, window_len, head_width // HEAD_DIM, HEAD_DIM
    )
    scale = HEAD_DIM ** (-0.5)

    def one_block(block_args):
        block, log_block, grad_block, len_block = block_args
        queries, key_rows, values = (block[:, :, 0], block[:, :, 1], block[:, :, 2])
        scores = window_scores(queries, key_rows, len_block)
        attn_weights = jnp.exp(scores - log_block[..., None])
        grad_values = jnp.einsum(
            "bhqk,bqhd->bkhd",
            attn_weights.astype(jnp.bfloat16),
            grad_block,
            preferred_element_type=jnp.float32,
        )
        grad_probs = jnp.einsum(
            "bqhd,bkhd->bhqk", grad_block, values, preferred_element_type=jnp.float32
        )
        row_inner = jnp.sum(attn_weights * grad_probs, axis=-1, keepdims=True)
        grad_scores = (attn_weights * (grad_probs - row_inner)).astype(jnp.bfloat16)
        grad_queries = (
            jnp.einsum("bhqk,bkhd->bqhd", grad_scores, key_rows, preferred_element_type=jnp.float32)
            * scale
        )
        grad_keys = (
            jnp.einsum("bhqk,bqhd->bkhd", grad_scores, queries, preferred_element_type=jnp.float32)
            * scale
        )
        return jnp.stack([grad_queries, grad_keys, grad_values], 2).astype(jnp.bfloat16)

    joined = lax.map(one_block, (shaped, log_total, grad_blocks, len_blocks))
    return joined.reshape(windows, window_len, 3, head_width)


def local(
    long_tokens,
    short_tokens,
    long_cot,
    short_cot,
    long_lengths,
    short_lengths,
    w_query,
    w_key,
    w_value,
    w_out,
    w_up,
    w_down,
    pos_table,
    norm_gain,
    norm_bias,
):
    seq_place = lax.axis_index("seq")
    model_width = w_key.shape[1]
    rows_full = (
        lax.all_gather(w_query, ("dp", "seq"), axis=0, tiled=True),
        lax.all_gather(w_key, ("dp", "seq"), axis=0, tiled=True),
        lax.all_gather(w_value, ("dp", "seq"), axis=0, tiled=True),
        lax.all_gather(w_out, ("dp", "seq"), axis=0, tiled=True),
        lax.all_gather(w_up, ("dp", "seq"), axis=0, tiled=True),
    )
    cols_full = (
        lax.all_gather(w_down, ("dp", "seq"), axis=1, tiled=True),
        lax.all_gather(pos_table, ("dp", "seq"), axis=1, tiled=True),
        lax.all_gather(norm_gain, ("dp", "seq"), axis=1, tiled=True),
        lax.all_gather(norm_bias, ("dp", "seq"), axis=1, tiled=True),
    )
    joint_weight = jnp.concatenate(rows_full[:3], axis=1)
    long_start = seq_place * long_tokens.shape[1]
    short_start = seq_place * short_tokens.shape[1]

    def enter(tokens, start):
        windows, local_len, _ = tokens.shape
        pos_rows = lax.dynamic_slice_in_dim(cols_full[1], start, local_len, 0)
        first = tokens.astype(jnp.float32) + pos_rows[None].astype(jnp.float32)
        first_low = first.astype(jnp.bfloat16)
        joined = jnp.dot(
            first_low.reshape(-1, model_width), joint_weight, preferred_element_type=jnp.float32
        )
        return (
            first,
            first_low,
            joined.astype(jnp.bfloat16).reshape(windows, local_len, 3, model_width),
        )

    long_first, long_low, long_joint = enter(long_tokens, long_start)
    short_first, short_low, short_joint = enter(short_tokens, short_start)
    long_heads, short_heads = (
        lax.all_to_all(long_joint, "seq", split_axis=3, concat_axis=1, tiled=True),
        lax.all_to_all(short_joint, "seq", split_axis=3, concat_axis=1, tiled=True),
    )
    long_mixed, long_log = attend(long_heads, long_lengths)
    short_mixed, short_log = attend(short_heads, short_lengths)
    long_blocks, short_blocks = (
        lax.all_to_all(long_mixed, "seq", split_axis=1, concat_axis=2, tiled=True),
        lax.all_to_all(short_mixed, "seq", split_axis=1, concat_axis=2, tiled=True),
    )
    gains = cols_full[2].astype(jnp.float32)
    biases = cols_full[3].astype(jnp.float32)

    def finish(first, blocks):
        first_sum = first.reshape(-1, model_width) + jnp.dot(
            blocks.reshape(-1, model_width), rows_full[3], preferred_element_type=jnp.float32
        )
        normed = layer_norm(first_sum, gains[0], biases[0])
        normed_low = normed.astype(jnp.bfloat16)
        hidden = jnp.dot(normed_low, rows_full[4], preferred_element_type=jnp.float32)
        act_low = exact_gelu(hidden).astype(jnp.bfloat16)
        second = normed + jnp.dot(act_low, cols_full[0], preferred_element_type=jnp.float32)
        result = layer_norm(second, gains[1], biases[1]).astype(jnp.bfloat16).reshape(first.shape)
        return (result, (first_sum, normed_low, hidden, act_low, second))

    long_out, long_kept = finish(long_first, long_blocks)
    short_out, short_kept = finish(short_first, short_blocks)
    rows_back = (
        lax.all_gather(w_query, ("dp", "seq"), axis=0, tiled=True),
        lax.all_gather(w_key, ("dp", "seq"), axis=0, tiled=True),
        lax.all_gather(w_value, ("dp", "seq"), axis=0, tiled=True),
        lax.all_gather(w_out, ("dp", "seq"), axis=0, tiled=True),
        lax.all_gather(w_up, ("dp", "seq"), axis=0, tiled=True),
    )
    cols_back = (
        lax.all_gather(w_down, ("dp", "seq"), axis=1, tiled=True),
        lax.all_gather(pos_table, ("dp", "seq"), axis=1, tiled=True),
        lax.all_gather(norm_gain, ("dp", "seq"), axis=1, tiled=True),
        lax.all_gather(norm_bias, ("dp", "seq"), axis=1, tiled=True),
    )
    joint_back = jnp.concatenate(rows_back[:3], axis=1)
    gains_back = cols_back[2].astype(jnp.float32)
    biases_back = cols_back[3].astype(jnp.float32)

    def tail_back(cotangent, kept, blocks):
        first_sum, normed_low, hidden, act_low, second = kept
        grad_result = cotangent.reshape(-1, model_width).astype(jnp.float32)
        grad_second, gain_two, bias_two = jax.vjp(
            layer_norm, second, gains_back[1], biases_back[1]
        )[1](grad_result)
        second_low = grad_second.astype(jnp.bfloat16)
        grad_down = rows_product(act_low, second_low)
        grad_act = back_product(second_low, cols_back[0])
        grad_hidden = jax.vjp(exact_gelu, hidden)[1](grad_act)[0]
        hidden_low = grad_hidden.astype(jnp.bfloat16)
        grad_up = rows_product(normed_low, hidden_low)
        grad_normed = grad_second + back_product(hidden_low, rows_back[4])
        grad_sum, gain_one, bias_one = jax.vjp(
            layer_norm, first_sum, gains_back[0], biases_back[0]
        )[1](grad_normed)
        sum_low = grad_sum.astype(jnp.bfloat16)
        grad_outw = rows_product(blocks.reshape(-1, model_width), sum_low)
        grad_blocks = back_product(sum_low, rows_back[3]).astype(jnp.bfloat16).reshape(blocks.shape)
        weight_terms = (
            grad_outw,
            grad_up,
            grad_down,
            jnp.stack([gain_one, gain_two]),
            jnp.stack([bias_one, bias_two]),
        )
        return (grad_sum, grad_blocks, weight_terms)

    long_sum, long_gblocks, long_terms = tail_back(long_cot, long_kept, long_blocks)
    short_sum, short_gblocks, short_terms = tail_back(short_cot, short_kept, short_blocks)
    long_gheads, short_gheads = (
        lax.all_to_all(long_gblocks, "seq", split_axis=2, concat_axis=1, tiled=True),
        lax.all_to_all(short_gblocks, "seq", split_axis=2, concat_axis=1, tiled=True),
    )
    long_gjoint = attend_back(long_heads, long_log, long_gheads, long_lengths)
    short_gjoint = attend_back(short_heads, short_log, short_gheads, short_lengths)
    long_gback, short_gback = (
        lax.all_to_all(long_gjoint, "seq", split_axis=1, concat_axis=3, tiled=True),
        lax.all_to_all(short_gjoint, "seq", split_axis=1, concat_axis=3, tiled=True),
    )

    def leave(first_low, grad_sum, grad_joint):
        flat_joint = grad_joint.reshape(-1, 3 * model_width)
        grad_weight = rows_product(first_low.reshape(-1, model_width), flat_joint)
        grad_first = grad_sum + back_product(flat_joint, joint_back)
        return (grad_first.reshape(first_low.shape), grad_weight)

    long_gfirst, long_gweight = leave(long_low, long_sum, long_gback)
    short_gfirst, short_gweight = leave(short_low, short_sum, short_gback)
    joint_grad = long_gweight + short_gweight
    table_zeros = jnp.zeros((cols_full[1].shape[0], model_width), jnp.float32)
    pos_term = lax.dynamic_update_slice(
        table_zeros, jnp.sum(long_gfirst, axis=0), (long_start, seq_place * 0)
    )
    pos_term = pos_term + lax.dynamic_update_slice(
        table_zeros, jnp.sum(short_gfirst, axis=0), (short_start, seq_place * 0)
    )
    grad_query, grad_key, grad_value, grad_out, grad_up = (
        lax.psum_scatter(
            joint_grad[:, :model_width], ("dp", "seq"), scatter_dimension=0, tiled=True
        ),
        lax.psum_scatter(
            joint_grad[:, model_width : 2 * model_width],
            ("dp", "seq"),
            scatter_dimension=0,
            tiled=True,
        ),
        lax.psum_scatter(
            joint_grad[:, 2 * model_width :], ("dp", "seq"), scatter_dimension=0, tiled=True
        ),
        lax.psum_scatter(
            long_terms[0] + short_terms[0], ("dp", "seq"), scatter_dimension=0, tiled=True
        ),
        lax.psum_scatter(
            long_terms[1] + short_terms[1], ("dp", "seq"), scatter_dimension=0, tiled=True
        ),
    )
    grad_down, grad_pos, grad_gain, grad_bias = (
        lax.psum_scatter(
            long_terms[2] + short_terms[2], ("dp", "seq"), scatter_dimension=1, tiled=True
        ),
        lax.psum_scatter(pos_term, ("dp", "seq"), scatter_dimension=1, tiled=True),
        lax.psum_scatter(
            long_terms[3] + short_terms[3], ("dp", "seq"), scatter_dimension=1, tiled=True
        ),
        lax.psum_scatter(
            long_terms[4] + short_terms[4], ("dp", "seq"), scatter_dimension=1, tiled=True
        ),
    )
    long_grad = long_gfirst.astype(jnp.bfloat16)
    short_grad = short_gfirst.astype(jnp.bfloat16)
    return (
        long_out,
        short_out,
        long_grad,
        short_grad,
        grad_query,
        grad_key,
        grad_value,
        grad_out,
        grad_up,
        grad_down,
        grad_pos,
        grad_gain,
        grad_bias,
    )


def solution(mesh):
    return jax.shard_map(
        local,
        mesh=mesh,
        in_specs=(
            P("dp", "seq", None),
            P("dp", "seq", None),
            P("dp", "seq", None),
            P("dp", "seq", None),
            P("dp"),
            P("dp"),
            P(("dp", "seq"), None),
            P(("dp", "seq"), None),
            P(("dp", "seq"), None),
            P(("dp", "seq"), None),
            P(("dp", "seq"), None),
            P(None, ("dp", "seq")),
            P(None, ("dp", "seq")),
            P(None, ("dp", "seq")),
            P(None, ("dp", "seq")),
        ),
        out_specs=(
            P("dp", "seq", None),
            P("dp", "seq", None),
            P("dp", "seq", None),
            P("dp", "seq", None),
            P(("dp", "seq"), None),
            P(("dp", "seq"), None),
            P(("dp", "seq"), None),
            P(("dp", "seq"), None),
            P(("dp", "seq"), None),
            P(None, ("dp", "seq")),
            P(None, ("dp", "seq")),
            P(None, ("dp", "seq")),
            P(None, ("dp", "seq")),
        ),
        check_vma=False,
    )
```

profile of v0, /device:TPU:0, one launch (start us, length us, event | category | flops | bytes accessed | tf_op | source)
XLA Modules:
  0.0 1811.5 jit_solution(15583290334554209147)
XLA Ops:
  7.9 74.7 %all_gather.34 = bf16[512,512]{0,1:T(8,128)(2,1)S(1)} all-gather(bf16[512,16]{0,1:T(8,128)(2,1)} %param.27), channel_id=1, replica_groups=mesh['dp'=8,'seq'=4] {'dp','seq'}, dimensions={1}, use_global_device_ids=true | all-gather | bytes 540672 | tf_op jit(solution)/shard_map/all_gather | solution.py:146
  82.8 68.1 %all_gather.35 = bf16[512,512]{1,0:T(8,128)(2,1)S(1)} all-gather(bf16[16,512]{1,0:T(8,128)(2,1)} %param.21), channel_id=1, replica_groups=mesh['dp'=8,'seq'=4] {'dp','seq'}, dimensions={0}, use_global_device_ids=true | all-gather | bytes 540672 | tf_op jit(solution)/shard_map/all_gather | solution.py:138
  151.0 69.4 %all_gather.36 = bf16[512,512]{1,0:T(8,128)(2,1)S(1)} all-gather(bf16[16,512]{1,0:T(8,128)(2,1)S(1)} %copy-done.49), channel_id=1, replica_groups=mesh['dp'=8,'seq'=4] {'dp','seq'}, dimensions={0}, use_global_device_ids=true | all-gather | bytes 540672 | tf_op jit(solution)/shard_map/all_gather | solution.py:139
  220.5 67.9 %all_gather.37 = bf16[512,512]{1,0:T(8,128)(2,1)S(1)} all-gather(bf16[16,512]{1,0:T(8,128)(2,1)S(1)} %copy-done.50), channel_id=1, replica_groups=mesh['dp'=8,'seq'=4] {'dp','seq'}, dimensions={0}, use_global_device_ids=true | all-gather | bytes 540672 | tf_op jit(solution)/shard_map/all_gather | solution.py:140
  295.1 65.4 %all-gather = bf16[32,16,2]{1,2,0:T(2,128)(2,1)S(1)} all-gather(bf16[1,16,2]{1,2,0:T(2,128)(2,1)S(1)} %bitcast.320), channel_id=1, replica_groups=mesh['dp'=8,'seq'=4] {'dp','seq'}, dimensions={0}, use_global_device_ids=true | all-gather | bytes 2112 | tf_op jit(solution)/shard_map/all_gather | solution.py:147
  361.4 63.0 %all-gather.1 = bf16[32,16,2]{1,2,0:T(2,128)(2,1)S(1)} all-gather(bf16[1,16,2]{1,2,0:T(2,128)(2,1)S(1)} %bitcast.321), channel_id=1, replica_groups=mesh['dp'=8,'seq'=4] {'dp','seq'}, dimensions={0}, use_global_device_ids=true | all-gather | bytes 2112 | tf_op jit(solution)/shard_map/all_gather | solution.py:148
  431.4 74.8 %all_gather.38 = bf16[512,512]{1,0:T(8,128)(2,1)} all-gather(bf16[16,512]{1,0:T(8,128)(2,1)S(1)} %copy-done.51), channel_id=1, replica_groups=mesh['dp'=8,'seq'=4] {'dp','seq'}, dimensions={0}, use_global_device_ids=true | all-gather | bytes 540672 | tf_op jit(solution)/shard_map/all_gather | solution.py:141
  506.3 4.1 all-to-all-start.2
  532.5 5.1 all-to-all-start.3
  549.1 5.6 multiply_convert_fusion.3
  580.2 4.0 all-to-all-start.6
  600.8 5.0 all-to-all-start.4
  616.3 5.1 all-to-all-start.7
  634.7 5.1 all-to-all-start.5
  643.3 7.1 all-to-all-done.5
  672.0 30.5 %reduce-scatter.30.cloned.1.call-done = f32[16,2]{1,0:T(8,128)} async-done(((f32[512,2]{1,0:T(8,128)}), f32[16,2]{1,0:T(8,128)}) %reduce-scatter.30.cloned.1.call-update) | async-done | bytes 144
  703.8 131.0 %reduce-scatter.32.cloned.1.call-done = f32[16,2]{1,0:T(8,128)} async-done(((f32[512,2]{1,0:T(8,128)}), f32[16,2]{1,0:T(8,128)}) %reduce-scatter.32.cloned.1.call-update) | async-done | bytes 144
  836.2 133.4 %reduce-scatter.22.cloned.1.call-done = f32[16,512]{1,0:T(8,128)} async-done(((f32[512,512]{1,0:T(8,128)}), f32[16,512]{1,0:T(8,128)}) %reduce-scatter.22.cloned.1.call-update) | async-done | bytes 32784 | tf_op jit(solution)/shard_map/reduce_scatter | solution.py:284
  969.6 134.8 %reduce-scatter.28.cloned.1.call-done = f32[16,512]{1,0:T(8,128)} async-done(((f32[512,512]{1,0:T(8,128)}), f32[16,512]{1,0:T(8,128)}) %reduce-scatter.28.cloned.1.call-update) | async-done | bytes 32784
  1104.4 134.7 %reduce-scatter.16.cloned.1.call-done = f32[16,512]{1,0:T(8,128)} async-done(((f32[512,512]{1,0:T(8,128)}), f32[16,512]{1,0:T(8,128)}) %reduce-scatter.16.cloned.1.call-update) | async-done | bytes 32784 | tf_op jit(solution)/shard_map/reduce_scatter | solution.py:272
  1239.1 134.9 %reduce-scatter.18.cloned.1.call-done = f32[16,512]{1,0:T(8,128)} async-done(((f32[512,512]{1,0:T(8,128)}), f32[16,512]{1,0:T(8,128)}) %reduce-scatter.18.cloned.1.call-update) | async-done | bytes 32784 | tf_op jit(solution)/shard_map/reduce_scatter | solution.py:275
  1374.0 134.7 %reduce-scatter.20.cloned.1.call-done = f32[16,512]{1,0:T(8,128)} async-done(((f32[512,512]{1,0:T(8,128)}), f32[16,512]{1,0:T(8,128)}) %reduce-scatter.20.cloned.1.call-update) | async-done | bytes 32784 | tf_op jit(solution)/shard_map/reduce_scatter | solution.py:281
  1508.8 147.2 %reduce-scatter.26.cloned.1.call-done = f32[2048,16]{0,1:T(8,128)} async-done(((f32[2048,512]{0,1:T(8,128)}), f32[2048,16]{0,1:T(8,128)}) %reduce-scatter.26.cloned.1.call-update) | async-done | bytes 131088 | tf_op jit(solution)/shard_map/reduce_scatter | solution.py:292
  1655.9 149.1 %reduce-scatter.24.cloned.1.call-done = f32[16,2048]{1,0:T(8,128)} async-done(((f32[512,2048]{1,0:T(8,128)}), f32[16,2048]{1,0:T(8,128)}) %reduce-scatter.24.cloned.1.call-update) | async-done | bytes 131088 | tf_op jit(solution)/shard_map/reduce_scatter | solution.py:287
  (333 shorter events, 141.0 us)
Async XLA Ops:
  7.2 143.8 %copy-start.49 = (bf16[16,512]{1,0:T(8,128)(2,1)S(1)}, bf16[16,512]{1,0:T(8,128)(2,1)}, u32[]{:S(2)}) copy-start(bf16[16,512]{1,0:T(8,128)(2,1)} %param.22) | copy-start | bytes 49156
  7.2 541.9 %all-gather.5.cloned.1.call-start = ((), (), s32[]{:S(2)}) async-start(), calls=%async_computation.17 | async-start | bytes 2162688 | tf_op jit(solution)/shard_map/all_gather | solution.py:142
  7.9 212.5 %copy-start.50 = (bf16[16,512]{1,0:T(8,128)(2,1)S(1)}, bf16[16,512]{1,0:T(8,128)(2,1)}, u32[]{:S(2)}) copy-start(bf16[16,512]{1,0:T(8,128)(2,1)} %param.23) | copy-start | bytes 49156
  150.9 137.5 %copy-start.35 = (bf16[1,128,512]{2,1,0:T(8,128)(2,1)S(1)}, bf16[1,128,512]{2,1,0:T(8,128)(2,1)}, u32[]{:S(2)}) copy-start(bf16[1,128,512]{2,1,0:T(8,128)(2,1)} %param.15) | copy-start | bytes 393220
  288.4 137.9 %copy-start = (bf16[512,1536]{1,0:T(8,128)(2,1)}, bf16[512,1536]{1,0:T(8,128)(2,1)S(1)}, u32[]{:S(2)}) copy-start(bf16[512,1536]{1,0:T(8,128)(2,1)S(1)} %constant_dynamic-update-slice_fusion) | copy-start | bytes 4718596
  288.8 136.7 %copy-start.43 = (bf16[2,64,512]{2,1,0:T(8,128)(2,1)S(1)}, bf16[2,64,512]{2,1,0:T(8,128)(2,1)}, u32[]{:S(2)}) copy-start(bf16[2,64,512]{2,1,0:T(8,128)(2,1)} %param.16) | copy-start | bytes 393220
  290.2 216.0 %all-to-all-start = ((bf16[1,128,3,512]{1,2,0,3:T(4,128)(2,1)}), bf16[1,128,3,512]{1,2,0,3:T(4,128)(2,1)S(1)}, u32[]{:S(2)}, u32[]{:S(2)}) async-start(bf16[1,128,3,512]{1,2,0,3:T(4,128)(2,1)} %copy.242), calls=%async_computation | async-start | bytes 1048576 | tf_op jit(solution)/shard_map/all_to_all | solution.py:171
  293.7 261.0 %all-gather.7.cloned.1.call-start = ((), (), s32[]{:S(2)}) async-start(), calls=%async_computation.18 | async-start | bytes 2162688 | tf_op jit(solution)/shard_map/all_gather | solution.py:145
  506.3 13.1 all-to-all-start.2
  519.3 13.1 all-to-all-start.1
  532.5 11.1 all-to-all-start.3
  537.6 164.9 %reduce-scatter.30.cloned.1.call-start = ((), (), s32[]{:S(2)}) async-start(), calls=%async_computation.26 | async-start | bytes 270336
  580.2 20.6 %all-to-all-start.6 = ((bf16[4,2,8192]{2,1,0:T(2,128)(2,1)}), bf16[4,2,8192]{2,1,0:T(2,128)(2,1)}, u32[]{:S(2)}, u32[]{:S(2)}) async-start(bf16[4,2,8192]{2,1,0:T(2,128)(2,1)} %reshape.573), calls=%async_computation.6 | async-start | bytes 262144 | tf_op jit(solution)/shard_map/all_to_all | solution.py:246
  584.2 250.7 %reduce-scatter.32.cloned.1.call-start = ((), (), s32[]{:S(2)}) async-start(), calls=%async_computation.27 | async-start | bytes 270336
  592.0 377.6 %reduce-scatter.22.cloned.1.call-start = ((), (), s32[]{:S(2)}) async-start(), calls=%async_computation.22 | async-start | bytes 1081344 | tf_op jit(solution)/shard_map/reduce_scatter | solution.py:284
  600.8 15.5 all-to-all-start.4
  616.3 18.4 %all-to-all-start.7 = ((bf16[2,256,3,128]{3,0,2,1:T(2,128)(2,1)}), bf16[2,256,3,128]{3,0,2,1:T(2,128)(2,1)}, u32[]{:S(2)}, u32[]{:S(2)}) async-start(bf16[2,256,3,128]{3,0,2,1:T(2,128)(2,1)} %pad_maximum_fusion.1), calls=%async_computation.7 | async-start | bytes 786432 | tf_op jit(solution)/shard_map/all_to_all | solution.py:252
  634.7 15.7 all-to-all-start.5
  639.8 464.6 %reduce-scatter.28.cloned.1.call-start = ((), (), s32[]{:S(2)}) async-start(), calls=%async_computation.25 | async-start | bytes 1081344
  658.3 580.8 %reduce-scatter.16.cloned.1.call-start = ((), (), s32[]{:S(2)}) async-start(), calls=%async_computation.19 | async-start | bytes 1081344 | tf_op jit(solution)/shard_map/reduce_scatter | solution.py:272
  661.8 712.2 %reduce-scatter.18.cloned.1.call-start = ((), (), s32[]{:S(2)}) async-start(), calls=%async_computation.20 | async-start | bytes 1081344 | tf_op jit(solution)/shard_map/reduce_scatter | solution.py:275
  662.6 846.2 %reduce-scatter.20.cloned.1.call-start = ((), (), s32[]{:S(2)}) async-start(), calls=%async_computation.21 | async-start | bytes 1081344 | tf_op jit(solution)/shard_map/reduce_scatter | solution.py:281
  663.3 992.6 %reduce-scatter.26.cloned.1.call-start = ((), (), s32[]{:S(2)}) async-start(), calls=%async_computation.24 | async-start | bytes 4325376 | tf_op jit(solution)/shard_map/reduce_scatter | solution.py:292
  667.4 1137.6 %reduce-scatter.24.cloned.1.call-start = ((), (), s32[]{:S(2)}) async-start(), calls=%async_computation.23 | async-start | bytes 4325376 | tf_op jit(solution)/shard_map/reduce_scatter | solution.py:287
  (73 other events, 258.7 us)
Sparse Core Ops, SparseCore 0:
  11.0 59.7 all-gather.4
  297.5 56.5 all-gather.6
  570.1 132.3 reduce-scatter.29
  704.7 130.1 reduce-scatter.31
  837.5 132.0 reduce-scatter.21
  972.4 131.9 reduce-scatter.27
  1107.2 131.8 reduce-scatter.15
  1242.0 131.9 reduce-scatter.17
  1376.8 131.8 reduce-scatter.19
  1511.6 144.3 reduce-scatter.25
  1658.9 146.0 reduce-scatter.23
where the time goes:
time: 1810 us
  waiting for transfers between devices  1150 us (64%)
  blocking collectives  483 us (27%)
  local copies, waits for them, and re-layouts  55 us (3%)
  matrix products  52.2 us (3%)
  starting transfers between devices  36 us (2%)
  other arithmetic  22.8 us (1%)
    unnamed x14, waiting for transfers between devices  299 us
    reduce_scatter x1, waiting for transfers between devices, local(): lax.psum_scatter(long_terms[1] + short_terms[1], ('dp', 'seq'), scatter_d...  149 us
    reduce_scatter x1, waiting for transfers between devices, local(): lax.psum_scatter(long_terms[2] + short_terms[2], ('dp', 'seq'), scatter_d...  147 us
    reduce_scatter x1, waiting for transfers between devices, local(): lax.psum_scatter(joint_grad[:, model_width:2 * model_width], ('dp', 'seq'...  135 us
    reduce_scatter x1, waiting for transfers between devices, local(): lax.psum_scatter(joint_grad[:, 2 * model_width:], ('dp', 'seq'), scatter_...  135 us
    reduce_scatter x1, waiting for transfers between devices, local(): lax.psum_scatter(joint_grad[:, :model_width], ('dp', 'seq'), scatter_dime...  135 us
    reduce_scatter x1, waiting for transfers between devices, local(): lax.psum_scatter(long_terms[0] + short_terms[0], ('dp', 'seq'), scatter_d...  133 us
    all_gather x1, blocking collectives, local(): lax.all_gather(w_out, ('dp', 'seq'), axis=0, tiled=True)  74.8 us
  transfers between devices with their start and end apart: 19, of which 12 were waited for; matrix products, arithmetic and copies ran while one was open for 6% of the time, Pallas kernels for 0%

commit v1 on v0

v1 whole, which is shorter than its diff:
```python
import functools
import math

import jax
import jax.numpy as jnp
from jax import lax
from jax.experimental import pallas as pl
from jax.experimental.pallas import tpu as pltpu
from jax.sharding import PartitionSpec as P

HEAD_DIM = 64
LANES = 128
BAND = 16
BF = jnp.bfloat16
F32 = jnp.float32
VMEM = pl.BlockSpec(memory_space=pltpu.VMEM)
SMEM = pl.BlockSpec(memory_space=pltpu.SMEM)
ANY = pl.BlockSpec(memory_space=pl.ANY)
NN = (((1,), (0,)), ((), ()))
NT = (((1,), (1,)), ((), ()))
TN = (((0,), (0,)), ((), ()))


def mm(left, right, dims=NN):
    return lax.dot_general(left, right, dims, preferred_element_type=F32)


def call(body, outs, ins, scratch, flops, moved, name):
    return pl.pallas_call(
        body,
        out_shape=[jax.ShapeDtypeStruct(shape, dtype) for shape, dtype, _ in outs],
        out_specs=[spec for _, _, spec in outs],
        in_specs=ins,
        scratch_shapes=scratch,
        compiler_params=pltpu.CompilerParams(vmem_limit_bytes=50 * 1024 * 1024),
        cost_estimate=pl.CostEstimate(flops=flops, bytes_accessed=moved, transcendentals=0),
        name=name,
    )


def slot_device(slot, slots, me):
    half = slots // 2
    core, rest = divmod(slot, half)
    layer, place = divmod(rest, 4)
    return lax.bitwise_xor(jnp.int32((layer * 2 + core) * 4 + place), me)


def fetch_weights(near, far, weights, sem, me):
    half = near.shape[0]
    for slot in range(2 * half):
        start = pl.multiple_of(slot_device(slot, 2 * half, me) * BAND, BAND)
        source = near if slot < half else far
        pltpu.make_async_copy(
            source.at[slot % half], weights.at[:, pl.ds(start, BAND), :], sem
        ).start()


def store_slots(grads, near, far, sem, me):
    half = near.shape[0]
    for slot in range(2 * half):
        start = pl.multiple_of(slot_device(slot, 2 * half, me) * BAND, BAND)
        target = near if slot < half else far
        pltpu.make_async_copy(
            grads.at[:, pl.ds(start, BAND), :], target.at[slot % half], sem
        ).start()
    pltpu.make_async_copy(grads, grads, sem).wait()


def split_rows(seq_count, long_len, short_len, short_win):
    total_long = seq_count * long_len

    def parts(k):
        found = [(k * long_len, long_len)]
        for w in range(short_win):
            found.append((total_long + (w * seq_count + k) * short_len, short_len))
        return found

    return parts


def stack_heads(block, lane):
    zero = jnp.zeros_like(block)
    return jnp.concatenate([jnp.where(lane, block, zero), jnp.where(lane, zero, block)], 0)


def join_heads(stacked, lane):
    half = stacked.shape[0] // 2
    return jnp.where(lane, stacked[:half], stacked[half:])


def attend_body(dims, ids, long_len, short_len, *refs):
    seq_count, n_long, n_short, short_win = dims
    tokens = refs[:seq_count]
    near, far = refs[seq_count : seq_count + 2]
    first_o, low_o, q_o, k_o, v_o, pl_o, ps_o, mix_o = refs[seq_count + 2 : seq_count + 10]
    weights, table, sem = refs[seq_count + 10 :]
    me, seq = (ids[0], ids[1])
    width = first_o.shape[1]
    fetch_weights(near, far, weights, sem, me)
    pltpu.make_async_copy(weights, weights, sem).wait()
    table[...] = weights[3].astype(F32).T
    parts = split_rows(seq_count, n_long, n_short, short_win)
    for k in range(seq_count):
        owner = lax.bitwise_xor(seq, jnp.int32(k))
        rows_in = 0
        for at, size in parts(k):
            place = pl.multiple_of(owner * size, size)
            first = tokens[k][rows_in : rows_in + size, :].astype(F32) + table[pl.ds(place, size), :]
            low_o[at : at + size, :] = first.astype(BF)
            if k == 0:
                first_o[rows_in : rows_in + size, :] = first
            rows_in += size
    k_o[...] = mm(low_o[...], weights[1]).astype(BF)
    v_o[...] = mm(low_o[...], weights[2]).astype(BF)
    own = jnp.concatenate([low_o[at : at + size, :] for at, size in parts(0)], 0)
    q_o[...] = mm(own, weights[0]).astype(BF) * BF(HEAD_DIM**-0.5)
    lane = lax.broadcasted_iota(jnp.int32, (1, LANES), 1) < HEAD_DIM
    groups = width // LANES

    def window(row, size, key_at, length, save):
        keys = seq_count * size
        row_pos = seq * size + lax.broadcasted_iota(jnp.int32, (size, keys), 0)
        col = lax.broadcasted_iota(jnp.int32, (size, keys), 1)
        col_pos = lax.bitwise_xor(col // size, jnp.full_like(col, seq)) * size + col % size
        allowed = (col_pos <= row_pos) & (col_pos < length)
        allowed = jnp.concatenate([allowed.astype(jnp.int32)] * 2, 0) > 0
        for g in range(groups):
            cols = slice(g * LANES, (g + 1) * LANES)
            queries = stack_heads(q_o[row : row + size, cols], lane)
            scores = mm(queries, k_o[key_at : key_at + keys, cols], NT)
            scores = jnp.where(allowed, scores, -1e30)
            top = jnp.max(scores, axis=-1, keepdims=True)
            shifted = jnp.exp(scores - top)
            probs = (shifted / jnp.sum(shifted, axis=-1, keepdims=True)).astype(BF)
            save(g, probs)
            mixed = mm(probs, v_o[key_at : key_at + keys, cols])
            mix_o[row : row + size, cols] = join_heads(mixed, lane).astype(BF)

    def save_long(g, probs):
        pl_o[g] = probs

    window(0, n_long, 0, long_len[0], save_long)
    for w in range(short_win):

        def save_short(g, probs, w=w):
            ps_o[w, g] = probs

        window(
            n_long + w * n_short,
            n_short,
            seq_count * (n_long + w * n_short),
            short_len[w],
            save_short,
        )


def norm_parts(values):
    mean = jnp.mean(values, axis=-1, keepdims=True)
    centred = values - mean
    scale = lax.rsqrt(jnp.mean(centred * centred, axis=-1, keepdims=True) + 1e-05)
    return centred * scale, scale


def norm_back(cot, gain, xhat, scale):
    scaled = cot * gain
    mean = jnp.mean(scaled, axis=-1, keepdims=True)
    inner = jnp.mean(scaled * xhat, axis=-1, keepdims=True)
    return scale * (scaled - mean - xhat * inner)


def middle_body(ids, first, mixed, cot, near, far, out_o, gsum_o, gmix_o, gnear, gfar, weights, grads, act, slope, sem):
    me = ids[0]
    fetch_weights(near, far, weights, sem, me)
    pltpu.make_async_copy(weights, weights, sem).wait()
    width = first.shape[1]
    chunks = (weights.shape[0] - 2) // 2
    norm = weights.shape[0] - 1
    vectors = jnp.sum(weights[norm].astype(F32).reshape(-1, BAND, width), axis=0)
    gain0, gain1, bias0, bias1 = (vectors[i : i + 1] for i in range(4))
    mixed_low = mixed[...]
    xhat0, scale0 = norm_parts(first[...] + mm(mixed_low, weights[0]))
    normed = xhat0 * gain0 + bias0
    normed_low = normed.astype(BF)
    second = normed
    for c in range(chunks):
        hidden = mm(normed_low, weights[1 + c])
        cdf = 0.5 + 0.5 * lax.erf(hidden * (0.5**0.5))
        slope[c] = cdf + hidden * jnp.exp(-0.5 * hidden * hidden) * ((2 * math.pi) ** -0.5)
        act[c] = (hidden * cdf).astype(BF)
        second = second + mm(act[c], weights[1 + chunks + c], NT)
    xhat1, scale1 = norm_parts(second)
    out_o[...] = (xhat1 * gain1 + bias1).astype(BF)
    cot_wide = cot[...].astype(F32)
    grad_second = norm_back(cot_wide, gain1, xhat1, scale1)
    second_low = grad_second.astype(BF)
    grad_normed = grad_second
    for c in range(chunks):
        hidden_low = (mm(second_low, weights[1 + chunks + c]) * slope[c]).astype(BF)
        grads[1 + chunks + c] = mm(second_low, act[c], TN).astype(BF)
        grads[1 + c] = mm(normed_low, hidden_low, TN).astype(BF)
        grad_normed = grad_normed + mm(hidden_low, weights[1 + c], NT)
    grad_sum = norm_back(grad_normed, gain0, xhat0, scale0)
    gsum_o[...] = grad_sum
    sum_low = grad_sum.astype(BF)
    gmix_o[...] = mm(sum_low, weights[0], NT).astype(BF)
    grads[0] = mm(mixed_low, sum_low, TN).astype(BF)
    terms = jnp.concatenate(
        [
            jnp.sum(grad_normed * xhat0, axis=0, keepdims=True),
            jnp.sum(cot_wide * xhat1, axis=0, keepdims=True),
            jnp.sum(grad_normed, axis=0, keepdims=True),
            jnp.sum(cot_wide, axis=0, keepdims=True),
            jnp.zeros((BAND - 4, width), F32),
        ],
        0,
    ).astype(BF)
    for d in range(width // BAND):
        grads[norm, d * BAND : (d + 1) * BAND, :] = terms
    store_slots(grads, gnear, gfar, sem, me)


def attend_back_body(dims, gmix, q, k, v, pl_i, ps_i, dq_o, dk_o, dv_o):
    seq_count, n_long, n_short, short_win = dims
    lane = lax.broadcasted_iota(jnp.int32, (1, LANES), 1) < HEAD_DIM
    groups = gmix.shape[1] // LANES
    scale = HEAD_DIM**-0.5

    def window(row, size, key_at, load):
        keys = seq_count * size
        for g in range(groups):
            cols = slice(g * LANES, (g + 1) * LANES)
            grads = stack_heads(gmix[row : row + size, cols], lane)
            queries = stack_heads(q[row : row + size, cols], lane)
            probs = load(g)
            grad_probs = mm(grads, v[key_at : key_at + keys, cols], NT)
            wide = probs.astype(F32)
            inner = jnp.sum(wide * grad_probs, axis=-1, keepdims=True)
            grad_scores = (wide * (grad_probs - inner)).astype(BF)
            grad_q = mm(grad_scores, k[key_at : key_at + keys, cols])
            dq_o[row : row + size, cols] = (join_heads(grad_q, lane) * scale).astype(BF)
            dk_o[key_at : key_at + keys, cols] = mm(grad_scores, queries, TN).astype(BF)
            dv_o[key_at : key_at + keys, cols] = mm(probs, grads, TN).astype(BF)

    window(0, n_long, 0, lambda g: pl_i[g])
    for w in range(short_win):
        window(
            n_long + w * n_short,
            n_short,
            seq_count * (n_long + w * n_short),
            lambda g, w=w: ps_i[w, g],
        )


def leave_body(dims, ids, low, dq, dk, dv, gsum, near, far, *refs):
    seq_count, n_long, n_short, short_win = dims
    own_o = refs[0]
    sent = refs[1:seq_count]
    gnear, gfar, weights, grads, table, sem = refs[seq_count:]
    me, seq = (ids[0], ids[1])
    fetch_weights(near, far, weights, sem, me)
    parts = split_rows(seq_count, n_long, n_short, short_win)
    own = jnp.concatenate([low[at : at + size, :] for at, size in parts(0)], 0)
    grads[0] = mm(own, dq[...], TN).astype(BF)
    grads[1] = mm(low[...], dk[...], TN).astype(BF)
    grads[2] = mm(low[...], dv[...], TN).astype(BF)
    pltpu.make_async_copy(weights, weights, sem).wait()
    back = mm(dk[...], weights[1], NT) + mm(dv[...], weights[2], NT)
    from_q = gsum[...] + mm(dq[...], weights[0], NT)
    order = []
    for k in range(seq_count):
        owner = lax.bitwise_xor(seq, jnp.int32(k))
        rows_in = 0
        for which, (at, size) in enumerate(parts(k)):
            piece = back[at : at + size]
            if k == 0:
                piece = piece + from_q[rows_in : rows_in + size]
                own_o[rows_in : rows_in + size, :] = piece
            else:
                sent[k - 1][rows_in : rows_in + size, :] = piece.astype(BF)
            order.append((min(which, 1), pl.multiple_of(owner * size, size), size, piece))
            rows_in += size
    table[...] = jnp.zeros_like(table)
    for which in range(2):
        for kind, place, size, piece in order:
            if kind == which:
                table[pl.ds(place, size), :] += piece
    grads[3] = table[...].T.astype(BF)
    store_slots(grads, gnear, gfar, sem, me)


def sum_stage(parts, groups, name):
    count, pieces, band, width = parts[0].shape
    size = count // groups

    def body(*refs):
        ins, outs = (refs[: len(parts)], refs[len(parts) :])
        for g in range(groups):
            rows = slice(g * size, (g + 1) * size)
            total = ins[0][rows].astype(F32)
            for item in ins[1:]:
                total = total + item[rows].astype(F32)
            outs[g][...] = total.astype(outs[g].dtype)

    def block(n):
        return pl.BlockSpec((n, 1, band, width), lambda i: (0, i, 0, 0))

    return pl.pallas_call(
        body,
        grid=(pieces,),
        out_shape=[
            jax.ShapeDtypeStruct((size, pieces, band, width), F32 if g == 0 else BF)
            for g in range(groups)
        ],
        in_specs=[block(count)] * len(parts),
        out_specs=[block(size)] * groups,
        compiler_params=pltpu.CompilerParams(vmem_limit_bytes=50 * 1024 * 1024),
        cost_estimate=pl.CostEstimate(
            flops=count * pieces * band * width * len(parts),
            bytes_accessed=2 * count * pieces * band * width * (len(parts) + 1),
            transcendentals=0,
        ),
        name=name,
    )(*parts)


def swap(value, axis, size, mask, keep=lambda source, target: True):
    pairs = [(i, i ^ mask) for i in range(size) if keep(i, i ^ mask)]
    return lax.ppermute(value, axis, pairs)


def local(
    dp_count,
    seq_count,
    long_tokens,
    short_tokens,
    long_cot,
    short_cot,
    long_lengths,
    short_lengths,
    w_query,
    w_key,
    w_value,
    w_out,
    w_up,
    w_down,
    pos_table,
    norm_gain,
    norm_bias,
):
    width = w_key.shape[1]
    hidden = w_up.shape[1]
    chunks = hidden // width
    shard = w_key.shape[0]
    slots = width // BAND
    direct = shard == BAND and seq_count == 4
    device = lax.axis_index("dp") * seq_count + lax.axis_index("seq")
    seq = lax.axis_index("seq")
    ids = jnp.stack([device if direct else device * 0, seq]).astype(jnp.int32)

    n_long, n_short, short_win = (long_tokens.shape[1], short_tokens.shape[1], short_tokens.shape[0])
    dims = (seq_count, n_long, n_short, short_win)
    rows = n_long + short_win * n_short
    group_rows = seq_count * rows

    def flat(long_part, short_part):
        return jnp.concatenate([long_part.reshape(-1, width), short_part.reshape(-1, width)], 0)

    vectors = jnp.concatenate([norm_gain, norm_bias], 0)
    norm_rows = lax.dynamic_update_slice(
        jnp.zeros((shard if direct else 8, width), BF), vectors, (0, device * shard)
    )
    early = jnp.stack([w_query, w_key, w_value, pos_table.T])

    def columns(weight):
        return weight.reshape(weight.shape[0], chunks, width).transpose(1, 0, 2)

    late = [w_out[None], columns(w_up), columns(w_down.T)]

    def gather(piece):
        layer = jnp.stack([piece] + [swap(piece, "seq", seq_count, k) for k in range(1, seq_count)])
        near = jnp.concatenate(
            [layer] + [swap(layer, "dp", dp_count, k) for k in range(2, dp_count, 2)], 0
        )
        return near, swap(near, "dp", dp_count, 1)

    def gather_plain(piece):
        whole = lax.all_gather(piece, ("dp", "seq"), axis=1, tiled=True)
        return to_slots(whole)

    def to_slots(whole):
        count = whole.shape[0]
        cut = whole.reshape(count, slots // 8, 2, 4, BAND, width).transpose(2, 1, 3, 0, 4, 5)
        cut = cut.reshape(2, slots // 2, count, BAND, width)
        return cut[0], cut[1]

    def from_slots(near, far):
        count = near.shape[1]
        cut = jnp.stack([near, far]).reshape(2, slots // 8, 4, count, BAND, width)
        return cut.transpose(3, 1, 0, 2, 4, 5).reshape(count, width, width)

    tokens = flat(long_tokens, short_tokens)
    cots = flat(long_cot, short_cot)
    if direct:
        early_full = gather(early)
    else:
        early_full = gather_plain(early)
    group_tokens = [tokens] + [
        swap(tokens, "seq", seq_count, k, lambda source, target: source < target)
        for k in range(1, seq_count)
    ]
    if direct:
        late_full = gather(jnp.concatenate(late + [norm_rows[None]], 0))
    else:
        norm_whole = lax.psum(norm_rows.astype(F32), ("dp", "seq")).astype(BF)
        norm_slots = to_slots(jnp.pad(norm_whole, ((0, width - 8), (0, 0)))[None])
        late_full = [
            jnp.concatenate([a, b], 1)
            for a, b in zip(gather_plain(jnp.concatenate(late, 0)), norm_slots)
        ]

    groups = width // LANES
    long_probs = (groups, 2 * n_long, seq_count * n_long)
    short_probs = (short_win, groups, 2 * n_short, seq_count * n_short)
    square = width * width
    early_pieces, late_pieces = (4, 2 + 2 * chunks)
    first, low, queries, key_rows, values, p_long, p_short, mixed = call(
        functools.partial(attend_body, dims),
        [
            ((rows, width), F32, VMEM),
            ((group_rows, width), BF, VMEM),
            ((rows, width), BF, VMEM),
            ((group_rows, width), BF, VMEM),
            ((group_rows, width), BF, VMEM),
            (long_probs, BF, VMEM),
            (short_probs, BF, VMEM),
            ((rows, width), BF, VMEM),
        ],
        [SMEM] * 3 + [VMEM] * seq_count + [ANY] * 2,
        [
            pltpu.VMEM((early_pieces, width, width), BF),
            pltpu.VMEM((width, width), F32),
            pltpu.SemaphoreType.DMA,
        ],
        6 * group_rows * square,
        20 * 1024 * 1024,
        "attend",
    )(ids, long_lengths, short_lengths, *group_tokens, *early_full)

    slot_half = (slots // 2, late_pieces, BAND, width)
    out, grad_sum, grad_mixed, late_near, late_far = call(
        middle_body,
        [
            ((rows, width), BF, VMEM),
            ((rows, width), F32, VMEM),
            ((rows, width), BF, VMEM),
            (slot_half, BF, ANY),
            (slot_half, BF, ANY),
        ],
        [SMEM] + [VMEM] * 3 + [ANY] * 2,
        [
            pltpu.VMEM((late_pieces, width, width), BF),
            pltpu.VMEM((late_pieces, width, width), BF),
            pltpu.VMEM((chunks, rows, width), BF),
            pltpu.VMEM((chunks, rows, width), F32),
            pltpu.SemaphoreType.DMA,
        ],
        12 * rows * square * chunks,
        20 * 1024 * 1024,
        "middle",
    )(ids, first, mixed, cots, *late_full)

    grad_q, grad_k, grad_v = call(
        functools.partial(attend_back_body, dims),
        [
            ((rows, width), BF, VMEM),
            ((group_rows, width), BF, VMEM),
            ((group_rows, width), BF, VMEM),
        ],
        [VMEM] * 6,
        [],
        4 * group_rows * square,
        16 * 1024 * 1024,
        "attend_back",
    )(grad_mixed, queries, key_rows, values, p_long, p_short)
    slot_half = (slots // 2, early_pieces, BAND, width)
    leave_outs = call(
        functools.partial(leave_body, dims),
        [((rows, width), F32, VMEM)]
        + [((rows, width), BF, VMEM)] * (seq_count - 1)
        + [(slot_half, BF, ANY)] * 2,
        [SMEM] + [VMEM] * 5 + [ANY] * 2,
        [
            pltpu.VMEM((early_pieces, width, width), BF),
            pltpu.VMEM((early_pieces, width, width), BF),
            pltpu.VMEM((width, width), F32),
            pltpu.SemaphoreType.DMA,
        ],
        8 * group_rows * square,
        16 * 1024 * 1024,
        "leave",
    )(ids, low, grad_q, grad_k, grad_v, grad_sum, *early_full)
    grad_first, sent = (leave_outs[0], leave_outs[1:seq_count])
    early_near, early_far = leave_outs[seq_count:]

    for k in range(1, seq_count):
        grad_first = grad_first + swap(
            sent[k - 1], "seq", seq_count, k, lambda source, target: source > target
        ).astype(F32)
    grads = grad_first.astype(BF)

    def scatter(near, far, name):
        arrived = swap(far, "dp", dp_count, 1)
        layers = sum_stage([near, arrived], dp_count // 2, name + "_core")
        layers = [layers[0]] + [
            swap(layers[k], "dp", dp_count, 2 * k) for k in range(1, dp_count // 2)
        ]
        places = sum_stage(layers, seq_count, name + "_layer")
        total = places[0].astype(F32)
        for k in range(1, seq_count):
            total = total + swap(places[k], "seq", seq_count, k).astype(F32)
        return total[0]

    def scatter_plain(near, far):
        return lax.psum_scatter(
            from_slots(near, far).astype(F32), ("dp", "seq"), scatter_dimension=1, tiled=True
        )

    if direct:
        late_sum = scatter(late_near, late_far, "late")
        early_sum = scatter(early_near, early_far, "early")
        norm_sum = late_sum[-1]
    else:
        late_sum = scatter_plain(late_near, late_far)
        early_sum = scatter_plain(early_near, early_far)
        norm_sum = lax.psum(from_slots(late_near, late_far)[-1, :8].astype(F32), ("dp", "seq"))
    norm_sum = lax.dynamic_slice(norm_sum, (0, device * shard), (4, shard))

    def join(pieces):
        return pieces.transpose(1, 0, 2).reshape(shard, hidden)

    return (
        out[:n_long].reshape(long_tokens.shape),
        out[n_long:].reshape(short_tokens.shape),
        grads[:n_long].reshape(long_tokens.shape),
        grads[n_long:].reshape(short_tokens.shape),
        early_sum[0],
        early_sum[1],
        early_sum[2],
        late_sum[0],
        join(late_sum[1 : 1 + chunks]),
        join(late_sum[1 + chunks : 1 + 2 * chunks]).T,
        early_sum[3].T,
        norm_sum[:2],
        norm_sum[2:],
    )


def solution(mesh):
    rows = P(("dp", "seq"), None)
    cols = P(None, ("dp", "seq"))
    acts = P("dp", "seq", None)
    return jax.shard_map(
        functools.partial(local, mesh.shape["dp"], mesh.shape["seq"]),
        mesh=mesh,
        in_specs=(acts,) * 4 + (P("dp"),) * 2 + (rows,) * 5 + (cols,) * 4,
        out_specs=(acts,) * 4 + (rows,) * 5 + (cols,) * 4,
        check_vma=False,
    )
```

time: 1810 us -> 215 us (0.12)
  waiting for transfers between devices: 1150 us -> 103 us
  blocking collectives: 483 us -> 0 us
  matrix products: 52.2 us -> 0 us
  local copies, waits for them, and re-layouts: 55 us -> 13.2 us
  Pallas kernels: 0 us -> 38 us
  starting transfers between devices: 36 us -> 56.2 us
  other arithmetic: 22.8 us -> 2.66 us
    reduce_scatter x6 -> x0, waiting for transfers between devices: 834 us -> none  [the longest x1 149 us: local(): lax.psum_scatter(long_terms[1] + short_terms[1], ('dp', 'seq'), scatter_d...]
    all_gather x7 -> x0, blocking collectives: 483 us -> none  [the longest x1 74.8 us: local(): lax.all_gather(w_out, ('dp', 'seq'), axis=0, tiled=True)]
    unnamed x14 -> x0, waiting for transfers between devices: 299 us -> none
    ppermute x0 -> x34, waiting for transfers between devices: none -> 103 us  [swap(): return lax.ppermute(value, axis, pairs)]
    ppermute x0 -> x34, starting transfers between devices: none -> 56.2 us  [swap(): return lax.ppermute(value, axis, pairs)]
    dot_general x36 -> x0, matrix products: 52.2 us -> none  [the longest x8 12.5 us: back_product(): lax.dot_general(grad_rows, weight, (((1,), (1,)), ((), ())), preferred_el...]
    pallas_call x0 -> x8, Pallas kernels: none -> 38 us  [the longest x1 10.9 us: local(): call(middle_body, [((rows, width), BF, VMEM), ((rows, width), F32, VMEM),...]
    all_to_all x8 -> x0, starting transfers between devices: 35.1 us -> none  [the longest x1 5.09 us: local(): lax.all_to_all(long_gjoint, 'seq', split_axis=1, concat_axis=3, tiled=True)]
  transfers between devices with their start and end apart: 19 -> 34, of which waited for: 12 -> 19; matrix products, arithmetic and copies ran while one was open for 6% -> 2% of each run, Pallas kernels for 0% -> 12%
where the time goes in v1:
time: 215 us
  waiting for transfers between devices  103 us (48%)
  starting transfers between devices  56.2 us (26%)
  Pallas kernels  38 us (18%)
  local copies, waits for them, and re-layouts  13.2 us (6%)
  other arithmetic  2.66 us (1%)
    ppermute x34, waiting for transfers between devices, swap(): return lax.ppermute(value, axis, pairs)  103 us
    ppermute x34, starting transfers between devices, swap(): return lax.ppermute(value, axis, pairs)  56.2 us
    pallas_call x1, Pallas kernels, local(): call(middle_body, [((rows, width), BF, VMEM), ((rows, width), F32, VMEM),...  10.9 us
    pallas_call x4, Pallas kernels, sum_stage(): pl.pallas_call(body, grid=(pieces,), out_shape=[jax.ShapeDtypeStruct((siz...  7.53 us
    unnamed x45, local copies, waits for them, and re-layouts  7.28 us
    pallas_call x1, Pallas kernels, local(): call(functools.partial(leave_body, dims), [((rows, width), F32, VMEM)] +...  6.7 us
    pallas_call x1, Pallas kernels, local(): call(functools.partial(attend_body, dims), [((rows, width), F32, VMEM), (...  6.46 us
    pallas_call x1, Pallas kernels, local(): call(functools.partial(attend_back_body, dims), [((rows, width), BF, VMEM...  6.45 us
  transfers between devices with their start and end apart: 34, of which 19 were waited for; matrix products, arithmetic and copies ran while one was open for 2% of the time, Pallas kernels for 12%

profile of v1, /device:TPU:0, one launch (start us, length us, event | category | flops | bytes accessed | tf_op | source)
XLA Modules:
  0.0 214.8 jit_solution(18034147837383067999)
XLA Ops:
  3.3 4.3 %collective-permute-start.11 = (bf16[10,16,512]{2,1,0:T(8,128)(2,1)S(1)}, bf16[10,16,512]{2,1,0:T(8,128)(2,1)S(1)}, u32[]{:S(2)}, u32[]{:S(2)}) collective-permute-start(bf16[10,16,512]{2,1,0:T(8,128)(2,1)S(1)} %get-tuple-element.98), channel_id=1, source_target_pairs={{0,2},{1,3},{2,0},{3,1},{4,6},{5,7},{6,4},{7,5},{8,10},{9,11},{10,... | collective-permute-start | bytes 491528 | tf_op jit(solution)/shard_map/ppermute | solution.py:328
  9.9 7.0 %collective-permute-done.11 = bf16[10,16,512]{2,1,0:T(8,128)(2,1)S(1)} collective-permute-done((bf16[10,16,512]{2,1,0:T(8,128)(2,1)S(1)}, bf16[10,16,512]{2,1,0:T(8,128)(2,1)S(1)}, u32[]{:S(2)}, u32[]{:S(2)}) %collective-permute-start.11) | collective-permute-done | bytes 163872 | tf_op jit(solution)/shard_map/ppermute | solution.py:328
  17.0 3.1 %collective-permute-done.12 = bf16[10,16,512]{2,1,0:T(8,128)(2,1)S(1)} collective-permute-done((bf16[10,16,512]{2,1,0:T(8,128)(2,1)S(1)}, bf16[10,16,512]{2,1,0:T(8,128)(2,1)S(1)}, u32[]{:S(2)}, u32[]{:S(2)}) %collective-permute-start.12) | collective-permute-done | bytes 163872 | tf_op jit(solution)/shard_map/ppermute | solution.py:328
  23.8 27.1 %collective-permute-done.13 = bf16[4,10,16,512]{3,2,1,0:T(8,128)(2,1)S(1)} collective-permute-done((bf16[4,10,16,512]{3,2,1,0:T(8,128)(2,1)S(1)}, bf16[4,10,16,512]{3,2,1,0:T(8,128)(2,1)S(1)}, u32[]{:S(2)}, u32[]{:S(2)}) %collective-permute-start.13) | collective-permute-done | bytes 655392 | tf_op jit(solution)/shard_map/ppermute | solution.py:328
  51.3 6.1 %collective-permute-start.4 = (bf16[4,16,512]{2,1,0:T(8,128)(2,1)S(1)}, bf16[4,16,512]{2,1,0:T(8,128)(2,1)S(1)}, u32[]{:S(2)}, u32[]{:S(2)}) collective-permute-start(bf16[4,16,512]{2,1,0:T(8,128)(2,1)S(1)} %get-tuple-element.104), channel_id=1, source_target_pairs={{0,2},{1,3},{2,0},{3,1},{4,6},{5,7},{6,4},{7,5},{8,10},{9,11},{10,... | collective-permute-start | bytes 196616 | tf_op jit(solution)/shard_map/ppermute | solution.py:328
  58.9 2.7 %collective-permute-done.4 = bf16[4,16,512]{2,1,0:T(8,128)(2,1)S(1)} collective-permute-done((bf16[4,16,512]{2,1,0:T(8,128)(2,1)S(1)}, bf16[4,16,512]{2,1,0:T(8,128)(2,1)S(1)}, u32[]{:S(2)}, u32[]{:S(2)}) %collective-permute-start.4) | collective-permute-done | bytes 65568 | tf_op jit(solution)/shard_map/ppermute | solution.py:328
  67.6 10.9 %collective-permute-done.6 = bf16[4,4,16,512]{3,2,1,0:T(8,128)(2,1)S(1)} collective-permute-done((bf16[4,4,16,512]{3,2,1,0:T(8,128)(2,1)S(1)}, bf16[4,4,16,512]{3,2,1,0:T(8,128)(2,1)S(1)}, u32[]{:S(2)}, u32[]{:S(2)}) %collective-permute-start.6) | collective-permute-done | bytes 262176 | tf_op jit(solution)/shard_map/ppermute | solution.py:328
  78.8 4.2 %collective-permute-start.2 = (bf16[256,512]{1,0:T(8,128)(2,1)S(1)}, bf16[256,512]{1,0:T(8,128)(2,1)S(1)}, u32[]{:S(2)}, u32[]{:S(2)}) collective-permute-start(bf16[256,512]{1,0:T(8,128)(2,1)S(1)} %pad_maximum_fusion.1.refs_0_), channel_id=1, source_target_pairs={{0,3},{1,2},{4,7},{5,6},{8,11},{9,10},{12,15},{13,14},{16,19},{17,... | collective-permute-start | bytes 786440 | tf_op jit(solution)/shard_map/ppermute | solution.py:328
  89.7 5.6 %collective-permute-done.1.refs_2_ = bf16[256,512]{1,0:T(8,128)(2,1)S(1)} collective-permute-done((bf16[256,512]{1,0:T(8,128)(2,1)S(1)}, bf16[256,512]{1,0:T(8,128)(2,1)S(1)}, u32[]{:S(2)}, u32[]{:S(2)}) %collective-permute-start.1) | collective-permute-done | bytes 262176 | tf_op jit(solution)/shard_map/ppermute | solution.py:328
  95.3 5.2 %collective-permute-done.refs_1_ = bf16[256,512]{1,0:T(8,128)(2,1)S(1)} collective-permute-done((bf16[256,512]{1,0:T(8,128)(2,1)S(1)}, bf16[256,512]{1,0:T(8,128)(2,1)S(1)}, u32[]{:S(2)}, u32[]{:S(2)}) %collective-permute-start) | collective-permute-done | bytes 262176 | tf_op jit(solution)/shard_map/ppermute | solution.py:328
  101.6 6.5 %attend.1 = (f32[256,512]{1,0:T(8,128)S(1)}, bf16[1024,512]{1,0:T(8,128)(2,1)S(1)}, bf16[256,512]{1,0:T(8,128)(2,1)S(1)}, bf16[1024,512]{1,0:T(8,128)(2,1)}, bf1...) custom-call(s32[2]{0:T(128)S(1)} %pad_add_fusion.ids, ...), custom_call_target="tpu_custom_call" | custom-call | flops 1610612736 | bytes 20971520 | tf_op jit(solution)/shard_map/attend/pallas_call | solution.py:426
  110.6 10.9 %middle.1 = (bf16[256,512]{1,0:T(8,128)(2,1)S(1)}, f32[256,512]{1,0:T(8,128)S(1)}, bf16[256,512]{1,0:T(8,128)(2,1)S(1)}, bf16[16,10,16,512]{3,2,1,0:T(8,128)(2,1)}, bf16[16,10,16,512]{3,2,1,0:T(8,128)(2,1)}) custom-call(s32[2]{0:T(128)S(1)} %pad_add_fusion.ids, f32[256,512]{1,0:T(8,128)S(1)} %get-tuple-element.51.first, ...), custom_call_target="tpu_custom_call" | custom-call | flops 3221225472 | bytes 20971520 | tf_op jit(solution)/shard_map/middle/pallas_call | solution.py:450
  121.5 6.5 %attend_back.1 = (bf16[256,512]{1,0:T(8,128)(2,1)S(1)}, bf16[1024,512]{1,0:T(8,128)(2,1)S(1)}, bf16[1024,512]{1,0:T(8,128)(2,1)S(1)}) custom-call(bf16[256,512]{1,0:T(8,128)(2,1)S(1)} %get-tuple-element.55.gmix, bf16[256,512]{1,0:T(8,128)(2,1)S(1)} %get-tuple-element.56.q, bf16[1024,512]{1,0:T(8,128)(2,1)} %get-tuple-element.57.k, ...), custom_call_target="tpu_custom_call" | custom-call | flops 1073741824 | bytes 16777216 | tf_op jit(solution)/shard_map/attend_back/pallas_call | solution.py:472
  130.0 6.7 %leave.1 = (f32[256,512]{1,0:T(8,128)S(1)}, bf16[256,512]{1,0:T(8,128)(2,1)S(1)}, bf16[256,512]{1,0:T(8,128)(2,1)S(1)}, bf16[256,512]{1,0:T(8,128)(2,1)S(1)}, bf...) custom-call(s32[2]{0:T(128)S(1)} %pad_add_fusion.ids, bf16[1024,512]{1,0:T(8,128)(2,1)} %copy-done.3, ...), custom_call_target="tpu_custom_call" | custom-call | flops 2147483648 | bytes 16777216 | tf_op jit(solution)/shard_map/leave/pallas_call | solution.py:486
  145.2 4.3 %collective-permute-done.21.refs_1_ = bf16[4,4,16,512]{3,2,1,0:T(8,128)(2,1)S(1)} collective-permute-done((bf16[4,4,16,512]{3,2,1,0:T(8,128)(2,1)S(1)}, bf16[4,4,16,512]{3,2,1,0:T(8,128)(2,1)S(1)}, u32[]{:S(2)}, u32[]{:S(2)}) %collective-permute-start.21) | collective-permute-done | bytes 262176 | tf_op jit(solution)/shard_map/ppermute | solution.py:328
  150.8 4.9 %collective-permute-done.22.refs_2_ = bf16[4,4,16,512]{3,2,1,0:T(8,128)(2,1)S(1)} collective-permute-done((bf16[4,4,16,512]{3,2,1,0:T(8,128)(2,1)S(1)}, bf16[4,4,16,512]{3,2,1,0:T(8,128)(2,1)S(1)}, u32[]{:S(2)}, u32[]{:S(2)}) %collective-permute-start.22) | collective-permute-done | bytes 262176 | tf_op jit(solution)/shard_map/ppermute | solution.py:328
  158.1 4.5 %collective-permute-start.24 = (bf16[1,4,16,512]{3,2,1,0:T(8,128)(2,1)S(1)}, bf16[1,4,16,512]{3,2,1,0:T(8,128)(2,1)S(1)}, u32[]{:S(2)}, u32[]{:S(2)}) collective-permute-start(bf16[1,4,16,512]{3,2,1,0:T(8,128)(2,1)S(1)} %get-tuple-element.76), channel_id=1, source_target_pairs={{0,1},{1,0},{2,3},{3,2},{4,5},{5,4},{6,7},{7,6},{8,9},{9,8},{10,11... | collective-permute-start | bytes 196616 | tf_op jit(solution)/shard_map/ppermute | solution.py:328
  164.1 5.9 %late_core.1 = (f32[4,10,16,512]{3,2,1,0:T(8,128)S(1)}, bf16[4,10,16,512]{3,2,1,0:T(8,128)(2,1)S(1)}, bf16[4,10,16,512]{3,2,1,0:T(8,128)(2,1)S(1)}, bf16[4,10,16,512]{3,2,1,0:T(8,128)(2,1)S(1)}) custom-call(bf16[16,10,16,512]{3,2,1,0:T(8,128)(2,1)} %get-tuple-element.79.refs_0_, bf16[16,10,16,512]{3,2,1,0:T(8,128)(2,1)} %copy-done.4), custom_call_target="tpu_custom_call" | custom-call | flops 2621440 | bytes 7864320 | tf_op jit(solution)/shard_map/late_core/pallas_call | solution.py:307
  173.8 3.4 %collective-permute-start.25 = (bf16[1,4,16,512]{3,2,1,0:T(8,128)(2,1)S(1)}, bf16[1,4,16,512]{3,2,1,0:T(8,128)(2,1)S(1)}, u32[]{:S(2)}, u32[]{:S(2)}) collective-permute-start(bf16[1,4,16,512]{3,2,1,0:T(8,128)(2,1)S(1)} %get-tuple-element.77), channel_id=1, source_target_pairs={{0,2},{1,3},{2,0},{3,1},{4,6},{5,7},{6,4},{7,5},{8,10},{9,11},{10,... | collective-permute-start | bytes 196616 | tf_op jit(solution)/shard_map/ppermute | solution.py:328
  177.2 2.9 %collective-permute-start.26 = (bf16[1,4,16,512]{3,2,1,0:T(8,128)(2,1)S(1)}, bf16[1,4,16,512]{3,2,1,0:T(8,128)(2,1)S(1)}, u32[]{:S(2)}, u32[]{:S(2)}) collective-permute-start(bf16[1,4,16,512]{3,2,1,0:T(8,128)(2,1)S(1)} %get-tuple-element.78), channel_id=1, source_target_pairs={{0,3},{1,2},{2,1},{3,0},{4,7},{5,6},{6,5},{7,4},{8,11},{9,10},{10,... | collective-permute-start | bytes 196616 | tf_op jit(solution)/shard_map/ppermute | solution.py:328
  183.3 4.4 %collective-permute-done.28.refs_1_ = bf16[4,10,16,512]{3,2,1,0:T(8,128)(2,1)S(1)} collective-permute-done((bf16[4,10,16,512]{3,2,1,0:T(8,128)(2,1)S(1)}, bf16[4,10,16,512]{3,2,1,0:T(8,128)(2,1)S(1)}, u32[]{:S(2)}, u32[]{:S(2)}) %collective-permute-start.28) | collective-permute-done | bytes 655392 | tf_op jit(solution)/shard_map/ppermute | solution.py:328
  187.8 10.5 %collective-permute-done.29.refs_2_ = bf16[4,10,16,512]{3,2,1,0:T(8,128)(2,1)S(1)} collective-permute-done((bf16[4,10,16,512]{3,2,1,0:T(8,128)(2,1)S(1)}, bf16[4,10,16,512]{3,2,1,0:T(8,128)(2,1)S(1)}, u32[]{:S(2)}, u32[]{:S(2)}) %collective-permute-start.29) | collective-permute-done | bytes 655392 | tf_op jit(solution)/shard_map/ppermute | solution.py:328
  199.3 3.4 %collective-permute-start.32 = (bf16[1,10,16,512]{3,2,1,0:T(8,128)(2,1)S(1)}, bf16[1,10,16,512]{3,2,1,0:T(8,128)(2,1)S(1)}, u32[]{:S(2)}, u32[]{:S(2)}) collective-permute-start(bf16[1,10,16,512]{3,2,1,0:T(8,128)(2,1)S(1)} %get-tuple-element.87), channel_id=1, source_target_pairs={{0,2},{1,3},{2,0},{3,1},{4,6},{5,7},{6,4},{7,5},{8,10},{9,11},{10,... | collective-permute-start | bytes 491528 | tf_op jit(solution)/shard_map/ppermute | solution.py:328
  206.7 5.4 %collective-permute-done.32 = bf16[1,10,16,512]{3,2,1,0:T(8,128)(2,1)S(1)} collective-permute-done((bf16[1,10,16,512]{3,2,1,0:T(8,128)(2,1)S(1)}, bf16[1,10,16,512]{3,2,1,0:T(8,128)(2,1)S(1)}, u32[]{:S(2)}, u32[]{:S(2)}) %collective-permute-start.32) | collective-permute-done | bytes 163872 | tf_op jit(solution)/shard_map/ppermute | solution.py:328
  (123 shorter events, 56.6 us)
Async XLA Ops:
  3.3 13.7 %collective-permute-start.11 = (bf16[10,16,512]{2,1,0:T(8,128)(2,1)S(1)}, bf16[10,16,512]{2,1,0:T(8,128)(2,1)S(1)}, u32[]{:S(2)}, u32[]{:S(2)}) collective-permute-start(bf16[10,16,512]{2,1,0:T(8,128)(2,1)S(1)} %get-tuple-element.98), channel_id=1, source_target_pairs={{0,2},{1,3},{2,0},{3,1},{4,6},{5,7},{6,4},{7,5},{8,10},{9,11},{10,... | collective-permute-start | bytes 491528 | tf_op jit(solution)/shard_map/ppermute | solution.py:328
  9.2 10.9 %collective-permute-start.12 = (bf16[10,16,512]{2,1,0:T(8,128)(2,1)S(1)}, bf16[10,16,512]{2,1,0:T(8,128)(2,1)S(1)}, u32[]{:S(2)}, u32[]{:S(2)}) collective-permute-start(bf16[10,16,512]{2,1,0:T(8,128)(2,1)S(1)} %get-tuple-element.98), channel_id=1, source_target_pairs={{0,3},{1,2},{2,1},{3,0},{4,7},{5,6},{6,5},{7,4},{8,11},{9,10},{10,... | collective-permute-start | bytes 491528 | tf_op jit(solution)/shard_map/ppermute | solution.py:328
  20.2 30.9 %collective-permute-start.15 = (bf16[4,10,16,512]{3,2,1,0:T(8,128)(2,1)S(1)}, bf16[4,10,16,512]{3,2,1,0:T(8,128)(2,1)S(1)}, u32[]{:S(2)}, u32[]{:S(2)}) collective-permute-start(bf16[4,10,16,512]{3,2,1,0:T(8,128)(2,1)S(1)} %pad_maximum_fusion), channel_id=1, source_target_pairs={{0,24},{4,28},{8,16},{12,20},{16,8},{20,12},{24,0},{28,4},{1,25},{... | collective-permute-start | bytes 1966088 | tf_op jit(solution)/shard_map/ppermute | solution.py:328
  22.7 28.3 %collective-permute-start.14 = (bf16[4,10,16,512]{3,2,1,0:T(8,128)(2,1)S(1)}, bf16[4,10,16,512]{3,2,1,0:T(8,128)(2,1)S(1)}, u32[]{:S(2)}, u32[]{:S(2)}) collective-permute-start(bf16[4,10,16,512]{3,2,1,0:T(8,128)(2,1)S(1)} %pad_maximum_fusion), channel_id=1, source_target_pairs={{0,16},{4,20},{8,24},{12,28},{16,0},{20,4},{24,8},{28,12},{1,17},{... | collective-permute-start | bytes 1966088 | tf_op jit(solution)/shard_map/ppermute | solution.py:328
  23.2 27.7 %collective-permute-start.13 = (bf16[4,10,16,512]{3,2,1,0:T(8,128)(2,1)S(1)}, bf16[4,10,16,512]{3,2,1,0:T(8,128)(2,1)S(1)}, u32[]{:S(2)}, u32[]{:S(2)}) collective-permute-start(bf16[4,10,16,512]{3,2,1,0:T(8,128)(2,1)S(1)} %pad_maximum_fusion), channel_id=1, source_target_pairs={{0,8},{4,12},{8,0},{12,4},{16,24},{20,28},{24,16},{28,20},{1,9},{5... | collective-permute-start | bytes 1966088 | tf_op jit(solution)/shard_map/ppermute | solution.py:328
  51.1 57.9 %collective-permute-start.16 = (bf16[16,10,16,512]{3,2,1,0:T(8,128)(2,1)S(1)}, bf16[16,10,16,512]{3,2,1,0:T(8,128)(2,1)S(1)}, u32[]{:S(2)}, u32[]{:S(2)}) collective-permute-start(bf16[16,10,16,512]{3,2,1,0:T(8,128)(2,1)S(1)} %constant_dynamic-update-slice_fusion.7.near), channel_id=1, source_target_pairs={{0,4},{4,0},{8,12},{12,8},{16,20},{20,16},{24,28},{28,24},{1,5},{5... | collective-permute-start | bytes 7864328 | tf_op jit(solution)/shard_map/ppermute | solution.py:328
  64.0 14.6 %collective-permute-start.8 = (bf16[4,4,16,512]{3,2,1,0:T(8,128)(2,1)S(1)}, bf16[4,4,16,512]{3,2,1,0:T(8,128)(2,1)S(1)}, u32[]{:S(2)}, u32[]{:S(2)}) collective-permute-start(bf16[4,4,16,512]{3,2,1,0:T(8,128)(2,1)S(1)} %pad_maximum_fusion.2), channel_id=1, source_target_pairs={{0,24},{4,28},{8,16},{12,20},{16,8},{20,12},{24,0},{28,4},{1,25},{... | collective-permute-start | bytes 786440 | tf_op jit(solution)/shard_map/ppermute | solution.py:328
  65.7 12.9 %collective-permute-start.7 = (bf16[4,4,16,512]{3,2,1,0:T(8,128)(2,1)S(1)}, bf16[4,4,16,512]{3,2,1,0:T(8,128)(2,1)S(1)}, u32[]{:S(2)}, u32[]{:S(2)}) collective-permute-start(bf16[4,4,16,512]{3,2,1,0:T(8,128)(2,1)S(1)} %pad_maximum_fusion.2), channel_id=1, source_target_pairs={{0,16},{4,20},{8,24},{12,28},{16,0},{20,4},{24,8},{28,12},{1,17},{... | collective-permute-start | bytes 786440 | tf_op jit(solution)/shard_map/ppermute | solution.py:328
  67.0 11.5 %collective-permute-start.6 = (bf16[4,4,16,512]{3,2,1,0:T(8,128)(2,1)S(1)}, bf16[4,4,16,512]{3,2,1,0:T(8,128)(2,1)S(1)}, u32[]{:S(2)}, u32[]{:S(2)}) collective-permute-start(bf16[4,4,16,512]{3,2,1,0:T(8,128)(2,1)S(1)} %pad_maximum_fusion.2), channel_id=1, source_target_pairs={{0,8},{4,12},{8,0},{12,4},{16,24},{20,28},{24,16},{28,20},{1,9},{5... | collective-permute-start | bytes 786440 | tf_op jit(solution)/shard_map/ppermute | solution.py:328
  78.7 21.9 %collective-permute-start.9 = (bf16[16,4,16,512]{3,2,1,0:T(8,128)(2,1)S(1)}, bf16[16,4,16,512]{3,2,1,0:T(8,128)(2,1)S(1)}, u32[]{:S(2)}, u32[]{:S(2)}) collective-permute-start(bf16[16,4,16,512]{3,2,1,0:T(8,128)(2,1)S(1)} %constant_dynamic-update-slice_fusion.refs_4_.near), channel_id=1, source_target_pairs={{0,4},{4,0},{8,12},{12,8},{16,20},{20,16},{24,28},{28,24},{1,5},{5... | collective-permute-start | bytes 3145736 | tf_op jit(solution)/shard_map/ppermute | solution.py:328
  78.8 10.9 %collective-permute-start.2 = (bf16[256,512]{1,0:T(8,128)(2,1)S(1)}, bf16[256,512]{1,0:T(8,128)(2,1)S(1)}, u32[]{:S(2)}, u32[]{:S(2)}) collective-permute-start(bf16[256,512]{1,0:T(8,128)(2,1)S(1)} %pad_maximum_fusion.1.refs_0_), channel_id=1, source_target_pairs={{0,3},{1,2},{4,7},{5,6},{8,11},{9,10},{12,15},{13,14},{16,19},{17,... | collective-permute-start | bytes 786440 | tf_op jit(solution)/shard_map/ppermute | solution.py:328
  83.0 12.3 %collective-permute-start.1 = (bf16[256,512]{1,0:T(8,128)(2,1)S(1)}, bf16[256,512]{1,0:T(8,128)(2,1)S(1)}, u32[]{:S(2)}, u32[]{:S(2)}) collective-permute-start(bf16[256,512]{1,0:T(8,128)(2,1)S(1)} %pad_maximum_fusion.1.refs_0_), channel_id=1, source_target_pairs={{0,2},{1,3},{4,6},{5,7},{8,10},{9,11},{12,14},{13,15},{16,18},{17,... | collective-permute-start | bytes 786440 | tf_op jit(solution)/shard_map/ppermute | solution.py:328
  84.4 16.2 %collective-permute-start = (bf16[256,512]{1,0:T(8,128)(2,1)S(1)}, bf16[256,512]{1,0:T(8,128)(2,1)S(1)}, u32[]{:S(2)}, u32[]{:S(2)}) collective-permute-start(bf16[256,512]{1,0:T(8,128)(2,1)S(1)} %pad_maximum_fusion.1.refs_0_), channel_id=1, source_target_pairs={{0,1},{2,3},{4,5},{6,7},{8,9},{10,11},{12,13},{14,15},{16,17},{18,... | collective-permute-start | bytes 786440 | tf_op jit(solution)/shard_map/ppermute | solution.py:328
  121.5 41.2 %collective-permute-start.27 = (bf16[16,10,16,512]{3,2,1,0:T(8,128)(2,1)}, bf16[16,10,16,512]{3,2,1,0:T(8,128)(2,1)S(1)}, u32[]{:S(2)}, u32[]{:S(2)}) collective-permute-start(bf16[16,10,16,512]{3,2,1,0:T(8,128)(2,1)} %get-tuple-element.80), channel_id=1, source_target_pairs={{0,4},{4,0},{8,12},{12,8},{16,20},{20,16},{24,28},{28,24},{1,5},{5... | collective-permute-start | bytes 7864328 | tf_op jit(solution)/shard_map/ppermute | solution.py:328
  141.8 13.9 %collective-permute-start.22 = (bf16[4,4,16,512]{3,2,1,0:T(8,128)(2,1)S(1)}, bf16[4,4,16,512]{3,2,1,0:T(8,128)(2,1)S(1)}, u32[]{:S(2)}, u32[]{:S(2)}) collective-permute-start(bf16[4,4,16,512]{3,2,1,0:T(8,128)(2,1)S(1)} %get-tuple-element.73), channel_id=1, source_target_pairs={{0,16},{4,20},{8,24},{12,28},{16,0},{20,4},{24,8},{28,12},{1,17},{... | collective-permute-start | bytes 786440 | tf_op jit(solution)/shard_map/ppermute | solution.py:328
  142.5 15.2 %collective-permute-start.23 = (bf16[4,4,16,512]{3,2,1,0:T(8,128)(2,1)S(1)}, bf16[4,4,16,512]{3,2,1,0:T(8,128)(2,1)S(1)}, u32[]{:S(2)}, u32[]{:S(2)}) collective-permute-start(bf16[4,4,16,512]{3,2,1,0:T(8,128)(2,1)S(1)} %get-tuple-element.74), channel_id=1, source_target_pairs={{0,24},{4,28},{8,16},{12,20},{16,8},{20,12},{24,0},{28,4},{1,25},{... | collective-permute-start | bytes 786440 | tf_op jit(solution)/shard_map/ppermute | solution.py:328
  143.9 26.8 %collective-permute-start.17 = (bf16[256,512]{1,0:T(8,128)(2,1)S(1)}, bf16[256,512]{1,0:T(8,128)(2,1)S(1)}, u32[]{:S(2)}, u32[]{:S(2)}) collective-permute-start(bf16[256,512]{1,0:T(8,128)(2,1)S(1)} %get-tuple-element.66), channel_id=1, source_target_pairs={{1,0},{3,2},{5,4},{7,6},{9,8},{11,10},{13,12},{15,14},{17,16},{19,... | collective-permute-start | bytes 786440 | tf_op jit(solution)/shard_map/ppermute | solution.py:328
  149.5 22.6 %collective-permute-start.18 = (bf16[256,512]{1,0:T(8,128)(2,1)S(1)}, bf16[256,512]{1,0:T(8,128)(2,1)S(1)}, u32[]{:S(2)}, u32[]{:S(2)}) collective-permute-start(bf16[256,512]{1,0:T(8,128)(2,1)S(1)} %get-tuple-element.67), channel_id=1, source_target_pairs={{2,0},{3,1},{6,4},{7,5},{10,8},{11,9},{14,12},{15,13},{18,16},{19,... | collective-permute-start | bytes 786440 | tf_op jit(solution)/shard_map/ppermute | solution.py:328
  155.7 18.0 %collective-permute-start.19 = (bf16[256,512]{1,0:T(8,128)(2,1)S(1)}, bf16[256,512]{1,0:T(8,128)(2,1)S(1)}, u32[]{:S(2)}, u32[]{:S(2)}) collective-permute-start(bf16[256,512]{1,0:T(8,128)(2,1)S(1)} %get-tuple-element.68), channel_id=1, source_target_pairs={{2,1},{3,0},{6,5},{7,4},{10,9},{11,8},{14,13},{15,12},{18,17},{19,... | collective-permute-start | bytes 786440 | tf_op jit(solution)/shard_map/ppermute | solution.py:328
  158.1 19.2 %collective-permute-start.24 = (bf16[1,4,16,512]{3,2,1,0:T(8,128)(2,1)S(1)}, bf16[1,4,16,512]{3,2,1,0:T(8,128)(2,1)S(1)}, u32[]{:S(2)}, u32[]{:S(2)}) collective-permute-start(bf16[1,4,16,512]{3,2,1,0:T(8,128)(2,1)S(1)} %get-tuple-element.76), channel_id=1, source_target_pairs={{0,1},{1,0},{2,3},{3,2},{4,5},{5,4},{6,7},{7,6},{8,9},{9,8},{10,11... | collective-permute-start | bytes 196616 | tf_op jit(solution)/shard_map/ppermute | solution.py:328
  170.0 17.7 %collective-permute-start.28 = (bf16[4,10,16,512]{3,2,1,0:T(8,128)(2,1)S(1)}, bf16[4,10,16,512]{3,2,1,0:T(8,128)(2,1)S(1)}, u32[]{:S(2)}, u32[]{:S(2)}) collective-permute-start(bf16[4,10,16,512]{3,2,1,0:T(8,128)(2,1)S(1)} %get-tuple-element.82), channel_id=1, source_target_pairs={{0,8},{4,12},{8,0},{12,4},{16,24},{20,28},{24,16},{28,20},{1,9},{5... | collective-permute-start | bytes 1966088 | tf_op jit(solution)/shard_map/ppermute | solution.py:328
  170.7 27.5 %collective-permute-start.29 = (bf16[4,10,16,512]{3,2,1,0:T(8,128)(2,1)S(1)}, bf16[4,10,16,512]{3,2,1,0:T(8,128)(2,1)S(1)}, u32[]{:S(2)}, u32[]{:S(2)}) collective-permute-start(bf16[4,10,16,512]{3,2,1,0:T(8,128)(2,1)S(1)} %get-tuple-element.83), channel_id=1, source_target_pairs={{0,16},{4,20},{8,24},{12,28},{16,0},{20,4},{24,8},{28,12},{1,17},{... | collective-permute-start | bytes 1966088 | tf_op jit(solution)/shard_map/ppermute | solution.py:328
  172.1 26.1 %collective-permute-start.30 = (bf16[4,10,16,512]{3,2,1,0:T(8,128)(2,1)S(1)}, bf16[4,10,16,512]{3,2,1,0:T(8,128)(2,1)S(1)}, u32[]{:S(2)}, u32[]{:S(2)}) collective-permute-start(bf16[4,10,16,512]{3,2,1,0:T(8,128)(2,1)S(1)} %get-tuple-element.84), channel_id=1, source_target_pairs={{0,24},{4,28},{8,16},{12,20},{16,8},{20,12},{24,0},{28,4},{1,25},{... | collective-permute-start | bytes 1966088 | tf_op jit(solution)/shard_map/ppermute | solution.py:328
  199.3 12.8 %collective-permute-start.32 = (bf16[1,10,16,512]{3,2,1,0:T(8,128)(2,1)S(1)}, bf16[1,10,16,512]{3,2,1,0:T(8,128)(2,1)S(1)}, u32[]{:S(2)}, u32[]{:S(2)}) collective-permute-start(bf16[1,10,16,512]{3,2,1,0:T(8,128)(2,1)S(1)} %get-tuple-element.87), channel_id=1, source_target_pairs={{0,2},{1,3},{2,0},{3,1},{4,6},{5,7},{6,4},{7,5},{8,10},{9,11},{10,... | collective-permute-start | bytes 491528 | tf_op jit(solution)/shard_map/ppermute | solution.py:328
  (27 other events, 465.3 us)

commit v2 on v1

v2 whole, which is shorter than its diff:
```python
import functools
import math

import jax
import jax.numpy as jnp
from jax import lax
from jax.experimental import pallas as pl
from jax.experimental.pallas import tpu as pltpu
from jax.sharding import PartitionSpec as P

HEAD_DIM = 64
LANES = 128
BAND = 16
MIB = 1024 * 1024
BF = jnp.bfloat16
F32 = jnp.float32
VMEM = pl.BlockSpec(memory_space=pltpu.VMEM)
SMEM = pl.BlockSpec(memory_space=pltpu.SMEM)
HBM = pl.BlockSpec(memory_space=pltpu.HBM)
NN = (((1,), (0,)), ((), ()))
NT = (((1,), (1,)), ((), ()))
TN = (((0,), (0,)), ((), ()))


def mm(left, right, dims=NN, precision=None):
    return lax.dot_general(left, right, dims, precision, preferred_element_type=F32)


def call(body, outs, ins, scratch, cost, name, limit):
    flops, moved = cost
    return pl.pallas_call(
        body,
        out_shape=[jax.ShapeDtypeStruct(shape, dtype) for shape, dtype, _ in outs],
        out_specs=[spec for _, _, spec in outs],
        in_specs=ins,
        scratch_shapes=scratch,
        compiler_params=pltpu.CompilerParams(vmem_limit_bytes=limit * MIB),
        cost_estimate=pl.CostEstimate(flops=flops, bytes_accessed=moved, transcendentals=0),
        name=name,
    )


def slot_rows(core, layer, place, me):
    device = lax.bitwise_xor(jnp.int32((layer * 2 + core) * 4 + place), me)
    return pl.ds(pl.multiple_of(device * BAND, BAND), BAND)


def each_slot(parts, by_layer, me):
    for i, part in enumerate(parts):
        core, outer = divmod(i, len(parts) // 2)
        for inner in range(part.shape[0]):
            layer, place = (outer, inner) if by_layer else (inner, outer)
            yield part.at[inner], slot_rows(core, layer, place, me)


def fetch_weights(parts, by_layer, weights, sem, me):
    for slot, rows in each_slot(parts, by_layer, me):
        pltpu.make_async_copy(slot, weights.at[:, rows, :], sem).start()


def cut_last(parts):
    return list(parts[:-1]) + [parts[-1].at[pl.ds(4 * k, 4)] for k in range(len(parts) - 1)]


def store_slots(grads, parts, by_layer, sem, me):
    for slot, rows in each_slot(cut_last(parts), by_layer, me):
        pltpu.make_async_copy(grads.at[:, rows, :], slot, sem).start()
    pltpu.make_async_copy(grads, grads, sem).wait()


def pick(seq, *options):
    chosen = options[-1]
    for i in range(len(options) - 2, -1, -1):
        chosen = jnp.where(seq == i, options[i], chosen)
    return chosen


def pad_rows(part, rows):
    return jnp.concatenate([part, jnp.zeros((rows - part.shape[0], part.shape[1]), part.dtype)], 0)


def pack_body(with_weights, ids, *refs):
    seq = ids[1]
    count = 11 if with_weights else 4
    sources, refs = (refs[:count], refs[count:])
    if with_weights:
        norms, refs = (refs[0], refs[1:])
    outs = 6 if with_weights else 4
    targets, held, sem = (refs[:outs], refs[outs : outs + count], refs[-1])
    pay1, pay_u2, pay_u3, pay_d = targets[:4]
    ins = [
        pltpu.make_async_copy(source, there, sem.at[i])
        for i, (source, there) in enumerate(zip(sources, held))
    ]
    for item in ins:
        item.start()
    long_tok, short_tok, long_cot, short_cot = held[:4]
    n_long, n_short = (long_tok.shape[1], short_tok.shape[1])
    copies = []

    def copy(source, target):
        item = pltpu.make_async_copy(source, target, sem.at[len(copies)])
        item.start()
        copies.append(item)

    if with_weights:
        early, late = targets[4:]
        row = refs[outs + count]
        width = early.shape[2]
        shard = norms.shape[1]
        col = lax.broadcasted_iota(jnp.int32, (shard, width), 1)
        at = lax.broadcasted_iota(jnp.int32, (shard, width), 0)
        spread = (col == at + ids[0] * shard).astype(BF)
        row[...] = pad_rows(mm(norms[...], spread), BAND).astype(BF)
    for item in ins:
        item.wait()
    if with_weights:
        wq, wk, wv, pos, wo, up, down = held[4:]
        chunks = up.shape[1] // width
        for i, weight in enumerate((wq, wk, wv, pos)):
            copy(weight, early.at[i])
        copy(wo, late.at[0])
        for c in range(chunks):
            cols = pl.ds(c * width, width)
            copy(up.at[:, cols], late.at[1 + c])
            copy(down.at[:, cols], late.at[1 + chunks + c])
        copy(row, late.at[1 + 2 * chunks])
    first = (seq > 0).astype(jnp.int32)
    for i, (longs, shorts) in enumerate(((long_tok, short_tok), (long_cot, short_cot))):
        copy(shorts.at[first], pay_u2.at[pl.ds(i * n_short, n_short), :])
        copy(shorts.at[1 - first], pay_u3.at[pl.ds(i * n_short, n_short), :])
        copy(longs.at[0], pay_d.at[pl.ds(i * n_long, n_long), :])
    last = len(copies)

    def both(sources, rows):
        ends = [
            pltpu.make_async_copy(source, pay1.at[pl.ds(i * n_long, rows), :], sem.at[last + i])
            for i, source in enumerate(sources)
        ]
        for item in ends:
            item.start()
        for item in ends:
            item.wait()

    @pl.when(seq < 2)
    def _():
        both((long_tok.at[0], long_cot.at[0]), n_long)

    @pl.when(seq > 1)
    def _():
        both((short_tok.at[3 - seq], short_cot.at[3 - seq]), n_short)

    for item in copies:
        item.wait()


def stack_heads(block, lane):
    zero = jnp.zeros_like(block)
    return jnp.concatenate([jnp.where(lane, block, zero), jnp.where(lane, zero, block)], 0)


def join_heads(stacked, lane):
    half = stacked.shape[0] // 2
    return jnp.where(lane, stacked[:half], stacked[half:])


def head_lanes():
    return lax.broadcasted_iota(jnp.int32, (1, LANES), 1) < HEAD_DIM


def block_base(seq, k, size):
    owner = lax.bitwise_xor(seq, jnp.int32(k))
    return pl.multiple_of(owner * jnp.where(seq < 2, size, size // 2), size // 2)


def gather_queries(seq, source, target):
    size = source.shape[0] // 4
    half = size // 2

    @pl.when(seq == 0)
    def _():
        target[...] = source[: 2 * size, :]

    @pl.when(seq == 1)
    def _():
        target[:size, :] = source[3 * size :, :]
        target[size:, :] = source[2 * size : 3 * size, :]

    @pl.when(seq > 1)
    def _():
        for k in range(4):
            target[k * half : (k + 1) * half, :] = source[k * size : k * size + half, :]


def spread_queries(seq, value, target):
    size = target.shape[0] // 4
    half = size // 2

    @pl.when(seq == 0)
    def _():
        target[: 2 * size, :] += value

    @pl.when(seq == 1)
    def _():
        target[3 * size :, :] += value[:size]
        target[2 * size : 3 * size, :] += value[size:]

    @pl.when(seq > 1)
    def _():
        for k in range(4):
            target[k * size : k * size + half, :] += value[k * half : (k + 1) * half]


def attend_body(layers, ids, long_len, short_len, *refs):
    long_tok, short_tok, long_cot, short_cot, got1, got_u2, got_u3, got_d2, got_d3 = refs[:9]
    parts = refs[9 : 9 + 2 * layers]
    first_o, cot_o, low_o, lowq_o, q_o, k_o, v_o, probs_o, mix_o = refs[9 + 2 * layers : 18 + 2 * layers]
    weights, table, first, cots, sem = refs[18 + 2 * layers :]
    me, seq = (ids[0], ids[1])
    fetch_weights(parts, True, weights, sem, me)
    n_long, n_short = (long_tok.shape[1], short_tok.shape[1])
    longs = seq < 2
    for i, (target, whole, shorts) in enumerate(
        ((first, long_tok, short_tok), (cots, long_cot, short_cot))
    ):
        big = slice(i * n_long, (i + 1) * n_long)
        small = slice(i * n_short, (i + 1) * n_short)
        own_short = pad_rows(jnp.where(seq == 2, shorts[0], shorts[1]), n_long)
        blocks = (
            jnp.where(longs, whole[0], own_short),
            jnp.where(longs, got1[big, :], pad_rows(got1[i * n_long : i * n_long + n_short, :], n_long)),
            jnp.where(longs, got_d2[big, :], pad_rows(got_u2[small, :], n_long)),
            jnp.where(longs, got_d3[big, :], pad_rows(got_u3[small, :], n_long)),
        )
        for k, block in enumerate(blocks):
            target[k * n_long : (k + 1) * n_long, :] = block.astype(target.dtype)
    gather_queries(seq, cots, cot_o)
    pltpu.make_async_copy(weights, weights, sem).wait()
    table[...] = weights[3].astype(F32).T
    for k in range(4):
        rows = slice(k * n_long, (k + 1) * n_long)
        first[rows, :] += table[pl.ds(block_base(seq, k, n_long), n_long), :]
    gather_queries(seq, first, first_o)
    lowq_o[...] = first_o[...].astype(BF)
    low_o[...] = first[...].astype(BF)
    k_o[...] = mm(low_o[...], weights[1]).astype(BF)
    v_o[...] = mm(low_o[...], weights[2]).astype(BF)
    q_o[...] = mm(lowq_o[...], weights[0]).astype(BF) * BF(HEAD_DIM**-0.5)
    rows, keys = (first_o.shape[0], first.shape[0])
    row = lax.broadcasted_iota(jnp.int32, (rows, 1), 0)
    row_pos = jnp.where(
        longs,
        row + seq * rows,
        lax.bitwise_xor(row // n_short, jnp.full_like(row, seq)) * n_short + row % n_short,
    )
    row_pos = jnp.concatenate([row_pos, row_pos], 0)
    col = lax.broadcasted_iota(jnp.int32, (1, keys), 1)
    owner = lax.bitwise_xor(col // n_long, jnp.full_like(col, seq))
    inner = col % n_long
    col_pos = jnp.where(longs, owner * n_long + inner, owner * n_short + inner)
    length = pick(seq, long_len[0], long_len[0], short_len[0], short_len[1])
    seen = (col_pos < length) & (longs | (inner < n_short))
    col_pos = jnp.where(seen, col_pos, jnp.int32(1 << 20))
    allowed = col_pos <= row_pos
    lane = head_lanes()
    for g in range(first_o.shape[1] // LANES):
        cols = slice(g * LANES, (g + 1) * LANES)
        scores = mm(stack_heads(q_o[:, cols], lane), k_o[:, cols], NT)
        scores = jnp.where(allowed, scores, -1e30)
        shifted = jnp.exp(scores - jnp.max(scores, axis=-1, keepdims=True))
        probs_o[g] = (shifted / jnp.sum(shifted, axis=-1, keepdims=True)).astype(BF)
        mix_o[:, cols] = join_heads(mm(probs_o[g], v_o[:, cols]), lane).astype(BF)


def norm_parts(values):
    mean = jnp.mean(values, axis=-1, keepdims=True)
    centred = values - mean
    scale = lax.rsqrt(jnp.mean(centred * centred, axis=-1, keepdims=True) + 1e-05)
    return centred * scale, scale


def norm_back(cot, gain, xhat, scale):
    scaled = cot * gain
    mean = jnp.mean(scaled, axis=-1, keepdims=True)
    inner = jnp.mean(scaled * xhat, axis=-1, keepdims=True)
    return scale * (scaled - mean - xhat * inner)


def middle_body(layers, ids, first, mixed, cot, *refs):
    parts = refs[: 2 * layers]
    block_outs = refs[2 * layers : 2 * layers + 4]
    gsum_o, gmix_o = refs[2 * layers + 4 : 2 * layers + 6]
    grad_parts = refs[2 * layers + 6 : 3 * layers + 7]
    weights, grads, act, slope, blocks, sem = refs[3 * layers + 7 :]
    me, seq = (ids[0], ids[1])
    fetch_weights(parts, True, weights, sem, me)
    blocks[...] = jnp.zeros_like(blocks)
    pltpu.make_async_copy(weights, weights, sem).wait()
    width = first.shape[1]
    chunks = (weights.shape[0] - 2) // 2
    norm = weights.shape[0] - 1
    vectors = jnp.sum(weights[norm].astype(F32).reshape(-1, BAND, width), axis=0)
    gain0, gain1, bias0, bias1 = (vectors[i : i + 1] for i in range(4))
    mixed_low = mixed[...]
    xhat0, scale0 = norm_parts(first[...] + mm(mixed_low, weights[0]))
    normed = xhat0 * gain0 + bias0
    normed_low = normed.astype(BF)
    second = normed
    for c in range(chunks):
        hidden = mm(normed_low, weights[1 + c])
        cdf = 0.5 + 0.5 * lax.erf(hidden * (0.5**0.5))
        slope[c] = cdf + hidden * jnp.exp(-0.5 * hidden * hidden) * ((2 * math.pi) ** -0.5)
        act[c] = (hidden * cdf).astype(BF)
        second = second + mm(act[c], weights[1 + chunks + c], NT)
    xhat1, scale1 = norm_parts(second)
    spread_queries(seq, xhat1 * gain1 + bias1, blocks)
    size = block_outs[0].shape[0]
    for k, target in enumerate(block_outs):
        target[...] = blocks[k * size : (k + 1) * size, :].astype(BF)
    cot_wide = cot[...].astype(F32)
    grad_second = norm_back(cot_wide, gain1, xhat1, scale1)
    second_low = grad_second.astype(BF)
    grad_normed = grad_second
    for c in range(chunks):
        hidden_low = (mm(second_low, weights[1 + chunks + c]) * slope[c]).astype(BF)
        grads[1 + chunks + c] = mm(second_low, act[c], TN).astype(BF)
        grads[1 + c] = mm(normed_low, hidden_low, TN).astype(BF)
        grad_normed = grad_normed + mm(hidden_low, weights[1 + c], NT)
    grad_sum = norm_back(grad_normed, gain0, xhat0, scale0)
    gsum_o[...] = grad_sum
    sum_low = grad_sum.astype(BF)
    gmix_o[...] = mm(sum_low, weights[0], NT).astype(BF)
    grads[0] = mm(mixed_low, sum_low, TN).astype(BF)
    terms = jnp.concatenate(
        [
            jnp.sum(grad_normed * xhat0, axis=0, keepdims=True),
            jnp.sum(cot_wide * xhat1, axis=0, keepdims=True),
            jnp.sum(grad_normed, axis=0, keepdims=True),
            jnp.sum(cot_wide, axis=0, keepdims=True),
            jnp.zeros((BAND - 4, width), F32),
        ],
        0,
    ).astype(BF)
    for d in range(width // BAND):
        grads[norm, d * BAND : (d + 1) * BAND, :] = terms
    store_slots(grads, grad_parts, True, sem, me)


def attend_back_body(gmix, q, k, v, probs_i, dq_o, dk_o, dv_o):
    lane = head_lanes()
    scale = HEAD_DIM**-0.5
    for g in range(gmix.shape[1] // LANES):
        cols = slice(g * LANES, (g + 1) * LANES)
        grads = stack_heads(gmix[:, cols], lane)
        queries = stack_heads(q[:, cols], lane)
        probs = probs_i[g]
        grad_probs = mm(grads, v[:, cols], NT)
        wide = probs.astype(F32)
        inner = jnp.sum(wide * grad_probs, axis=-1, keepdims=True)
        grad_scores = (wide * (grad_probs - inner)).astype(BF)
        grad_q = mm(grad_scores, k[:, cols])
        dq_o[:, cols] = (join_heads(grad_q, lane) * scale).astype(BF)
        dk_o[:, cols] = mm(grad_scores, queries, TN).astype(BF)
        dv_o[:, cols] = mm(probs, grads, TN).astype(BF)


def leave_body(layers, ids, low, lowq, dq, dk, dv, gsum, *refs):
    parts = refs[: 2 * layers]
    own_o, sent1_o, sent2_o, sent3_o = refs[2 * layers : 2 * layers + 4]
    grad_parts = refs[2 * layers + 4 : 3 * layers + 5]
    weights, grads, table, back, sem = refs[3 * layers + 5 :]
    me, seq = (ids[0], ids[1])
    fetch_weights(parts, True, weights, sem, me)
    grads[0] = mm(lowq[...], dq[...], TN).astype(BF)
    grads[1] = mm(low[...], dk[...], TN).astype(BF)
    grads[2] = mm(low[...], dv[...], TN).astype(BF)
    pltpu.make_async_copy(weights, weights, sem).wait()
    back[...] = mm(dk[...], weights[1], NT) + mm(dv[...], weights[2], NT)
    spread_queries(seq, gsum[...] + mm(dq[...], weights[0], NT), back)
    size = own_o.shape[0]
    table[...] = jnp.zeros_like(table)
    for k, target in enumerate((own_o, sent1_o, sent2_o, sent3_o)):
        piece = back[k * size : (k + 1) * size, :]
        target[...] = piece.astype(target.dtype)
        table[pl.ds(block_base(seq, k, size), size), :] += piece
    grads[3] = table[...].T.astype(BF)
    store_slots(grads, grad_parts, True, sem, me)


def return_rows(ids, *refs):
    seq = ids[1]
    for i in range(2):
        mine, one, two, three = (item[...].astype(F32) for item in refs[4 * i : 4 * i + 4])
        long_o, short_o = refs[8 + 2 * i : 10 + 2 * i]
        half = short_o.shape[1]
        long_o[0] = jnp.where(seq < 2, mine + one, two + three).astype(BF)
        mine, one, two, three = (item[:half] for item in (mine, one, two, three))
        short_o[0] = pick(seq, two, three, mine, one).astype(BF)
        short_o[1] = pick(seq, three, two, one, mine).astype(BF)


def four_body(*refs):
    ins, outs = (refs[:-4], refs[-4:])
    for place, out in enumerate(outs):
        total = ins[0][place].astype(F32)
        for item in ins[1:]:
            total = total + item[place].astype(F32)
        out[...] = total.astype(out.dtype)


def four_sums(parts, name):
    _, pieces, band, width = parts[0].shape
    step = 2
    block_in = pl.BlockSpec((4, step, band, width), lambda i: (0, i, 0, 0))
    block_out = pl.BlockSpec((step, band, width), lambda i: (i, 0, 0))
    return pl.pallas_call(
        four_body,
        grid=(pieces // step,),
        out_shape=[
            jax.ShapeDtypeStruct((pieces, band, width), F32 if place == 0 else BF)
            for place in range(4)
        ],
        in_specs=[block_in] * len(parts),
        out_specs=[block_out] * 4,
        compiler_params=pltpu.CompilerParams(vmem_limit_bytes=16 * MIB),
        name=name,
    )(*parts)


def finish_body(ids, *refs):
    late, early, rows = (refs[:4], refs[4:8], refs[8:16])
    row_outs, early_outs = (refs[16:20], refs[20:24])
    out_o, up_o, down_o, norm_o = refs[24:]
    width = out_o.shape[1]
    chunks = up_o.shape[1] // width

    def total(parts, i):
        own, one, two, three = parts
        return own[i] + (one[i].astype(F32) + two[i].astype(F32) + three[i].astype(F32))

    return_rows(ids, *rows, *row_outs)
    out_o[...] = total(late, 0)
    for c in range(chunks):
        up_o[:, c * width : (c + 1) * width] = total(late, 1 + c)
        down_o[:, c * width : (c + 1) * width] = total(late, 1 + chunks + c)
    shard = norm_o.shape[1]
    row = lax.broadcasted_iota(jnp.int32, (width, shard), 0)
    col = lax.broadcasted_iota(jnp.int32, (width, shard), 1)
    chosen = (row == col + ids[0] * shard).astype(F32)
    norm_o[...] = mm(total(late, 1 + 2 * chunks), chosen, NN, lax.Precision.HIGHEST)
    for i, out in enumerate(early_outs):
        out[...] = total(early, i)


def after(value, *others):
    return lax.optimization_barrier((value,) + others)[0]


def local(
    dp_count,
    seq_count,
    long_tokens,
    short_tokens,
    long_cot,
    short_cot,
    long_lengths,
    short_lengths,
    w_query,
    w_key,
    w_value,
    w_out,
    w_up,
    w_down,
    pos_table,
    norm_gain,
    norm_bias,
):
    width = w_key.shape[1]
    hidden = w_up.shape[1]
    chunks = hidden // width
    shard = w_key.shape[0]
    direct = shard == BAND and dp_count == 8
    layers = 4
    device = lax.axis_index("dp") * seq_count + lax.axis_index("seq")
    seq = lax.axis_index("seq")
    true_ids = jnp.stack([device, seq]).astype(jnp.int32)
    ids = true_ids if direct else jnp.stack([device * 0, seq]).astype(jnp.int32)
    n_long, n_short = (long_tokens.shape[1], short_tokens.shape[1])
    rows, keys = (2 * n_long, 4 * n_long)
    square = width * width
    early_pieces, late_pieces = (4, 2 + 2 * chunks)

    def swap_seq(value, mask, keep=lambda source, target: True):
        pairs = [(i, i ^ mask) for i in range(seq_count) if keep(i, i ^ mask)]
        return lax.ppermute(value, "seq", pairs)

    def swap_dp(value, mask):
        return lax.ppermute(value, "dp", [(i, i ^ mask) for i in range(dp_count)])

    acts = [long_tokens, short_tokens, long_cot, short_cot]
    packed = [
        ((2 * n_long, width), BF, HBM),
        ((2 * n_short, width), BF, HBM),
        ((2 * n_short, width), BF, HBM),
        ((2 * n_long, width), BF, HBM),
    ]
    own, specs, scratch = ([], [HBM] * 4, [])
    held = list(acts)
    if direct:
        own = [w_query, w_key, w_value, pos_table.T, w_out, w_up, w_down.T]
        held += own
        own.append(jnp.concatenate([norm_gain, norm_bias], 0))
        packed += [((count, BAND, width), BF, HBM) for count in (early_pieces, late_pieces)]
        specs += [HBM] * 7 + [VMEM]
        scratch = [pltpu.VMEM((BAND, width), BF)]
    pays = call(
        functools.partial(pack_body, direct),
        packed,
        [SMEM] + specs,
        [pltpu.VMEM(item.shape, BF) for item in held] + scratch + [pltpu.SemaphoreType.DMA((32,))],
        (0, 4 * MIB),
        "pack",
        60,
    )(true_ids, *acts, *own)
    pay1, pay_u2, pay_u3, pay_d = pays[:4]

    def to_slots(whole, by_layer):
        count = whole.shape[0]
        order = (2, 1, 3, 0, 4, 5) if by_layer else (2, 3, 1, 0, 4, 5)
        cut = whole.reshape(count, 4, 2, 4, BAND, width).transpose(*order)
        return [cut[core, outer] for core in range(2) for outer in range(4)]

    def slot_outs(pieces):
        near = ((4, pieces, BAND, width), BF, HBM)
        return [near] * layers + [((4 * layers, pieces, BAND, width), BF, HBM)]

    def from_slots(parts, by_layer):
        count = parts[0].shape[1]
        cut = jnp.concatenate(parts, 0).reshape(2, 4, 4, count, BAND, width)
        order = (3, 1, 0, 2, 4, 5) if by_layer else (3, 2, 0, 1, 4, 5)
        return cut.transpose(*order).reshape(count, width, width)

    def places(piece):
        return [piece] + [swap_seq(piece, k) for k in range(1, 4)]

    def spread(column):
        near = [column] + [swap_dp(column, 2 * k) for k in range(1, layers)]
        return near

    def cross(near):
        return list(near) + [swap_dp(part, 1) for part in near]

    if direct:
        early, late = pays[4:]
        early_places = places(early)
        pay1, pay_u2, pay_u3, pay_d, late = lax.optimization_barrier(
            (pay1, pay_u2, pay_u3, pay_d, late, *early_places)
        )[:5]
    up_only = lambda source, target: source < target and source < 2 and target > 1
    down_only = lambda source, target: source > 1 and target == 1
    got = [
        swap_seq(pay1, 1),
        swap_seq(pay_u2, 2, up_only),
        swap_seq(pay_u3, 3, up_only),
        swap_seq(pay_d, 2, down_only),
        swap_seq(pay_d, 3, down_only),
    ]
    if direct:
        late_places = places(late)
        early_near = spread(jnp.stack(early_places))
        late_column = after(jnp.stack(late_places), *early_near)
        early_full = cross(early_near)
        late_full = cross(spread(late_column))
    else:

        def columns(weight):
            return weight.reshape(weight.shape[0], chunks, width).transpose(1, 0, 2)

        def whole(pieces):
            return lax.all_gather(pieces, ("dp", "seq"), axis=1, tiled=True)

        early_full = to_slots(whole(jnp.stack([w_query, w_key, w_value, pos_table.T])), True)
        vectors = jnp.concatenate([norm_gain, norm_bias], 0)
        vectors = lax.all_gather(vectors, ("dp", "seq"), axis=1, tiled=True)
        vectors = jnp.pad(vectors, ((0, width - 4), (0, 0)))
        late_whole = whole(jnp.concatenate([w_out[None], columns(w_up), columns(w_down.T)], 0))
        late_full = to_slots(jnp.concatenate([late_whole, vectors[None]], 0), True)

    groups = width // LANES
    first, cots, low, low_queries, queries, key_rows, values, probs, mixed = call(
        functools.partial(attend_body, layers),
        [
            ((rows, width), F32, VMEM),
            ((rows, width), BF, VMEM),
            ((keys, width), BF, VMEM),
            ((rows, width), BF, VMEM),
            ((rows, width), BF, VMEM),
            ((keys, width), BF, VMEM),
            ((keys, width), BF, VMEM),
            ((groups, 2 * rows, keys), BF, VMEM),
            ((rows, width), BF, VMEM),
        ],
        [SMEM] * 3 + [VMEM] * 9 + [HBM] * (2 * layers),
        [
            pltpu.VMEM((early_pieces, width, width), BF),
            pltpu.VMEM((width, width), F32),
            pltpu.VMEM((keys, width), F32),
            pltpu.VMEM((keys, width), BF),
            pltpu.SemaphoreType.DMA,
        ],
        (8 * keys * square, 10 * MIB),
        "attend",
        24,
    )(ids, long_lengths, short_lengths, *acts, *got, *early_full)

    block = (n_long, width)
    middle_outs = call(
        functools.partial(middle_body, layers),
        [(block, BF, VMEM)] * 4
        + [((rows, width), F32, VMEM), ((rows, width), BF, VMEM)]
        + slot_outs(late_pieces),
        [SMEM] + [VMEM] * 3 + [HBM] * (2 * layers),
        [
            pltpu.VMEM((late_pieces, width, width), BF),
            pltpu.VMEM((late_pieces, width, width), BF),
            pltpu.VMEM((chunks, rows, width), BF),
            pltpu.VMEM((chunks, rows, width), F32),
            pltpu.VMEM((keys, width), F32),
            pltpu.SemaphoreType.DMA,
        ],
        (16 * rows * square * chunks, 20 * MIB),
        "middle",
        32,
    )(ids, first, mixed, cots, *late_full)
    out_blocks, (grad_sum, grad_mixed) = (middle_outs[:4], middle_outs[4:6])
    late_parts = middle_outs[6:]

    def core_sums(parts, arrived):
        return [
            (parts[k].astype(F32) + arrived[4 * k : 4 * k + 4].astype(F32)).astype(BF)
            for k in range(1, layers)
        ]

    if direct:
        late_arrived = swap_dp(late_parts[-1], 1)

    grad_q, grad_k, grad_v = call(
        attend_back_body,
        [
            ((rows, width), BF, VMEM),
            ((keys, width), BF, VMEM),
            ((keys, width), BF, VMEM),
        ],
        [VMEM] * 5,
        [],
        (8 * keys * square, 8 * MIB),
        "attend_back",
        24,
    )(grad_mixed, queries, key_rows, values, probs)
    leave_outs = call(
        functools.partial(leave_body, layers),
        [(block, F32, VMEM)] + [(block, BF, VMEM)] * 3 + slot_outs(early_pieces),
        [SMEM] + [VMEM] * 6 + [HBM] * (2 * layers),
        [
            pltpu.VMEM((early_pieces, width, width), BF),
            pltpu.VMEM((early_pieces, width, width), BF),
            pltpu.VMEM((width, width), F32),
            pltpu.VMEM((keys, width), F32),
            pltpu.SemaphoreType.DMA,
        ],
        (10 * keys * square, 8 * MIB),
        "leave",
        24,
    )(ids, low, low_queries, grad_q, grad_k, grad_v, grad_sum, *early_full)
    grad_blocks, early_parts = (leave_outs[:4], leave_outs[4:])

    def rows_back(blocks):
        back = lambda source, target: (source > 1 and target < 2) or (source == 1 and target > 1)
        return [swap_seq(blocks[1], 1)] + [swap_seq(blocks[k], k, back) for k in (2, 3)]

    got = rows_back(grad_blocks)
    got_out = rows_back(out_blocks)
    row_ins = [grad_blocks[0], *got, out_blocks[0], *got_out]
    row_outs = [(item.shape, BF, VMEM) for item in (long_tokens, short_tokens)] * 2
    if direct:
        late_sums = core_sums(late_parts, late_arrived)
        late_layers = [swap_dp(part, 2 * k) for k, part in enumerate(late_sums, 1)]
        early_far = after(early_parts[-1], *late_sums)
        early_arrived = swap_dp(early_far, 1)
        early_sums = core_sums(early_parts, early_arrived)
        late_layers, early_sums, got = lax.optimization_barrier((late_layers, early_sums, got))
        row_ins[1:4] = got
        late_cut = four_sums([late_parts[0], late_arrived] + late_layers, "late_sum")
        early_layers = [swap_dp(part, 2 * k) for k, part in enumerate(early_sums, 1)]
        late_ends = [late_cut[0]] + [swap_seq(late_cut[k], k) for k in range(1, 4)]
        late_ends, early_layers = lax.optimization_barrier((late_ends, early_layers))
        early_cut = four_sums([early_parts[0], early_arrived] + early_layers, "early_sum")
        early_ends = [early_cut[0]] + [swap_seq(early_cut[k], k) for k in range(1, 4)]
        ends = call(
            finish_body,
            row_outs
            + [((shard, width), F32, VMEM)] * 5
            + [((shard, hidden), F32, VMEM)] * 2
            + [((BAND, shard), F32, VMEM)],
            [SMEM] + [VMEM] * 16,
            [],
            (0, MIB),
            "finish",
            16,
        )(ids, *late_ends, *early_ends, *row_ins)
        row_grads, early_sum, (grad_out, grad_up, grad_down, norms) = (ends[:4], ends[4:8], ends[8:])
    else:

        def scatter(parts, by_layer):
            wide = from_slots(parts, by_layer).astype(F32)
            return lax.psum_scatter(wide, ("dp", "seq"), scatter_dimension=1, tiled=True)

        def join(pieces):
            return pieces.transpose(1, 0, 2).reshape(shard, hidden)

        late_sum = scatter(late_parts, True)
        early_sum = scatter(early_parts, True)
        grad_out, grad_up, grad_down = (
            late_sum[0],
            join(late_sum[1 : 1 + chunks]),
            join(late_sum[1 + chunks : 1 + 2 * chunks]),
        )
        norms = lax.psum(from_slots(late_parts, True)[-1, :BAND].astype(F32), ("dp", "seq"))
        norms = lax.dynamic_slice(norms, (0, device * shard), (BAND, shard))
        row_grads = call(
            return_rows, row_outs, [SMEM] + [VMEM] * 8, [], (0, MIB), "return", 16
        )(ids, *row_ins)
    long_grad, short_grad, long_out, short_out = row_grads
    return (
        long_out,
        short_out,
        long_grad,
        short_grad,
        early_sum[0],
        early_sum[1],
        early_sum[2],
        grad_out,
        grad_up,
        grad_down.T,
        early_sum[3].T,
        norms[:2],
        norms[2:4],
    )


def solution(mesh):
    rows = P(("dp", "seq"), None)
    cols = P(None, ("dp", "seq"))
    acts = P("dp", "seq", None)
    return jax.shard_map(
        functools.partial(local, mesh.shape["dp"], mesh.shape["seq"]),
        mesh=mesh,
        in_specs=(acts,) * 4 + (P("dp"),) * 2 + (rows,) * 5 + (cols,) * 4,
        out_specs=(acts,) * 4 + (rows,) * 5 + (cols,) * 4,
        check_vma=False,
    )
```

time: 215 us -> 172 us (0.80)
  waiting for transfers between devices: 103 us -> 83.7 us
  local copies, waits for them, and re-layouts: 13.2 us -> 0.62 us
  Pallas kernels: 38 us -> 27.6 us
  starting transfers between devices: 56.2 us -> 52.7 us
  other arithmetic: 2.66 us -> 4.93 us
    ppermute x34 -> x45, waiting for transfers between devices: 103 us -> 83.7 us  [the longest x23 52.9 us: swap_seq(): return lax.ppermute(value, 'seq', pairs)]
    pallas_call x8, Pallas kernels: 38 us -> 27.6 us  [the longest x1 8.7 us: local(): call(functools.partial(middle_body, layers), [(block, BF, VMEM)] * 4 + [(...]
    unnamed x45 -> x18, local copies, waits for them, and re-layouts: 7.28 us -> 0.05 us
    ppermute x34 -> x45, starting transfers between devices: 56.2 us -> 52.7 us  [the longest x23 35.7 us: swap_seq(): return lax.ppermute(value, 'seq', pairs)]
  transfers between devices with their start and end apart: 34 -> 45, of which waited for: 19 -> 19; matrix products, arithmetic and copies ran while one was open for 2% -> 1% of each run, Pallas kernels for 12% -> 8%
where the time goes in v2:
time: 172 us; the launch traced here: 171 us
  waiting for transfers between devices  83.7 us (49%)
  starting transfers between devices  52.7 us (31%)
  Pallas kernels  27.6 us (16%)
  other arithmetic  4.93 us (3%)
    ppermute x23, waiting for transfers between devices, swap_seq(): return lax.ppermute(value, 'seq', pairs)  52.9 us
    ppermute x23, starting transfers between devices, swap_seq(): return lax.ppermute(value, 'seq', pairs)  35.7 us
    ppermute x22, waiting for transfers between devices, swap_dp(): return lax.ppermute(value, 'dp', [(i, i ^ mask) for i in range(dp_count)])  30.8 us
    ppermute x22, starting transfers between devices, swap_dp(): return lax.ppermute(value, 'dp', [(i, i ^ mask) for i in range(dp_count)])  17 us
    pallas_call x1, Pallas kernels, local(): call(functools.partial(middle_body, layers), [(block, BF, VMEM)] * 4 + [(...  8.7 us
    pallas_call x1, Pallas kernels, local(): call(functools.partial(attend_body, layers), [((rows, width), F32, VMEM),...  4.89 us
    pallas_call x1, Pallas kernels, local(): call(functools.partial(leave_body, layers), [(block, F32, VMEM)] + [(bloc...  4.41 us
    pallas_call x1, Pallas kernels, local(): call(attend_back_body, [((rows, width), BF, VMEM), ((keys, width), BF, VM...  3.44 us
  transfers between devices with their start and end apart: 45, of which 19 were waited for; matrix products, arithmetic and copies ran while one was open for 1% of the time, Pallas kernels for 8%

profile of v2, /device:TPU:0, one launch (start us, length us, event | category | flops | bytes accessed | tf_op | source)
XLA Modules:
  0.0 171.2 jit_solution(1069729635663334403)
XLA Ops:
  2.6 3.2 %pack.1 = (bf16[256,512]{1,0:T(8,128)(2,1)}, bf16[128,512]{1,0:T(8,128)(2,1)}, bf16[128,512]{1,0:T(8,128)(2,1)}, bf16[256,512]{1,0:T(8,128)(2,1)}, bf16[4,16,512...) custom-call(s32[2]{0:T(128)} %pad_add_fusion.ids, bf16[1,128,512]{2,1,0:T(8,128)(2,1)} %refs_0_.3, ...), custom_call_target="tpu_custom_call" | custom-call | bytes 4194304 | tf_op jit(solution)/shard_map/pack/pallas_call | solution.py:516
  5.8 5.1 %collective-permute-start.2 = (bf16[4,16,512]{2,1,0:T(8,128)(2,1)}, bf16[4,16,512]{2,1,0:T(8,128)(2,1)S(1)}, u32[]{:S(2)}, u32[]{:S(2)}) collective-permute-start(bf16[4,16,512]{2,1,0:T(8,128)(2,1)} %get-tuple-element.99), channel_id=1, source_target_pairs={{0,3},{1,2},{2,1},{3,0},{4,7},{5,6},{6,5},{7,4},{8,11},{9,10},{10,... | collective-permute-start | bytes 196616 | tf_op jit(solution)/shard_map/ppermute | solution.py:495
  13.7 3.0 %collective-permute-done.1 = bf16[4,16,512]{2,1,0:T(8,128)(2,1)S(1)} collective-permute-done((bf16[4,16,512]{2,1,0:T(8,128)(2,1)}, bf16[4,16,512]{2,1,0:T(8,128)(2,1)S(1)}, u32[]{:S(2)}, u32[]{:S(2)}) %collective-permute-start.1) | collective-permute-done | bytes 65568 | tf_op jit(solution)/shard_map/ppermute | solution.py:495
  16.7 2.7 %collective-permute-start.17 = (bf16[10,16,512]{2,1,0:T(8,128)(2,1)}, bf16[10,16,512]{2,1,0:T(8,128)(2,1)S(1)}, u32[]{:S(2)}, u32[]{:S(2)}) collective-permute-start(bf16[10,16,512]{2,1,0:T(8,128)(2,1)} %get-tuple-element.107), channel_id=1, source_target_pairs={{0,3},{1,2},{2,1},{3,0},{4,7},{5,6},{6,5},{7,4},{8,11},{9,10},{10,... | collective-permute-start | bytes 491528 | tf_op jit(solution)/shard_map/ppermute | solution.py:495
  22.0 2.5 %collective-permute-start.10 = (bf16[4,4,16,512]{3,2,1,0:T(8,128)(2,1)S(1)}, bf16[4,4,16,512]{3,2,1,0:T(8,128)(2,1)S(1)}, u32[]{:S(2)}, u32[]{:S(2)}) collective-permute-start(bf16[4,4,16,512]{3,2,1,0:T(8,128)(2,1)S(1)} %pad_maximum_fusion.1.refs_9_.refs_0_), channel_id=1, source_target_pairs={{0,24},{4,28},{8,16},{12,20},{16,8},{20,12},{24,0},{28,4},{1,25},{... | collective-permute-start | bytes 786440 | tf_op jit(solution)/shard_map/ppermute | solution.py:498
  27.4 5.9 %collective-permute-done.16 = bf16[10,16,512]{2,1,0:T(8,128)(2,1)S(1)} collective-permute-done((bf16[10,16,512]{2,1,0:T(8,128)(2,1)}, bf16[10,16,512]{2,1,0:T(8,128)(2,1)S(1)}, u32[]{:S(2)}, u32[]{:S(2)}) %collective-permute-start.16) | collective-permute-done | bytes 163872 | tf_op jit(solution)/shard_map/ppermute | solution.py:495
  36.7 2.5 %collective-permute-start.5 = (bf16[128,512]{1,0:T(8,128)(2,1)S(1)}, bf16[128,512]{1,0:T(8,128)(2,1)S(1)}, u32[]{:S(2)}, u32[]{:S(2)}) collective-permute-start(bf16[128,512]{1,0:T(8,128)(2,1)S(1)} %copy-done.8), channel_id=1, source_target_pairs={{0,3},{1,2},{4,7},{5,6},{8,11},{9,10},{12,15},{13,14},{16,19},{17,... | collective-permute-start | bytes 393224 | tf_op jit(solution)/shard_map/ppermute | solution.py:495
  39.2 2.5 %collective-permute-start.20 = (bf16[4,10,16,512]{3,2,1,0:T(8,128)(2,1)S(1)}, bf16[4,10,16,512]{3,2,1,0:T(8,128)(2,1)S(1)}, u32[]{:S(2)}, u32[]{:S(2)}) collective-permute-start(bf16[4,10,16,512]{3,2,1,0:T(8,128)(2,1)S(1)} %pad_maximum_fusion.refs_0_), channel_id=1, source_target_pairs={{0,24},{4,28},{8,16},{12,20},{16,8},{20,12},{24,0},{28,4},{1,25},{... | collective-permute-start | bytes 1966088 | tf_op jit(solution)/shard_map/ppermute | solution.py:498
  42.8 3.9 %collective-permute-start.3 = (bf16[256,512]{1,0:T(8,128)(2,1)S(1)}, bf16[256,512]{1,0:T(8,128)(2,1)S(1)}, u32[]{:S(2)}, u32[]{:S(2)}) collective-permute-start(bf16[256,512]{1,0:T(8,128)(2,1)S(1)} %copy-done.7), channel_id=1, source_target_pairs={{0,1},{1,0},{2,3},{3,2},{4,5},{5,4},{6,7},{7,6},{8,9},{9,8},{10,11... | collective-permute-start | bytes 786440 | tf_op jit(solution)/shard_map/ppermute | solution.py:495
  47.4 5.5 %collective-permute-done.3.refs_4_ = bf16[256,512]{1,0:T(8,128)(2,1)S(1)} collective-permute-done((bf16[256,512]{1,0:T(8,128)(2,1)S(1)}, bf16[256,512]{1,0:T(8,128)(2,1)S(1)}, u32[]{:S(2)}, u32[]{:S(2)}) %collective-permute-start.3) | collective-permute-done | bytes 262176 | tf_op jit(solution)/shard_map/ppermute | solution.py:495
  54.2 3.6 %collective-permute-done.20.refs_3_ = bf16[4,10,16,512]{3,2,1,0:T(8,128)(2,1)S(1)} collective-permute-done((bf16[4,10,16,512]{3,2,1,0:T(8,128)(2,1)S(1)}, bf16[4,10,16,512]{3,2,1,0:T(8,128)(2,1)S(1)}, u32[]{:S(2)}, u32[]{:S(2)}) %collective-permute-start.20) | collective-permute-done | bytes 655392 | tf_op jit(solution)/shard_map/ppermute | solution.py:498
  57.8 13.3 %collective-permute-done.19.refs_2_ = bf16[4,10,16,512]{3,2,1,0:T(8,128)(2,1)S(1)} collective-permute-done((bf16[4,10,16,512]{3,2,1,0:T(8,128)(2,1)S(1)}, bf16[4,10,16,512]{3,2,1,0:T(8,128)(2,1)S(1)}, u32[]{:S(2)}, u32[]{:S(2)}) %collective-permute-start.19) | collective-permute-done | bytes 655392 | tf_op jit(solution)/shard_map/ppermute | solution.py:498
  71.7 2.8 %collective-permute-done.13.refs_15_.refs_6_ = bf16[4,4,16,512]{3,2,1,0:T(8,128)(2,1)S(1)} collective-permute-done((bf16[4,4,16,512]{3,2,1,0:T(8,128)(2,1)S(1)}, bf16[4,4,16,512]{3,2,1,0:T(8,128)(2,1)S(1)}, u32[]{:S(2)}, u32[]{:S(2)}) %collective-permute-start.13) | collective-permute-done | bytes 262176 | tf_op jit(solution)/shard_map/ppermute | solution.py:498
  76.1 4.9 %attend.1 = (f32[256,512]{1,0:T(8,128)S(1)}, bf16[256,512]{1,0:T(8,128)(2,1)S(1)}, bf16[512,512]{1,0:T(8,128)(2,1)S(1)}, bf16[256,512]{1,0:T(8,128)(2,1)S(1)}, b...) custom-call(s32[2]{0:T(128)S(1)} %copy-done.4, ...), custom_call_target="tpu_custom_call" | custom-call | flops 1073741824 | bytes 10485760 | tf_op jit(solution)/shard_map/attend/pallas_call | solution.py:590
  81.0 8.7 %middle.1 = (bf16[128,512]{1,0:T(8,128)(2,1)S(1)}, bf16[128,512]{1,0:T(8,128)(2,1)S(1)}, bf16[128,512]{1,0:T(8,128)(2,1)S(1)}, bf16[128,512]{1,0:T(8,128)(2,1)S(...) custom-call(s32[2]{0:T(128)S(1)} %copy-done.4, ...), custom_call_target="tpu_custom_call" | custom-call | flops 4294967296 | bytes 20971520 | tf_op jit(solution)/shard_map/middle/pallas_call | solution.py:617
  89.9 3.4 %attend_back.1 = (bf16[256,512]{1,0:T(8,128)(2,1)S(1)}, bf16[512,512]{1,0:T(8,128)(2,1)S(1)}, bf16[512,512]{1,0:T(8,128)(2,1)S(1)}) custom-call(bf16[256,512]{1,0:T(8,128)(2,1)S(1)} %get-tuple-element.116.gmix, bf16[256,512]{1,0:T(8,128)(2,1)S(1)} %get-tuple-element.117.q, bf16[512,512]{1,0:T(8,128)(2,1)S(1)} %get-tuple-element.118.k, ...), custom_call_target="tpu_custom_call" | custom-call | flops 1073741824 | bytes 8388608 | tf_op jit(solution)/shard_map/attend_back/pallas_call | solution.py:647
  93.4 4.4 %leave.1 = (f32[128,512]{1,0:T(8,128)S(1)}, bf16[128,512]{1,0:T(8,128)(2,1)S(1)}, bf16[128,512]{1,0:T(8,128)(2,1)S(1)}, bf16[128,512]{1,0:T(8,128)(2,1)S(1)}, bf...) custom-call(s32[2]{0:T(128)S(1)} %copy-done.4, ...), custom_call_target="tpu_custom_call" | custom-call | flops 1342177280 | bytes 8388608 | tf_op jit(solution)/shard_map/leave/pallas_call | solution.py:660
  103.5 4.1 %collective-permute-done.30.refs_9_ = bf16[128,512]{1,0:T(8,128)(2,1)S(1)} collective-permute-done((bf16[128,512]{1,0:T(8,128)(2,1)S(1)}, bf16[128,512]{1,0:T(8,128)(2,1)S(1)}, u32[]{:S(2)}, u32[]{:S(2)}) %collective-permute-start.30) | collective-permute-done | bytes 131104 | tf_op jit(solution)/shard_map/ppermute | solution.py:495
  110.5 10.2 %collective-permute-done.31.refs_10_ = bf16[128,512]{1,0:T(8,128)(2,1)S(1)} collective-permute-done((bf16[128,512]{1,0:T(8,128)(2,1)S(1)}, bf16[128,512]{1,0:T(8,128)(2,1)S(1)}, u32[]{:S(2)}, u32[]{:S(2)}) %collective-permute-start.31) | collective-permute-done | bytes 131104 | tf_op jit(solution)/shard_map/ppermute | solution.py:495
  120.7 10.1 %collective-permute-done.27.refs_3_ = bf16[4,10,16,512]{3,2,1,0:T(8,128)(2,1)S(1)} collective-permute-done((bf16[4,10,16,512]{3,2,1,0:T(8,128)(2,1)S(1)}, bf16[4,10,16,512]{3,2,1,0:T(8,128)(2,1)S(1)}, u32[]{:S(2)}, u32[]{:S(2)}) %collective-permute-start.27) | collective-permute-done | bytes 655392 | tf_op jit(solution)/shard_map/ppermute | solution.py:498
  139.7 8.6 %collective-permute-done.34.refs_2_ = bf16[10,16,512]{2,1,0:T(8,128)(2,1)S(1)} collective-permute-done((bf16[10,16,512]{2,1,0:T(8,128)(2,1)S(1)}, bf16[10,16,512]{2,1,0:T(8,128)(2,1)S(1)}, u32[]{:S(2)}, u32[]{:S(2)}) %collective-permute-start.34) | collective-permute-done | bytes 163872 | tf_op jit(solution)/shard_map/ppermute | solution.py:495
  151.3 4.8 %collective-permute-start.39 = (bf16[4,16,512]{2,1,0:T(8,128)(2,1)S(1)}, bf16[4,16,512]{2,1,0:T(8,128)(2,1)S(1)}, u32[]{:S(2)}, u32[]{:S(2)}) collective-permute-start(bf16[4,16,512]{2,1,0:T(8,128)(2,1)S(1)} %get-tuple-element.152), channel_id=1, source_target_pairs={{0,1},{1,0},{2,3},{3,2},{4,5},{5,4},{6,7},{7,6},{8,9},{9,8},{10,11... | collective-permute-start | bytes 196616 | tf_op jit(solution)/shard_map/ppermute | solution.py:495
  160.6 2.5 %collective-permute-done.44.refs_15_ = bf16[128,512]{1,0:T(8,128)(2,1)S(1)} collective-permute-done((bf16[128,512]{1,0:T(8,128)(2,1)S(1)}, bf16[128,512]{1,0:T(8,128)(2,1)S(1)}, u32[]{:S(2)}, u32[]{:S(2)}) %collective-permute-start.44) | collective-permute-done | bytes 131104 | tf_op jit(solution)/shard_map/ppermute | solution.py:495
  163.1 5.7 %collective-permute-done.40.refs_6_ = bf16[4,16,512]{2,1,0:T(8,128)(2,1)S(1)} collective-permute-done((bf16[4,16,512]{2,1,0:T(8,128)(2,1)S(1)}, bf16[4,16,512]{2,1,0:T(8,128)(2,1)S(1)}, u32[]{:S(2)}, u32[]{:S(2)}) %collective-permute-start.40) | collective-permute-done | bytes 65568 | tf_op jit(solution)/shard_map/ppermute | solution.py:495
  (99 shorter events, 45.4 us)
Async XLA Ops:
  19.4 13.8 %collective-permute-start.16 = (bf16[10,16,512]{2,1,0:T(8,128)(2,1)}, bf16[10,16,512]{2,1,0:T(8,128)(2,1)S(1)}, u32[]{:S(2)}, u32[]{:S(2)}) collective-permute-start(bf16[10,16,512]{2,1,0:T(8,128)(2,1)} %get-tuple-element.107), channel_id=1, source_target_pairs={{0,2},{1,3},{2,0},{3,1},{4,6},{5,7},{6,4},{7,5},{8,10},{9,11},{10,... | collective-permute-start | bytes 491528 | tf_op jit(solution)/shard_map/ppermute | solution.py:495
  19.4 16.1 %collective-permute-start.15 = (bf16[10,16,512]{2,1,0:T(8,128)(2,1)}, bf16[10,16,512]{2,1,0:T(8,128)(2,1)S(1)}, u32[]{:S(2)}, u32[]{:S(2)}) collective-permute-start(bf16[10,16,512]{2,1,0:T(8,128)(2,1)} %get-tuple-element.107), channel_id=1, source_target_pairs={{0,1},{1,0},{2,3},{3,2},{4,5},{5,4},{6,7},{7,6},{8,9},{9,8},{10,11... | collective-permute-start | bytes 491528 | tf_op jit(solution)/shard_map/ppermute | solution.py:495
  22.0 14.7 %collective-permute-start.10 = (bf16[4,4,16,512]{3,2,1,0:T(8,128)(2,1)S(1)}, bf16[4,4,16,512]{3,2,1,0:T(8,128)(2,1)S(1)}, u32[]{:S(2)}, u32[]{:S(2)}) collective-permute-start(bf16[4,4,16,512]{3,2,1,0:T(8,128)(2,1)S(1)} %pad_maximum_fusion.1.refs_9_.refs_0_), channel_id=1, source_target_pairs={{0,24},{4,28},{8,16},{12,20},{16,8},{20,12},{24,0},{28,4},{1,25},{... | collective-permute-start | bytes 786440 | tf_op jit(solution)/shard_map/ppermute | solution.py:498
  24.5 14.7 %collective-permute-start.9 = (bf16[4,4,16,512]{3,2,1,0:T(8,128)(2,1)S(1)}, bf16[4,4,16,512]{3,2,1,0:T(8,128)(2,1)S(1)}, u32[]{:S(2)}, u32[]{:S(2)}) collective-permute-start(bf16[4,4,16,512]{3,2,1,0:T(8,128)(2,1)S(1)} %pad_maximum_fusion.1.refs_9_.refs_0_), channel_id=1, source_target_pairs={{0,16},{4,20},{8,24},{12,28},{16,0},{20,4},{24,8},{28,12},{1,17},{... | collective-permute-start | bytes 786440 | tf_op jit(solution)/shard_map/ppermute | solution.py:498
  25.9 13.3 %collective-permute-start.8 = (bf16[4,4,16,512]{3,2,1,0:T(8,128)(2,1)S(1)}, bf16[4,4,16,512]{3,2,1,0:T(8,128)(2,1)S(1)}, u32[]{:S(2)}, u32[]{:S(2)}) collective-permute-start(bf16[4,4,16,512]{3,2,1,0:T(8,128)(2,1)S(1)} %pad_maximum_fusion.1.refs_9_.refs_0_), channel_id=1, source_target_pairs={{0,8},{4,12},{8,0},{12,4},{16,24},{20,28},{24,16},{28,20},{1,9},{5... | collective-permute-start | bytes 786440 | tf_op jit(solution)/shard_map/ppermute | solution.py:498
  39.2 18.6 %collective-permute-start.20 = (bf16[4,10,16,512]{3,2,1,0:T(8,128)(2,1)S(1)}, bf16[4,10,16,512]{3,2,1,0:T(8,128)(2,1)S(1)}, u32[]{:S(2)}, u32[]{:S(2)}) collective-permute-start(bf16[4,10,16,512]{3,2,1,0:T(8,128)(2,1)S(1)} %pad_maximum_fusion.refs_0_), channel_id=1, source_target_pairs={{0,24},{4,28},{8,16},{12,20},{16,8},{20,12},{24,0},{28,4},{1,25},{... | collective-permute-start | bytes 1966088 | tf_op jit(solution)/shard_map/ppermute | solution.py:498
  41.7 29.3 %collective-permute-start.19 = (bf16[4,10,16,512]{3,2,1,0:T(8,128)(2,1)S(1)}, bf16[4,10,16,512]{3,2,1,0:T(8,128)(2,1)S(1)}, u32[]{:S(2)}, u32[]{:S(2)}) collective-permute-start(bf16[4,10,16,512]{3,2,1,0:T(8,128)(2,1)S(1)} %pad_maximum_fusion.refs_0_), channel_id=1, source_target_pairs={{0,16},{4,20},{8,24},{12,28},{16,0},{20,4},{24,8},{28,12},{1,17},{... | collective-permute-start | bytes 1966088 | tf_op jit(solution)/shard_map/ppermute | solution.py:498
  42.3 28.9 %collective-permute-start.18 = (bf16[4,10,16,512]{3,2,1,0:T(8,128)(2,1)S(1)}, bf16[4,10,16,512]{3,2,1,0:T(8,128)(2,1)S(1)}, u32[]{:S(2)}, u32[]{:S(2)}) collective-permute-start(bf16[4,10,16,512]{3,2,1,0:T(8,128)(2,1)S(1)} %pad_maximum_fusion.refs_0_), channel_id=1, source_target_pairs={{0,8},{4,12},{8,0},{12,4},{16,24},{20,28},{24,16},{28,20},{1,9},{5... | collective-permute-start | bytes 1966088 | tf_op jit(solution)/shard_map/ppermute | solution.py:498
  53.6 18.0 %collective-permute-start.14 = (bf16[4,4,16,512]{3,2,1,0:T(8,128)(2,1)S(1)}, bf16[4,4,16,512]{3,2,1,0:T(8,128)(2,1)S(1)}, u32[]{:S(2)}, u32[]{:S(2)}) collective-permute-start(bf16[4,4,16,512]{3,2,1,0:T(8,128)(2,1)S(1)} %collective-permute-done.10.refs_12_.refs_3_), channel_id=1, source_target_pairs={{0,4},{4,0},{8,12},{12,8},{16,20},{20,16},{24,28},{28,24},{1,5},{5... | collective-permute-start | bytes 786440 | tf_op jit(solution)/shard_map/ppermute | solution.py:498
  53.7 27.3 %collective-permute-start.21 = (bf16[4,10,16,512]{3,2,1,0:T(8,128)(2,1)S(1)}, bf16[4,10,16,512]{3,2,1,0:T(8,128)(2,1)S(1)}, u32[]{:S(2)}, u32[]{:S(2)}) collective-permute-start(bf16[4,10,16,512]{3,2,1,0:T(8,128)(2,1)S(1)} %pad_maximum_fusion.refs_0_), channel_id=1, source_target_pairs={{0,4},{4,0},{8,12},{12,8},{16,20},{20,16},{24,28},{28,24},{1,5},{5... | collective-permute-start | bytes 1966088 | tf_op jit(solution)/shard_map/ppermute | solution.py:498
  57.8 23.2 %collective-permute-start.24 = (bf16[4,10,16,512]{3,2,1,0:T(8,128)(2,1)S(1)}, bf16[4,10,16,512]{3,2,1,0:T(8,128)(2,1)S(1)}, u32[]{:S(2)}, u32[]{:S(2)}) collective-permute-start(bf16[4,10,16,512]{3,2,1,0:T(8,128)(2,1)S(1)} %collective-permute-done.20.refs_3_), channel_id=1, source_target_pairs={{0,4},{4,0},{8,12},{12,8},{16,20},{20,16},{24,28},{28,24},{1,5},{5... | collective-permute-start | bytes 1966088 | tf_op jit(solution)/shard_map/ppermute | solution.py:498
  99.2 21.6 %collective-permute-start.28 = (bf16[4,10,16,512]{3,2,1,0:T(8,128)(2,1)S(1)}, bf16[4,10,16,512]{3,2,1,0:T(8,128)(2,1)S(1)}, u32[]{:S(2)}, u32[]{:S(2)}) collective-permute-start(bf16[4,10,16,512]{3,2,1,0:T(8,128)(2,1)S(1)} %get-tuple-element.175), channel_id=1, source_target_pairs={{0,24},{4,28},{8,16},{12,20},{16,8},{20,12},{24,0},{28,4},{1,25},{... | collective-permute-start | bytes 1966088 | tf_op jit(solution)/shard_map/ppermute | solution.py:498
  100.9 30.0 %collective-permute-start.27 = (bf16[4,10,16,512]{3,2,1,0:T(8,128)(2,1)S(1)}, bf16[4,10,16,512]{3,2,1,0:T(8,128)(2,1)S(1)}, u32[]{:S(2)}, u32[]{:S(2)}) collective-permute-start(bf16[4,10,16,512]{3,2,1,0:T(8,128)(2,1)S(1)} %get-tuple-element.176), channel_id=1, source_target_pairs={{0,16},{4,20},{8,24},{12,28},{16,0},{20,4},{24,8},{28,12},{1,17},{... | collective-permute-start | bytes 1966088 | tf_op jit(solution)/shard_map/ppermute | solution.py:498
  102.1 28.9 %collective-permute-start.26 = (bf16[4,10,16,512]{3,2,1,0:T(8,128)(2,1)S(1)}, bf16[4,10,16,512]{3,2,1,0:T(8,128)(2,1)S(1)}, u32[]{:S(2)}, u32[]{:S(2)}) collective-permute-start(bf16[4,10,16,512]{3,2,1,0:T(8,128)(2,1)S(1)} %get-tuple-element.177), channel_id=1, source_target_pairs={{0,8},{4,12},{8,0},{12,4},{16,24},{20,28},{24,16},{28,20},{1,9},{5... | collective-permute-start | bytes 1966088 | tf_op jit(solution)/shard_map/ppermute | solution.py:498
  107.6 13.1 %collective-permute-start.31 = (bf16[128,512]{1,0:T(8,128)(2,1)S(1)}, bf16[128,512]{1,0:T(8,128)(2,1)S(1)}, u32[]{:S(2)}, u32[]{:S(2)}) collective-permute-start(bf16[128,512]{1,0:T(8,128)(2,1)S(1)} %get-tuple-element.131), channel_id=1, source_target_pairs={{1,3},{2,0},{3,1},{5,7},{6,4},{7,5},{9,11},{10,8},{11,9},{13,15},{... | collective-permute-start | bytes 393224 | tf_op jit(solution)/shard_map/ppermute | solution.py:495
  108.9 11.8 %collective-permute-start.32 = (bf16[128,512]{1,0:T(8,128)(2,1)S(1)}, bf16[128,512]{1,0:T(8,128)(2,1)S(1)}, u32[]{:S(2)}, u32[]{:S(2)}) collective-permute-start(bf16[128,512]{1,0:T(8,128)(2,1)S(1)} %get-tuple-element.132), channel_id=1, source_target_pairs={{1,2},{2,1},{3,0},{5,6},{6,5},{7,4},{9,10},{10,9},{11,8},{13,14},{... | collective-permute-start | bytes 393224 | tf_op jit(solution)/shard_map/ppermute | solution.py:495
  132.7 17.0 %collective-permute-start.36 = (bf16[4,4,16,512]{3,2,1,0:T(8,128)(2,1)S(1)}, bf16[4,4,16,512]{3,2,1,0:T(8,128)(2,1)S(1)}, u32[]{:S(2)}, u32[]{:S(2)}) collective-permute-start(bf16[4,4,16,512]{3,2,1,0:T(8,128)(2,1)S(1)} %get-tuple-element.140), channel_id=1, source_target_pairs={{0,8},{4,12},{8,0},{12,4},{16,24},{20,28},{24,16},{28,20},{1,9},{5... | collective-permute-start | bytes 786440 | tf_op jit(solution)/shard_map/ppermute | solution.py:498
  134.1 14.3 %collective-permute-start.34 = (bf16[10,16,512]{2,1,0:T(8,128)(2,1)S(1)}, bf16[10,16,512]{2,1,0:T(8,128)(2,1)S(1)}, u32[]{:S(2)}, u32[]{:S(2)}) collective-permute-start(bf16[10,16,512]{2,1,0:T(8,128)(2,1)S(1)} %get-tuple-element.138), channel_id=1, source_target_pairs={{0,2},{1,3},{2,0},{3,1},{4,6},{5,7},{6,4},{7,5},{8,10},{9,11},{10,... | collective-permute-start | bytes 491528 | tf_op jit(solution)/shard_map/ppermute | solution.py:495
  134.1 16.9 %collective-permute-start.37 = (bf16[4,4,16,512]{3,2,1,0:T(8,128)(2,1)S(1)}, bf16[4,4,16,512]{3,2,1,0:T(8,128)(2,1)S(1)}, u32[]{:S(2)}, u32[]{:S(2)}) collective-permute-start(bf16[4,4,16,512]{3,2,1,0:T(8,128)(2,1)S(1)} %get-tuple-element.141), channel_id=1, source_target_pairs={{0,16},{4,20},{8,24},{12,28},{16,0},{20,4},{24,8},{28,12},{1,17},{... | collective-permute-start | bytes 786440 | tf_op jit(solution)/shard_map/ppermute | solution.py:498
  134.9 16.1 %collective-permute-start.38 = (bf16[4,4,16,512]{3,2,1,0:T(8,128)(2,1)S(1)}, bf16[4,4,16,512]{3,2,1,0:T(8,128)(2,1)S(1)}, u32[]{:S(2)}, u32[]{:S(2)}) collective-permute-start(bf16[4,4,16,512]{3,2,1,0:T(8,128)(2,1)S(1)} %get-tuple-element.142), channel_id=1, source_target_pairs={{0,24},{4,28},{8,16},{12,20},{16,8},{20,12},{24,0},{28,4},{1,25},{... | collective-permute-start | bytes 786440 | tf_op jit(solution)/shard_map/ppermute | solution.py:498
  148.3 12.3 %collective-permute-start.43 = (bf16[128,512]{1,0:T(8,128)(2,1)S(1)}, bf16[128,512]{1,0:T(8,128)(2,1)S(1)}, u32[]{:S(2)}, u32[]{:S(2)}) collective-permute-start(bf16[128,512]{1,0:T(8,128)(2,1)S(1)} %get-tuple-element.161), channel_id=1, source_target_pairs={{1,3},{2,0},{3,1},{5,7},{6,4},{7,5},{9,11},{10,8},{11,9},{13,15},{... | collective-permute-start | bytes 393224 | tf_op jit(solution)/shard_map/ppermute | solution.py:495
  149.6 13.5 %collective-permute-start.44 = (bf16[128,512]{1,0:T(8,128)(2,1)S(1)}, bf16[128,512]{1,0:T(8,128)(2,1)S(1)}, u32[]{:S(2)}, u32[]{:S(2)}) collective-permute-start(bf16[128,512]{1,0:T(8,128)(2,1)S(1)} %get-tuple-element.162), channel_id=1, source_target_pairs={{1,2},{2,1},{3,0},{5,6},{6,5},{7,4},{9,10},{10,9},{11,8},{13,14},{... | collective-permute-start | bytes 393224 | tf_op jit(solution)/shard_map/ppermute | solution.py:495
  151.3 11.8 %collective-permute-start.39 = (bf16[4,16,512]{2,1,0:T(8,128)(2,1)S(1)}, bf16[4,16,512]{2,1,0:T(8,128)(2,1)S(1)}, u32[]{:S(2)}, u32[]{:S(2)}) collective-permute-start(bf16[4,16,512]{2,1,0:T(8,128)(2,1)S(1)} %get-tuple-element.152), channel_id=1, source_target_pairs={{0,1},{1,0},{2,3},{3,2},{4,5},{5,4},{6,7},{7,6},{8,9},{9,8},{10,11... | collective-permute-start | bytes 196616 | tf_op jit(solution)/shard_map/ppermute | solution.py:495
  156.1 12.8 %collective-permute-start.40 = (bf16[4,16,512]{2,1,0:T(8,128)(2,1)S(1)}, bf16[4,16,512]{2,1,0:T(8,128)(2,1)S(1)}, u32[]{:S(2)}, u32[]{:S(2)}) collective-permute-start(bf16[4,16,512]{2,1,0:T(8,128)(2,1)S(1)} %get-tuple-element.153), channel_id=1, source_target_pairs={{0,2},{1,3},{2,0},{3,1},{4,6},{5,7},{6,4},{7,5},{8,10},{9,11},{10,... | collective-permute-start | bytes 196616 | tf_op jit(solution)/shard_map/ppermute | solution.py:495
  (30 other events, 717.6 us)

commit v3 on v2

v3 whole, which is shorter than its diff:
```python
import functools
import math

import jax
import jax.numpy as jnp
from jax import lax
from jax.experimental import pallas as pl
from jax.experimental.pallas import tpu as pltpu
from jax.sharding import PartitionSpec as P

HEAD_DIM = 64
LANES = 128
BAND = 16
MIB = 1024 * 1024
BF = jnp.bfloat16
F32 = jnp.float32
VMEM = pl.BlockSpec(memory_space=pltpu.VMEM)
SMEM = pl.BlockSpec(memory_space=pltpu.SMEM)
HBM = pl.BlockSpec(memory_space=pltpu.HBM)
NN = (((1,), (0,)), ((), ()))
NT = (((1,), (1,)), ((), ()))
TN = (((0,), (0,)), ((), ()))


def mm(left, right, dims=NN, precision=None):
    return lax.dot_general(left, right, dims, precision, preferred_element_type=F32)


def call(body, outs, ins, scratch, cost, name, limit):
    flops, moved = cost
    return pl.pallas_call(
        body,
        out_shape=[jax.ShapeDtypeStruct(shape, dtype) for shape, dtype, _ in outs],
        out_specs=[spec for _, _, spec in outs],
        in_specs=ins,
        scratch_shapes=scratch,
        compiler_params=pltpu.CompilerParams(vmem_limit_bytes=limit * MIB),
        cost_estimate=pl.CostEstimate(flops=flops, bytes_accessed=moved, transcendentals=0),
        name=name,
    )


def own_place():
    seq = lax.axis_index("seq")
    return lax.axis_index("dp") * 4 + seq, seq


def slot_rows(core, layer, place, me):
    device = lax.bitwise_xor(jnp.int32((layer * 2 + core) * 4 + place), me)
    return pl.ds(pl.multiple_of(device * BAND, BAND), BAND)


def plain_layout(pieces):
    return [(core, layer, 0, pieces) for core in range(2) for layer in range(4)]


def split_layout(pieces):
    half = pieces // 2
    per_core = [(layer, 0, pieces) for layer in range(3)] + [(3, 0, half), (3, half, half)]
    return [(core,) + item for core in range(2) for item in per_core]


def fetch_weights(layout, parts, weights, sem, me):
    for (core, layer, first, count), part in zip(layout, parts):
        for place in range(4):
            rows = slot_rows(core, layer, place, me)
            target = weights.at[pl.ds(first, count), rows, :]
            pltpu.make_async_copy(part.at[place], target, sem).start()


def store_slots(grads, parts, sem, me):
    for core in range(2):
        for layer in range(4):
            for place in range(4):
                slot = parts[4].at[layer * 4 + place] if core else parts[layer].at[place]
                rows = slot_rows(core, layer, place, me)
                pltpu.make_async_copy(grads.at[:, rows, :], slot, sem).start()
    pltpu.make_async_copy(grads, grads, sem).wait()


def has_long(seq):
    return (seq == 1) | (seq == 2)


def pick(seq, *options):
    chosen = options[-1]
    for i in range(len(options) - 2, -1, -1):
        chosen = jnp.where(seq == i, options[i], chosen)
    return chosen


def pad_rows(part, rows):
    return jnp.concatenate([part, jnp.zeros((rows - part.shape[0], part.shape[1]), part.dtype)], 0)


def pack_body(with_weights, *refs):
    me, seq = own_place()
    count = 13 if with_weights else 4
    sources, refs = (refs[:count], refs[count:])
    outs = 5 if with_weights else 3
    targets, held, sem = (refs[:outs], refs[outs : outs + count], refs[-1])
    pay1, pay2, pay3 = targets[:3]
    ins = [
        pltpu.make_async_copy(source, there, sem.at[i])
        for i, (source, there) in enumerate(zip(sources, held))
    ]
    for item in ins:
        item.start()
    long_tok, short_tok, long_cot, short_cot = held[:4]
    n_long, n_short = (long_tok.shape[1], short_tok.shape[1])
    copies = []

    def copy(source, target):
        item = pltpu.make_async_copy(source, target, sem.at[len(copies)])
        item.start()
        copies.append(item)

    if with_weights:
        early, late = targets[3:]
        row = refs[outs + count]
        width = early.shape[2]
        gain, bias = held[11:]
        shard = gain.shape[1]
        col = lax.broadcasted_iota(jnp.int32, (shard, width), 1)
        at = lax.broadcasted_iota(jnp.int32, (shard, width), 0)
        spread = (col == at + me * shard).astype(BF)
    for item in ins:
        item.wait()
    if with_weights:
        wq, wk, wv, pos, wo, up, down = held[4:11]
        chunks = up.shape[1] // width
        vectors = jnp.concatenate([mm(gain[...], spread), mm(bias[...], spread)], 0)
        row[...] = pad_rows(vectors, BAND).astype(BF)
        for i, weight in enumerate((wq, wk, wv, pos)):
            copy(weight, early.at[i])
        copy(wo, late.at[0])
        for c in range(chunks):
            cols = pl.ds(c * width, width)
            copy(up.at[:, cols], late.at[1 + c])
            copy(down.at[:, cols], late.at[1 + chunks + c])
        copy(row, late.at[1 + 2 * chunks])
    last = len(copies)

    def rest(pairs):
        ends = [
            pltpu.make_async_copy(source, target, sem.at[last + i])
            for i, (source, target) in enumerate(pairs)
        ]
        for item in ends:
            item.start()
        for item in ends:
            item.wait()

    def halves(pay, one, two, rows):
        half = pay.shape[0] // 2
        return [(one, pay.at[pl.ds(0, rows), :]), (two, pay.at[pl.ds(half, rows), :])]

    longs = [long_tok.at[0], long_cot.at[0], n_long]
    zeros, ones = ([short_tok.at[i], short_cot.at[i], n_short] for i in range(2))
    plans = (
        halves(pay1, *longs) + [(long_tok.at[0], pay2)] + halves(pay3, *ones),
        halves(pay1, *zeros) + halves(pay2, *ones) + [(long_tok.at[0], pay3)],
        halves(pay1, *ones) + halves(pay2, *zeros),
        halves(pay1, *longs) + halves(pay3, *zeros),
    )
    for place, plan in enumerate(plans):

        @pl.when(seq == place)
        def _(plan=plan):
            rest(plan)

    for item in copies:
        item.wait()


def stack_heads(block, lane):
    zero = jnp.zeros_like(block)
    return jnp.concatenate([jnp.where(lane, block, zero), jnp.where(lane, zero, block)], 0)


def join_heads(stacked, lane):
    half = stacked.shape[0] // 2
    return jnp.where(lane, stacked[:half], stacked[half:])


def head_lanes():
    return lax.broadcasted_iota(jnp.int32, (1, LANES), 1) < HEAD_DIM


def block_base(seq, k, size):
    owner = lax.bitwise_xor(seq, jnp.int32(k))
    return pl.multiple_of(owner * jnp.where(has_long(seq), size, size // 2), size // 2)


def gather_queries(seq, source, target):
    size = source.shape[0] // 4
    half = size // 2

    @pl.when(seq == 1)
    def _():
        target[:size, :] = source[size : 2 * size, :]
        target[size:, :] = source[:size, :]

    @pl.when(seq == 2)
    def _():
        target[...] = source[: 2 * size, :]

    @pl.when((seq == 0) | (seq == 3))
    def _():
        for k in range(4):
            target[k * half : (k + 1) * half, :] = source[k * size : k * size + half, :]


def spread_queries(seq, value, target):
    size = target.shape[0] // 4
    half = size // 2

    @pl.when(seq == 1)
    def _():
        target[size : 2 * size, :] += value[:size]
        target[:size, :] += value[size:]

    @pl.when(seq == 2)
    def _():
        target[: 2 * size, :] += value

    @pl.when((seq == 0) | (seq == 3))
    def _():
        for k in range(4):
            target[k * size : k * size + half, :] += value[k * half : (k + 1) * half]


def row_blocks(seq, whole, shorts, one, two, three):
    rows, half = (whole.shape[1], shorts.shape[1])
    longs = has_long(seq)
    own_short = pad_rows(jnp.where(seq == 0, shorts[0], shorts[1]), rows)
    return (
        jnp.where(longs, whole[0], own_short),
        jnp.where(longs, one, pad_rows(one[:half], rows)),
        two,
        three,
    )


def attend_body(direct, layout, long_len, short_len, *refs):
    count = len(layout)
    long_tok, short_tok, got1, got2, got3 = refs[:5]
    parts, refs = (refs[5 : 5 + count], refs[5 + count :])
    first_o, low_o, lowq_o, q_o, k_o, v_o, probs_o, mix_o = refs[:8]
    weights, table, first, sem = refs[8:]
    me, seq = own_place()
    me = me if direct else jnp.int32(0)
    fetch_weights(layout, parts, weights, sem, me)
    n_long, n_short = (long_tok.shape[1], short_tok.shape[1])
    longs = has_long(seq)
    two, three = (
        jnp.where(longs, got[...], pad_rows(got[:n_short, :], n_long)) for got in (got2, got3)
    )
    blocks = row_blocks(seq, long_tok, short_tok, got1[:n_long, :], two, three)
    for k, block in enumerate(blocks):
        first[k * n_long : (k + 1) * n_long, :] = block.astype(F32)
    pltpu.make_async_copy(weights, weights, sem).wait()
    table[...] = weights[3].astype(F32).T
    for k in range(4):
        rows = slice(k * n_long, (k + 1) * n_long)
        first[rows, :] += table[pl.ds(block_base(seq, k, n_long), n_long), :]
    gather_queries(seq, first, first_o)
    lowq_o[...] = first_o[...].astype(BF)
    low_o[...] = first[...].astype(BF)
    k_o[...] = mm(low_o[...], weights[1]).astype(BF)
    v_o[...] = mm(low_o[...], weights[2]).astype(BF)
    q_o[...] = mm(lowq_o[...], weights[0]).astype(BF) * BF(HEAD_DIM**-0.5)
    rows, keys = (first_o.shape[0], first.shape[0])
    row = lax.broadcasted_iota(jnp.int32, (rows, 1), 0)
    row_pos = jnp.where(
        longs,
        row + (seq - 1) * rows,
        lax.bitwise_xor(row // n_short, jnp.full_like(row, seq)) * n_short + row % n_short,
    )
    row_pos = jnp.concatenate([row_pos, row_pos], 0)
    col = lax.broadcasted_iota(jnp.int32, (1, keys), 1)
    owner = lax.bitwise_xor(col // n_long, jnp.full_like(col, seq))
    inner = col % n_long
    col_pos = jnp.where(longs, owner * n_long + inner, owner * n_short + inner)
    length = pick(seq, short_len[0], long_len[0], long_len[0], short_len[1])
    seen = (col_pos < length) & (longs | (inner < n_short))
    col_pos = jnp.where(seen, col_pos, jnp.int32(1 << 20))
    allowed = col_pos <= row_pos
    lane = head_lanes()
    for g in range(first_o.shape[1] // LANES):
        cols = slice(g * LANES, (g + 1) * LANES)
        scores = mm(stack_heads(q_o[:, cols], lane), k_o[:, cols], NT)
        scores = jnp.where(allowed, scores, -1e30)
        shifted = jnp.exp(scores - jnp.max(scores, axis=-1, keepdims=True))
        probs_o[g] = (shifted / jnp.sum(shifted, axis=-1, keepdims=True)).astype(BF)
        mix_o[:, cols] = join_heads(mm(probs_o[g], v_o[:, cols]), lane).astype(BF)


def norm_parts(values):
    mean = jnp.mean(values, axis=-1, keepdims=True)
    centred = values - mean
    scale = lax.rsqrt(jnp.mean(centred * centred, axis=-1, keepdims=True) + 1e-05)
    return centred * scale, scale


def norm_back(cot, gain, xhat, scale):
    scaled = cot * gain
    mean = jnp.mean(scaled, axis=-1, keepdims=True)
    inner = jnp.mean(scaled * xhat, axis=-1, keepdims=True)
    return scale * (scaled - mean - xhat * inner)


def middle_body(direct, layout, first, mixed, long_cot, short_cot, *refs):
    count = len(layout)
    got1, got2, got3 = refs[:3]
    parts, refs = (refs[3 : 3 + count], refs[3 + count :])
    out_o, gsum_o, gmix_o = refs[:3]
    grad_parts = refs[3:8]
    weights, grads, act, slope, blocks, cots, sem = refs[8:]
    me, seq = own_place()
    me = me if direct else jnp.int32(0)
    fetch_weights(layout, parts, weights, sem, me)
    n_long, n_short = (long_cot.shape[1], short_cot.shape[1])
    two, three = (pad_rows(got[n_short:, :], n_long) for got in (got2, got3))
    found = row_blocks(seq, long_cot, short_cot, got1[n_long:, :], two, three)
    for k, block in enumerate(found):
        blocks[k * n_long : (k + 1) * n_long, :] = block.astype(F32)
    gather_queries(seq, blocks, cots)
    blocks[...] = jnp.zeros_like(blocks)
    pltpu.make_async_copy(weights, weights, sem).wait()
    width = first.shape[1]
    chunks = (weights.shape[0] - 2) // 2
    norm = weights.shape[0] - 1
    vectors = jnp.sum(weights[norm].astype(F32).reshape(-1, BAND, width), axis=0)
    gain0, gain1, bias0, bias1 = (vectors[i : i + 1] for i in range(4))
    mixed_low = mixed[...]
    xhat0, scale0 = norm_parts(first[...] + mm(mixed_low, weights[0]))
    normed = xhat0 * gain0 + bias0
    normed_low = normed.astype(BF)
    second = normed
    for c in range(chunks):
        hidden = mm(normed_low, weights[1 + c])
        cdf = 0.5 + 0.5 * lax.erf(hidden * (0.5**0.5))
        slope[c] = cdf + hidden * jnp.exp(-0.5 * hidden * hidden) * ((2 * math.pi) ** -0.5)
        act[c] = (hidden * cdf).astype(BF)
        second = second + mm(act[c], weights[1 + chunks + c], NT)
    xhat1, scale1 = norm_parts(second)
    spread_queries(seq, xhat1 * gain1 + bias1, blocks)
    out_o[...] = blocks[...].astype(BF)
    cot_wide = cots[...]
    grad_second = norm_back(cot_wide, gain1, xhat1, scale1)
    second_low = grad_second.astype(BF)
    grad_normed = grad_second
    for c in range(chunks):
        hidden_low = (mm(second_low, weights[1 + chunks + c]) * slope[c]).astype(BF)
        grads[1 + chunks + c] = mm(second_low, act[c], TN).astype(BF)
        grads[1 + c] = mm(normed_low, hidden_low, TN).astype(BF)
        grad_normed = grad_normed + mm(hidden_low, weights[1 + c], NT)
    grad_sum = norm_back(grad_normed, gain0, xhat0, scale0)
    gsum_o[...] = grad_sum
    sum_low = grad_sum.astype(BF)
    gmix_o[...] = mm(sum_low, weights[0], NT).astype(BF)
    grads[0] = mm(mixed_low, sum_low, TN).astype(BF)
    terms = jnp.concatenate(
        [
            jnp.sum(grad_normed * xhat0, axis=0, keepdims=True),
            jnp.sum(cot_wide * xhat1, axis=0, keepdims=True),
            jnp.sum(grad_normed, axis=0, keepdims=True),
            jnp.sum(cot_wide, axis=0, keepdims=True),
            jnp.zeros((BAND - 4, width), F32),
        ],
        0,
    ).astype(BF)
    for d in range(width // BAND):
        grads[norm, d * BAND : (d + 1) * BAND, :] = terms
    store_slots(grads, grad_parts, sem, me)


def attend_back_body(gmix, q, k, v, probs_i, dq_o, dk_o, dv_o):
    lane = head_lanes()
    scale = HEAD_DIM**-0.5
    for g in range(gmix.shape[1] // LANES):
        cols = slice(g * LANES, (g + 1) * LANES)
        grads = stack_heads(gmix[:, cols], lane)
        queries = stack_heads(q[:, cols], lane)
        probs = probs_i[g]
        grad_probs = mm(grads, v[:, cols], NT)
        wide = probs.astype(F32)
        inner = jnp.sum(wide * grad_probs, axis=-1, keepdims=True)
        grad_scores = (wide * (grad_probs - inner)).astype(BF)
        grad_q = mm(grad_scores, k[:, cols])
        dq_o[:, cols] = (join_heads(grad_q, lane) * scale).astype(BF)
        dk_o[:, cols] = mm(grad_scores, queries, TN).astype(BF)
        dv_o[:, cols] = mm(probs, grads, TN).astype(BF)


def leave_body(direct, layout, low, lowq, dq, dk, dv, gsum, outs, *refs):
    count = len(layout)
    parts, refs = (refs[:count], refs[count:])
    own_o, sent1_o, sent2_o, sent3_o = refs[:4]
    grad_parts = refs[4:9]
    weights, grads, table, back, sem = refs[9:]
    me, seq = own_place()
    me = me if direct else jnp.int32(0)
    fetch_weights(layout, parts, weights, sem, me)
    grads[0] = mm(lowq[...], dq[...], TN).astype(BF)
    grads[1] = mm(low[...], dk[...], TN).astype(BF)
    grads[2] = mm(low[...], dv[...], TN).astype(BF)
    pltpu.make_async_copy(weights, weights, sem).wait()
    back[...] = mm(dk[...], weights[1], NT) + mm(dv[...], weights[2], NT)
    spread_queries(seq, gsum[...] + mm(dq[...], weights[0], NT), back)
    size = own_o.shape[0]
    table[...] = jnp.zeros_like(table)
    for k, target in enumerate((own_o, sent1_o, sent2_o, sent3_o)):
        piece = back[k * size : (k + 1) * size, :]
        target[:size, :] = piece.astype(target.dtype)
        if k == 1:
            target[size:, :] = outs[size : 2 * size, :]
        elif k > 1:
            both = jnp.concatenate([piece[: size // 2].astype(BF), outs[k * size : k * size + size // 2, :]], 0)
            target[...] = jnp.where(has_long(seq), piece.astype(BF), both)
        table[pl.ds(block_base(seq, k, size), size), :] += piece
    grads[3] = table[...].T.astype(BF)
    store_slots(grads, grad_parts, sem, me)


def return_rows(own, outs, got1, got2, got3, long_grad, short_grad, long_out, short_out):
    seq = own_place()[1]
    size, half = (long_grad.shape[1], short_grad.shape[1])
    for i, (mine, long_o, short_o) in enumerate(((own, long_grad, short_grad), (outs, long_out, short_out))):
        mine = mine[:size, :].astype(F32)
        one = got1[i * size : (i + 1) * size, :].astype(F32)
        if i == 0:
            two, three = (got[...].astype(F32) for got in (got2, got3))
            long_o[0] = pick(seq, one + two, mine + three, mine, one).astype(BF)
        else:
            long_o[0] = pick(seq, one, mine, mine, one).astype(BF)
        two, three = (got[i * half : (i + 1) * half, :].astype(F32) for got in (got2, got3))
        mine, one = (mine[:half], one[:half])
        short_o[0] = pick(seq, mine, one, two, three).astype(BF)
        short_o[1] = pick(seq, three, two, one, mine).astype(BF)


def wide(ref, *index):
    return ref[index].astype(F32)


def sum_call(body, outs, ins, blocks_in, steps, name):
    def spec(shape, axis):
        block = tuple(1 if i == axis else size for i, size in enumerate(shape))
        return pl.BlockSpec(block, lambda i: tuple(i if a == axis else 0 for a in range(len(shape))))

    return pl.pallas_call(
        body,
        grid=(steps,),
        out_shape=[jax.ShapeDtypeStruct(shape, dtype) for shape, dtype, _ in outs],
        in_specs=blocks_in,
        out_specs=[spec(shape, axis) for shape, _, axis in outs],
        compiler_params=pltpu.CompilerParams(vmem_limit_bytes=16 * MIB),
        name=name,
    )(*ins)


def one_place(part, layer=0):
    shape = part.shape
    return pl.BlockSpec((1,) + shape[1:], lambda i: (layer * 4 + i,) + (0,) * (len(shape) - 1))


def first_sums_body(half, near1, near2, near3, far1, far2, far3, to_x, to_y):
    to_y[0, 0] = (wide(near2, 0)[:half] + wide(far2, 0)[:half]).astype(BF)
    to_y[1, 0] = (wide(near3, 0)[:half] + wide(far3, 0)[:half]).astype(BF)
    to_x[0, 0] = (wide(near1, 0)[half:] + wide(far1, 0)[half:]).astype(BF)
    to_x[1, 0] = (wide(near3, 0)[half:] + wide(far3, 0)[half:]).astype(BF)


def second_sums_body(half, near1, near2, far1, far2, from_x, from_y, to_x, to_y):
    to_x[0] = (wide(near1, 0)[:half] + wide(far1, 0)[:half] + wide(from_y, 0, 0)).astype(BF)
    to_y[0] = (wide(near2, 0)[half:] + wide(far2, 0)[half:] + wide(from_x, 0, 0)).astype(BF)


def last_sums_body(half, near0, far0, from_x, from_y, then_x, then_y, *outs):
    for place, out in enumerate(outs):
        low = wide(near0, place)[:half] + wide(far0, place)[:half]
        low = low + (wide(from_y, 0, place) + wide(then_x, place))
        out[:half] = low.astype(out.dtype)
        high = wide(near0, place)[half:] + wide(far0, place)[half:]
        high = high + (wide(from_x, 0, place) + wide(then_y, place))
        out[half:] = high.astype(out.dtype)


def four_sums_body(*refs):
    ins, outs = (refs[:-4], refs[-4:])
    for place, out in enumerate(outs):
        total = wide(ins[0], place)
        for item in ins[1:]:
            total = total + wide(item, place)
        out[...] = total.astype(out.dtype)


def cut_sums(body, parts, pieces, name):
    _, _, band, width = parts[0].shape

    def whole(part):
        shape = part.shape
        shape = (1,) + shape[1:] if len(shape) == 5 else (4,) + shape[1:]
        return pl.BlockSpec(shape, lambda i: (0,) * len(shape))

    out = pl.BlockSpec((pieces, band, width), lambda i: (0, 0, 0))
    return pl.pallas_call(
        body,
        grid=(1,),
        out_shape=[
            jax.ShapeDtypeStruct((pieces, band, width), F32 if place == 0 else BF)
            for place in range(4)
        ],
        in_specs=[whole(part) for part in parts],
        out_specs=[out] * 4,
        compiler_params=pltpu.CompilerParams(vmem_limit_bytes=24 * MIB),
        name=name,
    )(*parts)


def finish_body(*refs):
    late, early, rows = (refs[:4], refs[4:8], refs[8:13])
    row_outs, early_outs = (refs[13:17], refs[17:21])
    out_o, up_o, down_o, norm_o = refs[21:]
    width = out_o.shape[1]
    chunks = up_o.shape[1] // width

    def total(parts, i):
        own, one, two, three = parts
        return own[i] + (one[i].astype(F32) + two[i].astype(F32) + three[i].astype(F32))

    return_rows(*rows, *row_outs)
    out_o[...] = total(late, 0)
    for c in range(chunks):
        up_o[:, c * width : (c + 1) * width] = total(late, 1 + c)
        down_o[:, c * width : (c + 1) * width] = total(late, 1 + chunks + c)
    shard = norm_o.shape[1]
    row = lax.broadcasted_iota(jnp.int32, (width, shard), 0)
    col = lax.broadcasted_iota(jnp.int32, (width, shard), 1)
    chosen = (row == col + own_place()[0] * shard).astype(F32)
    norm_o[...] = mm(total(late, 1 + 2 * chunks), chosen, NN, lax.Precision.HIGHEST)
    for i, out in enumerate(early_outs):
        out[...] = total(early, i)


def after(value, *others):
    return lax.optimization_barrier((value,) + others)[0]


def local(
    dp_count,
    seq_count,
    long_tokens,
    short_tokens,
    long_cot,
    short_cot,
    long_lengths,
    short_lengths,
    w_query,
    w_key,
    w_value,
    w_out,
    w_up,
    w_down,
    pos_table,
    norm_gain,
    norm_bias,
):
    width = w_key.shape[1]
    hidden = w_up.shape[1]
    chunks = hidden // width
    shard = w_key.shape[0]
    direct = shard == BAND and dp_count == 8
    layers = 4
    device = lax.axis_index("dp") * seq_count + lax.axis_index("seq")
    n_long, n_short = (long_tokens.shape[1], short_tokens.shape[1])
    rows, keys = (2 * n_long, 4 * n_long)
    square = width * width
    early_pieces, late_pieces = (4, 2 + 2 * chunks)

    def swap_seq(value, mask, keep=lambda source, target: True):
        pairs = [(i, i ^ mask) for i in range(seq_count) if keep(i, i ^ mask)]
        return lax.ppermute(value, "seq", pairs)

    def swap_dp(value, mask):
        return lax.ppermute(value, "dp", [(i, i ^ mask) for i in range(dp_count)])

    acts = [long_tokens, short_tokens, long_cot, short_cot]
    packed = [
        ((2 * n_long, width), BF, HBM),
        ((n_long, width), BF, HBM),
        ((n_long, width), BF, HBM),
    ]
    own, specs, scratch = ([], [HBM] * 4, [])
    held = list(acts)
    if direct:
        own = [w_query, w_key, w_value, pos_table.T, w_out, w_up, w_down.T]
        own += [norm_gain, norm_bias]
        held += own
        packed += [((count, BAND, width), BF, HBM) for count in (early_pieces, late_pieces)]
        specs += [HBM] * 9
        scratch = [pltpu.VMEM((BAND, width), BF)]
    pays = call(
        functools.partial(pack_body, direct),
        packed,
        specs,
        [pltpu.VMEM(item.shape, BF) for item in held] + scratch + [pltpu.SemaphoreType.DMA((32,))],
        (0, 4 * MIB),
        "pack",
        60,
    )(*acts, *own)
    pay1, pay2, pay3 = pays[:3]

    def to_slots(whole):
        count = whole.shape[0]
        cut = whole.reshape(count, 4, 2, 4, BAND, width).transpose(2, 1, 3, 0, 4, 5)
        return [cut[core, outer] for core in range(2) for outer in range(4)]

    def slot_outs(pieces):
        near = ((4, pieces, BAND, width), BF, HBM)
        return [near] * layers + [((4 * layers, pieces, BAND, width), BF, HBM)]

    def from_slots(parts):
        count = parts[0].shape[1]
        cut = jnp.concatenate(parts, 0).reshape(2, 4, 4, count, BAND, width)
        return cut.transpose(3, 1, 0, 2, 4, 5).reshape(count, width, width)

    def places(piece):
        return [piece] + [swap_seq(piece, k) for k in range(1, 4)]

    def spread(column):
        near = [column] + [swap_dp(column, 2 * k) for k in range(1, layers)]
        return near

    def cross(near):
        return list(near) + [swap_dp(part, 1) for part in near]

    early_layout = plain_layout(early_pieces)
    late_layout = split_layout(late_pieces) if direct else plain_layout(late_pieces)
    if direct:
        early, late = pays[3:]
        early_places = places(early)
        late = after(late, *early_places)
        late_places = places(late)
        early_near = spread(jnp.stack(early_places))
        column = jnp.stack(late_places)
        column = after(column, *early_near)
        pay1, pay2, pay3 = lax.optimization_barrier((pay1, pay2, pay3, *late_places))[:3]
        got1, got2, got3 = (
            swap_seq(pay1, 1),
            swap_seq(pay2, 2, lambda source, target: target != 1),
            swap_seq(pay3, 3, lambda source, target: target != 1),
        )
        early_full = early_near + cross(lax.optimization_barrier((early_near, got1, got2, got3))[0])[4:]
        half = late_pieces // 2
        near1, near2 = (swap_dp(column, 2), swap_dp(column, 4))
        near3 = [swap_dp(near1[:, :half], 4), swap_dp(near2[:, half:], 2)]
        late_full = cross([column, near1, near2] + near3)
    if not direct:
        got1, got2, got3 = (
            swap_seq(pay1, 1),
            swap_seq(pay2, 2, lambda source, target: target != 1),
            swap_seq(pay3, 3, lambda source, target: target != 1),
        )

        def columns(weight):
            return weight.reshape(weight.shape[0], chunks, width).transpose(1, 0, 2)

        def whole(pieces):
            return lax.all_gather(pieces, ("dp", "seq"), axis=1, tiled=True)

        early_full = to_slots(whole(jnp.stack([w_query, w_key, w_value, pos_table.T])))
        vectors = jnp.concatenate([norm_gain, norm_bias], 0)
        vectors = lax.all_gather(vectors, ("dp", "seq"), axis=1, tiled=True)
        vectors = jnp.pad(vectors, ((0, width - 4), (0, 0)))
        late_whole = whole(jnp.concatenate([w_out[None], columns(w_up), columns(w_down.T)], 0))
        late_full = to_slots(jnp.concatenate([late_whole, vectors[None]], 0))

    groups = width // LANES
    first, low, low_queries, queries, key_rows, values, probs, mixed = call(
        functools.partial(attend_body, direct, early_layout),
        [
            ((rows, width), F32, VMEM),
            ((keys, width), BF, VMEM),
            ((rows, width), BF, VMEM),
            ((rows, width), BF, VMEM),
            ((keys, width), BF, VMEM),
            ((keys, width), BF, VMEM),
            ((groups, 2 * rows, keys), BF, VMEM),
            ((rows, width), BF, VMEM),
        ],
        [SMEM] * 2 + [VMEM] * 5 + [HBM] * len(early_layout),
        [
            pltpu.VMEM((early_pieces, width, width), BF),
            pltpu.VMEM((width, width), F32),
            pltpu.VMEM((keys, width), F32),
            pltpu.SemaphoreType.DMA,
        ],
        (8 * keys * square, 10 * MIB),
        "attend",
        24,
    )(long_lengths, short_lengths, long_tokens, short_tokens, got1, got2, got3, *early_full)

    block = (n_long, width)
    middle_outs = call(
        functools.partial(middle_body, direct, late_layout),
        [((keys, width), BF, VMEM)]
        + [((rows, width), F32, VMEM), ((rows, width), BF, VMEM)]
        + slot_outs(late_pieces),
        [VMEM] * 7 + [HBM] * len(late_layout),
        [
            pltpu.VMEM((late_pieces, width, width), BF),
            pltpu.VMEM((late_pieces, width, width), BF),
            pltpu.VMEM((chunks, rows, width), BF),
            pltpu.VMEM((chunks, rows, width), F32),
            pltpu.VMEM((keys, width), F32),
            pltpu.VMEM((rows, width), F32),
            pltpu.SemaphoreType.DMA,
        ],
        (16 * rows * square * chunks, 20 * MIB),
        "middle",
        32,
    )(first, mixed, long_cot, short_cot, got1, got2, got3, *late_full)
    out_blocks, grad_sum, grad_mixed = middle_outs[:3]
    late_parts = middle_outs[3:]

    def core_sums(parts, arrived):
        return [
            (parts[k].astype(F32) + arrived[4 * k : 4 * k + 4].astype(F32)).astype(BF)
            for k in range(1, layers)
        ]

    if direct:
        late_arrived = swap_dp(late_parts[-1], 1)

    grad_q, grad_k, grad_v = call(
        attend_back_body,
        [
            ((rows, width), BF, VMEM),
            ((keys, width), BF, VMEM),
            ((keys, width), BF, VMEM),
        ],
        [VMEM] * 5,
        [],
        (8 * keys * square, 8 * MIB),
        "attend_back",
        24,
    )(grad_mixed, queries, key_rows, values, probs)
    leave_outs = call(
        functools.partial(leave_body, direct, early_layout),
        [(block, F32, VMEM), ((2 * n_long, width), BF, VMEM)] + [(block, BF, VMEM)] * 2 + slot_outs(early_pieces),
        [VMEM] * 7 + [HBM] * len(early_layout),
        [
            pltpu.VMEM((early_pieces, width, width), BF),
            pltpu.VMEM((early_pieces, width, width), BF),
            pltpu.VMEM((width, width), F32),
            pltpu.VMEM((keys, width), F32),
            pltpu.SemaphoreType.DMA,
        ],
        (10 * keys * square, 8 * MIB),
        "leave",
        24,
    )(low, low_queries, grad_q, grad_k, grad_v, grad_sum, out_blocks, *early_full)
    grad_blocks, early_parts = (leave_outs[:4], leave_outs[4:])

    back = lambda source, target: source != 1
    got = [swap_seq(grad_blocks[1], 1)] + [swap_seq(grad_blocks[k], k, back) for k in (2, 3)]
    row_outs = [(item.shape, BF, VMEM) for item in (long_tokens, short_tokens)] * 2
    if direct:
        half = late_pieces // 2
        near0, near1, near2, near3 = late_parts[:4]
        far = late_arrived
        pair = ((2, 4, half, BAND, width), BF, 1)
        single = ((4, half, BAND, width), BF, 0)
        to_x, to_y = sum_call(
            functools.partial(first_sums_body, half),
            [pair, pair],
            [near1, near2, near3, far, far, far],
            [one_place(item) for item in (near1, near2, near3)] + [one_place(far, k) for k in (1, 2, 3)],
            4,
            "late_sums_1",
        )
        from_x, from_y = (swap_dp(to_x, 2), swap_dp(to_y, 4))
        second = pl.BlockSpec((1, 1, half, BAND, width), lambda i: (1, i, 0, 0, 0))
        then_x, then_y = sum_call(
            functools.partial(second_sums_body, half),
            [single, single],
            [near1, near2, far, far, from_x, from_y],
            [one_place(near1), one_place(near2), one_place(far, 1), one_place(far, 2), second, second],
            4,
            "late_sums_2",
        )
        early_far = after(early_parts[-1], to_x)
        early_arrived = swap_dp(early_far, 1)
        early_sums = core_sums(early_parts, early_arrived)
        then_x, then_y, early_sums = lax.optimization_barrier((then_x, then_y, early_sums))
        then_x, then_y = (swap_dp(then_x, 2), swap_dp(then_y, 4))
        early_layers = [swap_dp(part, 2 * k) for k, part in enumerate(early_sums, 1)]
        then_x, then_y, got = lax.optimization_barrier((then_x, then_y, got))
        late_cut = cut_sums(
            functools.partial(last_sums_body, half),
            [near0, far, from_x, from_y, then_x, then_y],
            late_pieces,
            "late_sums_3",
        )
        late_ends = [late_cut[0]] + [swap_seq(late_cut[k], k) for k in range(1, 4)]
        early_cut = cut_sums(
            four_sums_body, [early_parts[0], early_arrived] + early_layers, early_pieces, "early_sums"
        )
        early_ends = [early_cut[0]] + [swap_seq(early_cut[k], k) for k in range(1, 4)]
        row_ins = [grad_blocks[0], out_blocks, *got]
        ends = call(
            finish_body,
            row_outs
            + [((shard, width), F32, VMEM)] * 5
            + [((shard, hidden), F32, VMEM)] * 2
            + [((BAND, shard), F32, VMEM)],
            [VMEM] * 13,
            [],
            (0, MIB),
            "finish",
            16,
        )(*late_ends, *early_ends, *row_ins)
        row_grads, early_sum, (grad_out, grad_up, grad_down, norms) = (ends[:4], ends[4:8], ends[8:])
    else:

        def scatter(parts):
            whole_sum = from_slots(parts).astype(F32)
            return lax.psum_scatter(whole_sum, ("dp", "seq"), scatter_dimension=1, tiled=True)

        def join(pieces):
            return pieces.transpose(1, 0, 2).reshape(shard, hidden)

        late_sum = scatter(late_parts)
        early_sum = scatter(early_parts)
        grad_out, grad_up, grad_down = (
            late_sum[0],
            join(late_sum[1 : 1 + chunks]),
            join(late_sum[1 + chunks : 1 + 2 * chunks]),
        )
        norms = lax.psum(from_slots(late_parts)[-1, :BAND].astype(F32), ("dp", "seq"))
        norms = lax.dynamic_slice(norms, (0, device * shard), (BAND, shard))
        row_grads = call(
            return_rows, row_outs, [VMEM] * 5, [], (0, MIB), "return", 16
        )(grad_blocks[0], out_blocks, *got)
    long_grad, short_grad, long_out, short_out = row_grads
    return (
        long_out,
        short_out,
        long_grad,
        short_grad,
        early_sum[0],
        early_sum[1],
        early_sum[2],
        grad_out,
        grad_up,
        grad_down.T,
        early_sum[3].T,
        norms[:2],
        norms[2:4],
    )


def solution(mesh):
    rows = P(("dp", "seq"), None)
    cols = P(None, ("dp", "seq"))
    acts = P("dp", "seq", None)
    return jax.shard_map(
        functools.partial(local, mesh.shape["dp"], mesh.shape["seq"]),
        mesh=mesh,
        in_specs=(acts,) * 4 + (P("dp"),) * 2 + (rows,) * 5 + (cols,) * 4,
        out_specs=(acts,) * 4 + (rows,) * 5 + (cols,) * 4,
        check_vma=False,
    )
```

time: 172 us -> 137 us (0.80)
  waiting for transfers between devices: 83.7 us -> 47.3 us
  starting transfers between devices: 52.7 us -> 60 us
  other arithmetic: 4.93 us -> 2.18 us
  Pallas kernels: 27.6 us -> 25.3 us
    ppermute x23 -> x18, waiting for transfers between devices: 52.9 us -> 23.7 us  [swap_seq(): return lax.ppermute(value, 'seq', pairs)]
    ppermute x22 -> x25, waiting for transfers between devices: 30.8 us -> 23.6 us  [swap_dp(): return lax.ppermute(value, 'dp', [(i, i ^ mask) for i in range(dp_count)])]
    ppermute x23 -> x18, starting transfers between devices: 35.7 us -> 41.9 us  [swap_seq(): return lax.ppermute(value, 'seq', pairs)]
    pallas_call x6 -> x8, Pallas kernels: 22.3 us -> 20.6 us  [the longest x1 8.38 us: local(): call(functools.partial(middle_body, direct, late_layout), [((keys, width)...]
    ppermute x22 -> x25, starting transfers between devices: 17 us -> 18 us  [swap_dp(): return lax.ppermute(value, 'dp', [(i, i ^ mask) for i in range(dp_count)])]
  transfers between devices with their start and end apart: 45 -> 43, of which waited for: 19 -> 21; matrix products, arithmetic and copies ran while one was open for 1% -> 2% of each run, Pallas kernels for 8% -> 9%
where the time goes in v3:
time: 137 us
  starting transfers between devices  60 us (44%)
  waiting for transfers between devices  47.3 us (35%)
  Pallas kernels  25.3 us (18%)
  other arithmetic  2.18 us (2%)
  between operations  1.59 us (1%)
    ppermute x18, starting transfers between devices, swap_seq(): return lax.ppermute(value, 'seq', pairs)  41.9 us
    ppermute x18, waiting for transfers between devices, swap_seq(): return lax.ppermute(value, 'seq', pairs)  23.7 us
    ppermute x25, waiting for transfers between devices, swap_dp(): return lax.ppermute(value, 'dp', [(i, i ^ mask) for i in range(dp_count)])  23.6 us
    ppermute x25, starting transfers between devices, swap_dp(): return lax.ppermute(value, 'dp', [(i, i ^ mask) for i in range(dp_count)])  18 us
    pallas_call x1, Pallas kernels, local(): call(functools.partial(middle_body, direct, late_layout), [((keys, width)...  8.38 us
    pallas_call x1, Pallas kernels, local(): call(functools.partial(attend_body, direct, early_layout), [((rows, width...  4.72 us
    pallas_call x1, Pallas kernels, local(): call(functools.partial(leave_body, direct, early_layout), [(block, F32, V...  3.89 us
    pallas_call x1, Pallas kernels, local(): call(attend_back_body, [((rows, width), BF, VMEM), ((keys, width), BF, VM...  3.4 us
  transfers between devices with their start and end apart: 43, of which 21 were waited for; matrix products, arithmetic and copies ran while one was open for 2% of the time, Pallas kernels for 9%

profile of v3, /device:TPU:0, one launch (start us, length us, event | category | flops | bytes accessed | tf_op | source)
XLA Modules:
  0.0 137.0 jit_solution(7661018474242889197)
XLA Ops:
  0.7 2.4 %pack.1 = (bf16[256,512]{1,0:T(8,128)(2,1)}, bf16[128,512]{1,0:T(8,128)(2,1)}, bf16[128,512]{1,0:T(8,128)(2,1)}, bf16[4,16,512]{2,1,0:T(8,128)(2,1)}, bf16[10,16,512]{2,1,0:T(8,128)(2,1)}) custom-call(bf16[1,128,512]{2,1,0:T(8,128)(2,1)} %refs_0_.3, bf16[2,64,512]{2,1,0:T(8,128)(2,1)} %refs_1_.3, bf16[1,128,512]{2,1,0:T(8,128)(2,1)} %long_cot.1, ...), custom_call_target="tpu_custom_call" | custom-call | bytes 4194304 | tf_op jit(solution)/shard_map/pack/pallas_call | solution.py:605
  3.1 5.1 %collective-permute-start.2 = (bf16[4,16,512]{2,1,0:T(8,128)(2,1)}, bf16[4,16,512]{2,1,0:T(8,128)(2,1)S(1)}, u32[]{:S(2)}, u32[]{:S(2)}) collective-permute-start(bf16[4,16,512]{2,1,0:T(8,128)(2,1)} %get-tuple-element.94), channel_id=1, source_target_pairs={{0,3},{1,2},{2,1},{3,0},{4,7},{5,6},{6,5},{7,4},{8,11},{9,10},{10,... | collective-permute-start | bytes 196616 | tf_op jit(solution)/shard_map/ppermute | solution.py:585
  8.8 2.2 %collective-permute-done.2 = bf16[4,16,512]{2,1,0:T(8,128)(2,1)S(1)} collective-permute-done((bf16[4,16,512]{2,1,0:T(8,128)(2,1)}, bf16[4,16,512]{2,1,0:T(8,128)(2,1)S(1)}, u32[]{:S(2)}, u32[]{:S(2)}) %collective-permute-start.2) | collective-permute-done | bytes 65568 | tf_op jit(solution)/shard_map/ppermute | solution.py:585
  11.0 3.0 %collective-permute-done.1 = bf16[4,16,512]{2,1,0:T(8,128)(2,1)S(1)} collective-permute-done((bf16[4,16,512]{2,1,0:T(8,128)(2,1)}, bf16[4,16,512]{2,1,0:T(8,128)(2,1)S(1)}, u32[]{:S(2)}, u32[]{:S(2)}) %collective-permute-start.1) | collective-permute-done | bytes 65568 | tf_op jit(solution)/shard_map/ppermute | solution.py:585
  14.0 2.7 %collective-permute-start.5 = (bf16[10,16,512]{2,1,0:T(8,128)(2,1)}, bf16[10,16,512]{2,1,0:T(8,128)(2,1)S(1)}, u32[]{:S(2)}, u32[]{:S(2)}) collective-permute-start(bf16[10,16,512]{2,1,0:T(8,128)(2,1)} %get-tuple-element.95), channel_id=1, source_target_pairs={{0,3},{1,2},{2,1},{3,0},{4,7},{5,6},{6,5},{7,4},{8,11},{9,10},{10,... | collective-permute-start | bytes 491528 | tf_op jit(solution)/shard_map/ppermute | solution.py:585
  19.3 2.5 %collective-permute-start.11 = (bf16[4,4,16,512]{3,2,1,0:T(8,128)(2,1)S(1)}, bf16[4,4,16,512]{3,2,1,0:T(8,128)(2,1)S(1)}, u32[]{:S(2)}, u32[]{:S(2)}) collective-permute-start(bf16[4,4,16,512]{3,2,1,0:T(8,128)(2,1)S(1)} %pad_maximum_fusion.1.refs_5_.refs_0_), channel_id=1, source_target_pairs={{0,24},{4,28},{8,16},{12,20},{16,8},{20,12},{24,0},{28,4},{1,25},{... | collective-permute-start | bytes 786440 | tf_op jit(solution)/shard_map/ppermute | solution.py:588
  24.7 5.8 %collective-permute-done.4 = bf16[10,16,512]{2,1,0:T(8,128)(2,1)S(1)} collective-permute-done((bf16[10,16,512]{2,1,0:T(8,128)(2,1)}, bf16[10,16,512]{2,1,0:T(8,128)(2,1)S(1)}, u32[]{:S(2)}, u32[]{:S(2)}) %collective-permute-start.4) | collective-permute-done | bytes 163872 | tf_op jit(solution)/shard_map/ppermute | solution.py:585
  35.3 3.3 %collective-permute-start.6 = (bf16[256,512]{1,0:T(8,128)(2,1)}, bf16[256,512]{1,0:T(8,128)(2,1)S(1)}, u32[]{:S(2)}, u32[]{:S(2)}) collective-permute-start(bf16[256,512]{1,0:T(8,128)(2,1)} %get-tuple-element.96), channel_id=1, source_target_pairs={{0,1},{1,0},{2,3},{3,2},{4,5},{5,4},{6,7},{7,6},{8,9},{9,8},{10,11... | collective-permute-start | bytes 786440 | tf_op jit(solution)/shard_map/ppermute | solution.py:585
  38.6 2.3 %collective-permute-start.7 = (bf16[128,512]{1,0:T(8,128)(2,1)}, bf16[128,512]{1,0:T(8,128)(2,1)S(1)}, u32[]{:S(2)}, u32[]{:S(2)}) collective-permute-start(bf16[128,512]{1,0:T(8,128)(2,1)} %get-tuple-element.97), channel_id=1, source_target_pairs={{0,2},{1,3},{2,0},{4,6},{5,7},{6,4},{8,10},{9,11},{10,8},{12,14},{... | collective-permute-start | bytes 393224 | tf_op jit(solution)/shard_map/ppermute | solution.py:585
  40.9 2.6 %collective-permute-start.8 = (bf16[128,512]{1,0:T(8,128)(2,1)}, bf16[128,512]{1,0:T(8,128)(2,1)S(1)}, u32[]{:S(2)}, u32[]{:S(2)}) collective-permute-start(bf16[128,512]{1,0:T(8,128)(2,1)} %get-tuple-element.98), channel_id=1, source_target_pairs={{0,3},{1,2},{3,0},{4,7},{5,6},{7,4},{8,11},{9,10},{11,8},{12,15},{... | collective-permute-start | bytes 393224 | tf_op jit(solution)/shard_map/ppermute | solution.py:585
  43.5 3.9 %collective-permute-done.7.refs_3_.refs_1_ = bf16[128,512]{1,0:T(8,128)(2,1)S(1)} collective-permute-done((bf16[128,512]{1,0:T(8,128)(2,1)}, bf16[128,512]{1,0:T(8,128)(2,1)S(1)}, u32[]{:S(2)}, u32[]{:S(2)}) %collective-permute-start.7) | collective-permute-done | bytes 131104 | tf_op jit(solution)/shard_map/ppermute | solution.py:585
  47.4 2.4 %collective-permute-done.8.refs_4_.refs_2_ = bf16[128,512]{1,0:T(8,128)(2,1)S(1)} collective-permute-done((bf16[128,512]{1,0:T(8,128)(2,1)}, bf16[128,512]{1,0:T(8,128)(2,1)S(1)}, u32[]{:S(2)}, u32[]{:S(2)}) %collective-permute-start.8) | collective-permute-done | bytes 131104 | tf_op jit(solution)/shard_map/ppermute | solution.py:585
  53.6 7.6 %collective-permute-done.19.refs_7_ = bf16[4,5,16,512]{3,2,1,0:T(8,128)(2,1)S(1)} collective-permute-done((bf16[4,5,16,512]{3,2,1,0:T(8,128)(2,1)S(1)}, bf16[4,5,16,512]{3,2,1,0:T(8,128)(2,1)S(1)}, u32[]{:S(2)}, u32[]{:S(2)}) %collective-permute-start.19) | collective-permute-done | bytes 327712 | tf_op jit(solution)/shard_map/ppermute | solution.py:588
  62.4 4.7 %attend.1 = (f32[256,512]{1,0:T(8,128)S(1)}, bf16[512,512]{1,0:T(8,128)(2,1)S(1)}, bf16[256,512]{1,0:T(8,128)(2,1)S(1)}, bf16[256,512]{1,0:T(8,128)(2,1)S(1)}, b...) custom-call(s32[1]{0:T(128)S(6)} %copy.28.long_len, ...), custom_call_target="tpu_custom_call" | custom-call | flops 1073741824 | bytes 10485760 | tf_op jit(solution)/shard_map/attend/pallas_call | solution.py:682
  67.2 8.4 %middle.1 = (bf16[512,512]{1,0:T(8,128)(2,1)S(1)}, f32[256,512]{1,0:T(8,128)S(1)}, bf16[256,512]{1,0:T(8,128)(2,1)S(1)}, bf16[4,10,16,512]{3,2,1,0:T(8,128)(2,1)...) custom-call(f32[256,512]{1,0:T(8,128)S(1)} %get-tuple-element.103.fi, ...), custom_call_target="tpu_custom_call" | custom-call | flops 4294967296 | bytes 20971520 | tf_op jit(solution)/shard_map/middle/pallas_call | solution.py:707
  76.0 3.4 %attend_back.1 = (bf16[256,512]{1,0:T(8,128)(2,1)S(1)}, bf16[512,512]{1,0:T(8,128)(2,1)S(1)}, bf16[512,512]{1,0:T(8,128)(2,1)S(1)}) custom-call(bf16[256,512]{1,0:T(8,128)(2,1)S(1)} %get-tuple-element.117.gmix, bf16[256,512]{1,0:T(8,128)(2,1)S(1)} %get-tuple-element.118.q, bf16[512,512]{1,0:T(8,128)(2,1)S(1)} %get-tuple-element.119.k, ...), custom_call_target="tpu_custom_call" | custom-call | flops 1073741824 | bytes 8388608 | tf_op jit(solution)/shard_map/attend_back/pallas_call | solution.py:738
  79.4 3.9 %leave.1 = (f32[128,512]{1,0:T(8,128)S(1)}, bf16[256,512]{1,0:T(8,128)(2,1)S(1)}, bf16[128,512]{1,0:T(8,128)(2,1)S(1)}, bf16[128,512]{1,0:T(8,128)(2,1)S(1)}, bf...) custom-call(bf16[512,512]{1,0:T(8,128)(2,1)S(1)} %get-tuple-element., ...), custom_call_target="tpu_custom_call" | custom-call | flops 1342177280 | bytes 8388608 | tf_op jit(solution)/shard_map/leave/pallas_call | solution.py:751
  86.0 4.9 %collective-permute-start.32 = (bf16[128,512]{1,0:T(8,128)(2,1)S(1)}, bf16[128,512]{1,0:T(8,128)(2,1)S(1)}, u32[]{:S(2)}, u32[]{:S(2)}) collective-permute-start(bf16[128,512]{1,0:T(8,128)(2,1)S(1)} %get-tuple-element.135), channel_id=1, source_target_pairs={{0,2},{2,0},{3,1},{4,6},{6,4},{7,5},{8,10},{10,8},{11,9},{12,14},{... | collective-permute-start | bytes 393224 | tf_op jit(solution)/shard_map/ppermute | solution.py:585
  90.9 2.5 %collective-permute-start.33 = (bf16[128,512]{1,0:T(8,128)(2,1)S(1)}, bf16[128,512]{1,0:T(8,128)(2,1)S(1)}, u32[]{:S(2)}, u32[]{:S(2)}) collective-permute-start(bf16[128,512]{1,0:T(8,128)(2,1)S(1)} %get-tuple-element.136), channel_id=1, source_target_pairs={{0,3},{2,1},{3,0},{4,7},{6,5},{7,4},{8,11},{10,9},{11,8},{12,15},{... | collective-permute-start | bytes 393224 | tf_op jit(solution)/shard_map/ppermute | solution.py:585
  93.4 7.6 %collective-permute-done.27.from_y = bf16[2,4,5,16,512]{4,3,2,1,0:T(8,128)(2,1)S(1)} collective-permute-done((bf16[2,4,5,16,512]{4,3,2,1,0:T(8,128)(2,1)S(1)}, bf16[2,4,5,16,512]{4,3,2,1,0:T(8,128)(2,1)S(1)}, u32[]{:S(2)}, u32[]{:S(2)}) %collective-permute-start.27) | collective-permute-done | bytes 655392 | tf_op jit(solution)/shard_map/ppermute | solution.py:588
  109.9 3.7 %collective-permute-done.29.then_x = bf16[4,5,16,512]{3,2,1,0:T(8,128)(2,1)S(1)} collective-permute-done((bf16[4,5,16,512]{3,2,1,0:T(8,128)(2,1)S(1)}, bf16[4,5,16,512]{3,2,1,0:T(8,128)(2,1)S(1)}, u32[]{:S(2)}, u32[]{:S(2)}) %collective-permute-start.29) | collective-permute-done | bytes 327712 | tf_op jit(solution)/shard_map/ppermute | solution.py:588
  116.2 2.3 %collective-permute-start.35 = (bf16[10,16,512]{2,1,0:T(8,128)(2,1)S(1)}, bf16[10,16,512]{2,1,0:T(8,128)(2,1)S(1)}, u32[]{:S(2)}, u32[]{:S(2)}) collective-permute-start(bf16[10,16,512]{2,1,0:T(8,128)(2,1)S(1)} %get-tuple-element.141), channel_id=1, source_target_pairs={{0,2},{1,3},{2,0},{3,1},{4,6},{5,7},{6,4},{7,5},{8,10},{9,11},{10,... | collective-permute-start | bytes 491528 | tf_op jit(solution)/shard_map/ppermute | solution.py:585
  119.3 3.3 %collective-permute-start.36 = (bf16[10,16,512]{2,1,0:T(8,128)(2,1)S(1)}, bf16[10,16,512]{2,1,0:T(8,128)(2,1)S(1)}, u32[]{:S(2)}, u32[]{:S(2)}) collective-permute-start(bf16[10,16,512]{2,1,0:T(8,128)(2,1)S(1)} %get-tuple-element.142), channel_id=1, source_target_pairs={{0,3},{1,2},{2,1},{3,0},{4,7},{5,6},{6,5},{7,4},{8,11},{9,10},{10,... | collective-permute-start | bytes 491528 | tf_op jit(solution)/shard_map/ppermute | solution.py:585
  128.9 3.9 %collective-permute-start.42 = (bf16[4,16,512]{2,1,0:T(8,128)(2,1)S(1)}, bf16[4,16,512]{2,1,0:T(8,128)(2,1)S(1)}, u32[]{:S(2)}, u32[]{:S(2)}) collective-permute-start(bf16[4,16,512]{2,1,0:T(8,128)(2,1)S(1)} %get-tuple-element.150), channel_id=1, source_target_pairs={{0,3},{1,2},{2,1},{3,0},{4,7},{5,6},{6,5},{7,4},{8,11},{9,10},{10,... | collective-permute-start | bytes 196616 | tf_op jit(solution)/shard_map/ppermute | solution.py:585
  (88 shorter events, 41.1 us)
Async XLA Ops:
  16.7 13.8 %collective-permute-start.4 = (bf16[10,16,512]{2,1,0:T(8,128)(2,1)}, bf16[10,16,512]{2,1,0:T(8,128)(2,1)S(1)}, u32[]{:S(2)}, u32[]{:S(2)}) collective-permute-start(bf16[10,16,512]{2,1,0:T(8,128)(2,1)} %get-tuple-element.95), channel_id=1, source_target_pairs={{0,2},{1,3},{2,0},{3,1},{4,6},{5,7},{6,4},{7,5},{8,10},{9,11},{10,... | collective-permute-start | bytes 491528 | tf_op jit(solution)/shard_map/ppermute | solution.py:585
  16.7 13.8 %collective-permute-start.3 = (bf16[10,16,512]{2,1,0:T(8,128)(2,1)}, bf16[10,16,512]{2,1,0:T(8,128)(2,1)S(1)}, u32[]{:S(2)}, u32[]{:S(2)}) collective-permute-start(bf16[10,16,512]{2,1,0:T(8,128)(2,1)} %get-tuple-element.95), channel_id=1, source_target_pairs={{0,1},{1,0},{2,3},{3,2},{4,5},{5,4},{6,7},{7,6},{8,9},{9,8},{10,11... | collective-permute-start | bytes 491528 | tf_op jit(solution)/shard_map/ppermute | solution.py:585
  19.3 12.3 %collective-permute-start.11 = (bf16[4,4,16,512]{3,2,1,0:T(8,128)(2,1)S(1)}, bf16[4,4,16,512]{3,2,1,0:T(8,128)(2,1)S(1)}, u32[]{:S(2)}, u32[]{:S(2)}) collective-permute-start(bf16[4,4,16,512]{3,2,1,0:T(8,128)(2,1)S(1)} %pad_maximum_fusion.1.refs_5_.refs_0_), channel_id=1, source_target_pairs={{0,24},{4,28},{8,16},{12,20},{16,8},{20,12},{24,0},{28,4},{1,25},{... | collective-permute-start | bytes 786440 | tf_op jit(solution)/shard_map/ppermute | solution.py:588
  21.8 11.1 %collective-permute-start.10 = (bf16[4,4,16,512]{3,2,1,0:T(8,128)(2,1)S(1)}, bf16[4,4,16,512]{3,2,1,0:T(8,128)(2,1)S(1)}, u32[]{:S(2)}, u32[]{:S(2)}) collective-permute-start(bf16[4,4,16,512]{3,2,1,0:T(8,128)(2,1)S(1)} %pad_maximum_fusion.1.refs_5_.refs_0_), channel_id=1, source_target_pairs={{0,16},{4,20},{8,24},{12,28},{16,0},{20,4},{24,8},{28,12},{1,17},{... | collective-permute-start | bytes 786440 | tf_op jit(solution)/shard_map/ppermute | solution.py:588
  23.2 9.9 %collective-permute-start.9 = (bf16[4,4,16,512]{3,2,1,0:T(8,128)(2,1)S(1)}, bf16[4,4,16,512]{3,2,1,0:T(8,128)(2,1)S(1)}, u32[]{:S(2)}, u32[]{:S(2)}) collective-permute-start(bf16[4,4,16,512]{3,2,1,0:T(8,128)(2,1)S(1)} %pad_maximum_fusion.1.refs_5_.refs_0_), channel_id=1, source_target_pairs={{0,8},{4,12},{8,0},{12,4},{16,24},{20,28},{24,16},{28,20},{1,9},{5... | collective-permute-start | bytes 786440 | tf_op jit(solution)/shard_map/ppermute | solution.py:588
  33.2 17.1 %collective-permute-start.17 = (bf16[4,10,16,512]{3,2,1,0:T(8,128)(2,1)S(1)}, bf16[4,10,16,512]{3,2,1,0:T(8,128)(2,1)S(1)}, u32[]{:S(2)}, u32[]{:S(2)}) collective-permute-start(bf16[4,10,16,512]{3,2,1,0:T(8,128)(2,1)S(1)} %pad_maximum_fusion.refs_3_), channel_id=1, source_target_pairs={{0,16},{4,20},{8,24},{12,28},{16,0},{20,4},{24,8},{28,12},{1,17},{... | collective-permute-start | bytes 1966088 | tf_op jit(solution)/shard_map/ppermute | solution.py:588
  34.6 16.4 %collective-permute-start.16 = (bf16[4,10,16,512]{3,2,1,0:T(8,128)(2,1)S(1)}, bf16[4,10,16,512]{3,2,1,0:T(8,128)(2,1)S(1)}, u32[]{:S(2)}, u32[]{:S(2)}) collective-permute-start(bf16[4,10,16,512]{3,2,1,0:T(8,128)(2,1)S(1)} %pad_maximum_fusion.refs_3_), channel_id=1, source_target_pairs={{0,8},{4,12},{8,0},{12,4},{16,24},{20,28},{24,16},{28,20},{1,9},{5... | collective-permute-start | bytes 1966088 | tf_op jit(solution)/shard_map/ppermute | solution.py:588
  35.3 14.5 %collective-permute-start.6 = (bf16[256,512]{1,0:T(8,128)(2,1)}, bf16[256,512]{1,0:T(8,128)(2,1)S(1)}, u32[]{:S(2)}, u32[]{:S(2)}) collective-permute-start(bf16[256,512]{1,0:T(8,128)(2,1)} %get-tuple-element.96), channel_id=1, source_target_pairs={{0,1},{1,0},{2,3},{3,2},{4,5},{5,4},{6,7},{7,6},{8,9},{9,8},{10,11... | collective-permute-start | bytes 786440 | tf_op jit(solution)/shard_map/ppermute | solution.py:585
  51.0 16.2 %collective-permute-start.20 = (bf16[4,10,16,512]{3,2,1,0:T(8,128)(2,1)S(1)}, bf16[4,10,16,512]{3,2,1,0:T(8,128)(2,1)S(1)}, u32[]{:S(2)}, u32[]{:S(2)}) collective-permute-start(bf16[4,10,16,512]{3,2,1,0:T(8,128)(2,1)S(1)} %pad_maximum_fusion.refs_3_), channel_id=1, source_target_pairs={{0,4},{4,0},{8,12},{12,8},{16,20},{20,16},{24,28},{28,24},{1,5},{5... | collective-permute-start | bytes 1966088 | tf_op jit(solution)/shard_map/ppermute | solution.py:588
  53.1 14.1 %collective-permute-start.22 = (bf16[4,10,16,512]{3,2,1,0:T(8,128)(2,1)S(1)}, bf16[4,10,16,512]{3,2,1,0:T(8,128)(2,1)S(1)}, u32[]{:S(2)}, u32[]{:S(2)}) collective-permute-start(bf16[4,10,16,512]{3,2,1,0:T(8,128)(2,1)S(1)} %collective-permute-done.17.refs_5_), channel_id=1, source_target_pairs={{0,4},{4,0},{8,12},{12,8},{16,20},{20,16},{24,28},{28,24},{1,5},{5... | collective-permute-start | bytes 1966088 | tf_op jit(solution)/shard_map/ppermute | solution.py:588
  53.1 14.1 %collective-permute-start.21 = (bf16[4,10,16,512]{3,2,1,0:T(8,128)(2,1)S(1)}, bf16[4,10,16,512]{3,2,1,0:T(8,128)(2,1)S(1)}, u32[]{:S(2)}, u32[]{:S(2)}) collective-permute-start(bf16[4,10,16,512]{3,2,1,0:T(8,128)(2,1)S(1)} %collective-permute-done.16.refs_4_), channel_id=1, source_target_pairs={{0,4},{4,0},{8,12},{12,8},{16,20},{20,16},{24,28},{28,24},{1,5},{5... | collective-permute-start | bytes 1966088 | tf_op jit(solution)/shard_map/ppermute | solution.py:588
  83.8 18.8 %collective-permute-start.28 = (bf16[16,4,16,512]{3,2,1,0:T(8,128)(2,1)S(1)}, bf16[16,4,16,512]{3,2,1,0:T(8,128)(2,1)S(1)}, u32[]{:S(2)}, u32[]{:S(2)}) collective-permute-start(bf16[16,4,16,512]{3,2,1,0:T(8,128)(2,1)S(1)} %get-tuple-element.129), channel_id=1, source_target_pairs={{0,4},{4,0},{8,12},{12,8},{16,20},{20,16},{24,28},{28,24},{1,5},{5... | collective-permute-start | bytes 3145736 | tf_op jit(solution)/shard_map/ppermute | solution.py:588
  84.0 17.0 %collective-permute-start.27 = (bf16[2,4,5,16,512]{4,3,2,1,0:T(8,128)(2,1)S(1)}, bf16[2,4,5,16,512]{4,3,2,1,0:T(8,128)(2,1)S(1)}, u32[]{:S(2)}, u32[]{:S(2)}) collective-permute-start(bf16[2,4,5,16,512]{4,3,2,1,0:T(8,128)(2,1)S(1)} %get-tuple-element.112), channel_id=1, source_target_pairs={{0,16},{4,20},{8,24},{12,28},{16,0},{20,4},{24,8},{28,12},{1,17},{... | collective-permute-start | bytes 1966088 | tf_op jit(solution)/shard_map/ppermute | solution.py:588
  85.3 17.0 %collective-permute-start.26 = (bf16[2,4,5,16,512]{4,3,2,1,0:T(8,128)(2,1)S(1)}, bf16[2,4,5,16,512]{4,3,2,1,0:T(8,128)(2,1)S(1)}, u32[]{:S(2)}, u32[]{:S(2)}) collective-permute-start(bf16[2,4,5,16,512]{4,3,2,1,0:T(8,128)(2,1)S(1)} %get-tuple-element.111), channel_id=1, source_target_pairs={{0,8},{4,12},{8,0},{12,4},{16,24},{20,28},{24,16},{28,20},{1,9},{5... | collective-permute-start | bytes 1966088 | tf_op jit(solution)/shard_map/ppermute | solution.py:588
  86.0 19.0 %collective-permute-start.32 = (bf16[128,512]{1,0:T(8,128)(2,1)S(1)}, bf16[128,512]{1,0:T(8,128)(2,1)S(1)}, u32[]{:S(2)}, u32[]{:S(2)}) collective-permute-start(bf16[128,512]{1,0:T(8,128)(2,1)S(1)} %get-tuple-element.135), channel_id=1, source_target_pairs={{0,2},{2,0},{3,1},{4,6},{6,4},{7,5},{8,10},{10,8},{11,9},{12,14},{... | collective-permute-start | bytes 393224 | tf_op jit(solution)/shard_map/ppermute | solution.py:585
  90.9 14.7 %collective-permute-start.33 = (bf16[128,512]{1,0:T(8,128)(2,1)S(1)}, bf16[128,512]{1,0:T(8,128)(2,1)S(1)}, u32[]{:S(2)}, u32[]{:S(2)}) collective-permute-start(bf16[128,512]{1,0:T(8,128)(2,1)S(1)} %get-tuple-element.136), channel_id=1, source_target_pairs={{0,3},{2,1},{3,0},{4,7},{6,5},{7,4},{8,11},{10,9},{11,8},{12,15},{... | collective-permute-start | bytes 393224 | tf_op jit(solution)/shard_map/ppermute | solution.py:585
  102.9 10.7 %collective-permute-start.29 = (bf16[4,5,16,512]{3,2,1,0:T(8,128)(2,1)S(1)}, bf16[4,5,16,512]{3,2,1,0:T(8,128)(2,1)S(1)}, u32[]{:S(2)}, u32[]{:S(2)}) collective-permute-start(bf16[4,5,16,512]{3,2,1,0:T(8,128)(2,1)S(1)} %get-tuple-element.132), channel_id=1, source_target_pairs={{0,8},{4,12},{8,0},{12,4},{16,24},{20,28},{24,16},{28,20},{1,9},{5... | collective-permute-start | bytes 983048 | tf_op jit(solution)/shard_map/ppermute | solution.py:588
  103.6 10.7 %collective-permute-start.30 = (bf16[4,5,16,512]{3,2,1,0:T(8,128)(2,1)S(1)}, bf16[4,5,16,512]{3,2,1,0:T(8,128)(2,1)S(1)}, u32[]{:S(2)}, u32[]{:S(2)}) collective-permute-start(bf16[4,5,16,512]{3,2,1,0:T(8,128)(2,1)S(1)} %get-tuple-element.133), channel_id=1, source_target_pairs={{0,16},{4,20},{8,24},{12,28},{16,0},{20,4},{24,8},{28,12},{1,17},{... | collective-permute-start | bytes 983048 | tf_op jit(solution)/shard_map/ppermute | solution.py:588
  105.0 14.3 %collective-permute-start.37 = (bf16[4,4,16,512]{3,2,1,0:T(8,128)(2,1)S(1)}, bf16[4,4,16,512]{3,2,1,0:T(8,128)(2,1)S(1)}, u32[]{:S(2)}, u32[]{:S(2)}) collective-permute-start(bf16[4,4,16,512]{3,2,1,0:T(8,128)(2,1)S(1)} %get-tuple-element.144), channel_id=1, source_target_pairs={{0,8},{4,12},{8,0},{12,4},{16,24},{20,28},{24,16},{28,20},{1,9},{5... | collective-permute-start | bytes 786440 | tf_op jit(solution)/shard_map/ppermute | solution.py:588
  105.6 17.8 %collective-permute-start.38 = (bf16[4,4,16,512]{3,2,1,0:T(8,128)(2,1)S(1)}, bf16[4,4,16,512]{3,2,1,0:T(8,128)(2,1)S(1)}, u32[]{:S(2)}, u32[]{:S(2)}) collective-permute-start(bf16[4,4,16,512]{3,2,1,0:T(8,128)(2,1)S(1)} %get-tuple-element.145), channel_id=1, source_target_pairs={{0,16},{4,20},{8,24},{12,28},{16,0},{20,4},{24,8},{28,12},{1,17},{... | collective-permute-start | bytes 786440 | tf_op jit(solution)/shard_map/ppermute | solution.py:588
  108.7 14.6 %collective-permute-start.39 = (bf16[4,4,16,512]{3,2,1,0:T(8,128)(2,1)S(1)}, bf16[4,4,16,512]{3,2,1,0:T(8,128)(2,1)S(1)}, u32[]{:S(2)}, u32[]{:S(2)}) collective-permute-start(bf16[4,4,16,512]{3,2,1,0:T(8,128)(2,1)S(1)} %get-tuple-element.146), channel_id=1, source_target_pairs={{0,24},{4,28},{8,16},{12,20},{16,8},{20,12},{24,0},{28,4},{1,25},{... | collective-permute-start | bytes 786440 | tf_op jit(solution)/shard_map/ppermute | solution.py:588
  114.5 20.6 %collective-permute-start.34 = (bf16[10,16,512]{2,1,0:T(8,128)(2,1)S(1)}, bf16[10,16,512]{2,1,0:T(8,128)(2,1)S(1)}, u32[]{:S(2)}, u32[]{:S(2)}) collective-permute-start(bf16[10,16,512]{2,1,0:T(8,128)(2,1)S(1)} %get-tuple-element.140), channel_id=1, source_target_pairs={{0,1},{1,0},{2,3},{3,2},{4,5},{5,4},{6,7},{7,6},{8,9},{9,8},{10,11... | collective-permute-start | bytes 491528 | tf_op jit(solution)/shard_map/ppermute | solution.py:585
  116.2 19.0 %collective-permute-start.35 = (bf16[10,16,512]{2,1,0:T(8,128)(2,1)S(1)}, bf16[10,16,512]{2,1,0:T(8,128)(2,1)S(1)}, u32[]{:S(2)}, u32[]{:S(2)}) collective-permute-start(bf16[10,16,512]{2,1,0:T(8,128)(2,1)S(1)} %get-tuple-element.141), channel_id=1, source_target_pairs={{0,2},{1,3},{2,0},{3,1},{4,6},{5,7},{6,4},{7,5},{8,10},{9,11},{10,... | collective-permute-start | bytes 491528 | tf_op jit(solution)/shard_map/ppermute | solution.py:585
  119.3 15.9 %collective-permute-start.36 = (bf16[10,16,512]{2,1,0:T(8,128)(2,1)S(1)}, bf16[10,16,512]{2,1,0:T(8,128)(2,1)S(1)}, u32[]{:S(2)}, u32[]{:S(2)}) collective-permute-start(bf16[10,16,512]{2,1,0:T(8,128)(2,1)S(1)} %get-tuple-element.142), channel_id=1, source_target_pairs={{0,3},{1,2},{2,1},{3,0},{4,7},{5,6},{6,5},{7,4},{8,11},{9,10},{10,... | collective-permute-start | bytes 491528 | tf_op jit(solution)/shard_map/ppermute | solution.py:585
  (24 other events, 371.5 us)

commit v4 on v3

--- a/solution.py
+++ b/solution.py
@@ -523,7 +523,7 @@
 def finish_body(*refs):
     late, early, rows = (refs[:4], refs[4:8], refs[8:13])
     row_outs, early_outs = (refs[13:17], refs[17:21])
-    out_o, up_o, down_o, norm_o = refs[21:]
+    out_o, up_o, down_o, gain_o, bias_o = refs[21:]
     width = out_o.shape[1]
     chunks = up_o.shape[1] // width
 
@@ -536,11 +536,13 @@
     for c in range(chunks):
         up_o[:, c * width : (c + 1) * width] = total(late, 1 + c)
         down_o[:, c * width : (c + 1) * width] = total(late, 1 + chunks + c)
-    shard = norm_o.shape[1]
+    shard = gain_o.shape[1]
     row = lax.broadcasted_iota(jnp.int32, (width, shard), 0)
     col = lax.broadcasted_iota(jnp.int32, (width, shard), 1)
     chosen = (row == col + own_place()[0] * shard).astype(F32)
-    norm_o[...] = mm(total(late, 1 + 2 * chunks), chosen, NN, lax.Precision.HIGHEST)
+    norms = mm(total(late, 1 + 2 * chunks), chosen, NN, lax.Precision.HIGHEST)
+    gain_o[...] = norms[:2]
+    bias_o[...] = norms[2:4]
     for i, out in enumerate(early_outs):
         out[...] = total(early, i)
 
@@ -642,7 +644,7 @@
     if direct:
         early, late = pays[3:]
         early_places = places(early)
-        late = after(late, *early_places)
+        late = after(late, early_places[1], early_places[2])
         late_places = places(late)
         early_near = spread(jnp.stack(early_places))
         column = jnp.stack(late_places)
@@ -657,7 +659,6 @@
         half = late_pieces // 2
         near1, near2 = (swap_dp(column, 2), swap_dp(column, 4))
         near3 = [swap_dp(near1[:, :half], 4), swap_dp(near2[:, half:], 2)]
-        late_full = cross([column, near1, near2] + near3)
     if not direct:
         got1, got2, got3 = (
             swap_seq(pay1, 1),
@@ -703,6 +704,11 @@
         24,
     )(long_lengths, short_lengths, long_tokens, short_tokens, got1, got2, got3, *early_full)
 
+    if direct:
+        near3, first = lax.optimization_barrier((near3, first))
+        late_near = [column, near1, near2]
+        late_far = [swap_dp(part, 1) for part in late_near + list(near3)]
+        late_full = late_near + list(near3) + late_far
     block = (n_long, width)
     middle_outs = call(
         functools.partial(middle_body, direct, late_layout),
@@ -816,14 +822,15 @@
             row_outs
             + [((shard, width), F32, VMEM)] * 5
             + [((shard, hidden), F32, VMEM)] * 2
-            + [((BAND, shard), F32, VMEM)],
+            + [((2, shard), F32, VMEM)] * 2,
             [VMEM] * 13,
             [],
             (0, MIB),
             "finish",
             16,
         )(*late_ends, *early_ends, *row_ins)
-        row_grads, early_sum, (grad_out, grad_up, grad_down, norms) = (ends[:4], ends[4:8], ends[8:])
+        row_grads, early_sum = (ends[:4], ends[4:8])
+        grad_out, grad_up, grad_down, grad_gain, grad_bias = ends[8:]
     else:
 
         def scatter(parts):
@@ -842,6 +849,7 @@
         )
         norms = lax.psum(from_slots(late_parts)[-1, :BAND].astype(F32), ("dp", "seq"))
         norms = lax.dynamic_slice(norms, (0, device * shard), (BAND, shard))
+        grad_gain, grad_bias = (norms[:2], norms[2:4])
         row_grads = call(
             return_rows, row_outs, [VMEM] * 5, [], (0, MIB), "return", 16
         )(grad_blocks[0], out_blocks, *got)
@@ -858,8 +866,8 @@
         grad_up,
         grad_down.T,
         early_sum[3].T,
-        norms[:2],
-        norms[2:4],
+        grad_gain,
+        grad_bias,
     )
 
 

time: 137 us -> 132 us (0.964)
  waiting for transfers between devices: 47.3 us -> 38.9 us
  starting transfers between devices: 60 us -> 63.5 us
    ppermute x25, waiting for transfers between devices: 23.6 us -> 17.5 us  [swap_dp(): return lax.ppermute(value, 'dp', [(i, i ^ mask) for i in range(dp_count)])]
    ppermute x18, waiting for transfers between devices: 23.7 us -> 21.4 us  [swap_seq(): return lax.ppermute(value, 'seq', pairs)]
    ppermute x18, starting transfers between devices: 41.9 us -> 44 us  [swap_seq(): return lax.ppermute(value, 'seq', pairs)]
    ppermute x25, starting transfers between devices: 18 us -> 19.5 us  [swap_dp(): return lax.ppermute(value, 'dp', [(i, i ^ mask) for i in range(dp_count)])]
  transfers between devices with their start and end apart: 43 -> 43, of which waited for: 21 -> 20; matrix products, arithmetic and copies ran while one was open for 2% -> 2% of each run, Pallas kernels for 9% -> 10%
where the time goes in v4:
time: 132 us
  starting transfers between devices  63.5 us (48%)
  waiting for transfers between devices  38.9 us (29%)
  Pallas kernels  25.3 us (19%)
  other arithmetic  2.18 us (2%)
  between operations  1.64 us (1%)
    ppermute x18, starting transfers between devices, swap_seq(): return lax.ppermute(value, 'seq', pairs)  44 us
    ppermute x18, waiting for transfers between devices, swap_seq(): return lax.ppermute(value, 'seq', pairs)  21.4 us
    ppermute x25, starting transfers between devices, swap_dp(): return lax.ppermute(value, 'dp', [(i, i ^ mask) for i in range(dp_count)])  19.5 us
    ppermute x25, waiting for transfers between devices, swap_dp(): return lax.ppermute(value, 'dp', [(i, i ^ mask) for i in range(dp_count)])  17.5 us
    pallas_call x1, Pallas kernels, local(): call(functools.partial(middle_body, direct, late_layout), [((keys, width)...  8.35 us
    pallas_call x1, Pallas kernels, local(): call(functools.partial(attend_body, direct, early_layout), [((rows, width...  4.72 us
    pallas_call x1, Pallas kernels, local(): call(functools.partial(leave_body, direct, early_layout), [(block, F32, V...  3.89 us
    pallas_call x1, Pallas kernels, local(): call(attend_back_body, [((rows, width), BF, VMEM), ((keys, width), BF, VM...  3.4 us
  transfers between devices with their start and end apart: 43, of which 20 were waited for; matrix products, arithmetic and copies ran while one was open for 2% of the time, Pallas kernels for 10%

profile of v4, /device:TPU:0, one launch (start us, length us, event | category | flops | bytes accessed | tf_op | source)
XLA Modules:
  0.0 131.6 jit_solution(4082691098338114269)
XLA Ops:
  0.7 2.4 %pack.1 = (bf16[256,512]{1,0:T(8,128)(2,1)}, bf16[128,512]{1,0:T(8,128)(2,1)}, bf16[128,512]{1,0:T(8,128)(2,1)}, bf16[4,16,512]{2,1,0:T(8,128)(2,1)}, bf16[10,16,512]{2,1,0:T(8,128)(2,1)}) custom-call(bf16[1,128,512]{2,1,0:T(8,128)(2,1)} %refs_0_.3, bf16[2,64,512]{2,1,0:T(8,128)(2,1)} %refs_1_.3, bf16[1,128,512]{2,1,0:T(8,128)(2,1)} %long_cot.1, ...), custom_call_target="tpu_custom_call" | custom-call | bytes 4194304 | tf_op jit(solution)/shard_map/pack/pallas_call | solution.py:607
  3.1 4.0 %collective-permute-start.1 = (bf16[4,16,512]{2,1,0:T(8,128)(2,1)}, bf16[4,16,512]{2,1,0:T(8,128)(2,1)S(1)}, u32[]{:S(2)}, u32[]{:S(2)}) collective-permute-start(bf16[4,16,512]{2,1,0:T(8,128)(2,1)} %get-tuple-element.95), channel_id=1, source_target_pairs={{0,2},{1,3},{2,0},{3,1},{4,6},{5,7},{6,4},{7,5},{8,10},{9,11},{10,... | collective-permute-start | bytes 196616 | tf_op jit(solution)/shard_map/ppermute | solution.py:587
  11.6 4.6 %collective-permute-start.4 = (bf16[10,16,512]{2,1,0:T(8,128)(2,1)}, bf16[10,16,512]{2,1,0:T(8,128)(2,1)S(1)}, u32[]{:S(2)}, u32[]{:S(2)}) collective-permute-start(bf16[10,16,512]{2,1,0:T(8,128)(2,1)} %get-tuple-element.96), channel_id=1, source_target_pairs={{0,3},{1,2},{2,1},{3,0},{4,7},{5,6},{6,5},{7,4},{8,11},{9,10},{10,... | collective-permute-start | bytes 491528 | tf_op jit(solution)/shard_map/ppermute | solution.py:587
  17.7 2.5 %collective-permute-start.8 = (bf16[4,4,16,512]{3,2,1,0:T(8,128)(2,1)S(1)}, bf16[4,4,16,512]{3,2,1,0:T(8,128)(2,1)S(1)}, u32[]{:S(2)}, u32[]{:S(2)}) collective-permute-start(bf16[4,4,16,512]{3,2,1,0:T(8,128)(2,1)S(1)} %pad_maximum_fusion.1.refs_5_.refs_0_), channel_id=1, source_target_pairs={{0,24},{4,28},{8,16},{12,20},{16,8},{20,12},{24,0},{28,4},{1,25},{... | collective-permute-start | bytes 786440 | tf_op jit(solution)/shard_map/ppermute | solution.py:590
  23.0 6.0 %collective-permute-done.3 = bf16[10,16,512]{2,1,0:T(8,128)(2,1)S(1)} collective-permute-done((bf16[10,16,512]{2,1,0:T(8,128)(2,1)}, bf16[10,16,512]{2,1,0:T(8,128)(2,1)S(1)}, u32[]{:S(2)}, u32[]{:S(2)}) %collective-permute-start.3) | collective-permute-done | bytes 163872 | tf_op jit(solution)/shard_map/ppermute | solution.py:587
  33.2 3.5 %collective-permute-start.13 = (bf16[256,512]{1,0:T(8,128)(2,1)}, bf16[256,512]{1,0:T(8,128)(2,1)S(1)}, u32[]{:S(2)}, u32[]{:S(2)}) collective-permute-start(bf16[256,512]{1,0:T(8,128)(2,1)} %get-tuple-element.101), channel_id=1, source_target_pairs={{0,1},{1,0},{2,3},{3,2},{4,5},{5,4},{6,7},{7,6},{8,9},{9,8},{10,11... | collective-permute-start | bytes 786440 | tf_op jit(solution)/shard_map/ppermute | solution.py:587
  36.7 2.2 %collective-permute-start.14 = (bf16[128,512]{1,0:T(8,128)(2,1)}, bf16[128,512]{1,0:T(8,128)(2,1)S(1)}, u32[]{:S(2)}, u32[]{:S(2)}) collective-permute-start(bf16[128,512]{1,0:T(8,128)(2,1)} %get-tuple-element.102), channel_id=1, source_target_pairs={{0,2},{1,3},{2,0},{4,6},{5,7},{6,4},{8,10},{9,11},{10,8},{12,14},{... | collective-permute-start | bytes 393224 | tf_op jit(solution)/shard_map/ppermute | solution.py:587
  38.9 2.6 %collective-permute-start.15 = (bf16[128,512]{1,0:T(8,128)(2,1)}, bf16[128,512]{1,0:T(8,128)(2,1)S(1)}, u32[]{:S(2)}, u32[]{:S(2)}) collective-permute-start(bf16[128,512]{1,0:T(8,128)(2,1)} %get-tuple-element.103), channel_id=1, source_target_pairs={{0,3},{1,2},{3,0},{4,7},{5,6},{7,4},{8,11},{9,10},{11,8},{12,15},{... | collective-permute-start | bytes 393224 | tf_op jit(solution)/shard_map/ppermute | solution.py:587
  41.6 4.2 %collective-permute-done.14.refs_3_.refs_1_ = bf16[128,512]{1,0:T(8,128)(2,1)S(1)} collective-permute-done((bf16[128,512]{1,0:T(8,128)(2,1)}, bf16[128,512]{1,0:T(8,128)(2,1)S(1)}, u32[]{:S(2)}, u32[]{:S(2)}) %collective-permute-start.14) | collective-permute-done | bytes 131104 | tf_op jit(solution)/shard_map/ppermute | solution.py:587
  45.7 2.1 %collective-permute-done.15.refs_4_.refs_2_ = bf16[128,512]{1,0:T(8,128)(2,1)S(1)} collective-permute-done((bf16[128,512]{1,0:T(8,128)(2,1)}, bf16[128,512]{1,0:T(8,128)(2,1)S(1)}, u32[]{:S(2)}, u32[]{:S(2)}) %collective-permute-start.15) | collective-permute-done | bytes 131104 | tf_op jit(solution)/shard_map/ppermute | solution.py:587
  51.7 4.7 %attend.1 = (f32[256,512]{1,0:T(8,128)S(1)}, bf16[512,512]{1,0:T(8,128)(2,1)S(1)}, bf16[256,512]{1,0:T(8,128)(2,1)S(1)}, bf16[256,512]{1,0:T(8,128)(2,1)S(1)}, b...) custom-call(s32[1]{0:T(128)S(6)} %copy.28.long_len, ...), custom_call_target="tpu_custom_call" | custom-call | flops 1073741824 | bytes 10485760 | tf_op jit(solution)/shard_map/attend/pallas_call | solution.py:683
  56.4 2.2 %collective-permute-done.12.refs_7_ = bf16[4,5,16,512]{3,2,1,0:T(8,128)(2,1)S(1)} collective-permute-done((bf16[4,5,16,512]{3,2,1,0:T(8,128)(2,1)S(1)}, bf16[4,5,16,512]{3,2,1,0:T(8,128)(2,1)S(1)}, u32[]{:S(2)}, u32[]{:S(2)}) %collective-permute-start.12) | collective-permute-done | bytes 327712 | tf_op jit(solution)/shard_map/ppermute | solution.py:590
  61.2 8.3 %middle.1 = (bf16[512,512]{1,0:T(8,128)(2,1)S(1)}, f32[256,512]{1,0:T(8,128)S(1)}, bf16[256,512]{1,0:T(8,128)(2,1)S(1)}, bf16[4,10,16,512]{3,2,1,0:T(8,128)(2,1)...) custom-call(f32[256,512]{1,0:T(8,128)S(1)} %get-tuple-element.109.fi, ...), custom_call_target="tpu_custom_call" | custom-call | flops 4294967296 | bytes 20971520 | tf_op jit(solution)/shard_map/middle/pallas_call | solution.py:713
  69.8 3.4 %attend_back.1 = (bf16[256,512]{1,0:T(8,128)(2,1)S(1)}, bf16[512,512]{1,0:T(8,128)(2,1)S(1)}, bf16[512,512]{1,0:T(8,128)(2,1)S(1)}) custom-call(bf16[256,512]{1,0:T(8,128)(2,1)S(1)} %get-tuple-element.124.gmix, bf16[256,512]{1,0:T(8,128)(2,1)S(1)} %get-tuple-element.125.q, bf16[512,512]{1,0:T(8,128)(2,1)S(1)} %get-tuple-element.126.k, ...), custom_call_target="tpu_custom_call" | custom-call | flops 1073741824 | bytes 8388608 | tf_op jit(solution)/shard_map/attend_back/pallas_call | solution.py:744
  73.2 3.9 %leave.1 = (f32[128,512]{1,0:T(8,128)S(1)}, bf16[256,512]{1,0:T(8,128)(2,1)S(1)}, bf16[128,512]{1,0:T(8,128)(2,1)S(1)}, bf16[128,512]{1,0:T(8,128)(2,1)S(1)}, bf...) custom-call(bf16[512,512]{1,0:T(8,128)(2,1)S(1)} %get-tuple-element., ...), custom_call_target="tpu_custom_call" | custom-call | flops 1342177280 | bytes 8388608 | tf_op jit(solution)/shard_map/leave/pallas_call | solution.py:757
  79.9 6.2 %collective-permute-start.32 = (bf16[128,512]{1,0:T(8,128)(2,1)S(1)}, bf16[128,512]{1,0:T(8,128)(2,1)S(1)}, u32[]{:S(2)}, u32[]{:S(2)}) collective-permute-start(bf16[128,512]{1,0:T(8,128)(2,1)S(1)} %get-tuple-element.142), channel_id=1, source_target_pairs={{0,2},{2,0},{3,1},{4,6},{6,4},{7,5},{8,10},{10,8},{11,9},{12,14},{... | collective-permute-start | bytes 393224 | tf_op jit(solution)/shard_map/ppermute | solution.py:587
  86.1 2.5 %collective-permute-start.33 = (bf16[128,512]{1,0:T(8,128)(2,1)S(1)}, bf16[128,512]{1,0:T(8,128)(2,1)S(1)}, u32[]{:S(2)}, u32[]{:S(2)}) collective-permute-start(bf16[128,512]{1,0:T(8,128)(2,1)S(1)} %get-tuple-element.143), channel_id=1, source_target_pairs={{0,3},{2,1},{3,0},{4,7},{6,5},{7,4},{8,11},{10,9},{11,8},{12,15},{... | collective-permute-start | bytes 393224 | tf_op jit(solution)/shard_map/ppermute | solution.py:587
  88.6 6.2 %collective-permute-done.27.from_y = bf16[2,4,5,16,512]{4,3,2,1,0:T(8,128)(2,1)S(1)} collective-permute-done((bf16[2,4,5,16,512]{4,3,2,1,0:T(8,128)(2,1)S(1)}, bf16[2,4,5,16,512]{4,3,2,1,0:T(8,128)(2,1)S(1)}, u32[]{:S(2)}, u32[]{:S(2)}) %collective-permute-start.27) | collective-permute-done | bytes 655392 | tf_op jit(solution)/shard_map/ppermute | solution.py:590
  94.8 2.0 %collective-permute-start.31 = (bf16[256,512]{1,0:T(8,128)(2,1)S(1)}, bf16[256,512]{1,0:T(8,128)(2,1)S(1)}, u32[]{:S(2)}, u32[]{:S(2)}) collective-permute-start(bf16[256,512]{1,0:T(8,128)(2,1)S(1)} %get-tuple-element.141), channel_id=1, source_target_pairs={{0,1},{1,0},{2,3},{3,2},{4,5},{5,4},{6,7},{7,6},{8,9},{9,8},{10,11... | collective-permute-start | bytes 786440 | tf_op jit(solution)/shard_map/ppermute | solution.py:587
  104.4 3.7 %collective-permute-done.29.then_x = bf16[4,5,16,512]{3,2,1,0:T(8,128)(2,1)S(1)} collective-permute-done((bf16[4,5,16,512]{3,2,1,0:T(8,128)(2,1)S(1)}, bf16[4,5,16,512]{3,2,1,0:T(8,128)(2,1)S(1)}, u32[]{:S(2)}, u32[]{:S(2)}) %collective-permute-start.29) | collective-permute-done | bytes 327712 | tf_op jit(solution)/shard_map/ppermute | solution.py:590
  110.7 2.4 %collective-permute-start.35 = (bf16[10,16,512]{2,1,0:T(8,128)(2,1)S(1)}, bf16[10,16,512]{2,1,0:T(8,128)(2,1)S(1)}, u32[]{:S(2)}, u32[]{:S(2)}) collective-permute-start(bf16[10,16,512]{2,1,0:T(8,128)(2,1)S(1)} %get-tuple-element.148), channel_id=1, source_target_pairs={{0,2},{1,3},{2,0},{3,1},{4,6},{5,7},{6,4},{7,5},{8,10},{9,11},{10,... | collective-permute-start | bytes 491528 | tf_op jit(solution)/shard_map/ppermute | solution.py:587
  113.7 3.3 %collective-permute-start.36 = (bf16[10,16,512]{2,1,0:T(8,128)(2,1)S(1)}, bf16[10,16,512]{2,1,0:T(8,128)(2,1)S(1)}, u32[]{:S(2)}, u32[]{:S(2)}) collective-permute-start(bf16[10,16,512]{2,1,0:T(8,128)(2,1)S(1)} %get-tuple-element.149), channel_id=1, source_target_pairs={{0,3},{1,2},{2,1},{3,0},{4,7},{5,6},{6,5},{7,4},{8,11},{9,10},{10,... | collective-permute-start | bytes 491528 | tf_op jit(solution)/shard_map/ppermute | solution.py:587
  119.4 3.1 %collective-permute-start.41 = (bf16[4,16,512]{2,1,0:T(8,128)(2,1)S(1)}, bf16[4,16,512]{2,1,0:T(8,128)(2,1)S(1)}, u32[]{:S(2)}, u32[]{:S(2)}) collective-permute-start(bf16[4,16,512]{2,1,0:T(8,128)(2,1)S(1)} %get-tuple-element.156), channel_id=1, source_target_pairs={{0,2},{1,3},{2,0},{3,1},{4,6},{5,7},{6,4},{7,5},{8,10},{9,11},{10,... | collective-permute-start | bytes 196616 | tf_op jit(solution)/shard_map/ppermute | solution.py:587
  124.1 3.2 %collective-permute-start.42 = (bf16[4,16,512]{2,1,0:T(8,128)(2,1)S(1)}, bf16[4,16,512]{2,1,0:T(8,128)(2,1)S(1)}, u32[]{:S(2)}, u32[]{:S(2)}) collective-permute-start(bf16[4,16,512]{2,1,0:T(8,128)(2,1)S(1)} %get-tuple-element.157), channel_id=1, source_target_pairs={{0,3},{1,2},{2,1},{3,0},{4,7},{5,6},{6,5},{7,4},{8,11},{9,10},{10,... | collective-permute-start | bytes 196616 | tf_op jit(solution)/shard_map/ppermute | solution.py:587
  (87 shorter events, 40.7 us)
Async XLA Ops:
  11.6 10.0 %collective-permute-start.4 = (bf16[10,16,512]{2,1,0:T(8,128)(2,1)}, bf16[10,16,512]{2,1,0:T(8,128)(2,1)S(1)}, u32[]{:S(2)}, u32[]{:S(2)}) collective-permute-start(bf16[10,16,512]{2,1,0:T(8,128)(2,1)} %get-tuple-element.96), channel_id=1, source_target_pairs={{0,3},{1,2},{2,1},{3,0},{4,7},{5,6},{6,5},{7,4},{8,11},{9,10},{10,... | collective-permute-start | bytes 491528 | tf_op jit(solution)/shard_map/ppermute | solution.py:587
  16.2 12.8 %collective-permute-start.3 = (bf16[10,16,512]{2,1,0:T(8,128)(2,1)}, bf16[10,16,512]{2,1,0:T(8,128)(2,1)S(1)}, u32[]{:S(2)}, u32[]{:S(2)}) collective-permute-start(bf16[10,16,512]{2,1,0:T(8,128)(2,1)} %get-tuple-element.96), channel_id=1, source_target_pairs={{0,2},{1,3},{2,0},{3,1},{4,6},{5,7},{6,4},{7,5},{8,10},{9,11},{10,... | collective-permute-start | bytes 491528 | tf_op jit(solution)/shard_map/ppermute | solution.py:587
  16.2 12.8 %collective-permute-start.2 = (bf16[10,16,512]{2,1,0:T(8,128)(2,1)}, bf16[10,16,512]{2,1,0:T(8,128)(2,1)S(1)}, u32[]{:S(2)}, u32[]{:S(2)}) collective-permute-start(bf16[10,16,512]{2,1,0:T(8,128)(2,1)} %get-tuple-element.96), channel_id=1, source_target_pairs={{0,1},{1,0},{2,3},{3,2},{4,5},{5,4},{6,7},{7,6},{8,9},{9,8},{10,11... | collective-permute-start | bytes 491528 | tf_op jit(solution)/shard_map/ppermute | solution.py:587
  17.7 12.4 %collective-permute-start.8 = (bf16[4,4,16,512]{3,2,1,0:T(8,128)(2,1)S(1)}, bf16[4,4,16,512]{3,2,1,0:T(8,128)(2,1)S(1)}, u32[]{:S(2)}, u32[]{:S(2)}) collective-permute-start(bf16[4,4,16,512]{3,2,1,0:T(8,128)(2,1)S(1)} %pad_maximum_fusion.1.refs_5_.refs_0_), channel_id=1, source_target_pairs={{0,24},{4,28},{8,16},{12,20},{16,8},{20,12},{24,0},{28,4},{1,25},{... | collective-permute-start | bytes 786440 | tf_op jit(solution)/shard_map/ppermute | solution.py:590
  20.2 9.9 %collective-permute-start.7 = (bf16[4,4,16,512]{3,2,1,0:T(8,128)(2,1)S(1)}, bf16[4,4,16,512]{3,2,1,0:T(8,128)(2,1)S(1)}, u32[]{:S(2)}, u32[]{:S(2)}) collective-permute-start(bf16[4,4,16,512]{3,2,1,0:T(8,128)(2,1)S(1)} %pad_maximum_fusion.1.refs_5_.refs_0_), channel_id=1, source_target_pairs={{0,16},{4,20},{8,24},{12,28},{16,0},{20,4},{24,8},{28,12},{1,17},{... | collective-permute-start | bytes 786440 | tf_op jit(solution)/shard_map/ppermute | solution.py:590
  30.3 18.0 %collective-permute-start.11 = (bf16[4,10,16,512]{3,2,1,0:T(8,128)(2,1)S(1)}, bf16[4,10,16,512]{3,2,1,0:T(8,128)(2,1)S(1)}, u32[]{:S(2)}, u32[]{:S(2)}) collective-permute-start(bf16[4,10,16,512]{3,2,1,0:T(8,128)(2,1)S(1)} %pad_maximum_fusion.refs_3_), channel_id=1, source_target_pairs={{0,16},{4,20},{8,24},{12,28},{16,0},{20,4},{24,8},{28,12},{1,17},{... | collective-permute-start | bytes 1966088 | tf_op jit(solution)/shard_map/ppermute | solution.py:590
  31.7 17.1 %collective-permute-start.9 = (bf16[4,10,16,512]{3,2,1,0:T(8,128)(2,1)S(1)}, bf16[4,10,16,512]{3,2,1,0:T(8,128)(2,1)S(1)}, u32[]{:S(2)}, u32[]{:S(2)}) collective-permute-start(bf16[4,10,16,512]{3,2,1,0:T(8,128)(2,1)S(1)} %pad_maximum_fusion.refs_3_), channel_id=1, source_target_pairs={{0,8},{4,12},{8,0},{12,4},{16,24},{20,28},{24,16},{28,20},{1,9},{5... | collective-permute-start | bytes 1966088 | tf_op jit(solution)/shard_map/ppermute | solution.py:590
  33.2 14.6 %collective-permute-start.13 = (bf16[256,512]{1,0:T(8,128)(2,1)}, bf16[256,512]{1,0:T(8,128)(2,1)S(1)}, u32[]{:S(2)}, u32[]{:S(2)}) collective-permute-start(bf16[256,512]{1,0:T(8,128)(2,1)} %get-tuple-element.101), channel_id=1, source_target_pairs={{0,1},{1,0},{2,3},{3,2},{4,5},{5,4},{6,7},{7,6},{8,9},{9,8},{10,11... | collective-permute-start | bytes 786440 | tf_op jit(solution)/shard_map/ppermute | solution.py:587
  48.9 9.7 %collective-permute-start.12 = (bf16[4,5,16,512]{3,2,1,0:T(8,128)(2,1)S(1)}, bf16[4,5,16,512]{3,2,1,0:T(8,128)(2,1)S(1)}, u32[]{:S(2)}, u32[]{:S(2)}) collective-permute-start(bf16[4,5,16,512]{3,2,1,0:T(8,128)(2,1)S(1)} %slice.21), channel_id=1, source_target_pairs={{0,8},{4,12},{8,0},{12,4},{16,24},{20,28},{24,16},{28,20},{1,9},{5... | collective-permute-start | bytes 983048 | tf_op jit(solution)/shard_map/ppermute | solution.py:590
  49.5 9.6 %collective-permute-start.10 = (bf16[4,5,16,512]{3,2,1,0:T(8,128)(2,1)S(1)}, bf16[4,5,16,512]{3,2,1,0:T(8,128)(2,1)S(1)}, u32[]{:S(2)}, u32[]{:S(2)}) collective-permute-start(bf16[4,5,16,512]{3,2,1,0:T(8,128)(2,1)S(1)} %slice.20), channel_id=1, source_target_pairs={{0,16},{4,20},{8,24},{12,28},{16,0},{20,4},{24,8},{28,12},{1,17},{... | collective-permute-start | bytes 983048 | tf_op jit(solution)/shard_map/ppermute | solution.py:590
  77.6 19.5 %collective-permute-start.28 = (bf16[16,4,16,512]{3,2,1,0:T(8,128)(2,1)S(1)}, bf16[16,4,16,512]{3,2,1,0:T(8,128)(2,1)S(1)}, u32[]{:S(2)}, u32[]{:S(2)}) collective-permute-start(bf16[16,4,16,512]{3,2,1,0:T(8,128)(2,1)S(1)} %get-tuple-element.136), channel_id=1, source_target_pairs={{0,4},{4,0},{8,12},{12,8},{16,20},{20,16},{24,28},{28,24},{1,5},{5... | collective-permute-start | bytes 3145736 | tf_op jit(solution)/shard_map/ppermute | solution.py:590
  78.0 16.8 %collective-permute-start.27 = (bf16[2,4,5,16,512]{4,3,2,1,0:T(8,128)(2,1)S(1)}, bf16[2,4,5,16,512]{4,3,2,1,0:T(8,128)(2,1)S(1)}, u32[]{:S(2)}, u32[]{:S(2)}) collective-permute-start(bf16[2,4,5,16,512]{4,3,2,1,0:T(8,128)(2,1)S(1)} %get-tuple-element.119), channel_id=1, source_target_pairs={{0,16},{4,20},{8,24},{12,28},{16,0},{20,4},{24,8},{28,12},{1,17},{... | collective-permute-start | bytes 1966088 | tf_op jit(solution)/shard_map/ppermute | solution.py:590
  78.6 18.1 %collective-permute-start.26 = (bf16[2,4,5,16,512]{4,3,2,1,0:T(8,128)(2,1)S(1)}, bf16[2,4,5,16,512]{4,3,2,1,0:T(8,128)(2,1)S(1)}, u32[]{:S(2)}, u32[]{:S(2)}) collective-permute-start(bf16[2,4,5,16,512]{4,3,2,1,0:T(8,128)(2,1)S(1)} %get-tuple-element.118), channel_id=1, source_target_pairs={{0,8},{4,12},{8,0},{12,4},{16,24},{20,28},{24,16},{28,20},{1,9},{5... | collective-permute-start | bytes 1966088 | tf_op jit(solution)/shard_map/ppermute | solution.py:590
  79.9 20.0 %collective-permute-start.32 = (bf16[128,512]{1,0:T(8,128)(2,1)S(1)}, bf16[128,512]{1,0:T(8,128)(2,1)S(1)}, u32[]{:S(2)}, u32[]{:S(2)}) collective-permute-start(bf16[128,512]{1,0:T(8,128)(2,1)S(1)} %get-tuple-element.142), channel_id=1, source_target_pairs={{0,2},{2,0},{3,1},{4,6},{6,4},{7,5},{8,10},{10,8},{11,9},{12,14},{... | collective-permute-start | bytes 393224 | tf_op jit(solution)/shard_map/ppermute | solution.py:587
  86.1 15.1 %collective-permute-start.33 = (bf16[128,512]{1,0:T(8,128)(2,1)S(1)}, bf16[128,512]{1,0:T(8,128)(2,1)S(1)}, u32[]{:S(2)}, u32[]{:S(2)}) collective-permute-start(bf16[128,512]{1,0:T(8,128)(2,1)S(1)} %get-tuple-element.143), channel_id=1, source_target_pairs={{0,3},{2,1},{3,0},{4,7},{6,5},{7,4},{8,11},{10,9},{11,8},{12,15},{... | collective-permute-start | bytes 393224 | tf_op jit(solution)/shard_map/ppermute | solution.py:587
  97.4 10.7 %collective-permute-start.29 = (bf16[4,5,16,512]{3,2,1,0:T(8,128)(2,1)S(1)}, bf16[4,5,16,512]{3,2,1,0:T(8,128)(2,1)S(1)}, u32[]{:S(2)}, u32[]{:S(2)}) collective-permute-start(bf16[4,5,16,512]{3,2,1,0:T(8,128)(2,1)S(1)} %get-tuple-element.139), channel_id=1, source_target_pairs={{0,8},{4,12},{8,0},{12,4},{16,24},{20,28},{24,16},{28,20},{1,9},{5... | collective-permute-start | bytes 983048 | tf_op jit(solution)/shard_map/ppermute | solution.py:590
  98.3 10.6 %collective-permute-start.30 = (bf16[4,5,16,512]{3,2,1,0:T(8,128)(2,1)S(1)}, bf16[4,5,16,512]{3,2,1,0:T(8,128)(2,1)S(1)}, u32[]{:S(2)}, u32[]{:S(2)}) collective-permute-start(bf16[4,5,16,512]{3,2,1,0:T(8,128)(2,1)S(1)} %get-tuple-element.140), channel_id=1, source_target_pairs={{0,16},{4,20},{8,24},{12,28},{16,0},{20,4},{24,8},{28,12},{1,17},{... | collective-permute-start | bytes 983048 | tf_op jit(solution)/shard_map/ppermute | solution.py:590
  99.9 13.8 %collective-permute-start.37 = (bf16[4,4,16,512]{3,2,1,0:T(8,128)(2,1)S(1)}, bf16[4,4,16,512]{3,2,1,0:T(8,128)(2,1)S(1)}, u32[]{:S(2)}, u32[]{:S(2)}) collective-permute-start(bf16[4,4,16,512]{3,2,1,0:T(8,128)(2,1)S(1)} %get-tuple-element.151), channel_id=1, source_target_pairs={{0,8},{4,12},{8,0},{12,4},{16,24},{20,28},{24,16},{28,20},{1,9},{5... | collective-permute-start | bytes 786440 | tf_op jit(solution)/shard_map/ppermute | solution.py:590
  101.2 15.8 %collective-permute-start.38 = (bf16[4,4,16,512]{3,2,1,0:T(8,128)(2,1)S(1)}, bf16[4,4,16,512]{3,2,1,0:T(8,128)(2,1)S(1)}, u32[]{:S(2)}, u32[]{:S(2)}) collective-permute-start(bf16[4,4,16,512]{3,2,1,0:T(8,128)(2,1)S(1)} %get-tuple-element.152), channel_id=1, source_target_pairs={{0,16},{4,20},{8,24},{12,28},{16,0},{20,4},{24,8},{28,12},{1,17},{... | collective-permute-start | bytes 786440 | tf_op jit(solution)/shard_map/ppermute | solution.py:590
  102.5 16.0 %collective-permute-start.39 = (bf16[4,4,16,512]{3,2,1,0:T(8,128)(2,1)S(1)}, bf16[4,4,16,512]{3,2,1,0:T(8,128)(2,1)S(1)}, u32[]{:S(2)}, u32[]{:S(2)}) collective-permute-start(bf16[4,4,16,512]{3,2,1,0:T(8,128)(2,1)S(1)} %get-tuple-element.153), channel_id=1, source_target_pairs={{0,24},{4,28},{8,16},{12,20},{16,8},{20,12},{24,0},{28,4},{1,25},{... | collective-permute-start | bytes 786440 | tf_op jit(solution)/shard_map/ppermute | solution.py:590
  109.3 20.9 %collective-permute-start.34 = (bf16[10,16,512]{2,1,0:T(8,128)(2,1)S(1)}, bf16[10,16,512]{2,1,0:T(8,128)(2,1)S(1)}, u32[]{:S(2)}, u32[]{:S(2)}) collective-permute-start(bf16[10,16,512]{2,1,0:T(8,128)(2,1)S(1)} %get-tuple-element.147), channel_id=1, source_target_pairs={{0,1},{1,0},{2,3},{3,2},{4,5},{5,4},{6,7},{7,6},{8,9},{9,8},{10,11... | collective-permute-start | bytes 491528 | tf_op jit(solution)/shard_map/ppermute | solution.py:587
  110.7 19.5 %collective-permute-start.35 = (bf16[10,16,512]{2,1,0:T(8,128)(2,1)S(1)}, bf16[10,16,512]{2,1,0:T(8,128)(2,1)S(1)}, u32[]{:S(2)}, u32[]{:S(2)}) collective-permute-start(bf16[10,16,512]{2,1,0:T(8,128)(2,1)S(1)} %get-tuple-element.148), channel_id=1, source_target_pairs={{0,2},{1,3},{2,0},{3,1},{4,6},{5,7},{6,4},{7,5},{8,10},{9,11},{10,... | collective-permute-start | bytes 491528 | tf_op jit(solution)/shard_map/ppermute | solution.py:587
  113.7 16.5 %collective-permute-start.36 = (bf16[10,16,512]{2,1,0:T(8,128)(2,1)S(1)}, bf16[10,16,512]{2,1,0:T(8,128)(2,1)S(1)}, u32[]{:S(2)}, u32[]{:S(2)}) collective-permute-start(bf16[10,16,512]{2,1,0:T(8,128)(2,1)S(1)} %get-tuple-element.149), channel_id=1, source_target_pairs={{0,3},{1,2},{2,1},{3,0},{4,7},{5,6},{6,5},{7,4},{8,11},{9,10},{10,... | collective-permute-start | bytes 491528 | tf_op jit(solution)/shard_map/ppermute | solution.py:587
  119.4 9.2 %collective-permute-start.41 = (bf16[4,16,512]{2,1,0:T(8,128)(2,1)S(1)}, bf16[4,16,512]{2,1,0:T(8,128)(2,1)S(1)}, u32[]{:S(2)}, u32[]{:S(2)}) collective-permute-start(bf16[4,16,512]{2,1,0:T(8,128)(2,1)S(1)} %get-tuple-element.156), channel_id=1, source_target_pairs={{0,2},{1,3},{2,0},{3,1},{4,6},{5,7},{6,4},{7,5},{8,10},{9,11},{10,... | collective-permute-start | bytes 196616 | tf_op jit(solution)/shard_map/ppermute | solution.py:587
  (24 other events, 322.0 us)

commit v5 on v4

--- a/solution.py
+++ b/solution.py
@@ -376,7 +376,12 @@
     store_slots(grads, grad_parts, sem, me)
 
 
-def attend_back_body(gmix, q, k, v, probs_i, dq_o, dk_o, dv_o):
+def attend_back_body(direct, layout, gmix, q, k, v, probs_i, gsum, outs, *refs):
+    count = len(layout)
+    parts, refs = (refs[:count], refs[count:])
+    dq_o, dk_o, dv_o, back_o, own_o, sent1_o, sent2_o, sent3_o, weights, sem = refs
+    me, seq = own_place()
+    fetch_weights(layout, parts, weights, sem, me if direct else jnp.int32(0))
     lane = head_lanes()
     scale = HEAD_DIM**-0.5
     for g in range(gmix.shape[1] // LANES):
@@ -385,41 +390,41 @@
         queries = stack_heads(q[:, cols], lane)
         probs = probs_i[g]
         grad_probs = mm(grads, v[:, cols], NT)
-        wide = probs.astype(F32)
-        inner = jnp.sum(wide * grad_probs, axis=-1, keepdims=True)
-        grad_scores = (wide * (grad_probs - inner)).astype(BF)
+        spread = probs.astype(F32)
+        inner = jnp.sum(spread * grad_probs, axis=-1, keepdims=True)
+        grad_scores = (spread * (grad_probs - inner)).astype(BF)
         grad_q = mm(grad_scores, k[:, cols])
         dq_o[:, cols] = (join_heads(grad_q, lane) * scale).astype(BF)
         dk_o[:, cols] = mm(grad_scores, queries, TN).astype(BF)
         dv_o[:, cols] = mm(probs, grads, TN).astype(BF)
-
-
-def leave_body(direct, layout, low, lowq, dq, dk, dv, gsum, outs, *refs):
-    count = len(layout)
-    parts, refs = (refs[:count], refs[count:])
-    own_o, sent1_o, sent2_o, sent3_o = refs[:4]
-    grad_parts = refs[4:9]
-    weights, grads, table, back, sem = refs[9:]
-    me, seq = own_place()
-    me = me if direct else jnp.int32(0)
-    fetch_weights(layout, parts, weights, sem, me)
-    grads[0] = mm(lowq[...], dq[...], TN).astype(BF)
-    grads[1] = mm(low[...], dk[...], TN).astype(BF)
-    grads[2] = mm(low[...], dv[...], TN).astype(BF)
     pltpu.make_async_copy(weights, weights, sem).wait()
-    back[...] = mm(dk[...], weights[1], NT) + mm(dv[...], weights[2], NT)
-    spread_queries(seq, gsum[...] + mm(dq[...], weights[0], NT), back)
+    back_o[...] = mm(dk_o[...], weights[1], NT) + mm(dv_o[...], weights[2], NT)
+    spread_queries(seq, gsum[...] + mm(dq_o[...], weights[0], NT), back_o)
     size = own_o.shape[0]
-    table[...] = jnp.zeros_like(table)
     for k, target in enumerate((own_o, sent1_o, sent2_o, sent3_o)):
-        piece = back[k * size : (k + 1) * size, :]
+        piece = back_o[k * size : (k + 1) * size, :]
         target[:size, :] = piece.astype(target.dtype)
         if k == 1:
             target[size:, :] = outs[size : 2 * size, :]
         elif k > 1:
-            both = jnp.concatenate([piece[: size // 2].astype(BF), outs[k * size : k * size + size // 2, :]], 0)
+            half = size // 2
+            both = jnp.concatenate(
+                [piece[:half].astype(BF), outs[k * size : k * size + half, :]], 0
+            )
             target[...] = jnp.where(has_long(seq), piece.astype(BF), both)
-        table[pl.ds(block_base(seq, k, size), size), :] += piece
+
+
+def leave_body(direct, low, lowq, dq, dk, dv, back, *refs):
+    grad_parts, (grads, table, sem) = (refs[:5], refs[5:])
+    me, seq = own_place()
+    me = me if direct else jnp.int32(0)
+    grads[0] = mm(lowq[...], dq[...], TN).astype(BF)
+    grads[1] = mm(low[...], dk[...], TN).astype(BF)
+    grads[2] = mm(low[...], dv[...], TN).astype(BF)
+    size = back.shape[0] // 4
+    table[...] = jnp.zeros_like(table)
+    for k in range(4):
+        table[pl.ds(block_base(seq, k, size), size), :] += back[k * size : (k + 1) * size, :]
     grads[3] = table[...].T.astype(BF)
     store_slots(grads, grad_parts, sem, me)
 
@@ -741,35 +746,37 @@
     if direct:
         late_arrived = swap_dp(late_parts[-1], 1)
 
-    grad_q, grad_k, grad_v = call(
-        attend_back_body,
+    grad_q, grad_k, grad_v, back_rows, *grad_blocks = call(
+        functools.partial(attend_back_body, direct, early_layout),
         [
             ((rows, width), BF, VMEM),
             ((keys, width), BF, VMEM),
             ((keys, width), BF, VMEM),
+            ((keys, width), F32, VMEM),
+            (block, F32, VMEM),
+            ((2 * n_long, width), BF, VMEM),
+            (block, BF, VMEM),
+            (block, BF, VMEM),
         ],
-        [VMEM] * 5,
-        [],
-        (8 * keys * square, 8 * MIB),
+        [VMEM] * 7 + [HBM] * len(early_layout),
+        [pltpu.VMEM((early_pieces, width, width), BF), pltpu.SemaphoreType.DMA],
+        (16 * keys * square, 12 * MIB),
         "attend_back",
         24,
-    )(grad_mixed, queries, key_rows, values, probs)
-    leave_outs = call(
-        functools.partial(leave_body, direct, early_layout),
-        [(block, F32, VMEM), ((2 * n_long, width), BF, VMEM)] + [(block, BF, VMEM)] * 2 + slot_outs(early_pieces),
-        [VMEM] * 7 + [HBM] * len(early_layout),
+    )(grad_mixed, queries, key_rows, values, probs, grad_sum, out_blocks, *early_full)
+    early_parts = call(
+        functools.partial(leave_body, direct),
+        slot_outs(early_pieces),
+        [VMEM] * 6,
         [
             pltpu.VMEM((early_pieces, width, width), BF),
-            pltpu.VMEM((early_pieces, width, width), BF),
             pltpu.VMEM((width, width), F32),
-            pltpu.VMEM((keys, width), F32),
             pltpu.SemaphoreType.DMA,
         ],
-        (10 * keys * square, 8 * MIB),
+        (6 * keys * square, 8 * MIB),
         "leave",
         24,
-    )(low, low_queries, grad_q, grad_k, grad_v, grad_sum, out_blocks, *early_full)
-    grad_blocks, early_parts = (leave_outs[:4], leave_outs[4:])
+    )(low, low_queries, grad_q, grad_k, grad_v, back_rows)
 
     back = lambda source, target: source != 1
     got = [swap_seq(grad_blocks[1], 1)] + [swap_seq(grad_blocks[k], k, back) for k in (2, 3)]
@@ -789,6 +796,10 @@
             "late_sums_1",
         )
         from_x, from_y = (swap_dp(to_x, 2), swap_dp(to_y, 4))
+        early_far = early_parts[-1]
+        early_arrived = swap_dp(early_far, 1)
+        early_sums = core_sums(early_parts, early_arrived)
+        from_x, from_y, early_sums = lax.optimization_barrier((from_x, from_y, early_sums))
         second = pl.BlockSpec((1, 1, half, BAND, width), lambda i: (1, i, 0, 0, 0))
         then_x, then_y = sum_call(
             functools.partial(second_sums_body, half),
@@ -798,10 +809,6 @@
             4,
             "late_sums_2",
         )
-        early_far = after(early_parts[-1], to_x)
-        early_arrived = swap_dp(early_far, 1)
-        early_sums = core_sums(early_parts, early_arrived)
-        then_x, then_y, early_sums = lax.optimization_barrier((then_x, then_y, early_sums))
         then_x, then_y = (swap_dp(then_x, 2), swap_dp(then_y, 4))
         early_layers = [swap_dp(part, 2 * k) for k, part in enumerate(early_sums, 1)]
         then_x, then_y, got = lax.optimization_barrier((then_x, then_y, got))

time: 132 us -> 130 us (0.985)
  starting transfers between devices: 63.5 us -> 61.7 us
    ppermute x25, waiting for transfers between devices: 17.5 us -> 19.2 us  [swap_dp(): return lax.ppermute(value, 'dp', [(i, i ^ mask) for i in range(dp_count)])]
    ppermute x18, waiting for transfers between devices: 21.4 us -> 19.7 us  [swap_seq(): return lax.ppermute(value, 'seq', pairs)]
  transfers between devices with their start and end apart: 43 -> 43, of which waited for: 20 -> 21; matrix products, arithmetic and copies ran while one was open for 2% -> 2% of each run, Pallas kernels for 10% -> 10%
where the time goes in v5:
time: 130 us; the launch traced here: 129 us
  starting transfers between devices  61.7 us (47%)
  waiting for transfers between devices  38.9 us (30%)
  Pallas kernels  24.9 us (19%)
  other arithmetic  2.18 us (2%)
  between operations  1.65 us (1%)
    ppermute x18, starting transfers between devices, swap_seq(): return lax.ppermute(value, 'seq', pairs)  42.9 us
    ppermute x18, waiting for transfers between devices, swap_seq(): return lax.ppermute(value, 'seq', pairs)  19.7 us
    ppermute x25, waiting for transfers between devices, swap_dp(): return lax.ppermute(value, 'dp', [(i, i ^ mask) for i in range(dp_count)])  19.2 us
    ppermute x25, starting transfers between devices, swap_dp(): return lax.ppermute(value, 'dp', [(i, i ^ mask) for i in range(dp_count)])  18.7 us
    pallas_call x1, Pallas kernels, local(): call(functools.partial(middle_body, direct, late_layout), [((keys, width)...  8.35 us
    pallas_call x1, Pallas kernels, local(): call(functools.partial(attend_back_body, direct, early_layout), [((rows,...  5.17 us
    pallas_call x1, Pallas kernels, local(): call(functools.partial(attend_body, direct, early_layout), [((rows, width...  4.72 us
  transfers between devices with their start and end apart: 43, of which 21 were waited for; matrix products, arithmetic and copies ran while one was open for 2% of the time, Pallas kernels for 10%

profile of v5, /device:TPU:0, one launch (start us, length us, event | category | flops | bytes accessed | tf_op | source)
XLA Modules:
  0.0 129.4 jit_solution(1190071671121591144)
XLA Ops:
  0.7 2.4 %pack.1 = (bf16[256,512]{1,0:T(8,128)(2,1)}, bf16[128,512]{1,0:T(8,128)(2,1)}, bf16[128,512]{1,0:T(8,128)(2,1)}, bf16[4,16,512]{2,1,0:T(8,128)(2,1)}, bf16[10,16,512]{2,1,0:T(8,128)(2,1)}) custom-call(bf16[1,128,512]{2,1,0:T(8,128)(2,1)} %refs_0_.3, bf16[2,64,512]{2,1,0:T(8,128)(2,1)} %refs_1_.3, bf16[1,128,512]{2,1,0:T(8,128)(2,1)} %long_cot.1, ...), custom_call_target="tpu_custom_call" | custom-call | bytes 4194304 | tf_op jit(solution)/shard_map/pack/pallas_call | solution.py:612
  3.1 4.0 %collective-permute-start.1 = (bf16[4,16,512]{2,1,0:T(8,128)(2,1)}, bf16[4,16,512]{2,1,0:T(8,128)(2,1)S(1)}, u32[]{:S(2)}, u32[]{:S(2)}) collective-permute-start(bf16[4,16,512]{2,1,0:T(8,128)(2,1)} %get-tuple-element.95), channel_id=1, source_target_pairs={{0,2},{1,3},{2,0},{3,1},{4,6},{5,7},{6,4},{7,5},{8,10},{9,11},{10,... | collective-permute-start | bytes 196616 | tf_op jit(solution)/shard_map/ppermute | solution.py:592
  11.6 4.6 %collective-permute-start.4 = (bf16[10,16,512]{2,1,0:T(8,128)(2,1)}, bf16[10,16,512]{2,1,0:T(8,128)(2,1)S(1)}, u32[]{:S(2)}, u32[]{:S(2)}) collective-permute-start(bf16[10,16,512]{2,1,0:T(8,128)(2,1)} %get-tuple-element.96), channel_id=1, source_target_pairs={{0,3},{1,2},{2,1},{3,0},{4,7},{5,6},{6,5},{7,4},{8,11},{9,10},{10,... | collective-permute-start | bytes 491528 | tf_op jit(solution)/shard_map/ppermute | solution.py:592
  17.7 2.5 %collective-permute-start.8 = (bf16[4,4,16,512]{3,2,1,0:T(8,128)(2,1)S(1)}, bf16[4,4,16,512]{3,2,1,0:T(8,128)(2,1)S(1)}, u32[]{:S(2)}, u32[]{:S(2)}) collective-permute-start(bf16[4,4,16,512]{3,2,1,0:T(8,128)(2,1)S(1)} %pad_maximum_fusion.1.refs_5_.refs_0_), channel_id=1, source_target_pairs={{0,24},{4,28},{8,16},{12,20},{16,8},{20,12},{24,0},{28,4},{1,25},{... | collective-permute-start | bytes 786440 | tf_op jit(solution)/shard_map/ppermute | solution.py:595
  23.0 6.0 %collective-permute-done.3 = bf16[10,16,512]{2,1,0:T(8,128)(2,1)S(1)} collective-permute-done((bf16[10,16,512]{2,1,0:T(8,128)(2,1)}, bf16[10,16,512]{2,1,0:T(8,128)(2,1)S(1)}, u32[]{:S(2)}, u32[]{:S(2)}) %collective-permute-start.3) | collective-permute-done | bytes 163872 | tf_op jit(solution)/shard_map/ppermute | solution.py:592
  33.2 3.5 %collective-permute-start.13 = (bf16[256,512]{1,0:T(8,128)(2,1)}, bf16[256,512]{1,0:T(8,128)(2,1)S(1)}, u32[]{:S(2)}, u32[]{:S(2)}) collective-permute-start(bf16[256,512]{1,0:T(8,128)(2,1)} %get-tuple-element.101), channel_id=1, source_target_pairs={{0,1},{1,0},{2,3},{3,2},{4,5},{5,4},{6,7},{7,6},{8,9},{9,8},{10,11... | collective-permute-start | bytes 786440 | tf_op jit(solution)/shard_map/ppermute | solution.py:592
  36.7 2.2 %collective-permute-start.14 = (bf16[128,512]{1,0:T(8,128)(2,1)}, bf16[128,512]{1,0:T(8,128)(2,1)S(1)}, u32[]{:S(2)}, u32[]{:S(2)}) collective-permute-start(bf16[128,512]{1,0:T(8,128)(2,1)} %get-tuple-element.102), channel_id=1, source_target_pairs={{0,2},{1,3},{2,0},{4,6},{5,7},{6,4},{8,10},{9,11},{10,8},{12,14},{... | collective-permute-start | bytes 393224 | tf_op jit(solution)/shard_map/ppermute | solution.py:592
  38.9 2.6 %collective-permute-start.15 = (bf16[128,512]{1,0:T(8,128)(2,1)}, bf16[128,512]{1,0:T(8,128)(2,1)S(1)}, u32[]{:S(2)}, u32[]{:S(2)}) collective-permute-start(bf16[128,512]{1,0:T(8,128)(2,1)} %get-tuple-element.103), channel_id=1, source_target_pairs={{0,3},{1,2},{3,0},{4,7},{5,6},{7,4},{8,11},{9,10},{11,8},{12,15},{... | collective-permute-start | bytes 393224 | tf_op jit(solution)/shard_map/ppermute | solution.py:592
  41.6 4.2 %collective-permute-done.14.refs_3_.refs_1_ = bf16[128,512]{1,0:T(8,128)(2,1)S(1)} collective-permute-done((bf16[128,512]{1,0:T(8,128)(2,1)}, bf16[128,512]{1,0:T(8,128)(2,1)S(1)}, u32[]{:S(2)}, u32[]{:S(2)}) %collective-permute-start.14) | collective-permute-done | bytes 131104 | tf_op jit(solution)/shard_map/ppermute | solution.py:592
  45.7 2.1 %collective-permute-done.15.refs_4_.refs_2_ = bf16[128,512]{1,0:T(8,128)(2,1)S(1)} collective-permute-done((bf16[128,512]{1,0:T(8,128)(2,1)}, bf16[128,512]{1,0:T(8,128)(2,1)S(1)}, u32[]{:S(2)}, u32[]{:S(2)}) %collective-permute-start.15) | collective-permute-done | bytes 131104 | tf_op jit(solution)/shard_map/ppermute | solution.py:592
  51.7 4.7 %attend.1 = (f32[256,512]{1,0:T(8,128)S(1)}, bf16[512,512]{1,0:T(8,128)(2,1)S(1)}, bf16[256,512]{1,0:T(8,128)(2,1)S(1)}, bf16[256,512]{1,0:T(8,128)(2,1)S(1)}, b...) custom-call(s32[1]{0:T(128)S(6)} %copy.28.long_len, ...), custom_call_target="tpu_custom_call" | custom-call | flops 1073741824 | bytes 10485760 | tf_op jit(solution)/shard_map/attend/pallas_call | solution.py:688
  56.4 2.2 %collective-permute-done.12.refs_7_ = bf16[4,5,16,512]{3,2,1,0:T(8,128)(2,1)S(1)} collective-permute-done((bf16[4,5,16,512]{3,2,1,0:T(8,128)(2,1)S(1)}, bf16[4,5,16,512]{3,2,1,0:T(8,128)(2,1)S(1)}, u32[]{:S(2)}, u32[]{:S(2)}) %collective-permute-start.12) | collective-permute-done | bytes 327712 | tf_op jit(solution)/shard_map/ppermute | solution.py:595
  61.2 8.3 %middle.1 = (bf16[512,512]{1,0:T(8,128)(2,1)S(1)}, f32[256,512]{1,0:T(8,128)S(1)}, bf16[256,512]{1,0:T(8,128)(2,1)S(1)}, bf16[4,10,16,512]{3,2,1,0:T(8,128)(2,1)...) custom-call(f32[256,512]{1,0:T(8,128)S(1)} %get-tuple-element.109.fi, ...), custom_call_target="tpu_custom_call" | custom-call | flops 4294967296 | bytes 20971520 | tf_op jit(solution)/shard_map/middle/pallas_call | solution.py:718
  69.8 5.2 %attend_back.1 = (bf16[256,512]{1,0:T(8,128)(2,1)S(1)}, bf16[512,512]{1,0:T(8,128)(2,1)S(1)}, bf16[512,512]{1,0:T(8,128)(2,1)S(1)}, f32[512,512]{1,0:T(8,128)S(1...) custom-call(bf16[256,512]{1,0:T(8,128)(2,1)S(1)} %get-tuple-element., ...), custom_call_target="tpu_custom_call" | custom-call | flops 2147483648 | bytes 12582912 | tf_op jit(solution)/shard_map/attend_back/pallas_call | solution.py:749
  79.5 6.2 %collective-permute-start.32 = (bf16[128,512]{1,0:T(8,128)(2,1)S(1)}, bf16[128,512]{1,0:T(8,128)(2,1)S(1)}, u32[]{:S(2)}, u32[]{:S(2)}) collective-permute-start(bf16[128,512]{1,0:T(8,128)(2,1)S(1)} %get-tuple-element.142), channel_id=1, source_target_pairs={{0,2},{2,0},{3,1},{4,6},{6,4},{7,5},{8,10},{10,8},{11,9},{12,14},{... | collective-permute-start | bytes 393224 | tf_op jit(solution)/shard_map/ppermute | solution.py:592
  85.8 2.5 %collective-permute-start.33 = (bf16[128,512]{1,0:T(8,128)(2,1)S(1)}, bf16[128,512]{1,0:T(8,128)(2,1)S(1)}, u32[]{:S(2)}, u32[]{:S(2)}) collective-permute-start(bf16[128,512]{1,0:T(8,128)(2,1)S(1)} %get-tuple-element.143), channel_id=1, source_target_pairs={{0,3},{2,1},{3,0},{4,7},{6,5},{7,4},{8,11},{10,9},{11,8},{12,15},{... | collective-permute-start | bytes 393224 | tf_op jit(solution)/shard_map/ppermute | solution.py:592
  88.7 5.8 %collective-permute-done.26.from_x = bf16[2,4,5,16,512]{4,3,2,1,0:T(8,128)(2,1)S(1)} collective-permute-done((bf16[2,4,5,16,512]{4,3,2,1,0:T(8,128)(2,1)S(1)}, bf16[2,4,5,16,512]{4,3,2,1,0:T(8,128)(2,1)S(1)}, u32[]{:S(2)}, u32[]{:S(2)}) %collective-permute-start.26) | collective-permute-done | bytes 655392 | tf_op jit(solution)/shard_map/ppermute | solution.py:595
  101.3 5.2 %collective-permute-done.29.then_x = bf16[4,5,16,512]{3,2,1,0:T(8,128)(2,1)S(1)} collective-permute-done((bf16[4,5,16,512]{3,2,1,0:T(8,128)(2,1)S(1)}, bf16[4,5,16,512]{3,2,1,0:T(8,128)(2,1)S(1)}, u32[]{:S(2)}, u32[]{:S(2)}) %collective-permute-start.29) | collective-permute-done | bytes 327712 | tf_op jit(solution)/shard_map/ppermute | solution.py:595
  107.5 2.0 %collective-permute-start.34 = (bf16[10,16,512]{2,1,0:T(8,128)(2,1)S(1)}, bf16[10,16,512]{2,1,0:T(8,128)(2,1)S(1)}, u32[]{:S(2)}, u32[]{:S(2)}) collective-permute-start(bf16[10,16,512]{2,1,0:T(8,128)(2,1)S(1)} %get-tuple-element.147), channel_id=1, source_target_pairs={{0,1},{1,0},{2,3},{3,2},{4,5},{5,4},{6,7},{7,6},{8,9},{9,8},{10,11... | collective-permute-start | bytes 491528 | tf_op jit(solution)/shard_map/ppermute | solution.py:592
  109.5 1.9 %collective-permute-start.35 = (bf16[10,16,512]{2,1,0:T(8,128)(2,1)S(1)}, bf16[10,16,512]{2,1,0:T(8,128)(2,1)S(1)}, u32[]{:S(2)}, u32[]{:S(2)}) collective-permute-start(bf16[10,16,512]{2,1,0:T(8,128)(2,1)S(1)} %get-tuple-element.148), channel_id=1, source_target_pairs={{0,2},{1,3},{2,0},{3,1},{4,6},{5,7},{6,4},{7,5},{8,10},{9,11},{10,... | collective-permute-start | bytes 491528 | tf_op jit(solution)/shard_map/ppermute | solution.py:592
  112.1 2.7 %collective-permute-start.36 = (bf16[10,16,512]{2,1,0:T(8,128)(2,1)S(1)}, bf16[10,16,512]{2,1,0:T(8,128)(2,1)S(1)}, u32[]{:S(2)}, u32[]{:S(2)}) collective-permute-start(bf16[10,16,512]{2,1,0:T(8,128)(2,1)S(1)} %get-tuple-element.149), channel_id=1, source_target_pairs={{0,3},{1,2},{2,1},{3,0},{4,7},{5,6},{6,5},{7,4},{8,11},{9,10},{10,... | collective-permute-start | bytes 491528 | tf_op jit(solution)/shard_map/ppermute | solution.py:592
  116.3 2.2 %collective-permute-start.40 = (bf16[4,16,512]{2,1,0:T(8,128)(2,1)S(1)}, bf16[4,16,512]{2,1,0:T(8,128)(2,1)S(1)}, u32[]{:S(2)}, u32[]{:S(2)}) collective-permute-start(bf16[4,16,512]{2,1,0:T(8,128)(2,1)S(1)} %get-tuple-element.155), channel_id=1, source_target_pairs={{0,1},{1,0},{2,3},{3,2},{4,5},{5,4},{6,7},{7,6},{8,9},{9,8},{10,11... | collective-permute-start | bytes 196616 | tf_op jit(solution)/shard_map/ppermute | solution.py:592
  118.5 1.9 %collective-permute-start.41 = (bf16[4,16,512]{2,1,0:T(8,128)(2,1)S(1)}, bf16[4,16,512]{2,1,0:T(8,128)(2,1)S(1)}, u32[]{:S(2)}, u32[]{:S(2)}) collective-permute-start(bf16[4,16,512]{2,1,0:T(8,128)(2,1)S(1)} %get-tuple-element.156), channel_id=1, source_target_pairs={{0,2},{1,3},{2,0},{3,1},{4,6},{5,7},{6,4},{7,5},{8,10},{9,11},{10,... | collective-permute-start | bytes 196616 | tf_op jit(solution)/shard_map/ppermute | solution.py:592
  121.3 4.3 %collective-permute-start.42 = (bf16[4,16,512]{2,1,0:T(8,128)(2,1)S(1)}, bf16[4,16,512]{2,1,0:T(8,128)(2,1)S(1)}, u32[]{:S(2)}, u32[]{:S(2)}) collective-permute-start(bf16[4,16,512]{2,1,0:T(8,128)(2,1)S(1)} %get-tuple-element.157), channel_id=1, source_target_pairs={{0,3},{1,2},{2,1},{3,0},{4,7},{5,6},{6,5},{7,4},{8,11},{9,10},{10,... | collective-permute-start | bytes 196616 | tf_op jit(solution)/shard_map/ppermute | solution.py:592
  (87 shorter events, 38.5 us)
Async XLA Ops:
  11.6 10.0 %collective-permute-start.4 = (bf16[10,16,512]{2,1,0:T(8,128)(2,1)}, bf16[10,16,512]{2,1,0:T(8,128)(2,1)S(1)}, u32[]{:S(2)}, u32[]{:S(2)}) collective-permute-start(bf16[10,16,512]{2,1,0:T(8,128)(2,1)} %get-tuple-element.96), channel_id=1, source_target_pairs={{0,3},{1,2},{2,1},{3,0},{4,7},{5,6},{6,5},{7,4},{8,11},{9,10},{10,... | collective-permute-start | bytes 491528 | tf_op jit(solution)/shard_map/ppermute | solution.py:592
  16.2 12.8 %collective-permute-start.3 = (bf16[10,16,512]{2,1,0:T(8,128)(2,1)}, bf16[10,16,512]{2,1,0:T(8,128)(2,1)S(1)}, u32[]{:S(2)}, u32[]{:S(2)}) collective-permute-start(bf16[10,16,512]{2,1,0:T(8,128)(2,1)} %get-tuple-element.96), channel_id=1, source_target_pairs={{0,2},{1,3},{2,0},{3,1},{4,6},{5,7},{6,4},{7,5},{8,10},{9,11},{10,... | collective-permute-start | bytes 491528 | tf_op jit(solution)/shard_map/ppermute | solution.py:592
  16.2 12.8 %collective-permute-start.2 = (bf16[10,16,512]{2,1,0:T(8,128)(2,1)}, bf16[10,16,512]{2,1,0:T(8,128)(2,1)S(1)}, u32[]{:S(2)}, u32[]{:S(2)}) collective-permute-start(bf16[10,16,512]{2,1,0:T(8,128)(2,1)} %get-tuple-element.96), channel_id=1, source_target_pairs={{0,1},{1,0},{2,3},{3,2},{4,5},{5,4},{6,7},{7,6},{8,9},{9,8},{10,11... | collective-permute-start | bytes 491528 | tf_op jit(solution)/shard_map/ppermute | solution.py:592
  17.7 12.4 %collective-permute-start.8 = (bf16[4,4,16,512]{3,2,1,0:T(8,128)(2,1)S(1)}, bf16[4,4,16,512]{3,2,1,0:T(8,128)(2,1)S(1)}, u32[]{:S(2)}, u32[]{:S(2)}) collective-permute-start(bf16[4,4,16,512]{3,2,1,0:T(8,128)(2,1)S(1)} %pad_maximum_fusion.1.refs_5_.refs_0_), channel_id=1, source_target_pairs={{0,24},{4,28},{8,16},{12,20},{16,8},{20,12},{24,0},{28,4},{1,25},{... | collective-permute-start | bytes 786440 | tf_op jit(solution)/shard_map/ppermute | solution.py:595
  20.2 9.9 %collective-permute-start.7 = (bf16[4,4,16,512]{3,2,1,0:T(8,128)(2,1)S(1)}, bf16[4,4,16,512]{3,2,1,0:T(8,128)(2,1)S(1)}, u32[]{:S(2)}, u32[]{:S(2)}) collective-permute-start(bf16[4,4,16,512]{3,2,1,0:T(8,128)(2,1)S(1)} %pad_maximum_fusion.1.refs_5_.refs_0_), channel_id=1, source_target_pairs={{0,16},{4,20},{8,24},{12,28},{16,0},{20,4},{24,8},{28,12},{1,17},{... | collective-permute-start | bytes 786440 | tf_op jit(solution)/shard_map/ppermute | solution.py:595
  30.3 18.0 %collective-permute-start.11 = (bf16[4,10,16,512]{3,2,1,0:T(8,128)(2,1)S(1)}, bf16[4,10,16,512]{3,2,1,0:T(8,128)(2,1)S(1)}, u32[]{:S(2)}, u32[]{:S(2)}) collective-permute-start(bf16[4,10,16,512]{3,2,1,0:T(8,128)(2,1)S(1)} %pad_maximum_fusion.refs_3_), channel_id=1, source_target_pairs={{0,16},{4,20},{8,24},{12,28},{16,0},{20,4},{24,8},{28,12},{1,17},{... | collective-permute-start | bytes 1966088 | tf_op jit(solution)/shard_map/ppermute | solution.py:595
  31.7 17.1 %collective-permute-start.9 = (bf16[4,10,16,512]{3,2,1,0:T(8,128)(2,1)S(1)}, bf16[4,10,16,512]{3,2,1,0:T(8,128)(2,1)S(1)}, u32[]{:S(2)}, u32[]{:S(2)}) collective-permute-start(bf16[4,10,16,512]{3,2,1,0:T(8,128)(2,1)S(1)} %pad_maximum_fusion.refs_3_), channel_id=1, source_target_pairs={{0,8},{4,12},{8,0},{12,4},{16,24},{20,28},{24,16},{28,20},{1,9},{5... | collective-permute-start | bytes 1966088 | tf_op jit(solution)/shard_map/ppermute | solution.py:595
  33.2 14.6 %collective-permute-start.13 = (bf16[256,512]{1,0:T(8,128)(2,1)}, bf16[256,512]{1,0:T(8,128)(2,1)S(1)}, u32[]{:S(2)}, u32[]{:S(2)}) collective-permute-start(bf16[256,512]{1,0:T(8,128)(2,1)} %get-tuple-element.101), channel_id=1, source_target_pairs={{0,1},{1,0},{2,3},{3,2},{4,5},{5,4},{6,7},{7,6},{8,9},{9,8},{10,11... | collective-permute-start | bytes 786440 | tf_op jit(solution)/shard_map/ppermute | solution.py:592
  48.9 9.7 %collective-permute-start.12 = (bf16[4,5,16,512]{3,2,1,0:T(8,128)(2,1)S(1)}, bf16[4,5,16,512]{3,2,1,0:T(8,128)(2,1)S(1)}, u32[]{:S(2)}, u32[]{:S(2)}) collective-permute-start(bf16[4,5,16,512]{3,2,1,0:T(8,128)(2,1)S(1)} %slice.21), channel_id=1, source_target_pairs={{0,8},{4,12},{8,0},{12,4},{16,24},{20,28},{24,16},{28,20},{1,9},{5... | collective-permute-start | bytes 983048 | tf_op jit(solution)/shard_map/ppermute | solution.py:595
  49.5 9.6 %collective-permute-start.10 = (bf16[4,5,16,512]{3,2,1,0:T(8,128)(2,1)S(1)}, bf16[4,5,16,512]{3,2,1,0:T(8,128)(2,1)S(1)}, u32[]{:S(2)}, u32[]{:S(2)}) collective-permute-start(bf16[4,5,16,512]{3,2,1,0:T(8,128)(2,1)S(1)} %slice.20), channel_id=1, source_target_pairs={{0,16},{4,20},{8,24},{12,28},{16,0},{20,4},{24,8},{28,12},{1,17},{... | collective-permute-start | bytes 983048 | tf_op jit(solution)/shard_map/ppermute | solution.py:595
  76.7 11.6 %collective-permute-start.28 = (bf16[16,4,16,512]{3,2,1,0:T(8,128)(2,1)S(1)}, bf16[16,4,16,512]{3,2,1,0:T(8,128)(2,1)S(1)}, u32[]{:S(2)}, u32[]{:S(2)}) collective-permute-start(bf16[16,4,16,512]{3,2,1,0:T(8,128)(2,1)S(1)} %get-tuple-element.134), channel_id=1, source_target_pairs={{0,4},{4,0},{8,12},{12,8},{16,20},{20,16},{24,28},{28,24},{1,5},{5... | collective-permute-start | bytes 3145736 | tf_op jit(solution)/shard_map/ppermute | solution.py:595
  77.6 16.9 %collective-permute-start.26 = (bf16[2,4,5,16,512]{4,3,2,1,0:T(8,128)(2,1)S(1)}, bf16[2,4,5,16,512]{4,3,2,1,0:T(8,128)(2,1)S(1)}, u32[]{:S(2)}, u32[]{:S(2)}) collective-permute-start(bf16[2,4,5,16,512]{4,3,2,1,0:T(8,128)(2,1)S(1)} %get-tuple-element.118), channel_id=1, source_target_pairs={{0,8},{4,12},{8,0},{12,4},{16,24},{20,28},{24,16},{28,20},{1,9},{5... | collective-permute-start | bytes 1966088 | tf_op jit(solution)/shard_map/ppermute | solution.py:595
  79.0 16.5 %collective-permute-start.27 = (bf16[2,4,5,16,512]{4,3,2,1,0:T(8,128)(2,1)S(1)}, bf16[2,4,5,16,512]{4,3,2,1,0:T(8,128)(2,1)S(1)}, u32[]{:S(2)}, u32[]{:S(2)}) collective-permute-start(bf16[2,4,5,16,512]{4,3,2,1,0:T(8,128)(2,1)S(1)} %get-tuple-element.119), channel_id=1, source_target_pairs={{0,16},{4,20},{8,24},{12,28},{16,0},{20,4},{24,8},{28,12},{1,17},{... | collective-permute-start | bytes 1966088 | tf_op jit(solution)/shard_map/ppermute | solution.py:595
  79.5 17.6 %collective-permute-start.32 = (bf16[128,512]{1,0:T(8,128)(2,1)S(1)}, bf16[128,512]{1,0:T(8,128)(2,1)S(1)}, u32[]{:S(2)}, u32[]{:S(2)}) collective-permute-start(bf16[128,512]{1,0:T(8,128)(2,1)S(1)} %get-tuple-element.142), channel_id=1, source_target_pairs={{0,2},{2,0},{3,1},{4,6},{6,4},{7,5},{8,10},{10,8},{11,9},{12,14},{... | collective-permute-start | bytes 393224 | tf_op jit(solution)/shard_map/ppermute | solution.py:592
  85.8 12.7 %collective-permute-start.33 = (bf16[128,512]{1,0:T(8,128)(2,1)S(1)}, bf16[128,512]{1,0:T(8,128)(2,1)S(1)}, u32[]{:S(2)}, u32[]{:S(2)}) collective-permute-start(bf16[128,512]{1,0:T(8,128)(2,1)S(1)} %get-tuple-element.143), channel_id=1, source_target_pairs={{0,3},{2,1},{3,0},{4,7},{6,5},{7,4},{8,11},{10,9},{11,8},{12,15},{... | collective-permute-start | bytes 393224 | tf_op jit(solution)/shard_map/ppermute | solution.py:592
  88.3 12.0 %collective-permute-start.31 = (bf16[256,512]{1,0:T(8,128)(2,1)S(1)}, bf16[256,512]{1,0:T(8,128)(2,1)S(1)}, u32[]{:S(2)}, u32[]{:S(2)}) collective-permute-start(bf16[256,512]{1,0:T(8,128)(2,1)S(1)} %get-tuple-element.141), channel_id=1, source_target_pairs={{0,1},{1,0},{2,3},{3,2},{4,5},{5,4},{6,7},{7,6},{8,9},{9,8},{10,11... | collective-permute-start | bytes 786440 | tf_op jit(solution)/shard_map/ppermute | solution.py:592
  95.8 10.7 %collective-permute-start.29 = (bf16[4,5,16,512]{3,2,1,0:T(8,128)(2,1)S(1)}, bf16[4,5,16,512]{3,2,1,0:T(8,128)(2,1)S(1)}, u32[]{:S(2)}, u32[]{:S(2)}) collective-permute-start(bf16[4,5,16,512]{3,2,1,0:T(8,128)(2,1)S(1)} %get-tuple-element.139), channel_id=1, source_target_pairs={{0,8},{4,12},{8,0},{12,4},{16,24},{20,28},{24,16},{28,20},{1,9},{5... | collective-permute-start | bytes 983048 | tf_op jit(solution)/shard_map/ppermute | solution.py:595
  96.5 10.6 %collective-permute-start.30 = (bf16[4,5,16,512]{3,2,1,0:T(8,128)(2,1)S(1)}, bf16[4,5,16,512]{3,2,1,0:T(8,128)(2,1)S(1)}, u32[]{:S(2)}, u32[]{:S(2)}) collective-permute-start(bf16[4,5,16,512]{3,2,1,0:T(8,128)(2,1)S(1)} %get-tuple-element.140), channel_id=1, source_target_pairs={{0,16},{4,20},{8,24},{12,28},{16,0},{20,4},{24,8},{28,12},{1,17},{... | collective-permute-start | bytes 983048 | tf_op jit(solution)/shard_map/ppermute | solution.py:595
  97.2 14.9 %collective-permute-start.37 = (bf16[4,4,16,512]{3,2,1,0:T(8,128)(2,1)S(1)}, bf16[4,4,16,512]{3,2,1,0:T(8,128)(2,1)S(1)}, u32[]{:S(2)}, u32[]{:S(2)}) collective-permute-start(bf16[4,4,16,512]{3,2,1,0:T(8,128)(2,1)S(1)} %get-tuple-element.151), channel_id=1, source_target_pairs={{0,8},{4,12},{8,0},{12,4},{16,24},{20,28},{24,16},{28,20},{1,9},{5... | collective-permute-start | bytes 786440 | tf_op jit(solution)/shard_map/ppermute | solution.py:595
  98.4 17.7 %collective-permute-start.38 = (bf16[4,4,16,512]{3,2,1,0:T(8,128)(2,1)S(1)}, bf16[4,4,16,512]{3,2,1,0:T(8,128)(2,1)S(1)}, u32[]{:S(2)}, u32[]{:S(2)}) collective-permute-start(bf16[4,4,16,512]{3,2,1,0:T(8,128)(2,1)S(1)} %get-tuple-element.152), channel_id=1, source_target_pairs={{0,16},{4,20},{8,24},{12,28},{16,0},{20,4},{24,8},{28,12},{1,17},{... | collective-permute-start | bytes 786440 | tf_op jit(solution)/shard_map/ppermute | solution.py:595
  100.2 15.9 %collective-permute-start.39 = (bf16[4,4,16,512]{3,2,1,0:T(8,128)(2,1)S(1)}, bf16[4,4,16,512]{3,2,1,0:T(8,128)(2,1)S(1)}, u32[]{:S(2)}, u32[]{:S(2)}) collective-permute-start(bf16[4,4,16,512]{3,2,1,0:T(8,128)(2,1)S(1)} %get-tuple-element.153), channel_id=1, source_target_pairs={{0,24},{4,28},{8,16},{12,20},{16,8},{20,12},{24,0},{28,4},{1,25},{... | collective-permute-start | bytes 786440 | tf_op jit(solution)/shard_map/ppermute | solution.py:595
  107.5 20.5 %collective-permute-start.34 = (bf16[10,16,512]{2,1,0:T(8,128)(2,1)S(1)}, bf16[10,16,512]{2,1,0:T(8,128)(2,1)S(1)}, u32[]{:S(2)}, u32[]{:S(2)}) collective-permute-start(bf16[10,16,512]{2,1,0:T(8,128)(2,1)S(1)} %get-tuple-element.147), channel_id=1, source_target_pairs={{0,1},{1,0},{2,3},{3,2},{4,5},{5,4},{6,7},{7,6},{8,9},{9,8},{10,11... | collective-permute-start | bytes 491528 | tf_op jit(solution)/shard_map/ppermute | solution.py:592
  109.5 18.4 %collective-permute-start.35 = (bf16[10,16,512]{2,1,0:T(8,128)(2,1)S(1)}, bf16[10,16,512]{2,1,0:T(8,128)(2,1)S(1)}, u32[]{:S(2)}, u32[]{:S(2)}) collective-permute-start(bf16[10,16,512]{2,1,0:T(8,128)(2,1)S(1)} %get-tuple-element.148), channel_id=1, source_target_pairs={{0,2},{1,3},{2,0},{3,1},{4,6},{5,7},{6,4},{7,5},{8,10},{9,11},{10,... | collective-permute-start | bytes 491528 | tf_op jit(solution)/shard_map/ppermute | solution.py:592
  112.1 15.9 %collective-permute-start.36 = (bf16[10,16,512]{2,1,0:T(8,128)(2,1)S(1)}, bf16[10,16,512]{2,1,0:T(8,128)(2,1)S(1)}, u32[]{:S(2)}, u32[]{:S(2)}) collective-permute-start(bf16[10,16,512]{2,1,0:T(8,128)(2,1)S(1)} %get-tuple-element.149), channel_id=1, source_target_pairs={{0,3},{1,2},{2,1},{3,0},{4,7},{5,6},{6,5},{7,4},{8,11},{9,10},{10,... | collective-permute-start | bytes 491528 | tf_op jit(solution)/shard_map/ppermute | solution.py:592
  (24 other events, 323.2 us)

commit v6 on v5

--- a/solution.py
+++ b/solution.py
@@ -95,9 +95,9 @@
 
 def pack_body(with_weights, *refs):
     me, seq = own_place()
-    count = 13 if with_weights else 4
+    count = 9 if with_weights else 4
     sources, refs = (refs[:count], refs[count:])
-    outs = 5 if with_weights else 3
+    outs = 4 if with_weights else 3
     targets, held, sem = (refs[:outs], refs[outs : outs + count], refs[-1])
     pay1, pay2, pay3 = targets[:3]
     ins = [
@@ -116,10 +116,10 @@
         copies.append(item)
 
     if with_weights:
-        early, late = targets[3:]
+        late = targets[3]
         row = refs[outs + count]
-        width = early.shape[2]
-        gain, bias = held[11:]
+        width = late.shape[2]
+        gain, bias = held[7:]
         shard = gain.shape[1]
         col = lax.broadcasted_iota(jnp.int32, (shard, width), 1)
         at = lax.broadcasted_iota(jnp.int32, (shard, width), 0)
@@ -127,12 +127,10 @@
     for item in ins:
         item.wait()
     if with_weights:
-        wq, wk, wv, pos, wo, up, down = held[4:11]
+        wo, up, down = held[4:7]
         chunks = up.shape[1] // width
         vectors = jnp.concatenate([mm(gain[...], spread), mm(bias[...], spread)], 0)
         row[...] = pad_rows(vectors, BAND).astype(BF)
-        for i, weight in enumerate((wq, wk, wv, pos)):
-            copy(weight, early.at[i])
         copy(wo, late.at[0])
         for c in range(chunks):
             cols = pl.ds(c * width, width)
@@ -171,6 +169,16 @@
 
     for item in copies:
         item.wait()
+
+
+def early_pack_body(*refs):
+    sources, early, held, sem = (refs[:4], refs[4], refs[5], refs[6])
+    for i, source in enumerate(sources):
+        pltpu.make_async_copy(source, held.at[i], sem.at[i]).start()
+    for i, source in enumerate(sources):
+        pltpu.make_async_copy(source, held.at[i], sem.at[i]).wait()
+    pltpu.make_async_copy(held, early, sem.at[0]).start()
+    pltpu.make_async_copy(held, early, sem.at[0]).wait()
 
 
 def stack_heads(block, lane):
@@ -316,17 +324,26 @@
     parts, refs = (refs[3 : 3 + count], refs[3 + count :])
     out_o, gsum_o, gmix_o = refs[:3]
     grad_parts = refs[3:8]
-    weights, grads, act, slope, blocks, cots, sem = refs[8:]
+    weights, grads, act, slope, cots, sem = refs[8:]
     me, seq = own_place()
     me = me if direct else jnp.int32(0)
     fetch_weights(layout, parts, weights, sem, me)
     n_long, n_short = (long_cot.shape[1], short_cot.shape[1])
-    two, three = (pad_rows(got[n_short:, :], n_long) for got in (got2, got3))
-    found = row_blocks(seq, long_cot, short_cot, got1[n_long:, :], two, three)
-    for k, block in enumerate(found):
-        blocks[k * n_long : (k + 1) * n_long, :] = block.astype(F32)
-    gather_queries(seq, blocks, cots)
-    blocks[...] = jnp.zeros_like(blocks)
+
+    @pl.when(has_long(seq))
+    def _():
+        own = pl.ds(jnp.where(seq == 1, n_long, 0), n_long)
+        other = pl.ds(jnp.where(seq == 1, 0, n_long), n_long)
+        cots[own, :] = long_cot[0].astype(F32)
+        cots[other, :] = got1[n_long:, :].astype(F32)
+
+    @pl.when((seq == 0) | (seq == 3))
+    def _():
+        own = jnp.where(seq == 0, short_cot[0], short_cot[1])
+        others = (got1[n_long : n_long + n_short, :], got2[n_short:, :], got3[n_short:, :])
+        for k, block in enumerate((own,) + others):
+            cots[k * n_short : (k + 1) * n_short, :] = block.astype(F32)
+
     pltpu.make_async_copy(weights, weights, sem).wait()
     width = first.shape[1]
     chunks = (weights.shape[0] - 2) // 2
@@ -345,8 +362,9 @@
         act[c] = (hidden * cdf).astype(BF)
         second = second + mm(act[c], weights[1 + chunks + c], NT)
     xhat1, scale1 = norm_parts(second)
-    spread_queries(seq, xhat1 * gain1 + bias1, blocks)
-    out_o[...] = blocks[...].astype(BF)
+    result = (xhat1 * gain1 + bias1).astype(BF)
+    out_o[...] = jnp.zeros_like(out_o)
+    spread_queries(seq, result, out_o)
     cot_wide = cots[...]
     grad_second = norm_back(cot_wide, gain1, xhat1, scale1)
     second_low = grad_second.astype(BF)
@@ -471,25 +489,25 @@
     return pl.BlockSpec((1,) + shape[1:], lambda i: (layer * 4 + i,) + (0,) * (len(shape) - 1))
 
 
-def first_sums_body(half, near1, near2, near3, far1, far2, far3, to_x, to_y):
-    to_y[0, 0] = (wide(near2, 0)[:half] + wide(far2, 0)[:half]).astype(BF)
-    to_y[1, 0] = (wide(near3, 0)[:half] + wide(far3, 0)[:half]).astype(BF)
-    to_x[0, 0] = (wide(near1, 0)[half:] + wide(far1, 0)[half:]).astype(BF)
-    to_x[1, 0] = (wide(near3, 0)[half:] + wide(far3, 0)[half:]).astype(BF)
+def first_sums_body(half, near1, near2, near3, far1, far2, far3, to_x, to_y, last_x, last_y):
+    to_y[0] = (wide(near3, 0)[:half] + wide(far3, 0)[:half]).astype(BF)
+    to_x[0] = (wide(near3, 0)[half:] + wide(far3, 0)[half:]).astype(BF)
+    last_y[0] = (wide(near2, 0)[:half] + wide(far2, 0)[:half]).astype(BF)
+    last_x[0] = (wide(near1, 0)[half:] + wide(far1, 0)[half:]).astype(BF)
 
 
 def second_sums_body(half, near1, near2, far1, far2, from_x, from_y, to_x, to_y):
-    to_x[0] = (wide(near1, 0)[:half] + wide(far1, 0)[:half] + wide(from_y, 0, 0)).astype(BF)
-    to_y[0] = (wide(near2, 0)[half:] + wide(far2, 0)[half:] + wide(from_x, 0, 0)).astype(BF)
+    to_x[0] = (wide(near1, 0)[:half] + wide(far1, 0)[:half] + wide(from_y, 0)).astype(BF)
+    to_y[0] = (wide(near2, 0)[half:] + wide(far2, 0)[half:] + wide(from_x, 0)).astype(BF)
 
 
 def last_sums_body(half, near0, far0, from_x, from_y, then_x, then_y, *outs):
     for place, out in enumerate(outs):
         low = wide(near0, place)[:half] + wide(far0, place)[:half]
-        low = low + (wide(from_y, 0, place) + wide(then_x, place))
+        low = low + (wide(from_y, place) + wide(then_x, place))
         out[:half] = low.astype(out.dtype)
         high = wide(near0, place)[half:] + wide(far0, place)[half:]
-        high = high + (wide(from_x, 0, place) + wide(then_y, place))
+        high = high + (wide(from_x, place) + wide(then_y, place))
         out[half:] = high.astype(out.dtype)
 
 
@@ -603,11 +621,11 @@
     own, specs, scratch = ([], [HBM] * 4, [])
     held = list(acts)
     if direct:
-        own = [w_query, w_key, w_value, pos_table.T, w_out, w_up, w_down.T]
+        own = [w_out, w_up, w_down.T]
         own += [norm_gain, norm_bias]
         held += own
-        packed += [((count, BAND, width), BF, HBM) for count in (early_pieces, late_pieces)]
-        specs += [HBM] * 9
+        packed += [((late_pieces, BAND, width), BF, HBM)]
+        specs += [HBM] * 5
         scratch = [pltpu.VMEM((BAND, width), BF)]
     pays = call(
         functools.partial(pack_body, direct),
@@ -647,7 +665,17 @@
     early_layout = plain_layout(early_pieces)
     late_layout = split_layout(late_pieces) if direct else plain_layout(late_pieces)
     if direct:
-        early, late = pays[3:]
+        late = pays[3]
+        shape = (early_pieces, BAND, width)
+        early = call(
+            early_pack_body,
+            [(shape, BF, HBM)],
+            [HBM] * 4,
+            [pltpu.VMEM(shape, BF), pltpu.SemaphoreType.DMA((4,))],
+            (0, MIB),
+            "early_pack",
+            60,
+        )(w_query, w_key, w_value, pos_table.T)[0]
         early_places = places(early)
         late = after(late, early_places[1], early_places[2])
         late_places = places(late)
@@ -726,7 +754,6 @@
             pltpu.VMEM((late_pieces, width, width), BF),
             pltpu.VMEM((chunks, rows, width), BF),
             pltpu.VMEM((chunks, rows, width), F32),
-            pltpu.VMEM((keys, width), F32),
             pltpu.VMEM((rows, width), F32),
             pltpu.SemaphoreType.DMA,
         ],
@@ -785,36 +812,36 @@
         half = late_pieces // 2
         near0, near1, near2, near3 = late_parts[:4]
         far = late_arrived
-        pair = ((2, 4, half, BAND, width), BF, 1)
         single = ((4, half, BAND, width), BF, 0)
-        to_x, to_y = sum_call(
+        to_x, to_y, last_x, last_y = sum_call(
             functools.partial(first_sums_body, half),
-            [pair, pair],
+            [single] * 4,
             [near1, near2, near3, far, far, far],
             [one_place(item) for item in (near1, near2, near3)] + [one_place(far, k) for k in (1, 2, 3)],
             4,
             "late_sums_1",
         )
         from_x, from_y = (swap_dp(to_x, 2), swap_dp(to_y, 4))
+        last_x, last_y = (swap_dp(last_x, 2), swap_dp(last_y, 4))
         early_far = early_parts[-1]
         early_arrived = swap_dp(early_far, 1)
         early_sums = core_sums(early_parts, early_arrived)
         from_x, from_y, early_sums = lax.optimization_barrier((from_x, from_y, early_sums))
-        second = pl.BlockSpec((1, 1, half, BAND, width), lambda i: (1, i, 0, 0, 0))
         then_x, then_y = sum_call(
             functools.partial(second_sums_body, half),
             [single, single],
             [near1, near2, far, far, from_x, from_y],
-            [one_place(near1), one_place(near2), one_place(far, 1), one_place(far, 2), second, second],
+            [one_place(near1), one_place(near2), one_place(far, 1), one_place(far, 2), one_place(from_x), one_place(from_y)],
             4,
             "late_sums_2",
         )
         then_x, then_y = (swap_dp(then_x, 2), swap_dp(then_y, 4))
+        early_sums = lax.optimization_barrier((early_sums, last_x, last_y))[0]
         early_layers = [swap_dp(part, 2 * k) for k, part in enumerate(early_sums, 1)]
         then_x, then_y, got = lax.optimization_barrier((then_x, then_y, got))
         late_cut = cut_sums(
             functools.partial(last_sums_body, half),
-            [near0, far, from_x, from_y, then_x, then_y],
+            [near0, far, last_x, last_y, then_x, then_y],
             late_pieces,
             "late_sums_3",
         )

time: 130 us -> 128 us (0.985)
  waiting for transfers between devices: 38.9 us -> 32.8 us
  starting transfers between devices: 61.7 us -> 65 us
    ppermute x25 -> x27, waiting for transfers between devices: 19.2 us -> 10.8 us  [swap_dp(): return lax.ppermute(value, 'dp', [(i, i ^ mask) for i in range(dp_count)])]
    ppermute x25 -> x27, starting transfers between devices: 18.7 us -> 21.7 us  [swap_dp(): return lax.ppermute(value, 'dp', [(i, i ^ mask) for i in range(dp_count)])]
    ppermute x18, waiting for transfers between devices: 19.7 us -> 22 us  [swap_seq(): return lax.ppermute(value, 'seq', pairs)]
    pallas_call x0 -> x1, Pallas kernels: none -> 1.47 us  [local(): call(early_pack_body, [(shape, BF, HBM)], [HBM] * 4, [pltpu.VMEM(shape, B...]
  transfers between devices with their start and end apart: 43 -> 45, of which waited for: 21 -> 20; matrix products, arithmetic and copies ran while one was open for 2% -> 2% of each run, Pallas kernels for 10% -> 12%
where the time goes in v6:
time: 128 us
  starting transfers between devices  65 us (51%)
  waiting for transfers between devices  32.8 us (26%)
  Pallas kernels  26.1 us (20%)
  other arithmetic  2.18 us (2%)
  between operations  1.67 us (1%)
    ppermute x18, starting transfers between devices, swap_seq(): return lax.ppermute(value, 'seq', pairs)  43.3 us
    ppermute x18, waiting for transfers between devices, swap_seq(): return lax.ppermute(value, 'seq', pairs)  22 us
    ppermute x27, starting transfers between devices, swap_dp(): return lax.ppermute(value, 'dp', [(i, i ^ mask) for i in range(dp_count)])  21.7 us
    ppermute x27, waiting for transfers between devices, swap_dp(): return lax.ppermute(value, 'dp', [(i, i ^ mask) for i in range(dp_count)])  10.8 us
    pallas_call x1, Pallas kernels, local(): call(functools.partial(middle_body, direct, late_layout), [((keys, width)...  8.16 us
    pallas_call x1, Pallas kernels, local(): call(functools.partial(attend_back_body, direct, early_layout), [((rows,...  5.17 us
    pallas_call x1, Pallas kernels, local(): call(functools.partial(attend_body, direct, early_layout), [((rows, width...  4.72 us
  transfers between devices with their start and end apart: 45, of which 20 were waited for; matrix products, arithmetic and copies ran while one was open for 2% of the time, Pallas kernels for 12%

profile of v6, /device:TPU:0, one launch (start us, length us, event | category | flops | bytes accessed | tf_op | source)
XLA Modules:
  0.0 127.7 jit_solution(13937345084191839363)
XLA Ops:
  2.2 4.1 %collective-permute-start.1 = (bf16[4,16,512]{2,1,0:T(8,128)(2,1)}, bf16[4,16,512]{2,1,0:T(8,128)(2,1)S(1)}, u32[]{:S(2)}, u32[]{:S(2)}) collective-permute-start(bf16[4,16,512]{2,1,0:T(8,128)(2,1)} %early_pack.1), channel_id=1, source_target_pairs={{0,2},{1,3},{2,0},{3,1},{4,6},{5,7},{6,4},{7,5},{8,10},{9,11},{10,... | collective-permute-start | bytes 196616 | tf_op jit(solution)/shard_map/ppermute | solution.py:610
  7.8 2.3 %pack.1 = (bf16[256,512]{1,0:T(8,128)(2,1)}, bf16[128,512]{1,0:T(8,128)(2,1)}, bf16[128,512]{1,0:T(8,128)(2,1)}, bf16[10,16,512]{2,1,0:T(8,128)(2,1)}) custom-call(bf16[1,128,512]{2,1,0:T(8,128)(2,1)} %refs_0_.5, bf16[2,64,512]{2,1,0:T(8,128)(2,1)} %refs_1_.5, bf16[1,128,512]{2,1,0:T(8,128)(2,1)} %long_cot.1, bf16[2,64,512]{2,1,0:T(8,128)(2,1)} %short_cot.1, ...), custom_call_target="tpu_custom_call" | custom-call | bytes 4194304 | tf_op jit(solution)/shard_map/pack/pallas_call | solution.py:630
  10.7 4.6 %collective-permute-start.4 = (bf16[10,16,512]{2,1,0:T(8,128)(2,1)}, bf16[10,16,512]{2,1,0:T(8,128)(2,1)S(1)}, u32[]{:S(2)}, u32[]{:S(2)}) collective-permute-start(bf16[10,16,512]{2,1,0:T(8,128)(2,1)} %get-tuple-element.99), channel_id=1, source_target_pairs={{0,3},{1,2},{2,1},{3,0},{4,7},{5,6},{6,5},{7,4},{8,11},{9,10},{10,... | collective-permute-start | bytes 491528 | tf_op jit(solution)/shard_map/ppermute | solution.py:610
  16.8 2.5 %collective-permute-start.8 = (bf16[4,4,16,512]{3,2,1,0:T(8,128)(2,1)S(1)}, bf16[4,4,16,512]{3,2,1,0:T(8,128)(2,1)S(1)}, u32[]{:S(2)}, u32[]{:S(2)}) collective-permute-start(bf16[4,4,16,512]{3,2,1,0:T(8,128)(2,1)S(1)} %pad_maximum_fusion.1.refs_5_.refs_0_), channel_id=1, source_target_pairs={{0,24},{4,28},{8,16},{12,20},{16,8},{20,12},{24,0},{28,4},{1,25},{... | collective-permute-start | bytes 786440 | tf_op jit(solution)/shard_map/ppermute | solution.py:613
  22.2 6.0 %collective-permute-done.3 = bf16[10,16,512]{2,1,0:T(8,128)(2,1)S(1)} collective-permute-done((bf16[10,16,512]{2,1,0:T(8,128)(2,1)}, bf16[10,16,512]{2,1,0:T(8,128)(2,1)S(1)}, u32[]{:S(2)}, u32[]{:S(2)}) %collective-permute-start.3) | collective-permute-done | bytes 163872 | tf_op jit(solution)/shard_map/ppermute | solution.py:610
  32.3 3.7 %collective-permute-start.13 = (bf16[256,512]{1,0:T(8,128)(2,1)}, bf16[256,512]{1,0:T(8,128)(2,1)S(1)}, u32[]{:S(2)}, u32[]{:S(2)}) collective-permute-start(bf16[256,512]{1,0:T(8,128)(2,1)} %get-tuple-element.104), channel_id=1, source_target_pairs={{0,1},{1,0},{2,3},{3,2},{4,5},{5,4},{6,7},{7,6},{8,9},{9,8},{10,11... | collective-permute-start | bytes 786440 | tf_op jit(solution)/shard_map/ppermute | solution.py:610
  36.0 2.1 %collective-permute-start.14 = (bf16[128,512]{1,0:T(8,128)(2,1)}, bf16[128,512]{1,0:T(8,128)(2,1)S(1)}, u32[]{:S(2)}, u32[]{:S(2)}) collective-permute-start(bf16[128,512]{1,0:T(8,128)(2,1)} %get-tuple-element.105), channel_id=1, source_target_pairs={{0,2},{1,3},{2,0},{4,6},{5,7},{6,4},{8,10},{9,11},{10,8},{12,14},{... | collective-permute-start | bytes 393224 | tf_op jit(solution)/shard_map/ppermute | solution.py:610
  38.1 2.6 %collective-permute-start.15 = (bf16[128,512]{1,0:T(8,128)(2,1)}, bf16[128,512]{1,0:T(8,128)(2,1)S(1)}, u32[]{:S(2)}, u32[]{:S(2)}) collective-permute-start(bf16[128,512]{1,0:T(8,128)(2,1)} %get-tuple-element.106), channel_id=1, source_target_pairs={{0,3},{1,2},{3,0},{4,7},{5,6},{7,4},{8,11},{9,10},{11,8},{12,15},{... | collective-permute-start | bytes 393224 | tf_op jit(solution)/shard_map/ppermute | solution.py:610
  40.7 4.2 %collective-permute-done.14.refs_3_.refs_1_ = bf16[128,512]{1,0:T(8,128)(2,1)S(1)} collective-permute-done((bf16[128,512]{1,0:T(8,128)(2,1)}, bf16[128,512]{1,0:T(8,128)(2,1)S(1)}, u32[]{:S(2)}, u32[]{:S(2)}) %collective-permute-start.14) | collective-permute-done | bytes 131104 | tf_op jit(solution)/shard_map/ppermute | solution.py:610
  44.9 2.1 %collective-permute-done.15.refs_4_.refs_2_ = bf16[128,512]{1,0:T(8,128)(2,1)S(1)} collective-permute-done((bf16[128,512]{1,0:T(8,128)(2,1)}, bf16[128,512]{1,0:T(8,128)(2,1)S(1)}, u32[]{:S(2)}, u32[]{:S(2)}) %collective-permute-start.15) | collective-permute-done | bytes 131104 | tf_op jit(solution)/shard_map/ppermute | solution.py:610
  50.7 4.7 %attend.1 = (f32[256,512]{1,0:T(8,128)S(1)}, bf16[512,512]{1,0:T(8,128)(2,1)S(1)}, bf16[256,512]{1,0:T(8,128)(2,1)S(1)}, bf16[256,512]{1,0:T(8,128)(2,1)S(1)}, b...) custom-call(s32[1]{0:T(128)S(6)} %copy.28.long_len, ...), custom_call_target="tpu_custom_call" | custom-call | flops 1073741824 | bytes 10485760 | tf_op jit(solution)/shard_map/attend/pallas_call | solution.py:716
  55.5 2.2 %collective-permute-done.12.refs_7_ = bf16[4,5,16,512]{3,2,1,0:T(8,128)(2,1)S(1)} collective-permute-done((bf16[4,5,16,512]{3,2,1,0:T(8,128)(2,1)S(1)}, bf16[4,5,16,512]{3,2,1,0:T(8,128)(2,1)S(1)}, u32[]{:S(2)}, u32[]{:S(2)}) %collective-permute-start.12) | collective-permute-done | bytes 327712 | tf_op jit(solution)/shard_map/ppermute | solution.py:613
  60.3 8.2 %middle.1 = (bf16[512,512]{1,0:T(8,128)(2,1)S(1)}, f32[256,512]{1,0:T(8,128)S(1)}, bf16[256,512]{1,0:T(8,128)(2,1)S(1)}, bf16[4,10,16,512]{3,2,1,0:T(8,128)(2,1)...) custom-call(f32[256,512]{1,0:T(8,128)S(1)} %get-tuple-element.112.fi, ...), custom_call_target="tpu_custom_call" | custom-call | flops 4294967296 | bytes 20971520 | tf_op jit(solution)/shard_map/middle/pallas_call | solution.py:746
  68.7 5.2 %attend_back.1 = (bf16[256,512]{1,0:T(8,128)(2,1)S(1)}, bf16[512,512]{1,0:T(8,128)(2,1)S(1)}, bf16[512,512]{1,0:T(8,128)(2,1)S(1)}, f32[512,512]{1,0:T(8,128)S(1...) custom-call(bf16[256,512]{1,0:T(8,128)(2,1)S(1)} %get-tuple-element., ...), custom_call_target="tpu_custom_call" | custom-call | flops 2147483648 | bytes 12582912 | tf_op jit(solution)/shard_map/attend_back/pallas_call | solution.py:776
  80.6 5.7 %collective-permute-start.34 = (bf16[128,512]{1,0:T(8,128)(2,1)S(1)}, bf16[128,512]{1,0:T(8,128)(2,1)S(1)}, u32[]{:S(2)}, u32[]{:S(2)}) collective-permute-start(bf16[128,512]{1,0:T(8,128)(2,1)S(1)} %get-tuple-element.147), channel_id=1, source_target_pairs={{0,2},{2,0},{3,1},{4,6},{6,4},{7,5},{8,10},{10,8},{11,9},{12,14},{... | collective-permute-start | bytes 393224 | tf_op jit(solution)/shard_map/ppermute | solution.py:610
  87.1 5.1 %collective-permute-start.35 = (bf16[128,512]{1,0:T(8,128)(2,1)S(1)}, bf16[128,512]{1,0:T(8,128)(2,1)S(1)}, u32[]{:S(2)}, u32[]{:S(2)}) collective-permute-start(bf16[128,512]{1,0:T(8,128)(2,1)S(1)} %get-tuple-element.148), channel_id=1, source_target_pairs={{0,3},{2,1},{3,0},{4,7},{6,5},{7,4},{8,11},{10,9},{11,8},{12,15},{... | collective-permute-start | bytes 393224 | tf_op jit(solution)/shard_map/ppermute | solution.py:610
  98.1 2.2 %collective-permute-done.33.refs_10_ = bf16[256,512]{1,0:T(8,128)(2,1)S(1)} collective-permute-done((bf16[256,512]{1,0:T(8,128)(2,1)S(1)}, bf16[256,512]{1,0:T(8,128)(2,1)S(1)}, u32[]{:S(2)}, u32[]{:S(2)}) %collective-permute-start.33) | collective-permute-done | bytes 262176 | tf_op jit(solution)/shard_map/ppermute | solution.py:610
  102.0 1.9 %collective-permute-done.31.then_x = bf16[4,5,16,512]{3,2,1,0:T(8,128)(2,1)S(1)} collective-permute-done((bf16[4,5,16,512]{3,2,1,0:T(8,128)(2,1)S(1)}, bf16[4,5,16,512]{3,2,1,0:T(8,128)(2,1)S(1)}, u32[]{:S(2)}, u32[]{:S(2)}) %collective-permute-start.31) | collective-permute-done | bytes 327712 | tf_op jit(solution)/shard_map/ppermute | solution.py:613
  105.6 1.9 %collective-permute-start.36 = (bf16[10,16,512]{2,1,0:T(8,128)(2,1)S(1)}, bf16[10,16,512]{2,1,0:T(8,128)(2,1)S(1)}, u32[]{:S(2)}, u32[]{:S(2)}) collective-permute-start(bf16[10,16,512]{2,1,0:T(8,128)(2,1)S(1)} %get-tuple-element.152), channel_id=1, source_target_pairs={{0,1},{1,0},{2,3},{3,2},{4,5},{5,4},{6,7},{7,6},{8,9},{9,8},{10,11... | collective-permute-start | bytes 491528 | tf_op jit(solution)/shard_map/ppermute | solution.py:610
  107.4 1.9 %collective-permute-start.37 = (bf16[10,16,512]{2,1,0:T(8,128)(2,1)S(1)}, bf16[10,16,512]{2,1,0:T(8,128)(2,1)S(1)}, u32[]{:S(2)}, u32[]{:S(2)}) collective-permute-start(bf16[10,16,512]{2,1,0:T(8,128)(2,1)S(1)} %get-tuple-element.153), channel_id=1, source_target_pairs={{0,2},{1,3},{2,0},{3,1},{4,6},{5,7},{6,4},{7,5},{8,10},{9,11},{10,... | collective-permute-start | bytes 491528 | tf_op jit(solution)/shard_map/ppermute | solution.py:610
  109.5 3.2 %collective-permute-start.38 = (bf16[10,16,512]{2,1,0:T(8,128)(2,1)S(1)}, bf16[10,16,512]{2,1,0:T(8,128)(2,1)S(1)}, u32[]{:S(2)}, u32[]{:S(2)}) collective-permute-start(bf16[10,16,512]{2,1,0:T(8,128)(2,1)S(1)} %get-tuple-element.154), channel_id=1, source_target_pairs={{0,3},{1,2},{2,1},{3,0},{4,7},{5,6},{6,5},{7,4},{8,11},{9,10},{10,... | collective-permute-start | bytes 491528 | tf_op jit(solution)/shard_map/ppermute | solution.py:610
  114.6 2.2 %collective-permute-start.42 = (bf16[4,16,512]{2,1,0:T(8,128)(2,1)S(1)}, bf16[4,16,512]{2,1,0:T(8,128)(2,1)S(1)}, u32[]{:S(2)}, u32[]{:S(2)}) collective-permute-start(bf16[4,16,512]{2,1,0:T(8,128)(2,1)S(1)} %get-tuple-element.163), channel_id=1, source_target_pairs={{0,1},{1,0},{2,3},{3,2},{4,5},{5,4},{6,7},{7,6},{8,9},{9,8},{10,11... | collective-permute-start | bytes 196616 | tf_op jit(solution)/shard_map/ppermute | solution.py:610
  120.2 2.1 %collective-permute-start.44 = (bf16[4,16,512]{2,1,0:T(8,128)(2,1)S(1)}, bf16[4,16,512]{2,1,0:T(8,128)(2,1)S(1)}, u32[]{:S(2)}, u32[]{:S(2)}) collective-permute-start(bf16[4,16,512]{2,1,0:T(8,128)(2,1)S(1)} %get-tuple-element.165), channel_id=1, source_target_pairs={{0,3},{1,2},{2,1},{3,0},{4,7},{5,6},{6,5},{7,4},{8,11},{9,10},{10,... | collective-permute-start | bytes 196616 | tf_op jit(solution)/shard_map/ppermute | solution.py:610
  122.3 4.0 %collective-permute-done.43.refs_6_ = bf16[4,16,512]{2,1,0:T(8,128)(2,1)S(1)} collective-permute-done((bf16[4,16,512]{2,1,0:T(8,128)(2,1)S(1)}, bf16[4,16,512]{2,1,0:T(8,128)(2,1)S(1)}, u32[]{:S(2)}, u32[]{:S(2)}) %collective-permute-start.43) | collective-permute-done | bytes 65568 | tf_op jit(solution)/shard_map/ppermute | solution.py:610
  (92 shorter events, 41.4 us)
Async XLA Ops:
  10.7 9.9 %collective-permute-start.4 = (bf16[10,16,512]{2,1,0:T(8,128)(2,1)}, bf16[10,16,512]{2,1,0:T(8,128)(2,1)S(1)}, u32[]{:S(2)}, u32[]{:S(2)}) collective-permute-start(bf16[10,16,512]{2,1,0:T(8,128)(2,1)} %get-tuple-element.99), channel_id=1, source_target_pairs={{0,3},{1,2},{2,1},{3,0},{4,7},{5,6},{6,5},{7,4},{8,11},{9,10},{10,... | collective-permute-start | bytes 491528 | tf_op jit(solution)/shard_map/ppermute | solution.py:610
  15.4 12.8 %collective-permute-start.3 = (bf16[10,16,512]{2,1,0:T(8,128)(2,1)}, bf16[10,16,512]{2,1,0:T(8,128)(2,1)S(1)}, u32[]{:S(2)}, u32[]{:S(2)}) collective-permute-start(bf16[10,16,512]{2,1,0:T(8,128)(2,1)} %get-tuple-element.99), channel_id=1, source_target_pairs={{0,2},{1,3},{2,0},{3,1},{4,6},{5,7},{6,4},{7,5},{8,10},{9,11},{10,... | collective-permute-start | bytes 491528 | tf_op jit(solution)/shard_map/ppermute | solution.py:610
  15.4 12.8 %collective-permute-start.2 = (bf16[10,16,512]{2,1,0:T(8,128)(2,1)}, bf16[10,16,512]{2,1,0:T(8,128)(2,1)S(1)}, u32[]{:S(2)}, u32[]{:S(2)}) collective-permute-start(bf16[10,16,512]{2,1,0:T(8,128)(2,1)} %get-tuple-element.99), channel_id=1, source_target_pairs={{0,1},{1,0},{2,3},{3,2},{4,5},{5,4},{6,7},{7,6},{8,9},{9,8},{10,11... | collective-permute-start | bytes 491528 | tf_op jit(solution)/shard_map/ppermute | solution.py:610
  16.8 12.4 %collective-permute-start.8 = (bf16[4,4,16,512]{3,2,1,0:T(8,128)(2,1)S(1)}, bf16[4,4,16,512]{3,2,1,0:T(8,128)(2,1)S(1)}, u32[]{:S(2)}, u32[]{:S(2)}) collective-permute-start(bf16[4,4,16,512]{3,2,1,0:T(8,128)(2,1)S(1)} %pad_maximum_fusion.1.refs_5_.refs_0_), channel_id=1, source_target_pairs={{0,24},{4,28},{8,16},{12,20},{16,8},{20,12},{24,0},{28,4},{1,25},{... | collective-permute-start | bytes 786440 | tf_op jit(solution)/shard_map/ppermute | solution.py:613
  19.3 9.9 %collective-permute-start.7 = (bf16[4,4,16,512]{3,2,1,0:T(8,128)(2,1)S(1)}, bf16[4,4,16,512]{3,2,1,0:T(8,128)(2,1)S(1)}, u32[]{:S(2)}, u32[]{:S(2)}) collective-permute-start(bf16[4,4,16,512]{3,2,1,0:T(8,128)(2,1)S(1)} %pad_maximum_fusion.1.refs_5_.refs_0_), channel_id=1, source_target_pairs={{0,16},{4,20},{8,24},{12,28},{16,0},{20,4},{24,8},{28,12},{1,17},{... | collective-permute-start | bytes 786440 | tf_op jit(solution)/shard_map/ppermute | solution.py:613
  29.3 18.2 %collective-permute-start.11 = (bf16[4,10,16,512]{3,2,1,0:T(8,128)(2,1)S(1)}, bf16[4,10,16,512]{3,2,1,0:T(8,128)(2,1)S(1)}, u32[]{:S(2)}, u32[]{:S(2)}) collective-permute-start(bf16[4,10,16,512]{3,2,1,0:T(8,128)(2,1)S(1)} %pad_maximum_fusion.refs_3_), channel_id=1, source_target_pairs={{0,16},{4,20},{8,24},{12,28},{16,0},{20,4},{24,8},{28,12},{1,17},{... | collective-permute-start | bytes 1966088 | tf_op jit(solution)/shard_map/ppermute | solution.py:613
  30.8 17.2 %collective-permute-start.9 = (bf16[4,10,16,512]{3,2,1,0:T(8,128)(2,1)S(1)}, bf16[4,10,16,512]{3,2,1,0:T(8,128)(2,1)S(1)}, u32[]{:S(2)}, u32[]{:S(2)}) collective-permute-start(bf16[4,10,16,512]{3,2,1,0:T(8,128)(2,1)S(1)} %pad_maximum_fusion.refs_3_), channel_id=1, source_target_pairs={{0,8},{4,12},{8,0},{12,4},{16,24},{20,28},{24,16},{28,20},{1,9},{5... | collective-permute-start | bytes 1966088 | tf_op jit(solution)/shard_map/ppermute | solution.py:613
  32.3 14.7 %collective-permute-start.13 = (bf16[256,512]{1,0:T(8,128)(2,1)}, bf16[256,512]{1,0:T(8,128)(2,1)S(1)}, u32[]{:S(2)}, u32[]{:S(2)}) collective-permute-start(bf16[256,512]{1,0:T(8,128)(2,1)} %get-tuple-element.104), channel_id=1, source_target_pairs={{0,1},{1,0},{2,3},{3,2},{4,5},{5,4},{6,7},{7,6},{8,9},{9,8},{10,11... | collective-permute-start | bytes 786440 | tf_op jit(solution)/shard_map/ppermute | solution.py:610
  48.0 9.7 %collective-permute-start.12 = (bf16[4,5,16,512]{3,2,1,0:T(8,128)(2,1)S(1)}, bf16[4,5,16,512]{3,2,1,0:T(8,128)(2,1)S(1)}, u32[]{:S(2)}, u32[]{:S(2)}) collective-permute-start(bf16[4,5,16,512]{3,2,1,0:T(8,128)(2,1)S(1)} %slice.21), channel_id=1, source_target_pairs={{0,8},{4,12},{8,0},{12,4},{16,24},{20,28},{24,16},{28,20},{1,9},{5... | collective-permute-start | bytes 983048 | tf_op jit(solution)/shard_map/ppermute | solution.py:613
  48.7 9.6 %collective-permute-start.10 = (bf16[4,5,16,512]{3,2,1,0:T(8,128)(2,1)S(1)}, bf16[4,5,16,512]{3,2,1,0:T(8,128)(2,1)S(1)}, u32[]{:S(2)}, u32[]{:S(2)}) collective-permute-start(bf16[4,5,16,512]{3,2,1,0:T(8,128)(2,1)S(1)} %slice.20), channel_id=1, source_target_pairs={{0,16},{4,20},{8,24},{12,28},{16,0},{20,4},{24,8},{28,12},{1,17},{... | collective-permute-start | bytes 983048 | tf_op jit(solution)/shard_map/ppermute | solution.py:613
  76.4 10.6 %collective-permute-start.28 = (bf16[4,5,16,512]{3,2,1,0:T(8,128)(2,1)S(1)}, bf16[4,5,16,512]{3,2,1,0:T(8,128)(2,1)S(1)}, u32[]{:S(2)}, u32[]{:S(2)}) collective-permute-start(bf16[4,5,16,512]{3,2,1,0:T(8,128)(2,1)S(1)} %get-tuple-element.123), channel_id=1, source_target_pairs={{0,8},{4,12},{8,0},{12,4},{16,24},{20,28},{24,16},{28,20},{1,9},{5... | collective-permute-start | bytes 983048 | tf_op jit(solution)/shard_map/ppermute | solution.py:613
  77.8 14.4 %collective-permute-start.29 = (bf16[4,5,16,512]{3,2,1,0:T(8,128)(2,1)S(1)}, bf16[4,5,16,512]{3,2,1,0:T(8,128)(2,1)S(1)}, u32[]{:S(2)}, u32[]{:S(2)}) collective-permute-start(bf16[4,5,16,512]{3,2,1,0:T(8,128)(2,1)S(1)} %get-tuple-element.124), channel_id=1, source_target_pairs={{0,16},{4,20},{8,24},{12,28},{16,0},{20,4},{24,8},{28,12},{1,17},{... | collective-permute-start | bytes 983048 | tf_op jit(solution)/shard_map/ppermute | solution.py:613
  78.4 14.9 %collective-permute-start.26 = (bf16[4,5,16,512]{3,2,1,0:T(8,128)(2,1)S(1)}, bf16[4,5,16,512]{3,2,1,0:T(8,128)(2,1)S(1)}, u32[]{:S(2)}, u32[]{:S(2)}) collective-permute-start(bf16[4,5,16,512]{3,2,1,0:T(8,128)(2,1)S(1)} %get-tuple-element.121), channel_id=1, source_target_pairs={{0,8},{4,12},{8,0},{12,4},{16,24},{20,28},{24,16},{28,20},{1,9},{5... | collective-permute-start | bytes 983048 | tf_op jit(solution)/shard_map/ppermute | solution.py:613
  79.1 15.5 %collective-permute-start.27 = (bf16[4,5,16,512]{3,2,1,0:T(8,128)(2,1)S(1)}, bf16[4,5,16,512]{3,2,1,0:T(8,128)(2,1)S(1)}, u32[]{:S(2)}, u32[]{:S(2)}) collective-permute-start(bf16[4,5,16,512]{3,2,1,0:T(8,128)(2,1)S(1)} %get-tuple-element.122), channel_id=1, source_target_pairs={{0,16},{4,20},{8,24},{12,28},{16,0},{20,4},{24,8},{28,12},{1,17},{... | collective-permute-start | bytes 983048 | tf_op jit(solution)/shard_map/ppermute | solution.py:613
  80.6 14.6 %collective-permute-start.34 = (bf16[128,512]{1,0:T(8,128)(2,1)S(1)}, bf16[128,512]{1,0:T(8,128)(2,1)S(1)}, u32[]{:S(2)}, u32[]{:S(2)}) collective-permute-start(bf16[128,512]{1,0:T(8,128)(2,1)S(1)} %get-tuple-element.147), channel_id=1, source_target_pairs={{0,2},{2,0},{3,1},{4,6},{6,4},{7,5},{8,10},{10,8},{11,9},{12,14},{... | collective-permute-start | bytes 393224 | tf_op jit(solution)/shard_map/ppermute | solution.py:610
  87.1 10.1 %collective-permute-start.35 = (bf16[128,512]{1,0:T(8,128)(2,1)S(1)}, bf16[128,512]{1,0:T(8,128)(2,1)S(1)}, u32[]{:S(2)}, u32[]{:S(2)}) collective-permute-start(bf16[128,512]{1,0:T(8,128)(2,1)S(1)} %get-tuple-element.148), channel_id=1, source_target_pairs={{0,3},{2,1},{3,0},{4,7},{6,5},{7,4},{8,11},{10,9},{11,8},{12,15},{... | collective-permute-start | bytes 393224 | tf_op jit(solution)/shard_map/ppermute | solution.py:610
  93.3 10.6 %collective-permute-start.31 = (bf16[4,5,16,512]{3,2,1,0:T(8,128)(2,1)S(1)}, bf16[4,5,16,512]{3,2,1,0:T(8,128)(2,1)S(1)}, u32[]{:S(2)}, u32[]{:S(2)}) collective-permute-start(bf16[4,5,16,512]{3,2,1,0:T(8,128)(2,1)S(1)} %get-tuple-element.144), channel_id=1, source_target_pairs={{0,8},{4,12},{8,0},{12,4},{16,24},{20,28},{24,16},{28,20},{1,9},{5... | collective-permute-start | bytes 983048 | tf_op jit(solution)/shard_map/ppermute | solution.py:613
  94.6 10.6 %collective-permute-start.32 = (bf16[4,5,16,512]{3,2,1,0:T(8,128)(2,1)S(1)}, bf16[4,5,16,512]{3,2,1,0:T(8,128)(2,1)S(1)}, u32[]{:S(2)}, u32[]{:S(2)}) collective-permute-start(bf16[4,5,16,512]{3,2,1,0:T(8,128)(2,1)S(1)} %get-tuple-element.145), channel_id=1, source_target_pairs={{0,16},{4,20},{8,24},{12,28},{16,0},{20,4},{24,8},{28,12},{1,17},{... | collective-permute-start | bytes 983048 | tf_op jit(solution)/shard_map/ppermute | solution.py:613
  95.2 14.3 %collective-permute-start.39 = (bf16[4,4,16,512]{3,2,1,0:T(8,128)(2,1)S(1)}, bf16[4,4,16,512]{3,2,1,0:T(8,128)(2,1)S(1)}, u32[]{:S(2)}, u32[]{:S(2)}) collective-permute-start(bf16[4,4,16,512]{3,2,1,0:T(8,128)(2,1)S(1)} %get-tuple-element.159), channel_id=1, source_target_pairs={{0,8},{4,12},{8,0},{12,4},{16,24},{20,28},{24,16},{28,20},{1,9},{5... | collective-permute-start | bytes 786440 | tf_op jit(solution)/shard_map/ppermute | solution.py:613
  97.2 17.3 %collective-permute-start.40 = (bf16[4,4,16,512]{3,2,1,0:T(8,128)(2,1)S(1)}, bf16[4,4,16,512]{3,2,1,0:T(8,128)(2,1)S(1)}, u32[]{:S(2)}, u32[]{:S(2)}) collective-permute-start(bf16[4,4,16,512]{3,2,1,0:T(8,128)(2,1)S(1)} %get-tuple-element.160), channel_id=1, source_target_pairs={{0,16},{4,20},{8,24},{12,28},{16,0},{20,4},{24,8},{28,12},{1,17},{... | collective-permute-start | bytes 786440 | tf_op jit(solution)/shard_map/ppermute | solution.py:613
  100.3 14.1 %collective-permute-start.41 = (bf16[4,4,16,512]{3,2,1,0:T(8,128)(2,1)S(1)}, bf16[4,4,16,512]{3,2,1,0:T(8,128)(2,1)S(1)}, u32[]{:S(2)}, u32[]{:S(2)}) collective-permute-start(bf16[4,4,16,512]{3,2,1,0:T(8,128)(2,1)S(1)} %get-tuple-element.161), channel_id=1, source_target_pairs={{0,24},{4,28},{8,16},{12,20},{16,8},{20,12},{24,0},{28,4},{1,25},{... | collective-permute-start | bytes 786440 | tf_op jit(solution)/shard_map/ppermute | solution.py:613
  105.6 20.8 %collective-permute-start.36 = (bf16[10,16,512]{2,1,0:T(8,128)(2,1)S(1)}, bf16[10,16,512]{2,1,0:T(8,128)(2,1)S(1)}, u32[]{:S(2)}, u32[]{:S(2)}) collective-permute-start(bf16[10,16,512]{2,1,0:T(8,128)(2,1)S(1)} %get-tuple-element.152), channel_id=1, source_target_pairs={{0,1},{1,0},{2,3},{3,2},{4,5},{5,4},{6,7},{7,6},{8,9},{9,8},{10,11... | collective-permute-start | bytes 491528 | tf_op jit(solution)/shard_map/ppermute | solution.py:610
  107.4 18.9 %collective-permute-start.37 = (bf16[10,16,512]{2,1,0:T(8,128)(2,1)S(1)}, bf16[10,16,512]{2,1,0:T(8,128)(2,1)S(1)}, u32[]{:S(2)}, u32[]{:S(2)}) collective-permute-start(bf16[10,16,512]{2,1,0:T(8,128)(2,1)S(1)} %get-tuple-element.153), channel_id=1, source_target_pairs={{0,2},{1,3},{2,0},{3,1},{4,6},{5,7},{6,4},{7,5},{8,10},{9,11},{10,... | collective-permute-start | bytes 491528 | tf_op jit(solution)/shard_map/ppermute | solution.py:610
  109.5 16.8 %collective-permute-start.38 = (bf16[10,16,512]{2,1,0:T(8,128)(2,1)S(1)}, bf16[10,16,512]{2,1,0:T(8,128)(2,1)S(1)}, u32[]{:S(2)}, u32[]{:S(2)}) collective-permute-start(bf16[10,16,512]{2,1,0:T(8,128)(2,1)S(1)} %get-tuple-element.154), channel_id=1, source_target_pairs={{0,3},{1,2},{2,1},{3,0},{4,7},{5,6},{6,5},{7,4},{8,11},{9,10},{10,... | collective-permute-start | bytes 491528 | tf_op jit(solution)/shard_map/ppermute | solution.py:610
  (26 other events, 335.0 us)

commit v7 on v6

--- a/solution.py
+++ b/solution.py
@@ -169,16 +169,6 @@
 
     for item in copies:
         item.wait()
-
-
-def early_pack_body(*refs):
-    sources, early, held, sem = (refs[:4], refs[4], refs[5], refs[6])
-    for i, source in enumerate(sources):
-        pltpu.make_async_copy(source, held.at[i], sem.at[i]).start()
-    for i, source in enumerate(sources):
-        pltpu.make_async_copy(source, held.at[i], sem.at[i]).wait()
-    pltpu.make_async_copy(held, early, sem.at[0]).start()
-    pltpu.make_async_copy(held, early, sem.at[0]).wait()
 
 
 def stack_heads(block, lane):
@@ -666,16 +656,7 @@
     late_layout = split_layout(late_pieces) if direct else plain_layout(late_pieces)
     if direct:
         late = pays[3]
-        shape = (early_pieces, BAND, width)
-        early = call(
-            early_pack_body,
-            [(shape, BF, HBM)],
-            [HBM] * 4,
-            [pltpu.VMEM(shape, BF), pltpu.SemaphoreType.DMA((4,))],
-            (0, MIB),
-            "early_pack",
-            60,
-        )(w_query, w_key, w_value, pos_table.T)[0]
+        early = jnp.stack([w_query, w_key, w_value, pos_table.T])
         early_places = places(early)
         late = after(late, early_places[1], early_places[2])
         late_places = places(late)

time: 128 us -> 127 us (level)
  waiting for transfers between devices: 32.8 us -> 37.5 us
  starting transfers between devices: 65 us -> 61 us
  Pallas kernels: 26.1 us -> 24.6 us
    ppermute x27, waiting for transfers between devices: 10.8 us -> 15 us  [swap_dp(): return lax.ppermute(value, 'dp', [(i, i ^ mask) for i in range(dp_count)])]
    ppermute x27, starting transfers between devices: 21.7 us -> 18.9 us  [swap_dp(): return lax.ppermute(value, 'dp', [(i, i ^ mask) for i in range(dp_count)])]
    pallas_call x1 -> x0, Pallas kernels: 1.47 us -> none  [local(): call(early_pack_body, [(shape, BF, HBM)], [HBM] * 4, [pltpu.VMEM(shape, B...]
  transfers between devices with their start and end apart: 45 -> 45, of which waited for: 20 -> 22; matrix products, arithmetic and copies ran while one was open for 2% -> 1% of each run, Pallas kernels for 12% -> 12%
where the time goes in v7:
time: 127 us
  starting transfers between devices  61 us (48%)
  waiting for transfers between devices  37.5 us (30%)
  Pallas kernels  24.6 us (19%)
  other arithmetic  2.17 us (2%)
  between operations  1.67 us (1%)
    ppermute x18, starting transfers between devices, swap_seq(): return lax.ppermute(value, 'seq', pairs)  42.1 us
    ppermute x18, waiting for transfers between devices, swap_seq(): return lax.ppermute(value, 'seq', pairs)  22.5 us
    ppermute x27, starting transfers between devices, swap_dp(): return lax.ppermute(value, 'dp', [(i, i ^ mask) for i in range(dp_count)])  18.9 us
    ppermute x27, waiting for transfers between devices, swap_dp(): return lax.ppermute(value, 'dp', [(i, i ^ mask) for i in range(dp_count)])  15 us
    pallas_call x1, Pallas kernels, local(): call(functools.partial(middle_body, direct, late_layout), [((keys, width)...  8.15 us
    pallas_call x1, Pallas kernels, local(): call(functools.partial(attend_back_body, direct, early_layout), [((rows,...  5.17 us
    pallas_call x1, Pallas kernels, local(): call(functools.partial(attend_body, direct, early_layout), [((rows, width...  4.72 us
  transfers between devices with their start and end apart: 45, of which 22 were waited for; matrix products, arithmetic and copies ran while one was open for 1% of the time, Pallas kernels for 12%

profile of v7, /device:TPU:0, one launch (start us, length us, event | category | flops | bytes accessed | tf_op | source)
XLA Modules:
  0.0 126.9 jit_solution(14324914863064664461)
XLA Ops:
  1.5 4.1 %collective-permute-start.1 = (bf16[4,16,512]{2,1,0:T(8,128)(2,1)S(1)}, bf16[4,16,512]{2,1,0:T(8,128)(2,1)S(1)}, u32[]{:S(2)}, u32[]{:S(2)}) collective-permute-start(bf16[4,16,512]{2,1,0:T(8,128)(2,1)S(1)} %get-tuple-element.187), channel_id=1, source_target_pairs={{0,2},{1,3},{2,0},{3,1},{4,6},{5,7},{6,4},{7,5},{8,10},{9,11},{10,... | collective-permute-start | bytes 196616 | tf_op jit(solution)/shard_map/ppermute | solution.py:600
  7.2 2.3 %pack.1 = (bf16[256,512]{1,0:T(8,128)(2,1)}, bf16[128,512]{1,0:T(8,128)(2,1)}, bf16[128,512]{1,0:T(8,128)(2,1)}, bf16[10,16,512]{2,1,0:T(8,128)(2,1)}) custom-call(bf16[1,128,512]{2,1,0:T(8,128)(2,1)} %refs_0_.3, bf16[2,64,512]{2,1,0:T(8,128)(2,1)} %refs_1_.3, bf16[1,128,512]{2,1,0:T(8,128)(2,1)} %long_cot.1, bf16[2,64,512]{2,1,0:T(8,128)(2,1)} %short_cot.1, ...), custom_call_target="tpu_custom_call" | custom-call | bytes 4194304 | tf_op jit(solution)/shard_map/pack/pallas_call | solution.py:620
  9.9 4.6 %collective-permute-start.4 = (bf16[10,16,512]{2,1,0:T(8,128)(2,1)}, bf16[10,16,512]{2,1,0:T(8,128)(2,1)S(1)}, u32[]{:S(2)}, u32[]{:S(2)}) collective-permute-start(bf16[10,16,512]{2,1,0:T(8,128)(2,1)} %get-tuple-element.99), channel_id=1, source_target_pairs={{0,3},{1,2},{2,1},{3,0},{4,7},{5,6},{6,5},{7,4},{8,11},{9,10},{10,... | collective-permute-start | bytes 491528 | tf_op jit(solution)/shard_map/ppermute | solution.py:600
  15.1 2.5 %collective-permute-start.8 = (bf16[4,4,16,512]{3,2,1,0:T(8,128)(2,1)S(1)}, bf16[4,4,16,512]{3,2,1,0:T(8,128)(2,1)S(1)}, u32[]{:S(2)}, u32[]{:S(2)}) collective-permute-start(bf16[4,4,16,512]{3,2,1,0:T(8,128)(2,1)S(1)} %pad_maximum_fusion.1.refs_5_.refs_0_), channel_id=1, source_target_pairs={{0,24},{4,28},{8,16},{12,20},{16,8},{20,12},{24,0},{28,4},{1,25},{... | collective-permute-start | bytes 786440 | tf_op jit(solution)/shard_map/ppermute | solution.py:603
  21.3 6.0 %collective-permute-done.3 = bf16[10,16,512]{2,1,0:T(8,128)(2,1)S(1)} collective-permute-done((bf16[10,16,512]{2,1,0:T(8,128)(2,1)}, bf16[10,16,512]{2,1,0:T(8,128)(2,1)S(1)}, u32[]{:S(2)}, u32[]{:S(2)}) %collective-permute-start.3) | collective-permute-done | bytes 163872 | tf_op jit(solution)/shard_map/ppermute | solution.py:600
  31.4 3.7 %collective-permute-start.13 = (bf16[256,512]{1,0:T(8,128)(2,1)}, bf16[256,512]{1,0:T(8,128)(2,1)S(1)}, u32[]{:S(2)}, u32[]{:S(2)}) collective-permute-start(bf16[256,512]{1,0:T(8,128)(2,1)} %get-tuple-element.104), channel_id=1, source_target_pairs={{0,1},{1,0},{2,3},{3,2},{4,5},{5,4},{6,7},{7,6},{8,9},{9,8},{10,11... | collective-permute-start | bytes 786440 | tf_op jit(solution)/shard_map/ppermute | solution.py:600
  35.1 2.7 %collective-permute-start.14 = (bf16[128,512]{1,0:T(8,128)(2,1)}, bf16[128,512]{1,0:T(8,128)(2,1)S(1)}, u32[]{:S(2)}, u32[]{:S(2)}) collective-permute-start(bf16[128,512]{1,0:T(8,128)(2,1)} %get-tuple-element.105), channel_id=1, source_target_pairs={{0,2},{1,3},{2,0},{4,6},{5,7},{6,4},{8,10},{9,11},{10,8},{12,14},{... | collective-permute-start | bytes 393224 | tf_op jit(solution)/shard_map/ppermute | solution.py:600
  37.8 2.6 %collective-permute-start.15 = (bf16[128,512]{1,0:T(8,128)(2,1)}, bf16[128,512]{1,0:T(8,128)(2,1)S(1)}, u32[]{:S(2)}, u32[]{:S(2)}) collective-permute-start(bf16[128,512]{1,0:T(8,128)(2,1)} %get-tuple-element.106), channel_id=1, source_target_pairs={{0,3},{1,2},{3,0},{4,7},{5,6},{7,4},{8,11},{9,10},{11,8},{12,15},{... | collective-permute-start | bytes 393224 | tf_op jit(solution)/shard_map/ppermute | solution.py:600
  40.5 3.6 %collective-permute-done.14.refs_3_.refs_1_ = bf16[128,512]{1,0:T(8,128)(2,1)S(1)} collective-permute-done((bf16[128,512]{1,0:T(8,128)(2,1)}, bf16[128,512]{1,0:T(8,128)(2,1)S(1)}, u32[]{:S(2)}, u32[]{:S(2)}) %collective-permute-start.14) | collective-permute-done | bytes 131104 | tf_op jit(solution)/shard_map/ppermute | solution.py:600
  44.1 2.6 %collective-permute-done.15.refs_4_.refs_2_ = bf16[128,512]{1,0:T(8,128)(2,1)S(1)} collective-permute-done((bf16[128,512]{1,0:T(8,128)(2,1)}, bf16[128,512]{1,0:T(8,128)(2,1)S(1)}, u32[]{:S(2)}, u32[]{:S(2)}) %collective-permute-start.15) | collective-permute-done | bytes 131104 | tf_op jit(solution)/shard_map/ppermute | solution.py:600
  50.2 4.7 %attend.1 = (f32[256,512]{1,0:T(8,128)S(1)}, bf16[512,512]{1,0:T(8,128)(2,1)S(1)}, bf16[256,512]{1,0:T(8,128)(2,1)S(1)}, bf16[256,512]{1,0:T(8,128)(2,1)S(1)}, b...) custom-call(s32[1]{0:T(128)S(6)} %copy.28.long_len, ...), custom_call_target="tpu_custom_call" | custom-call | flops 1073741824 | bytes 10485760 | tf_op jit(solution)/shard_map/attend/pallas_call | solution.py:697
  54.9 2.5 %collective-permute-done.12.refs_7_ = bf16[4,5,16,512]{3,2,1,0:T(8,128)(2,1)S(1)} collective-permute-done((bf16[4,5,16,512]{3,2,1,0:T(8,128)(2,1)S(1)}, bf16[4,5,16,512]{3,2,1,0:T(8,128)(2,1)S(1)}, u32[]{:S(2)}, u32[]{:S(2)}) %collective-permute-start.12) | collective-permute-done | bytes 327712 | tf_op jit(solution)/shard_map/ppermute | solution.py:603
  60.1 8.2 %middle.1 = (bf16[512,512]{1,0:T(8,128)(2,1)S(1)}, f32[256,512]{1,0:T(8,128)S(1)}, bf16[256,512]{1,0:T(8,128)(2,1)S(1)}, bf16[4,10,16,512]{3,2,1,0:T(8,128)(2,1)...) custom-call(f32[256,512]{1,0:T(8,128)S(1)} %get-tuple-element.112.fi, ...), custom_call_target="tpu_custom_call" | custom-call | flops 4294967296 | bytes 20971520 | tf_op jit(solution)/shard_map/middle/pallas_call | solution.py:727
  68.5 5.2 %attend_back.1 = (bf16[256,512]{1,0:T(8,128)(2,1)S(1)}, bf16[512,512]{1,0:T(8,128)(2,1)S(1)}, bf16[512,512]{1,0:T(8,128)(2,1)S(1)}, f32[512,512]{1,0:T(8,128)S(1...) custom-call(bf16[256,512]{1,0:T(8,128)(2,1)S(1)} %get-tuple-element., ...), custom_call_target="tpu_custom_call" | custom-call | flops 2147483648 | bytes 12582912 | tf_op jit(solution)/shard_map/attend_back/pallas_call | solution.py:757
  80.3 4.9 %collective-permute-start.34 = (bf16[128,512]{1,0:T(8,128)(2,1)S(1)}, bf16[128,512]{1,0:T(8,128)(2,1)S(1)}, u32[]{:S(2)}, u32[]{:S(2)}) collective-permute-start(bf16[128,512]{1,0:T(8,128)(2,1)S(1)} %get-tuple-element.147), channel_id=1, source_target_pairs={{0,2},{2,0},{3,1},{4,6},{6,4},{7,5},{8,10},{10,8},{11,9},{12,14},{... | collective-permute-start | bytes 393224 | tf_op jit(solution)/shard_map/ppermute | solution.py:600
  86.8 4.4 %collective-permute-start.35 = (bf16[128,512]{1,0:T(8,128)(2,1)S(1)}, bf16[128,512]{1,0:T(8,128)(2,1)S(1)}, u32[]{:S(2)}, u32[]{:S(2)}) collective-permute-start(bf16[128,512]{1,0:T(8,128)(2,1)S(1)} %get-tuple-element.148), channel_id=1, source_target_pairs={{0,3},{2,1},{3,0},{4,7},{6,5},{7,4},{8,11},{10,9},{11,8},{12,15},{... | collective-permute-start | bytes 393224 | tf_op jit(solution)/shard_map/ppermute | solution.py:600
  97.2 2.9 %collective-permute-done.33.refs_10_ = bf16[256,512]{1,0:T(8,128)(2,1)S(1)} collective-permute-done((bf16[256,512]{1,0:T(8,128)(2,1)S(1)}, bf16[256,512]{1,0:T(8,128)(2,1)S(1)}, u32[]{:S(2)}, u32[]{:S(2)}) %collective-permute-start.33) | collective-permute-done | bytes 262176 | tf_op jit(solution)/shard_map/ppermute | solution.py:600
  101.2 2.5 %collective-permute-done.31.then_x = bf16[4,5,16,512]{3,2,1,0:T(8,128)(2,1)S(1)} collective-permute-done((bf16[4,5,16,512]{3,2,1,0:T(8,128)(2,1)S(1)}, bf16[4,5,16,512]{3,2,1,0:T(8,128)(2,1)S(1)}, u32[]{:S(2)}, u32[]{:S(2)}) %collective-permute-start.31) | collective-permute-done | bytes 327712 | tf_op jit(solution)/shard_map/ppermute | solution.py:603
  106.6 1.9 %collective-permute-start.37 = (bf16[10,16,512]{2,1,0:T(8,128)(2,1)S(1)}, bf16[10,16,512]{2,1,0:T(8,128)(2,1)S(1)}, u32[]{:S(2)}, u32[]{:S(2)}) collective-permute-start(bf16[10,16,512]{2,1,0:T(8,128)(2,1)S(1)} %get-tuple-element.153), channel_id=1, source_target_pairs={{0,2},{1,3},{2,0},{3,1},{4,6},{5,7},{6,4},{7,5},{8,10},{9,11},{10,... | collective-permute-start | bytes 491528 | tf_op jit(solution)/shard_map/ppermute | solution.py:600
  109.3 2.5 %collective-permute-start.38 = (bf16[10,16,512]{2,1,0:T(8,128)(2,1)S(1)}, bf16[10,16,512]{2,1,0:T(8,128)(2,1)S(1)}, u32[]{:S(2)}, u32[]{:S(2)}) collective-permute-start(bf16[10,16,512]{2,1,0:T(8,128)(2,1)S(1)} %get-tuple-element.154), channel_id=1, source_target_pairs={{0,3},{1,2},{2,1},{3,0},{4,7},{5,6},{6,5},{7,4},{8,11},{9,10},{10,... | collective-permute-start | bytes 491528 | tf_op jit(solution)/shard_map/ppermute | solution.py:600
  111.8 2.4 %collective-permute-done.40.refs_3_ = bf16[4,4,16,512]{3,2,1,0:T(8,128)(2,1)S(1)} collective-permute-done((bf16[4,4,16,512]{3,2,1,0:T(8,128)(2,1)S(1)}, bf16[4,4,16,512]{3,2,1,0:T(8,128)(2,1)S(1)}, u32[]{:S(2)}, u32[]{:S(2)}) %collective-permute-start.40) | collective-permute-done | bytes 262176 | tf_op jit(solution)/shard_map/ppermute | solution.py:603
  115.6 1.9 %collective-permute-start.43 = (bf16[4,16,512]{2,1,0:T(8,128)(2,1)S(1)}, bf16[4,16,512]{2,1,0:T(8,128)(2,1)S(1)}, u32[]{:S(2)}, u32[]{:S(2)}) collective-permute-start(bf16[4,16,512]{2,1,0:T(8,128)(2,1)S(1)} %get-tuple-element.164), channel_id=1, source_target_pairs={{0,2},{1,3},{2,0},{3,1},{4,6},{5,7},{6,4},{7,5},{8,10},{9,11},{10,... | collective-permute-start | bytes 196616 | tf_op jit(solution)/shard_map/ppermute | solution.py:600
  119.0 3.9 %collective-permute-start.44 = (bf16[4,16,512]{2,1,0:T(8,128)(2,1)S(1)}, bf16[4,16,512]{2,1,0:T(8,128)(2,1)S(1)}, u32[]{:S(2)}, u32[]{:S(2)}) collective-permute-start(bf16[4,16,512]{2,1,0:T(8,128)(2,1)S(1)} %get-tuple-element.165), channel_id=1, source_target_pairs={{0,3},{1,2},{2,1},{3,0},{4,7},{5,6},{6,5},{7,4},{8,11},{9,10},{10,... | collective-permute-start | bytes 196616 | tf_op jit(solution)/shard_map/ppermute | solution.py:600
  122.9 2.6 %collective-permute-done.43.refs_6_ = bf16[4,16,512]{2,1,0:T(8,128)(2,1)S(1)} collective-permute-done((bf16[4,16,512]{2,1,0:T(8,128)(2,1)S(1)}, bf16[4,16,512]{2,1,0:T(8,128)(2,1)S(1)}, u32[]{:S(2)}, u32[]{:S(2)}) %collective-permute-start.43) | collective-permute-done | bytes 65568 | tf_op jit(solution)/shard_map/ppermute | solution.py:600
  (92 shorter events, 39.9 us)
Async XLA Ops:
  9.9 10.0 %collective-permute-start.4 = (bf16[10,16,512]{2,1,0:T(8,128)(2,1)}, bf16[10,16,512]{2,1,0:T(8,128)(2,1)S(1)}, u32[]{:S(2)}, u32[]{:S(2)}) collective-permute-start(bf16[10,16,512]{2,1,0:T(8,128)(2,1)} %get-tuple-element.99), channel_id=1, source_target_pairs={{0,3},{1,2},{2,1},{3,0},{4,7},{5,6},{6,5},{7,4},{8,11},{9,10},{10,... | collective-permute-start | bytes 491528 | tf_op jit(solution)/shard_map/ppermute | solution.py:600
  14.5 12.8 %collective-permute-start.3 = (bf16[10,16,512]{2,1,0:T(8,128)(2,1)}, bf16[10,16,512]{2,1,0:T(8,128)(2,1)S(1)}, u32[]{:S(2)}, u32[]{:S(2)}) collective-permute-start(bf16[10,16,512]{2,1,0:T(8,128)(2,1)} %get-tuple-element.99), channel_id=1, source_target_pairs={{0,2},{1,3},{2,0},{3,1},{4,6},{5,7},{6,4},{7,5},{8,10},{9,11},{10,... | collective-permute-start | bytes 491528 | tf_op jit(solution)/shard_map/ppermute | solution.py:600
  14.5 12.8 %collective-permute-start.2 = (bf16[10,16,512]{2,1,0:T(8,128)(2,1)}, bf16[10,16,512]{2,1,0:T(8,128)(2,1)S(1)}, u32[]{:S(2)}, u32[]{:S(2)}) collective-permute-start(bf16[10,16,512]{2,1,0:T(8,128)(2,1)} %get-tuple-element.99), channel_id=1, source_target_pairs={{0,1},{1,0},{2,3},{3,2},{4,5},{5,4},{6,7},{7,6},{8,9},{9,8},{10,11... | collective-permute-start | bytes 491528 | tf_op jit(solution)/shard_map/ppermute | solution.py:600
  15.1 13.2 %collective-permute-start.8 = (bf16[4,4,16,512]{3,2,1,0:T(8,128)(2,1)S(1)}, bf16[4,4,16,512]{3,2,1,0:T(8,128)(2,1)S(1)}, u32[]{:S(2)}, u32[]{:S(2)}) collective-permute-start(bf16[4,4,16,512]{3,2,1,0:T(8,128)(2,1)S(1)} %pad_maximum_fusion.1.refs_5_.refs_0_), channel_id=1, source_target_pairs={{0,24},{4,28},{8,16},{12,20},{16,8},{20,12},{24,0},{28,4},{1,25},{... | collective-permute-start | bytes 786440 | tf_op jit(solution)/shard_map/ppermute | solution.py:603
  17.6 10.7 %collective-permute-start.7 = (bf16[4,4,16,512]{3,2,1,0:T(8,128)(2,1)S(1)}, bf16[4,4,16,512]{3,2,1,0:T(8,128)(2,1)S(1)}, u32[]{:S(2)}, u32[]{:S(2)}) collective-permute-start(bf16[4,4,16,512]{3,2,1,0:T(8,128)(2,1)S(1)} %pad_maximum_fusion.1.refs_5_.refs_0_), channel_id=1, source_target_pairs={{0,16},{4,20},{8,24},{12,28},{16,0},{20,4},{24,8},{28,12},{1,17},{... | collective-permute-start | bytes 786440 | tf_op jit(solution)/shard_map/ppermute | solution.py:603
  28.3 18.9 %collective-permute-start.11 = (bf16[4,10,16,512]{3,2,1,0:T(8,128)(2,1)S(1)}, bf16[4,10,16,512]{3,2,1,0:T(8,128)(2,1)S(1)}, u32[]{:S(2)}, u32[]{:S(2)}) collective-permute-start(bf16[4,10,16,512]{3,2,1,0:T(8,128)(2,1)S(1)} %pad_maximum_fusion.refs_3_), channel_id=1, source_target_pairs={{0,16},{4,20},{8,24},{12,28},{16,0},{20,4},{24,8},{28,12},{1,17},{... | collective-permute-start | bytes 1966088 | tf_op jit(solution)/shard_map/ppermute | solution.py:603
  29.9 17.8 %collective-permute-start.9 = (bf16[4,10,16,512]{3,2,1,0:T(8,128)(2,1)S(1)}, bf16[4,10,16,512]{3,2,1,0:T(8,128)(2,1)S(1)}, u32[]{:S(2)}, u32[]{:S(2)}) collective-permute-start(bf16[4,10,16,512]{3,2,1,0:T(8,128)(2,1)S(1)} %pad_maximum_fusion.refs_3_), channel_id=1, source_target_pairs={{0,8},{4,12},{8,0},{12,4},{16,24},{20,28},{24,16},{28,20},{1,9},{5... | collective-permute-start | bytes 1966088 | tf_op jit(solution)/shard_map/ppermute | solution.py:603
  31.4 15.3 %collective-permute-start.13 = (bf16[256,512]{1,0:T(8,128)(2,1)}, bf16[256,512]{1,0:T(8,128)(2,1)S(1)}, u32[]{:S(2)}, u32[]{:S(2)}) collective-permute-start(bf16[256,512]{1,0:T(8,128)(2,1)} %get-tuple-element.104), channel_id=1, source_target_pairs={{0,1},{1,0},{2,3},{3,2},{4,5},{5,4},{6,7},{7,6},{8,9},{9,8},{10,11... | collective-permute-start | bytes 786440 | tf_op jit(solution)/shard_map/ppermute | solution.py:600
  48.6 9.9 %collective-permute-start.20 = (bf16[4,10,16,512]{3,2,1,0:T(8,128)(2,1)S(1)}, bf16[4,10,16,512]{3,2,1,0:T(8,128)(2,1)S(1)}, u32[]{:S(2)}, u32[]{:S(2)}) collective-permute-start(bf16[4,10,16,512]{3,2,1,0:T(8,128)(2,1)S(1)} %pad_maximum_fusion.refs_3_), channel_id=1, source_target_pairs={{0,4},{4,0},{8,12},{12,8},{16,20},{20,16},{24,28},{28,24},{1,5},{5... | collective-permute-start | bytes 1966088 | tf_op jit(solution)/shard_map/ppermute | solution.py:603
  76.2 10.6 %collective-permute-start.28 = (bf16[4,5,16,512]{3,2,1,0:T(8,128)(2,1)S(1)}, bf16[4,5,16,512]{3,2,1,0:T(8,128)(2,1)S(1)}, u32[]{:S(2)}, u32[]{:S(2)}) collective-permute-start(bf16[4,5,16,512]{3,2,1,0:T(8,128)(2,1)S(1)} %get-tuple-element.123), channel_id=1, source_target_pairs={{0,8},{4,12},{8,0},{12,4},{16,24},{20,28},{24,16},{28,20},{1,9},{5... | collective-permute-start | bytes 983048 | tf_op jit(solution)/shard_map/ppermute | solution.py:603
  77.6 13.7 %collective-permute-start.29 = (bf16[4,5,16,512]{3,2,1,0:T(8,128)(2,1)S(1)}, bf16[4,5,16,512]{3,2,1,0:T(8,128)(2,1)S(1)}, u32[]{:S(2)}, u32[]{:S(2)}) collective-permute-start(bf16[4,5,16,512]{3,2,1,0:T(8,128)(2,1)S(1)} %get-tuple-element.124), channel_id=1, source_target_pairs={{0,16},{4,20},{8,24},{12,28},{16,0},{20,4},{24,8},{28,12},{1,17},{... | collective-permute-start | bytes 983048 | tf_op jit(solution)/shard_map/ppermute | solution.py:603
  77.9 15.2 %collective-permute-start.26 = (bf16[4,5,16,512]{3,2,1,0:T(8,128)(2,1)S(1)}, bf16[4,5,16,512]{3,2,1,0:T(8,128)(2,1)S(1)}, u32[]{:S(2)}, u32[]{:S(2)}) collective-permute-start(bf16[4,5,16,512]{3,2,1,0:T(8,128)(2,1)S(1)} %get-tuple-element.121), channel_id=1, source_target_pairs={{0,8},{4,12},{8,0},{12,4},{16,24},{20,28},{24,16},{28,20},{1,9},{5... | collective-permute-start | bytes 983048 | tf_op jit(solution)/shard_map/ppermute | solution.py:603
  78.6 15.8 %collective-permute-start.27 = (bf16[4,5,16,512]{3,2,1,0:T(8,128)(2,1)S(1)}, bf16[4,5,16,512]{3,2,1,0:T(8,128)(2,1)S(1)}, u32[]{:S(2)}, u32[]{:S(2)}) collective-permute-start(bf16[4,5,16,512]{3,2,1,0:T(8,128)(2,1)S(1)} %get-tuple-element.122), channel_id=1, source_target_pairs={{0,16},{4,20},{8,24},{12,28},{16,0},{20,4},{24,8},{28,12},{1,17},{... | collective-permute-start | bytes 983048 | tf_op jit(solution)/shard_map/ppermute | solution.py:603
  80.3 14.3 %collective-permute-start.34 = (bf16[128,512]{1,0:T(8,128)(2,1)S(1)}, bf16[128,512]{1,0:T(8,128)(2,1)S(1)}, u32[]{:S(2)}, u32[]{:S(2)}) collective-permute-start(bf16[128,512]{1,0:T(8,128)(2,1)S(1)} %get-tuple-element.147), channel_id=1, source_target_pairs={{0,2},{2,0},{3,1},{4,6},{6,4},{7,5},{8,10},{10,8},{11,9},{12,14},{... | collective-permute-start | bytes 393224 | tf_op jit(solution)/shard_map/ppermute | solution.py:600
  86.8 10.1 %collective-permute-start.35 = (bf16[128,512]{1,0:T(8,128)(2,1)S(1)}, bf16[128,512]{1,0:T(8,128)(2,1)S(1)}, u32[]{:S(2)}, u32[]{:S(2)}) collective-permute-start(bf16[128,512]{1,0:T(8,128)(2,1)S(1)} %get-tuple-element.148), channel_id=1, source_target_pairs={{0,3},{2,1},{3,0},{4,7},{6,5},{7,4},{8,11},{10,9},{11,8},{12,15},{... | collective-permute-start | bytes 393224 | tf_op jit(solution)/shard_map/ppermute | solution.py:600
  93.0 10.6 %collective-permute-start.31 = (bf16[4,5,16,512]{3,2,1,0:T(8,128)(2,1)S(1)}, bf16[4,5,16,512]{3,2,1,0:T(8,128)(2,1)S(1)}, u32[]{:S(2)}, u32[]{:S(2)}) collective-permute-start(bf16[4,5,16,512]{3,2,1,0:T(8,128)(2,1)S(1)} %get-tuple-element.144), channel_id=1, source_target_pairs={{0,8},{4,12},{8,0},{12,4},{16,24},{20,28},{24,16},{28,20},{1,9},{5... | collective-permute-start | bytes 983048 | tf_op jit(solution)/shard_map/ppermute | solution.py:603
  94.3 10.6 %collective-permute-start.32 = (bf16[4,5,16,512]{3,2,1,0:T(8,128)(2,1)S(1)}, bf16[4,5,16,512]{3,2,1,0:T(8,128)(2,1)S(1)}, u32[]{:S(2)}, u32[]{:S(2)}) collective-permute-start(bf16[4,5,16,512]{3,2,1,0:T(8,128)(2,1)S(1)} %get-tuple-element.145), channel_id=1, source_target_pairs={{0,16},{4,20},{8,24},{12,28},{16,0},{20,4},{24,8},{28,12},{1,17},{... | collective-permute-start | bytes 983048 | tf_op jit(solution)/shard_map/ppermute | solution.py:603
  94.6 14.6 %collective-permute-start.39 = (bf16[4,4,16,512]{3,2,1,0:T(8,128)(2,1)S(1)}, bf16[4,4,16,512]{3,2,1,0:T(8,128)(2,1)S(1)}, u32[]{:S(2)}, u32[]{:S(2)}) collective-permute-start(bf16[4,4,16,512]{3,2,1,0:T(8,128)(2,1)S(1)} %get-tuple-element.159), channel_id=1, source_target_pairs={{0,8},{4,12},{8,0},{12,4},{16,24},{20,28},{24,16},{28,20},{1,9},{5... | collective-permute-start | bytes 786440 | tf_op jit(solution)/shard_map/ppermute | solution.py:603
  96.9 17.3 %collective-permute-start.40 = (bf16[4,4,16,512]{3,2,1,0:T(8,128)(2,1)S(1)}, bf16[4,4,16,512]{3,2,1,0:T(8,128)(2,1)S(1)}, u32[]{:S(2)}, u32[]{:S(2)}) collective-permute-start(bf16[4,4,16,512]{3,2,1,0:T(8,128)(2,1)S(1)} %get-tuple-element.160), channel_id=1, source_target_pairs={{0,16},{4,20},{8,24},{12,28},{16,0},{20,4},{24,8},{28,12},{1,17},{... | collective-permute-start | bytes 786440 | tf_op jit(solution)/shard_map/ppermute | solution.py:603
  100.1 14.1 %collective-permute-start.41 = (bf16[4,4,16,512]{3,2,1,0:T(8,128)(2,1)S(1)}, bf16[4,4,16,512]{3,2,1,0:T(8,128)(2,1)S(1)}, u32[]{:S(2)}, u32[]{:S(2)}) collective-permute-start(bf16[4,4,16,512]{3,2,1,0:T(8,128)(2,1)S(1)} %get-tuple-element.161), channel_id=1, source_target_pairs={{0,24},{4,28},{8,16},{12,20},{16,8},{20,12},{24,0},{28,4},{1,25},{... | collective-permute-start | bytes 786440 | tf_op jit(solution)/shard_map/ppermute | solution.py:603
  105.3 20.2 %collective-permute-start.36 = (bf16[10,16,512]{2,1,0:T(8,128)(2,1)S(1)}, bf16[10,16,512]{2,1,0:T(8,128)(2,1)S(1)}, u32[]{:S(2)}, u32[]{:S(2)}) collective-permute-start(bf16[10,16,512]{2,1,0:T(8,128)(2,1)S(1)} %get-tuple-element.152), channel_id=1, source_target_pairs={{0,1},{1,0},{2,3},{3,2},{4,5},{5,4},{6,7},{7,6},{8,9},{9,8},{10,11... | collective-permute-start | bytes 491528 | tf_op jit(solution)/shard_map/ppermute | solution.py:600
  106.6 18.9 %collective-permute-start.37 = (bf16[10,16,512]{2,1,0:T(8,128)(2,1)S(1)}, bf16[10,16,512]{2,1,0:T(8,128)(2,1)S(1)}, u32[]{:S(2)}, u32[]{:S(2)}) collective-permute-start(bf16[10,16,512]{2,1,0:T(8,128)(2,1)S(1)} %get-tuple-element.153), channel_id=1, source_target_pairs={{0,2},{1,3},{2,0},{3,1},{4,6},{5,7},{6,4},{7,5},{8,10},{9,11},{10,... | collective-permute-start | bytes 491528 | tf_op jit(solution)/shard_map/ppermute | solution.py:600
  109.3 16.2 %collective-permute-start.38 = (bf16[10,16,512]{2,1,0:T(8,128)(2,1)S(1)}, bf16[10,16,512]{2,1,0:T(8,128)(2,1)S(1)}, u32[]{:S(2)}, u32[]{:S(2)}) collective-permute-start(bf16[10,16,512]{2,1,0:T(8,128)(2,1)S(1)} %get-tuple-element.154), channel_id=1, source_target_pairs={{0,3},{1,2},{2,1},{3,0},{4,7},{5,6},{6,5},{7,4},{8,11},{9,10},{10,... | collective-permute-start | bytes 491528 | tf_op jit(solution)/shard_map/ppermute | solution.py:600
  115.6 9.8 %collective-permute-start.43 = (bf16[4,16,512]{2,1,0:T(8,128)(2,1)S(1)}, bf16[4,16,512]{2,1,0:T(8,128)(2,1)S(1)}, u32[]{:S(2)}, u32[]{:S(2)}) collective-permute-start(bf16[4,16,512]{2,1,0:T(8,128)(2,1)S(1)} %get-tuple-element.164), channel_id=1, source_target_pairs={{0,2},{1,3},{2,0},{3,1},{4,6},{5,7},{6,4},{7,5},{8,10},{9,11},{10,... | collective-permute-start | bytes 196616 | tf_op jit(solution)/shard_map/ppermute | solution.py:600
  (26 other events, 334.0 us)

commit v8 on v7

--- a/solution.py
+++ b/solution.py
@@ -658,7 +658,6 @@
         late = pays[3]
         early = jnp.stack([w_query, w_key, w_value, pos_table.T])
         early_places = places(early)
-        late = after(late, early_places[1], early_places[2])
         late_places = places(late)
         early_near = spread(jnp.stack(early_places))
         column = jnp.stack(late_places)

time: 127 us -> 127 us (level)
  waiting for transfers between devices: 37.5 us -> 36.1 us
    ppermute x27, starting transfers between devices: 18.9 us -> 20.3 us  [swap_dp(): return lax.ppermute(value, 'dp', [(i, i ^ mask) for i in range(dp_count)])]
  transfers between devices with their start and end apart: 45 -> 45, of which waited for: 22 -> 18; matrix products, arithmetic and copies ran while one was open for 1% -> 1% of each run, Pallas kernels for 12% -> 12%
where the time goes in v8:
time: 127 us; the launch traced here: 126 us
  starting transfers between devices  61.7 us (49%)
  waiting for transfers between devices  36.1 us (28%)
  Pallas kernels  24.6 us (19%)
  other arithmetic  2.17 us (2%)
  between operations  1.66 us (1%)
    ppermute x18, starting transfers between devices, swap_seq(): return lax.ppermute(value, 'seq', pairs)  41.4 us
    ppermute x18, waiting for transfers between devices, swap_seq(): return lax.ppermute(value, 'seq', pairs)  22.1 us
    ppermute x27, starting transfers between devices, swap_dp(): return lax.ppermute(value, 'dp', [(i, i ^ mask) for i in range(dp_count)])  20.3 us
    ppermute x27, waiting for transfers between devices, swap_dp(): return lax.ppermute(value, 'dp', [(i, i ^ mask) for i in range(dp_count)])  13.9 us
    pallas_call x1, Pallas kernels, local(): call(functools.partial(middle_body, direct, late_layout), [((keys, width)...  8.15 us
    pallas_call x1, Pallas kernels, local(): call(functools.partial(attend_back_body, direct, early_layout), [((rows,...  5.17 us
    pallas_call x1, Pallas kernels, local(): call(functools.partial(attend_body, direct, early_layout), [((rows, width...  4.72 us
  transfers between devices with their start and end apart: 45, of which 18 were waited for; matrix products, arithmetic and copies ran while one was open for 1% of the time, Pallas kernels for 12%

profile of v8, /device:TPU:0, one launch (start us, length us, event | category | flops | bytes accessed | tf_op | source)
XLA Modules:
  0.0 126.2 jit_solution(2185877225920496350)
XLA Ops:
  1.5 4.1 %collective-permute-start.4 = (bf16[4,16,512]{2,1,0:T(8,128)(2,1)S(1)}, bf16[4,16,512]{2,1,0:T(8,128)(2,1)S(1)}, u32[]{:S(2)}, u32[]{:S(2)}) collective-permute-start(bf16[4,16,512]{2,1,0:T(8,128)(2,1)S(1)} %get-tuple-element.185), channel_id=1, source_target_pairs={{0,2},{1,3},{2,0},{3,1},{4,6},{5,7},{6,4},{7,5},{8,10},{9,11},{10,... | collective-permute-start | bytes 196616 | tf_op jit(solution)/shard_map/ppermute | solution.py:600
  7.2 2.3 %pack.1 = (bf16[256,512]{1,0:T(8,128)(2,1)}, bf16[128,512]{1,0:T(8,128)(2,1)}, bf16[128,512]{1,0:T(8,128)(2,1)}, bf16[10,16,512]{2,1,0:T(8,128)(2,1)}) custom-call(bf16[1,128,512]{2,1,0:T(8,128)(2,1)} %refs_0_.3, bf16[2,64,512]{2,1,0:T(8,128)(2,1)} %refs_1_.3, bf16[1,128,512]{2,1,0:T(8,128)(2,1)} %long_cot.1, bf16[2,64,512]{2,1,0:T(8,128)(2,1)} %short_cot.1, ...), custom_call_target="tpu_custom_call" | custom-call | bytes 4194304 | tf_op jit(solution)/shard_map/pack/pallas_call | solution.py:620
  9.5 3.8 %collective-permute-start.2 = (bf16[10,16,512]{2,1,0:T(8,128)(2,1)}, bf16[10,16,512]{2,1,0:T(8,128)(2,1)S(1)}, u32[]{:S(2)}, u32[]{:S(2)}) collective-permute-start(bf16[10,16,512]{2,1,0:T(8,128)(2,1)} %get-tuple-element.97), channel_id=1, source_target_pairs={{0,3},{1,2},{2,1},{3,0},{4,7},{5,6},{6,5},{7,4},{8,11},{9,10},{10,... | collective-permute-start | bytes 491528 | tf_op jit(solution)/shard_map/ppermute | solution.py:600
  14.1 2.7 %collective-permute-start.8 = (bf16[4,4,16,512]{3,2,1,0:T(8,128)(2,1)S(1)}, bf16[4,4,16,512]{3,2,1,0:T(8,128)(2,1)S(1)}, u32[]{:S(2)}, u32[]{:S(2)}) collective-permute-start(bf16[4,4,16,512]{3,2,1,0:T(8,128)(2,1)S(1)} %pad_maximum_fusion.1.refs_5_.refs_0_), channel_id=1, source_target_pairs={{0,24},{4,28},{8,16},{12,20},{16,8},{20,12},{24,0},{28,4},{1,25},{... | collective-permute-start | bytes 786440 | tf_op jit(solution)/shard_map/ppermute | solution.py:603
  20.5 6.3 %collective-permute-done.1 = bf16[10,16,512]{2,1,0:T(8,128)(2,1)S(1)} collective-permute-done((bf16[10,16,512]{2,1,0:T(8,128)(2,1)}, bf16[10,16,512]{2,1,0:T(8,128)(2,1)S(1)}, u32[]{:S(2)}, u32[]{:S(2)}) %collective-permute-start.1) | collective-permute-done | bytes 163872 | tf_op jit(solution)/shard_map/ppermute | solution.py:600
  30.9 3.5 %collective-permute-start.13 = (bf16[256,512]{1,0:T(8,128)(2,1)}, bf16[256,512]{1,0:T(8,128)(2,1)S(1)}, u32[]{:S(2)}, u32[]{:S(2)}) collective-permute-start(bf16[256,512]{1,0:T(8,128)(2,1)} %get-tuple-element.102), channel_id=1, source_target_pairs={{0,1},{1,0},{2,3},{3,2},{4,5},{5,4},{6,7},{7,6},{8,9},{9,8},{10,11... | collective-permute-start | bytes 786440 | tf_op jit(solution)/shard_map/ppermute | solution.py:600
  34.4 2.8 %collective-permute-start.14 = (bf16[128,512]{1,0:T(8,128)(2,1)}, bf16[128,512]{1,0:T(8,128)(2,1)S(1)}, u32[]{:S(2)}, u32[]{:S(2)}) collective-permute-start(bf16[128,512]{1,0:T(8,128)(2,1)} %get-tuple-element.103), channel_id=1, source_target_pairs={{0,2},{1,3},{2,0},{4,6},{5,7},{6,4},{8,10},{9,11},{10,8},{12,14},{... | collective-permute-start | bytes 393224 | tf_op jit(solution)/shard_map/ppermute | solution.py:600
  37.2 2.6 %collective-permute-start.15 = (bf16[128,512]{1,0:T(8,128)(2,1)}, bf16[128,512]{1,0:T(8,128)(2,1)S(1)}, u32[]{:S(2)}, u32[]{:S(2)}) collective-permute-start(bf16[128,512]{1,0:T(8,128)(2,1)} %get-tuple-element.104), channel_id=1, source_target_pairs={{0,3},{1,2},{3,0},{4,7},{5,6},{7,4},{8,11},{9,10},{11,8},{12,15},{... | collective-permute-start | bytes 393224 | tf_op jit(solution)/shard_map/ppermute | solution.py:600
  39.9 3.9 %collective-permute-done.14.refs_3_.refs_1_ = bf16[128,512]{1,0:T(8,128)(2,1)S(1)} collective-permute-done((bf16[128,512]{1,0:T(8,128)(2,1)}, bf16[128,512]{1,0:T(8,128)(2,1)S(1)}, u32[]{:S(2)}, u32[]{:S(2)}) %collective-permute-start.14) | collective-permute-done | bytes 131104 | tf_op jit(solution)/shard_map/ppermute | solution.py:600
  43.7 2.4 %collective-permute-done.15.refs_4_.refs_2_ = bf16[128,512]{1,0:T(8,128)(2,1)S(1)} collective-permute-done((bf16[128,512]{1,0:T(8,128)(2,1)}, bf16[128,512]{1,0:T(8,128)(2,1)S(1)}, u32[]{:S(2)}, u32[]{:S(2)}) %collective-permute-start.15) | collective-permute-done | bytes 131104 | tf_op jit(solution)/shard_map/ppermute | solution.py:600
  49.6 4.7 %attend.1 = (f32[256,512]{1,0:T(8,128)S(1)}, bf16[512,512]{1,0:T(8,128)(2,1)S(1)}, bf16[256,512]{1,0:T(8,128)(2,1)S(1)}, bf16[256,512]{1,0:T(8,128)(2,1)S(1)}, b...) custom-call(s32[1]{0:T(128)S(6)} %copy.28.long_len, ...), custom_call_target="tpu_custom_call" | custom-call | flops 1073741824 | bytes 10485760 | tf_op jit(solution)/shard_map/attend/pallas_call | solution.py:696
  54.4 2.5 %collective-permute-done.12.refs_7_ = bf16[4,5,16,512]{3,2,1,0:T(8,128)(2,1)S(1)} collective-permute-done((bf16[4,5,16,512]{3,2,1,0:T(8,128)(2,1)S(1)}, bf16[4,5,16,512]{3,2,1,0:T(8,128)(2,1)S(1)}, u32[]{:S(2)}, u32[]{:S(2)}) %collective-permute-start.12) | collective-permute-done | bytes 327712 | tf_op jit(solution)/shard_map/ppermute | solution.py:603
  59.5 8.2 %middle.1 = (bf16[512,512]{1,0:T(8,128)(2,1)S(1)}, f32[256,512]{1,0:T(8,128)S(1)}, bf16[256,512]{1,0:T(8,128)(2,1)S(1)}, bf16[4,10,16,512]{3,2,1,0:T(8,128)(2,1)...) custom-call(f32[256,512]{1,0:T(8,128)S(1)} %get-tuple-element.110.fi, ...), custom_call_target="tpu_custom_call" | custom-call | flops 4294967296 | bytes 20971520 | tf_op jit(solution)/shard_map/middle/pallas_call | solution.py:726
  67.9 5.2 %attend_back.1 = (bf16[256,512]{1,0:T(8,128)(2,1)S(1)}, bf16[512,512]{1,0:T(8,128)(2,1)S(1)}, bf16[512,512]{1,0:T(8,128)(2,1)S(1)}, f32[512,512]{1,0:T(8,128)S(1...) custom-call(bf16[256,512]{1,0:T(8,128)(2,1)S(1)} %get-tuple-element., ...), custom_call_target="tpu_custom_call" | custom-call | flops 2147483648 | bytes 12582912 | tf_op jit(solution)/shard_map/attend_back/pallas_call | solution.py:756
  79.7 5.0 %collective-permute-start.34 = (bf16[128,512]{1,0:T(8,128)(2,1)S(1)}, bf16[128,512]{1,0:T(8,128)(2,1)S(1)}, u32[]{:S(2)}, u32[]{:S(2)}) collective-permute-start(bf16[128,512]{1,0:T(8,128)(2,1)S(1)} %get-tuple-element.145), channel_id=1, source_target_pairs={{0,2},{2,0},{3,1},{4,6},{6,4},{7,5},{8,10},{10,8},{11,9},{12,14},{... | collective-permute-start | bytes 393224 | tf_op jit(solution)/shard_map/ppermute | solution.py:600
  86.2 4.6 %collective-permute-start.35 = (bf16[128,512]{1,0:T(8,128)(2,1)S(1)}, bf16[128,512]{1,0:T(8,128)(2,1)S(1)}, u32[]{:S(2)}, u32[]{:S(2)}) collective-permute-start(bf16[128,512]{1,0:T(8,128)(2,1)S(1)} %get-tuple-element.146), channel_id=1, source_target_pairs={{0,3},{2,1},{3,0},{4,7},{6,5},{7,4},{8,11},{10,9},{11,8},{12,15},{... | collective-permute-start | bytes 393224 | tf_op jit(solution)/shard_map/ppermute | solution.py:600
  96.9 2.6 %collective-permute-done.33.refs_10_ = bf16[256,512]{1,0:T(8,128)(2,1)S(1)} collective-permute-done((bf16[256,512]{1,0:T(8,128)(2,1)S(1)}, bf16[256,512]{1,0:T(8,128)(2,1)S(1)}, u32[]{:S(2)}, u32[]{:S(2)}) %collective-permute-start.33) | collective-permute-done | bytes 262176 | tf_op jit(solution)/shard_map/ppermute | solution.py:600
  100.7 2.3 %collective-permute-done.31.then_x = bf16[4,5,16,512]{3,2,1,0:T(8,128)(2,1)S(1)} collective-permute-done((bf16[4,5,16,512]{3,2,1,0:T(8,128)(2,1)S(1)}, bf16[4,5,16,512]{3,2,1,0:T(8,128)(2,1)S(1)}, u32[]{:S(2)}, u32[]{:S(2)}) %collective-permute-start.31) | collective-permute-done | bytes 327712 | tf_op jit(solution)/shard_map/ppermute | solution.py:603
  105.7 1.9 %collective-permute-start.37 = (bf16[10,16,512]{2,1,0:T(8,128)(2,1)S(1)}, bf16[10,16,512]{2,1,0:T(8,128)(2,1)S(1)}, u32[]{:S(2)}, u32[]{:S(2)}) collective-permute-start(bf16[10,16,512]{2,1,0:T(8,128)(2,1)S(1)} %get-tuple-element.151), channel_id=1, source_target_pairs={{0,2},{1,3},{2,0},{3,1},{4,6},{5,7},{6,4},{7,5},{8,10},{9,11},{10,... | collective-permute-start | bytes 491528 | tf_op jit(solution)/shard_map/ppermute | solution.py:600
  108.7 2.7 %collective-permute-start.38 = (bf16[10,16,512]{2,1,0:T(8,128)(2,1)S(1)}, bf16[10,16,512]{2,1,0:T(8,128)(2,1)S(1)}, u32[]{:S(2)}, u32[]{:S(2)}) collective-permute-start(bf16[10,16,512]{2,1,0:T(8,128)(2,1)S(1)} %get-tuple-element.152), channel_id=1, source_target_pairs={{0,3},{1,2},{2,1},{3,0},{4,7},{5,6},{6,5},{7,4},{8,11},{9,10},{10,... | collective-permute-start | bytes 491528 | tf_op jit(solution)/shard_map/ppermute | solution.py:600
  111.4 2.2 %collective-permute-done.40.refs_3_ = bf16[4,4,16,512]{3,2,1,0:T(8,128)(2,1)S(1)} collective-permute-done((bf16[4,4,16,512]{3,2,1,0:T(8,128)(2,1)S(1)}, bf16[4,4,16,512]{3,2,1,0:T(8,128)(2,1)S(1)}, u32[]{:S(2)}, u32[]{:S(2)}) %collective-permute-start.40) | collective-permute-done | bytes 262176 | tf_op jit(solution)/shard_map/ppermute | solution.py:603
  114.8 1.9 %collective-permute-start.43 = (bf16[4,16,512]{2,1,0:T(8,128)(2,1)S(1)}, bf16[4,16,512]{2,1,0:T(8,128)(2,1)S(1)}, u32[]{:S(2)}, u32[]{:S(2)}) collective-permute-start(bf16[4,16,512]{2,1,0:T(8,128)(2,1)S(1)} %get-tuple-element.162), channel_id=1, source_target_pairs={{0,2},{1,3},{2,0},{3,1},{4,6},{5,7},{6,4},{7,5},{8,10},{9,11},{10,... | collective-permute-start | bytes 196616 | tf_op jit(solution)/shard_map/ppermute | solution.py:600
  118.2 4.1 %collective-permute-start.44 = (bf16[4,16,512]{2,1,0:T(8,128)(2,1)S(1)}, bf16[4,16,512]{2,1,0:T(8,128)(2,1)S(1)}, u32[]{:S(2)}, u32[]{:S(2)}) collective-permute-start(bf16[4,16,512]{2,1,0:T(8,128)(2,1)S(1)} %get-tuple-element.163), channel_id=1, source_target_pairs={{0,3},{1,2},{2,1},{3,0},{4,7},{5,6},{6,5},{7,4},{8,11},{9,10},{10,... | collective-permute-start | bytes 196616 | tf_op jit(solution)/shard_map/ppermute | solution.py:600
  122.2 2.5 %collective-permute-done.43.refs_6_ = bf16[4,16,512]{2,1,0:T(8,128)(2,1)S(1)} collective-permute-done((bf16[4,16,512]{2,1,0:T(8,128)(2,1)S(1)}, bf16[4,16,512]{2,1,0:T(8,128)(2,1)S(1)}, u32[]{:S(2)}, u32[]{:S(2)}) %collective-permute-start.43) | collective-permute-done | bytes 65568 | tf_op jit(solution)/shard_map/ppermute | solution.py:600
  (92 shorter events, 39.6 us)
Async XLA Ops:
  1.5 11.9 %collective-permute-start.4 = (bf16[4,16,512]{2,1,0:T(8,128)(2,1)S(1)}, bf16[4,16,512]{2,1,0:T(8,128)(2,1)S(1)}, u32[]{:S(2)}, u32[]{:S(2)}) collective-permute-start(bf16[4,16,512]{2,1,0:T(8,128)(2,1)S(1)} %get-tuple-element.185), channel_id=1, source_target_pairs={{0,2},{1,3},{2,0},{3,1},{4,6},{5,7},{6,4},{7,5},{8,10},{9,11},{10,... | collective-permute-start | bytes 196616 | tf_op jit(solution)/shard_map/ppermute | solution.py:600
  13.4 13.4 %collective-permute-start.1 = (bf16[10,16,512]{2,1,0:T(8,128)(2,1)}, bf16[10,16,512]{2,1,0:T(8,128)(2,1)S(1)}, u32[]{:S(2)}, u32[]{:S(2)}) collective-permute-start(bf16[10,16,512]{2,1,0:T(8,128)(2,1)} %get-tuple-element.97), channel_id=1, source_target_pairs={{0,2},{1,3},{2,0},{3,1},{4,6},{5,7},{6,4},{7,5},{8,10},{9,11},{10,... | collective-permute-start | bytes 491528 | tf_op jit(solution)/shard_map/ppermute | solution.py:600
  13.4 13.4 %collective-permute-start = (bf16[10,16,512]{2,1,0:T(8,128)(2,1)}, bf16[10,16,512]{2,1,0:T(8,128)(2,1)S(1)}, u32[]{:S(2)}, u32[]{:S(2)}) collective-permute-start(bf16[10,16,512]{2,1,0:T(8,128)(2,1)} %get-tuple-element.97), channel_id=1, source_target_pairs={{0,1},{1,0},{2,3},{3,2},{4,5},{5,4},{6,7},{7,6},{8,9},{9,8},{10,11... | collective-permute-start | bytes 491528 | tf_op jit(solution)/shard_map/ppermute | solution.py:600
  14.1 13.7 %collective-permute-start.8 = (bf16[4,4,16,512]{3,2,1,0:T(8,128)(2,1)S(1)}, bf16[4,4,16,512]{3,2,1,0:T(8,128)(2,1)S(1)}, u32[]{:S(2)}, u32[]{:S(2)}) collective-permute-start(bf16[4,4,16,512]{3,2,1,0:T(8,128)(2,1)S(1)} %pad_maximum_fusion.1.refs_5_.refs_0_), channel_id=1, source_target_pairs={{0,24},{4,28},{8,16},{12,20},{16,8},{20,12},{24,0},{28,4},{1,25},{... | collective-permute-start | bytes 786440 | tf_op jit(solution)/shard_map/ppermute | solution.py:603
  16.8 11.0 %collective-permute-start.7 = (bf16[4,4,16,512]{3,2,1,0:T(8,128)(2,1)S(1)}, bf16[4,4,16,512]{3,2,1,0:T(8,128)(2,1)S(1)}, u32[]{:S(2)}, u32[]{:S(2)}) collective-permute-start(bf16[4,4,16,512]{3,2,1,0:T(8,128)(2,1)S(1)} %pad_maximum_fusion.1.refs_5_.refs_0_), channel_id=1, source_target_pairs={{0,16},{4,20},{8,24},{12,28},{16,0},{20,4},{24,8},{28,12},{1,17},{... | collective-permute-start | bytes 786440 | tf_op jit(solution)/shard_map/ppermute | solution.py:603
  27.8 18.8 %collective-permute-start.11 = (bf16[4,10,16,512]{3,2,1,0:T(8,128)(2,1)S(1)}, bf16[4,10,16,512]{3,2,1,0:T(8,128)(2,1)S(1)}, u32[]{:S(2)}, u32[]{:S(2)}) collective-permute-start(bf16[4,10,16,512]{3,2,1,0:T(8,128)(2,1)S(1)} %pad_maximum_fusion.refs_3_), channel_id=1, source_target_pairs={{0,16},{4,20},{8,24},{12,28},{16,0},{20,4},{24,8},{28,12},{1,17},{... | collective-permute-start | bytes 1966088 | tf_op jit(solution)/shard_map/ppermute | solution.py:603
  29.4 17.7 %collective-permute-start.9 = (bf16[4,10,16,512]{3,2,1,0:T(8,128)(2,1)S(1)}, bf16[4,10,16,512]{3,2,1,0:T(8,128)(2,1)S(1)}, u32[]{:S(2)}, u32[]{:S(2)}) collective-permute-start(bf16[4,10,16,512]{3,2,1,0:T(8,128)(2,1)S(1)} %pad_maximum_fusion.refs_3_), channel_id=1, source_target_pairs={{0,8},{4,12},{8,0},{12,4},{16,24},{20,28},{24,16},{28,20},{1,9},{5... | collective-permute-start | bytes 1966088 | tf_op jit(solution)/shard_map/ppermute | solution.py:603
  30.9 15.2 %collective-permute-start.13 = (bf16[256,512]{1,0:T(8,128)(2,1)}, bf16[256,512]{1,0:T(8,128)(2,1)S(1)}, u32[]{:S(2)}, u32[]{:S(2)}) collective-permute-start(bf16[256,512]{1,0:T(8,128)(2,1)} %get-tuple-element.102), channel_id=1, source_target_pairs={{0,1},{1,0},{2,3},{3,2},{4,5},{5,4},{6,7},{7,6},{8,9},{9,8},{10,11... | collective-permute-start | bytes 786440 | tf_op jit(solution)/shard_map/ppermute | solution.py:600
  47.2 9.7 %collective-permute-start.12 = (bf16[4,5,16,512]{3,2,1,0:T(8,128)(2,1)S(1)}, bf16[4,5,16,512]{3,2,1,0:T(8,128)(2,1)S(1)}, u32[]{:S(2)}, u32[]{:S(2)}) collective-permute-start(bf16[4,5,16,512]{3,2,1,0:T(8,128)(2,1)S(1)} %slice.21), channel_id=1, source_target_pairs={{0,8},{4,12},{8,0},{12,4},{16,24},{20,28},{24,16},{28,20},{1,9},{5... | collective-permute-start | bytes 983048 | tf_op jit(solution)/shard_map/ppermute | solution.py:603
  75.6 10.6 %collective-permute-start.28 = (bf16[4,5,16,512]{3,2,1,0:T(8,128)(2,1)S(1)}, bf16[4,5,16,512]{3,2,1,0:T(8,128)(2,1)S(1)}, u32[]{:S(2)}, u32[]{:S(2)}) collective-permute-start(bf16[4,5,16,512]{3,2,1,0:T(8,128)(2,1)S(1)} %get-tuple-element.121), channel_id=1, source_target_pairs={{0,8},{4,12},{8,0},{12,4},{16,24},{20,28},{24,16},{28,20},{1,9},{5... | collective-permute-start | bytes 983048 | tf_op jit(solution)/shard_map/ppermute | solution.py:603
  77.0 13.8 %collective-permute-start.29 = (bf16[4,5,16,512]{3,2,1,0:T(8,128)(2,1)S(1)}, bf16[4,5,16,512]{3,2,1,0:T(8,128)(2,1)S(1)}, u32[]{:S(2)}, u32[]{:S(2)}) collective-permute-start(bf16[4,5,16,512]{3,2,1,0:T(8,128)(2,1)S(1)} %get-tuple-element.122), channel_id=1, source_target_pairs={{0,16},{4,20},{8,24},{12,28},{16,0},{20,4},{24,8},{28,12},{1,17},{... | collective-permute-start | bytes 983048 | tf_op jit(solution)/shard_map/ppermute | solution.py:603
  77.5 14.9 %collective-permute-start.26 = (bf16[4,5,16,512]{3,2,1,0:T(8,128)(2,1)S(1)}, bf16[4,5,16,512]{3,2,1,0:T(8,128)(2,1)S(1)}, u32[]{:S(2)}, u32[]{:S(2)}) collective-permute-start(bf16[4,5,16,512]{3,2,1,0:T(8,128)(2,1)S(1)} %get-tuple-element.119), channel_id=1, source_target_pairs={{0,8},{4,12},{8,0},{12,4},{16,24},{20,28},{24,16},{28,20},{1,9},{5... | collective-permute-start | bytes 983048 | tf_op jit(solution)/shard_map/ppermute | solution.py:603
  78.2 15.5 %collective-permute-start.27 = (bf16[4,5,16,512]{3,2,1,0:T(8,128)(2,1)S(1)}, bf16[4,5,16,512]{3,2,1,0:T(8,128)(2,1)S(1)}, u32[]{:S(2)}, u32[]{:S(2)}) collective-permute-start(bf16[4,5,16,512]{3,2,1,0:T(8,128)(2,1)S(1)} %get-tuple-element.120), channel_id=1, source_target_pairs={{0,16},{4,20},{8,24},{12,28},{16,0},{20,4},{24,8},{28,12},{1,17},{... | collective-permute-start | bytes 983048 | tf_op jit(solution)/shard_map/ppermute | solution.py:603
  79.7 14.5 %collective-permute-start.34 = (bf16[128,512]{1,0:T(8,128)(2,1)S(1)}, bf16[128,512]{1,0:T(8,128)(2,1)S(1)}, u32[]{:S(2)}, u32[]{:S(2)}) collective-permute-start(bf16[128,512]{1,0:T(8,128)(2,1)S(1)} %get-tuple-element.145), channel_id=1, source_target_pairs={{0,2},{2,0},{3,1},{4,6},{6,4},{7,5},{8,10},{10,8},{11,9},{12,14},{... | collective-permute-start | bytes 393224 | tf_op jit(solution)/shard_map/ppermute | solution.py:600
  86.2 10.1 %collective-permute-start.35 = (bf16[128,512]{1,0:T(8,128)(2,1)S(1)}, bf16[128,512]{1,0:T(8,128)(2,1)S(1)}, u32[]{:S(2)}, u32[]{:S(2)}) collective-permute-start(bf16[128,512]{1,0:T(8,128)(2,1)S(1)} %get-tuple-element.146), channel_id=1, source_target_pairs={{0,3},{2,1},{3,0},{4,7},{6,5},{7,4},{8,11},{10,9},{11,8},{12,15},{... | collective-permute-start | bytes 393224 | tf_op jit(solution)/shard_map/ppermute | solution.py:600
  92.4 10.6 %collective-permute-start.31 = (bf16[4,5,16,512]{3,2,1,0:T(8,128)(2,1)S(1)}, bf16[4,5,16,512]{3,2,1,0:T(8,128)(2,1)S(1)}, u32[]{:S(2)}, u32[]{:S(2)}) collective-permute-start(bf16[4,5,16,512]{3,2,1,0:T(8,128)(2,1)S(1)} %get-tuple-element.142), channel_id=1, source_target_pairs={{0,8},{4,12},{8,0},{12,4},{16,24},{20,28},{24,16},{28,20},{1,9},{5... | collective-permute-start | bytes 983048 | tf_op jit(solution)/shard_map/ppermute | solution.py:603
  93.7 10.6 %collective-permute-start.32 = (bf16[4,5,16,512]{3,2,1,0:T(8,128)(2,1)S(1)}, bf16[4,5,16,512]{3,2,1,0:T(8,128)(2,1)S(1)}, u32[]{:S(2)}, u32[]{:S(2)}) collective-permute-start(bf16[4,5,16,512]{3,2,1,0:T(8,128)(2,1)S(1)} %get-tuple-element.143), channel_id=1, source_target_pairs={{0,16},{4,20},{8,24},{12,28},{16,0},{20,4},{24,8},{28,12},{1,17},{... | collective-permute-start | bytes 983048 | tf_op jit(solution)/shard_map/ppermute | solution.py:603
  94.2 14.4 %collective-permute-start.39 = (bf16[4,4,16,512]{3,2,1,0:T(8,128)(2,1)S(1)}, bf16[4,4,16,512]{3,2,1,0:T(8,128)(2,1)S(1)}, u32[]{:S(2)}, u32[]{:S(2)}) collective-permute-start(bf16[4,4,16,512]{3,2,1,0:T(8,128)(2,1)S(1)} %get-tuple-element.157), channel_id=1, source_target_pairs={{0,8},{4,12},{8,0},{12,4},{16,24},{20,28},{24,16},{28,20},{1,9},{5... | collective-permute-start | bytes 786440 | tf_op jit(solution)/shard_map/ppermute | solution.py:603
  96.3 17.3 %collective-permute-start.40 = (bf16[4,4,16,512]{3,2,1,0:T(8,128)(2,1)S(1)}, bf16[4,4,16,512]{3,2,1,0:T(8,128)(2,1)S(1)}, u32[]{:S(2)}, u32[]{:S(2)}) collective-permute-start(bf16[4,4,16,512]{3,2,1,0:T(8,128)(2,1)S(1)} %get-tuple-element.158), channel_id=1, source_target_pairs={{0,16},{4,20},{8,24},{12,28},{16,0},{20,4},{24,8},{28,12},{1,17},{... | collective-permute-start | bytes 786440 | tf_op jit(solution)/shard_map/ppermute | solution.py:603
  99.5 14.1 %collective-permute-start.41 = (bf16[4,4,16,512]{3,2,1,0:T(8,128)(2,1)S(1)}, bf16[4,4,16,512]{3,2,1,0:T(8,128)(2,1)S(1)}, u32[]{:S(2)}, u32[]{:S(2)}) collective-permute-start(bf16[4,4,16,512]{3,2,1,0:T(8,128)(2,1)S(1)} %get-tuple-element.159), channel_id=1, source_target_pairs={{0,24},{4,28},{8,16},{12,20},{16,8},{20,12},{24,0},{28,4},{1,25},{... | collective-permute-start | bytes 786440 | tf_op jit(solution)/shard_map/ppermute | solution.py:603
  104.7 20.1 %collective-permute-start.36 = (bf16[10,16,512]{2,1,0:T(8,128)(2,1)S(1)}, bf16[10,16,512]{2,1,0:T(8,128)(2,1)S(1)}, u32[]{:S(2)}, u32[]{:S(2)}) collective-permute-start(bf16[10,16,512]{2,1,0:T(8,128)(2,1)S(1)} %get-tuple-element.150), channel_id=1, source_target_pairs={{0,1},{1,0},{2,3},{3,2},{4,5},{5,4},{6,7},{7,6},{8,9},{9,8},{10,11... | collective-permute-start | bytes 491528 | tf_op jit(solution)/shard_map/ppermute | solution.py:600
  105.7 19.1 %collective-permute-start.37 = (bf16[10,16,512]{2,1,0:T(8,128)(2,1)S(1)}, bf16[10,16,512]{2,1,0:T(8,128)(2,1)S(1)}, u32[]{:S(2)}, u32[]{:S(2)}) collective-permute-start(bf16[10,16,512]{2,1,0:T(8,128)(2,1)S(1)} %get-tuple-element.151), channel_id=1, source_target_pairs={{0,2},{1,3},{2,0},{3,1},{4,6},{5,7},{6,4},{7,5},{8,10},{9,11},{10,... | collective-permute-start | bytes 491528 | tf_op jit(solution)/shard_map/ppermute | solution.py:600
  108.7 16.1 %collective-permute-start.38 = (bf16[10,16,512]{2,1,0:T(8,128)(2,1)S(1)}, bf16[10,16,512]{2,1,0:T(8,128)(2,1)S(1)}, u32[]{:S(2)}, u32[]{:S(2)}) collective-permute-start(bf16[10,16,512]{2,1,0:T(8,128)(2,1)S(1)} %get-tuple-element.152), channel_id=1, source_target_pairs={{0,3},{1,2},{2,1},{3,0},{4,7},{5,6},{6,5},{7,4},{8,11},{9,10},{10,... | collective-permute-start | bytes 491528 | tf_op jit(solution)/shard_map/ppermute | solution.py:600
  114.8 10.0 %collective-permute-start.43 = (bf16[4,16,512]{2,1,0:T(8,128)(2,1)S(1)}, bf16[4,16,512]{2,1,0:T(8,128)(2,1)S(1)}, u32[]{:S(2)}, u32[]{:S(2)}) collective-permute-start(bf16[4,16,512]{2,1,0:T(8,128)(2,1)S(1)} %get-tuple-element.162), channel_id=1, source_target_pairs={{0,2},{1,3},{2,0},{3,1},{4,6},{5,7},{6,4},{7,5},{8,10},{9,11},{10,... | collective-permute-start | bytes 196616 | tf_op jit(solution)/shard_map/ppermute | solution.py:600
  (26 other events, 337.4 us)
